TPU v7x, 32 devices: a whole 2x2x4 slice. The times are simulated.
32 devices in a mesh: grp: 2 (over x), seq: 8 (over z, y), ten: 2 (over core).
Axes of the slice: x: 2, y: 2, z: 4, core: 2. Of those that a mesh axis runs over, the one named last changes fastest.
Arguments:
- queries: bfloat16 [1024, 4096], P(('grp', 'seq'), 'ten'), parts along dimension 0, may hold values from -128 to 128
- keys: bfloat16 [1024, 512], P(('grp', 'seq'), 'ten'), parts along dimension 0, may hold values from -6 to 6
- values: bfloat16 [1024, 512], P(('grp', 'seq'), 'ten'), parts along dimension 0, may hold values from -6 to 6
- hidden: bfloat16 [1024, 8192], P(('grp', 'seq')), parts along dimension 0, may hold values from -6 to 6
- norm_gain: float32 [8192], replicated, may hold values from 0.1 to 1.9
- retained_lists: int32 [1024], P(('grp', 'seq')), parts along dimension 0, may hold values from -1 to 63, as said below
- counts: int32 [16], P('grp'), parts along dimension 0, may hold values from 0 to 64, as said below
- affine_matrix: bfloat16 [8192, 5120], P('seq', 'ten'), may hold values from -0.0625 to 0.0625
- affine_offset_vector: float32 [5120], P('ten'), may hold values from -3 to 3
Outputs:
- context: float32 [1024, 4096], P(('grp', 'seq'), 'ten'), parts along dimension 0
- col_scores: float32 [1024], P(('grp', 'seq')), parts along dimension 0
- tier_third_mapped_triples: float32 [512, 5120], P(('grp', 'seq'), 'ten'), parts along dimension 0
There are 2 independent parts, one for each index of `grp`. A program takes and returns all parts, laid end to end along the dimension named above; an argument that names none is the same for every part. Nothing has to cross between parts.
Inputs may be any that keep to these rules, and one draw needn't show every extreme that they name: `retained_lists`: entries s*64 to (s+1)*64 - 1 hold, in their first counts[s] places, the kept local rows of shard s in rising order, and -1 after them. counts sum to 256; some shard keeps all its 64 rows.
All inputs are finite; a program needn't handle non-finite values.
Results may differ from a plain program's by a relative error of at most 0.0027.
Values may be sent and summed in bfloat16 or wider, within the bound.
No kernel may reach another device: no remote copies, remote signals or barrier semaphores. Data moves between devices by JAX's collectives and lax.ppermute only.
A program may use at most 64 MiB of HBM per device.

v0:
```python
import math

import jax
import jax.numpy as jnp
from jax import lax
from jax.sharding import PartitionSpec as P

HEAD_SIZE = 128
QUERY_HEADS = 32


def block_length(key_count):
    return math.gcd(key_count, 512)


def heads_first(queries, kv_heads):
    partition_inner_lines = queries.shape[0]
    group_width = queries.shape[1] // (HEAD_SIZE * kv_heads)
    return (
        queries.reshape(partition_inner_lines, kv_heads, group_width, HEAD_SIZE)
        .transpose(1, 2, 0, 3)
        .reshape(kv_heads, group_width * partition_inner_lines, HEAD_SIZE)
    )


def masked_scores(query_heads, query_pos, key_block, offset):
    key_count = key_block.shape[0]
    kv_heads = query_heads.shape[0]
    key_head_rows = key_block.reshape(key_count, kv_heads, HEAD_SIZE)
    scores = jnp.einsum(
        "hrd,nhd->hrn", query_heads, key_head_rows, preferred_element_type=jnp.float32
    ) * HEAD_SIZE ** (-0.5)
    key_pos = offset + jnp.arange(key_count, dtype=jnp.int32)
    allowed = key_pos[None, None, :] <= query_pos[None, :, None]
    return (scores, allowed)


def attend(carried, pieces, query_heads, query_pos):
    key_piece, value_piece = pieces
    key_count = key_piece.shape[0]
    block_rows = block_length(key_count)
    block_total = key_count // block_rows
    kv_heads = query_heads.shape[0]
    key_blocks = key_piece.reshape(block_total, block_rows, key_piece.shape[1])
    value_blocks = value_piece.reshape(block_total, block_rows, value_piece.shape[1])

    def attend_step_block(state, inputs):
        row_max, row_sum, accumulated = state
        key_block, value_block, token_count = inputs
        scores, allowed = masked_scores(query_heads, query_pos, key_block, token_count * block_rows)
        new_max = jnp.maximum(row_max, jnp.max(jnp.where(allowed, scores, -1e30), axis=2))
        weights = jnp.where(allowed, jnp.exp(scores - new_max[:, :, None]), 0.0)
        factor = jnp.exp(row_max - new_max)
        row_sum = row_sum * factor + jnp.sum(weights, axis=2)
        value_head_rows = value_block.reshape(block_rows, kv_heads, HEAD_SIZE)
        update = jnp.einsum(
            "hrn,nhd->hrd",
            weights.astype(jnp.bfloat16),
            value_head_rows,
            preferred_element_type=jnp.float32,
        )
        accumulated = accumulated * factor[:, :, None] + update
        return ((new_max, row_sum, accumulated), None)

    state, unused = lax.scan(
        attend_step_block,
        carried,
        (key_blocks, value_blocks, jnp.arange(block_total, dtype=jnp.int32)),
    )
    return state


def column_terms(key_piece, query_heads, query_pos, log_total):
    key_count = key_piece.shape[0]
    block_rows = block_length(key_count)
    block_total = key_count // block_rows
    key_blocks = key_piece.reshape(block_total, block_rows, key_piece.shape[1])

    def column_step_block(state, inputs):
        key_block, token_count = inputs
        scores, allowed = masked_scores(query_heads, query_pos, key_block, token_count * block_rows)
        weights = jnp.where(allowed, jnp.exp(scores - log_total[:, :, None]), 0.0)
        return (state, jnp.sum(weights, axis=(0, 1)))

    unused, sums = lax.scan(
        column_step_block, jnp.float32(0.0), (key_blocks, jnp.arange(block_total, dtype=jnp.int32))
    )
    return sums.reshape(key_count)


def shards(
    queries,
    keys,
    values,
    hidden,
    norm_gain,
    retained_lists,
    counts,
    affine_matrix,
    affine_offset_vector,
):
    partition_inner_lines = queries.shape[0]
    kv_heads = keys.shape[1] // HEAD_SIZE
    group_width = queries.shape[1] // keys.shape[1]
    seq_index = lax.axis_index("seq")
    query_heads = heads_first(queries, kv_heads)
    query_pos = seq_index * partition_inner_lines + jnp.tile(
        jnp.arange(partition_inner_lines, dtype=jnp.int32), group_width
    )
    packed_rows = group_width * partition_inner_lines
    initial = (
        jnp.full((kv_heads, packed_rows), -1e30, jnp.float32),
        jnp.zeros((kv_heads, packed_rows), jnp.float32),
        jnp.zeros((kv_heads, packed_rows, HEAD_SIZE), jnp.float32),
    )
    row_max, row_sum, accumulated = attend(
        initial,
        (
            lax.all_gather(keys, "seq", axis=0, tiled=True),
            lax.all_gather(values, "seq", axis=0, tiled=True),
        ),
        query_heads,
        query_pos,
    )
    log_total = row_max + jnp.log(row_sum)
    column_part = column_terms(
        lax.all_gather(keys, "seq", axis=0, tiled=True), query_heads, query_pos, log_total
    )
    context = (
        (accumulated / row_sum[:, :, None])
        .reshape(kv_heads, group_width, partition_inner_lines, HEAD_SIZE)
        .transpose(2, 0, 1, 3)
        .reshape(partition_inner_lines, queries.shape[1])
    )
    column_rows = lax.psum_scatter(column_part, "seq", scatter_dimension=0, tiled=True)
    col_scores = lax.psum(column_rows, "ten") / QUERY_HEADS
    hidden_f = hidden.astype(jnp.float32)
    rescaled_activations = (
        hidden_f
        * lax.rsqrt(jnp.mean(hidden_f * hidden_f, axis=1, keepdims=True) + 1e-06)
        * norm_gain
    ).astype(jnp.bfloat16)
    selector = (
        retained_lists[:, None] == jnp.arange(partition_inner_lines, dtype=jnp.int32)[None, :]
    ).astype(jnp.bfloat16)
    chosen = jnp.dot(selector, rescaled_activations, preferred_element_type=jnp.float32).astype(
        jnp.bfloat16
    )
    sequence_total = lax.axis_size("seq")
    retained_total = sequence_total * partition_inner_lines // 2
    retained_element = jnp.arange(retained_total, dtype=jnp.int32)
    partition_finish_marks = jnp.cumsum(counts)
    holder_partition = jnp.sum(
        (partition_finish_marks[None, :] <= retained_element[:, None]).astype(jnp.int32), axis=1
    )
    starts = partition_finish_marks - counts
    opening_marks = jnp.sum(
        jnp.where(
            jnp.arange(sequence_total, dtype=jnp.int32)[None, :] == holder_partition[:, None],
            starts[None, :],
            0,
        ),
        axis=1,
    )
    retained_place_number = retained_element - opening_marks
    received = lax.all_to_all(chosen, "seq", split_axis=1, concat_axis=0, tiled=True)
    provenance = holder_partition * partition_inner_lines + retained_place_number
    compact = jnp.take(received, provenance, axis=0)
    projected = lax.psum_scatter(
        jnp.dot(compact, affine_matrix, preferred_element_type=jnp.float32),
        "seq",
        scatter_dimension=0,
        tiled=True,
    )
    tier_third_mapped_triples = projected + affine_offset_vector
    return (context, col_scores, tier_third_mapped_triples)


def solution(mesh):
    in_specs = (
        P(("grp", "seq"), "ten"),
        P(("grp", "seq"), "ten"),
        P(("grp", "seq"), "ten"),
        P(("grp", "seq"), None),
        P(),
        P(("grp", "seq")),
        P("grp"),
        P("seq", "ten"),
        P("ten"),
    )
    out_specs = (P(("grp", "seq"), "ten"), P(("grp", "seq")), P(("grp", "seq"), "ten"))
    return jax.shard_map(shards, mesh=mesh, in_specs=in_specs, out_specs=out_specs, check_vma=False)
```

profile of v0, /device:TPU:0, one launch (start us, length us, event | category | flops | bytes accessed | tf_op | source)
XLA Modules:
  0.0 151.9 jit_solution(15588536419003187684)
XLA Ops:
  7.2 1.5 %fusion = f32[64]{0:T(128)S(1)} fusion(bf16[64,8192]{1,0:T(8,128)(2,1)} %param.12), kind=kLoop, calls=%fused_computation.4 | loop fusion | flops 1572800 | bytes 1048832 | tf_op jit(solution)/shard_map/reduce_sum | solution.py:140
  8.7 1.7 %convolution_convert_fusion = bf16[64,8192]{1,0:T(8,128)(2,1)S(1)} fusion(bf16[64,8192]{1,0:T(8,128)(2,1)} %param.12, f32[8192]{0:T(1024)} %param.13, f32[64]{0:T(128)S(1)} %add_rsqrt_fusion, s32[64]{0:T(128)} %param.14), kind=kOutput, calls=%fused_computation.1 | convolution fusion | flops 69734400 | bytes 2130432 | tf_op jit(solution)/shard_map/dot_general | solution.py:146
  10.5 0.0 copy-start.4
  10.5 1.1 copy.48
  11.6 7.3 %all-to-all-start = ((bf16[64,8,1024]{2,0,1:T(8,128)(2,1)}), bf16[64,8,1024]{2,0,1:T(8,128)(2,1)S(1)}, u32[]{:S(2)}, u32[]{:S(2)}) async-start(bf16[64,8,1024]{2,0,1:T(8,128)(2,1)} %bitcast.32), calls=%async_computation | async-start | bytes 2097152 | tf_op jit(solution)/shard_map/all_to_all | solution.py:166
  18.8 0.0 reduce-scatter.2.cloned.1.call-start
  18.9 0.0 copy-done.4
  18.9 0.2 reduce-window.8
  19.1 0.1 convert_reduce_fusion
  19.2 0.1 select_reduce_fusion.2
  19.3 25.3 %all-to-all-done = bf16[64,8,1024]{2,0,1:T(8,128)(2,1)S(1)} async-done(((bf16[64,8,1024]{2,0,1:T(8,128)(2,1)}), bf16[64,8,1024]{2,0,1:T(8,128)(2,1)S(1)}, u32[]{:S(2)}, u32[]{:S(2)}) %all-to-all-start) | async-done | bytes 1048608 | tf_op jit(solution)/shard_map/all_to_all | solution.py:166
  44.6 1.2 gather_fusion
  45.8 5.6 %fusion.14 = f32[256,2560]{1,0:T(8,128)} fusion(bf16[1024,2560]{1,0:T(8,128)(2,1)} %param.16, bf16[256,1024]{1,0:T(8,128)(2,1)S(1)} %gather_fusion, pred[256]{0:T(512)(128)(4,1)S(1)} %compare_and_fusion), kind=kOutput, calls=%fused_computation.23 | convolution fusion | flops 1342439424 | bytes 8388864 | tf_op jit(solution)/shard_map/dot_general | solution.py:170
  51.3 0.0 copy-start
  51.3 0.0 copy-start.1
  51.3 0.0 copy-start.2
  51.3 0.0 reduce-scatter.2.cloned.1.call-update
  51.4 0.1 add.110
  51.5 0.8 copy-done
  52.3 0.1 copy.32
  52.4 0.0 copy-done.1
  52.4 31.5 %all_gather.7 = bf16[512,256]{1,0:T(8,128)(2,1)S(1)} all-gather(bf16[64,256]{1,0:T(8,128)(2,1)S(1)} %copy-done.1), channel_id=1, replica_groups=mesh['grp'=2,'seq'=8,'ten'=2] {'seq'}, dimensions={0}, use_global_device_ids=true | all-gather | bytes 294912 | tf_op jit(solution)/shard_map/all_gather | solution.py:119
  83.9 0.1 copy.33
  84.1 0.0 copy-done.2
  84.1 31.4 %all_gather.8 = bf16[512,256]{1,0:T(8,128)(2,1)S(1)} all-gather(bf16[64,256]{1,0:T(8,128)(2,1)S(1)} %copy-done.2), channel_id=1, replica_groups=mesh['grp'=2,'seq'=8,'ten'=2] {'seq'}, dimensions={0}, use_global_device_ids=true | all-gather | bytes 294912 | tf_op jit(solution)/shard_map/all_gather | solution.py:120
  115.5 0.1 copy.35
  115.6 0.2 iota_compare_fusion
  115.8 0.6 select_reduce_fusion.1
  116.5 0.5 fusion.3
  117.0 0.9 fusion.5
  117.9 0.0 copy-start.5
  118.0 0.0 copy-start.3
  118.0 0.3 copy.38
  118.3 1.0 copy.49
  119.2 0.0 copy-done.5
  119.2 0.6 dynamic-slice.2
  120.5 0.6 select_reduce_fusion
  121.0 19.2 %all-reduce = f32[512]{0:T(512)S(1)} all-reduce(f32[512]{0:T(512)S(1)} %select_reduce_fusion), channel_id=2, replica_groups=mesh['grp'=2,'seq'=8,'ten'=2] {'seq'}, use_global_device_ids=true, to_apply=%region_3.4.clone | all-reduce | flops 512 | bytes 4096
  140.2 0.1 dynamic-slice.3
  140.3 2.4 %psum.7 = f32[64]{0:T(128)S(1)} all-reduce(f32[64]{0:T(128)S(1)} %dynamic-slice.3), channel_id=1, replica_groups=mesh['grp'=2,'seq'=8,'ten'=2] {'ten'}, use_global_device_ids=true, to_apply=%region_4.5 | all-reduce | flops 64 | bytes 512 | tf_op jit(solution)/shard_map/psum | solution.py:136
  142.8 0.5 broadcast_multiply_fusion.1
  143.3 0.0 reduce-scatter.2.cloned.1.call-done
  143.3 0.0 copy-done.3
  143.3 1.7 %broadcast_add_fusion = f32[32,2560]{1,0:T(8,128)} fusion(f32[32,2560]{1,0:T(8,128)} %reduce-scatter.2.cloned.1.call-done, f32[2560]{0:T(1024)S(1)} %copy-done.3), kind=kLoop, calls=%fused_computation.27 | loop fusion | flops 81920 | bytes 665600 | tf_op jit(solution)/shard_map/add | solution.py:175
  (10 shorter events, 0.1 us)
Async XLA Ops:
  10.5 8.4 %copy-start.4 = (s32[8]{0:T(128)S(1)}, s32[8]{0:T(128)}, u32[]{:S(2)}) copy-start(s32[8]{0:T(128)} %param.15) | copy-start | bytes 100
  11.6 33.0 %all-to-all-start = ((bf16[64,8,1024]{2,0,1:T(8,128)(2,1)}), bf16[64,8,1024]{2,0,1:T(8,128)(2,1)S(1)}, u32[]{:S(2)}, u32[]{:S(2)}) async-start(bf16[64,8,1024]{2,0,1:T(8,128)(2,1)} %bitcast.32), calls=%async_computation | async-start | bytes 2097152 | tf_op jit(solution)/shard_map/all_to_all | solution.py:166
  18.8 124.5 %reduce-scatter.2.cloned.1.call-start = ((), (), s32[]{:S(2)}) async-start(), calls=%async_computation.2 | async-start | bytes 2949120 | tf_op jit(solution)/shard_map/reduce_scatter | solution.py:169
  51.3 0.9 copy-start
  51.3 1.1 copy-start.1
  51.3 32.8 %copy-start.2 = (bf16[64,256]{1,0:T(8,128)(2,1)S(1)}, bf16[64,256]{1,0:T(8,128)(2,1)}, u32[]{:S(2)}) copy-start(bf16[64,256]{1,0:T(8,128)(2,1)} %param.11) | copy-start | bytes 98308
  117.9 1.3 copy-start.5
  118.0 25.3 %copy-start.3 = (f32[2560]{0:T(1024)S(1)}, f32[2560]{0:T(1024)}, u32[]{:S(2)}) copy-start(f32[2560]{0:T(1024)} %param.17) | copy-start | bytes 30724
Sparse Core Ops, SparseCore 0:
  51.5 70.7 reduce-scatter.1
where the time goes:
time: 152 us
  blocking collectives  84.6 us (56%)
  waiting for transfers between devices  25.3 us (17%)
  between operations  14.8 us (10%)
  matrix products  8.9 us (6%)
  starting transfers between devices  7.31 us (5%)
  local copies, waits for them, and re-layouts  5.49 us (4%)
  other arithmetic  5.4 us (4%)
    all_gather x1, blocking collectives, shards(): lax.all_gather(keys, 'seq', axis=0, tiled=True)  31.5 us
    all_gather x1, blocking collectives, shards(): lax.all_gather(values, 'seq', axis=0, tiled=True)  31.4 us
    all_to_all x1, waiting for transfers between devices, shards(): lax.all_to_all(chosen, 'seq', split_axis=1, concat_axis=0, tiled=True)  25.3 us
    unnamed x1, blocking collectives  19.2 us
    all_to_all x1, starting transfers between devices, shards(): lax.all_to_all(chosen, 'seq', split_axis=1, concat_axis=0, tiled=True)  7.27 us
    dot_general x1, matrix products, shards(): jnp.dot(compact, affine_matrix, preferred_element_type=jnp.float32)  5.57 us
  transfers between devices with their start and end apart: 2, of which 1 were waited for; matrix products, arithmetic and copies ran while one was open for 4% of the time, Pallas kernels for 0%

commit v1 on v0

v1 whole, which is shorter than its diff:
```python
import functools

import jax
import jax.numpy as jnp
from jax import lax
from jax.experimental import pallas as pl
from jax.experimental.pallas import tpu as pltpu
from jax.sharding import PartitionSpec as P

HEAD_SIZE = 128
QUERY_HEADS = 32
VMEM = pl.BlockSpec(memory_space=pltpu.VMEM)
SMEM = pl.BlockSpec(memory_space=pltpu.SMEM)
PARAMS = pltpu.CompilerParams(vmem_limit_bytes=48 * 1024 * 1024)


def norm_select_kernel(n, place, hidden, gain, kept, *outs):
    rows, width = hidden.shape
    block = width // n
    half = block // 2
    s, t = place[0], place[1]
    total = jnp.zeros((rows, block), jnp.float32)
    for i in range(n):
        part = hidden[:, i * block : (i + 1) * block].astype(jnp.float32)
        total += part * part
    scale = lax.rsqrt(jnp.sum(total, axis=1, keepdims=True) / width + 1e-06)
    selector = (kept[...] == lax.broadcasted_iota(jnp.int32, (rows, rows), 0)).astype(jnp.bfloat16)
    for k in range(n):
        start = pl.multiple_of(lax.rem(s + k, n) * block + t * half, half)
        columns = pl.ds(start, half)
        normed = (hidden[:, columns].astype(jnp.float32) * scale * gain[:, columns]).astype(jnp.bfloat16)
        outs[k][...] = lax.dot_general(
            selector, normed, (((0,), (0,)), ((), ())), preferred_element_type=jnp.float32
        ).astype(jnp.bfloat16)


def attention_kernel(n, kv_heads, place, queries, *refs):
    blocks, (context, columns) = refs[:n], refs[n:]
    rows = queries.shape[0]
    group = queries.shape[1] // (HEAD_SIZE * kv_heads)
    s = place[0]
    keys_total = n * rows
    row = lax.broadcasted_iota(jnp.int32, (rows, keys_total), 0)
    column = lax.broadcasted_iota(jnp.int32, (rows, keys_total), 1)
    diagonal = (column <= row) & (column < rows)
    earlier = (column >= rows) & (column < (s + 1) * rows)
    allowed = diagonal | earlier
    sums = jnp.zeros((1, keys_total), jnp.float32)
    for g in range(kv_heads):
        key = jnp.concatenate([b[:, g * HEAD_SIZE : (g + 1) * HEAD_SIZE] for b in blocks], axis=0)
        first = (kv_heads + g) * HEAD_SIZE
        value = jnp.concatenate([b[:, first : first + HEAD_SIZE] for b in blocks], axis=0)
        for h in range(g * group, (g + 1) * group):
            lanes = slice(h * HEAD_SIZE, (h + 1) * HEAD_SIZE)
            scores = lax.dot_general(
                queries[:, lanes], key, (((1,), (1,)), ((), ())), preferred_element_type=jnp.float32
            ) * HEAD_SIZE ** (-0.5)
            scores = jnp.where(allowed, scores, -1e30)
            row_max = jnp.max(scores, axis=1, keepdims=True)
            weights = jnp.where(allowed, jnp.exp(scores - row_max), 0.0)
            inverse = 1.0 / jnp.sum(weights, axis=1, keepdims=True)
            mixed = jnp.dot(weights.astype(jnp.bfloat16), value, preferred_element_type=jnp.float32)
            context[:, lanes] = mixed * inverse
            sums += jnp.sum(weights * inverse, axis=0, keepdims=True)
    columns[...] = sums


def compact_kernel(n, place, counts, *refs):
    blocks, out = refs[:n], refs[n]
    rows = blocks[0].shape[0]
    survivors = out.shape[0]
    s = place[0]
    slot_all = lax.broadcasted_iota(jnp.int32, (1, n * rows), 1)
    target = jnp.full((1, n * rows), -1, jnp.int32)
    for k in range(n):
        source = lax.rem(s - k + n, n)
        begin = jnp.int32(0)
        for i in range(n):
            begin += jnp.where(i < source, counts[i], 0)
        slot = slot_all - k * rows
        inside = (slot >= 0) & (slot < counts[source])
        target = jnp.where(inside, begin + slot, target)
    survivor = lax.broadcasted_iota(jnp.int32, (survivors, n * rows), 0) + s * (survivors // n)
    survivor = jnp.where(survivor >= survivors, survivor - survivors, survivor)
    pick = (survivor == target).astype(jnp.float32).astype(jnp.bfloat16)
    received = jnp.concatenate([b[...] for b in blocks], axis=0)
    out[...] = jnp.dot(pick, received, preferred_element_type=jnp.float32).astype(jnp.bfloat16)


def project_kernel(n, place, own, other, matrix, columns, columns_other, own_part, own_columns, *sent):
    outs = (None,) + sent
    t = place[1]
    survivors, half = own.shape
    width = matrix.shape[1]
    lines = survivors // n
    rows = columns.shape[1] // n
    first = t == 0
    low = jnp.where(first, own[...], other[...])
    high = jnp.where(first, other[...], own[...])
    features = jnp.concatenate([low, high], axis=1)
    tile = width // 5 if width % 640 == 0 else width
    for c in range(width // tile):
        lanes = slice(c * tile, (c + 1) * tile)
        part = jnp.dot(features, matrix[:, lanes], preferred_element_type=jnp.float32)
        own_part[:, lanes] = part[:lines]
        for k in range(1, n):
            outs[k][:, lanes] = part[k * lines : (k + 1) * lines].astype(jnp.bfloat16)
    total = columns[...] + columns_other[...]
    own_columns[...] = total[:, :rows]
    for k in range(1, n):
        j = n - k
        piece = total[:, j * rows : (j + 1) * rows]
        head = piece.astype(jnp.bfloat16)
        tail = (piece - head.astype(jnp.float32)).astype(jnp.bfloat16)
        outs[k][:, width : width + rows] = jnp.broadcast_to(head, (lines, rows))
        outs[k][:, width + rows :] = jnp.broadcast_to(tail, (lines, rows))


def finish_kernel(n, own, own_columns, bias, *refs):
    received, (out, scores) = refs[: n - 1], refs[n - 1 :]
    width = own.shape[1]
    rows = own_columns.shape[1]
    total = own[...]
    sums = own_columns[...]
    for r in received:
        total += r[:, :width].astype(jnp.float32)
        extra = r[:16, width:].astype(jnp.float32)
        sums += extra[:1, :rows] + extra[:1, rows:]
    out[...] = total + bias[...]
    scores[...] = sums / QUERY_HEADS


def shards(queries, keys, values, hidden, norm_gain, retained_lists, counts, affine_matrix, affine_offset_vector):
    n = lax.axis_size("seq")
    rows, model = hidden.shape
    kv_heads = keys.shape[1] // HEAD_SIZE
    half = affine_matrix.shape[0] // 2
    width = affine_matrix.shape[1]
    survivors = n * rows // 2
    lines = survivors // n
    s, t = lax.axis_index("seq"), lax.axis_index("ten")
    place = jnp.stack([s, t]).astype(jnp.int32)
    f32, bf16 = jnp.float32, jnp.bfloat16
    shape = jax.ShapeDtypeStruct

    def shift(x, k):
        return lax.ppermute(x, "seq", [(i, (i + k) % n) for i in range(n)])

    def swap(x):
        return lax.ppermute(x, "ten", [(0, 1), (1, 0)])

    pair = jnp.concatenate([keys, values], axis=1)
    pairs = [pair] + [shift(pair, k) for k in range(1, n)]

    chosen = pl.pallas_call(
        functools.partial(norm_select_kernel, n),
        out_shape=[shape((rows, half), bf16)] * n,
        in_specs=[SMEM, VMEM, VMEM, VMEM],
        out_specs=[VMEM] * n,
        compiler_params=PARAMS,
        cost_estimate=pl.CostEstimate(flops=4 * rows * model, bytes_accessed=3 * rows * model, transcendentals=0),
        name="norm_select",
    )(place, hidden, norm_gain.reshape(1, model), retained_lists.reshape(1, rows))
    received = [chosen[0]] + [shift(chosen[k], k) for k in range(1, n)]

    context, columns = pl.pallas_call(
        functools.partial(attention_kernel, n, kv_heads),
        out_shape=[shape(queries.shape, f32), shape((1, n * rows), f32)],
        in_specs=[SMEM, VMEM] + [VMEM] * n,
        out_specs=[VMEM] * 2,
        compiler_params=PARAMS,
        cost_estimate=pl.CostEstimate(
            flops=4 * rows * n * rows * queries.shape[1], bytes_accessed=6 * rows * queries.shape[1], transcendentals=0
        ),
        name="attention",
    )(place, queries, *pairs)
    columns_other = swap(columns)

    own = pl.pallas_call(
        functools.partial(compact_kernel, n),
        out_shape=shape((survivors, half), bf16),
        in_specs=[SMEM, SMEM] + [VMEM] * n,
        out_specs=VMEM,
        compiler_params=PARAMS,
        cost_estimate=pl.CostEstimate(flops=2 * survivors * n * rows * half, bytes_accessed=4 * n * rows * half, transcendentals=0),
        name="compact",
    )(place, counts, *received)
    other = swap(own)

    own_part, own_columns, *partial_sums = pl.pallas_call(
        functools.partial(project_kernel, n),
        out_shape=[shape((lines, width), f32), shape((1, rows), f32)]
        + [shape((lines, width + 2 * rows), bf16)] * (n - 1),
        in_specs=[SMEM] + [VMEM] * 5,
        out_specs=[VMEM] * (n + 1),
        compiler_params=PARAMS,
        cost_estimate=pl.CostEstimate(
            flops=4 * survivors * half * width, bytes_accessed=4 * half * width + 2 * survivors * width, transcendentals=0
        ),
        name="project",
    )(place, own, other, affine_matrix, columns, columns_other)
    arrived = [shift(partial_sums[k - 1], k) for k in range(1, n)]

    triples, scores = pl.pallas_call(
        functools.partial(finish_kernel, n),
        out_shape=[shape((lines, width), f32), shape((1, rows), f32)],
        in_specs=[VMEM] * (n + 2),
        out_specs=[VMEM] * 2,
        compiler_params=PARAMS,
        cost_estimate=pl.CostEstimate(flops=n * lines * width, bytes_accessed=2 * n * lines * width, transcendentals=0),
        name="finish",
    )(own_part, own_columns, affine_offset_vector.reshape(1, width), *arrived)
    return (context, scores.reshape(rows), triples)


def solution(mesh):
    in_specs = (
        P(("grp", "seq"), "ten"),
        P(("grp", "seq"), "ten"),
        P(("grp", "seq"), "ten"),
        P(("grp", "seq"), None),
        P(),
        P(("grp", "seq")),
        P("grp"),
        P("seq", "ten"),
        P("ten"),
    )
    out_specs = (P(("grp", "seq"), "ten"), P(("grp", "seq")), P(("grp", "seq"), "ten"))
    return jax.shard_map(shards, mesh=mesh, in_specs=in_specs, out_specs=out_specs, check_vma=False)
```

time: 152 us -> 87.5 us (0.58)
  the two profiles are of different devices: /device:TPU:0 before, /device:TPU:13 now
where the time goes in v1:
time: 87.5 us; the launch traced here: 87 us
  waiting for transfers between devices  39.5 us (45%)
  starting transfers between devices  28.3 us (32%)
  Pallas kernels  12.6 us (14%)
  local copies, waits for them, and re-layouts  5.77 us (7%)
    ppermute x21, waiting for transfers between devices, shift(): return lax.ppermute(x, 'seq', [(i, (i + k) % n) for i in range(n)])  38.7 us
    ppermute x21, starting transfers between devices, shift(): return lax.ppermute(x, 'seq', [(i, (i + k) % n) for i in range(n)])  25.4 us
    pallas_call x1, Pallas kernels, shards(): pl.pallas_call(functools.partial(attention_kernel, n, kv_heads), out_shap...  5.63 us
    unnamed x13, local copies, waits for them, and re-layouts  5.01 us
    pallas_call x1, Pallas kernels, shards(): pl.pallas_call(functools.partial(project_kernel, n), out_shape=[shape((li...  4.01 us
    ppermute x2, starting transfers between devices, swap(): return lax.ppermute(x, 'ten', [(0, 1), (1, 0)])  2.9 us
  transfers between devices with their start and end apart: 23, of which 11 were waited for; matrix products, arithmetic and copies ran while one was open for 2% of the time, Pallas kernels for 6%

profile of v1, /device:TPU:13, one launch (start us, length us, event | category | flops | bytes accessed | tf_op | source)
XLA Modules:
  0.0 87.0 jit_solution(17800521085657915397)
XLA Ops:
  0.6 0.1 pad_add_fusion.place
  0.7 1.2 %copy-done = bf16[64,8192]{1,0:T(8,128)(2,1)S(1)} copy-done((bf16[64,8192]{1,0:T(8,128)(2,1)S(1)}, bf16[64,8192]{1,0:T(8,128)(2,1)}, u32[]{:S(2)}) %copy-start) | copy-done | bytes 1048600
  1.9 0.8 copy-done.1
  2.7 0.7 copy-done.2
  3.4 1.1 %norm_select.1 = (bf16[64,512]{1,0:T(8,128)(2,1)S(1)}, bf16[64,512]{1,0:T(8,128)(2,1)S(1)}, bf16[64,512]{1,0:T(8,128)(2,1)S(1)}, bf16[64,512]{1,0:T(8,128)(2,1)S...) custom-call(s32[2]{0:T(128)S(1)} %pad_add_fusion.place, ...), custom_call_target="tpu_custom_call" | custom-call | flops 2097152 | bytes 1572864 | tf_op jit(solution)/shard_map/norm_select/pallas_call | solution.py:155
  4.5 1.3 %collective-permute-start.7 = (bf16[64,512]{1,0:T(8,128)(2,1)S(1)}, bf16[64,512]{1,0:T(8,128)(2,1)S(1)}, u32[]{:S(2)}, u32[]{:S(2)}) collective-permute-start(bf16[64,512]{1,0:T(8,128)(2,1)S(1)} %get-tuple-element.26), channel_id=1, source_target_pairs={{0,2},{2,4},{4,6},{6,8},{8,10},{10,12},{12,14},{14,0},{1,3},{3,5},... | collective-permute-start | bytes 196616 | tf_op jit(solution)/shard_map/ppermute | solution.py:147
  5.8 1.3 %collective-permute-start.8 = (bf16[64,512]{1,0:T(8,128)(2,1)S(1)}, bf16[64,512]{1,0:T(8,128)(2,1)S(1)}, u32[]{:S(2)}, u32[]{:S(2)}) collective-permute-start(bf16[64,512]{1,0:T(8,128)(2,1)S(1)} %get-tuple-element.27), channel_id=1, source_target_pairs={{0,4},{2,6},{4,8},{6,10},{8,12},{10,14},{12,0},{14,2},{1,5},{3,7},... | collective-permute-start | bytes 196616 | tf_op jit(solution)/shard_map/ppermute | solution.py:147
  7.1 1.0 %collective-permute-start.9 = (bf16[64,512]{1,0:T(8,128)(2,1)S(1)}, bf16[64,512]{1,0:T(8,128)(2,1)S(1)}, u32[]{:S(2)}, u32[]{:S(2)}) collective-permute-start(bf16[64,512]{1,0:T(8,128)(2,1)S(1)} %get-tuple-element.28), channel_id=1, source_target_pairs={{0,6},{2,8},{4,10},{6,12},{8,14},{10,0},{12,2},{14,4},{1,7},{3,9},... | collective-permute-start | bytes 196616 | tf_op jit(solution)/shard_map/ppermute | solution.py:147
  8.0 1.4 %collective-permute-start.10 = (bf16[64,512]{1,0:T(8,128)(2,1)S(1)}, bf16[64,512]{1,0:T(8,128)(2,1)S(1)}, u32[]{:S(2)}, u32[]{:S(2)}) collective-permute-start(bf16[64,512]{1,0:T(8,128)(2,1)S(1)} %get-tuple-element.29), channel_id=1, source_target_pairs={{0,8},{2,10},{4,12},{6,14},{8,0},{10,2},{12,4},{14,6},{1,9},{3,11}... | collective-permute-start | bytes 196616 | tf_op jit(solution)/shard_map/ppermute | solution.py:147
  9.4 1.0 %collective-permute-start.11 = (bf16[64,512]{1,0:T(8,128)(2,1)S(1)}, bf16[64,512]{1,0:T(8,128)(2,1)S(1)}, u32[]{:S(2)}, u32[]{:S(2)}) collective-permute-start(bf16[64,512]{1,0:T(8,128)(2,1)S(1)} %get-tuple-element.30), channel_id=1, source_target_pairs={{0,10},{2,12},{4,14},{6,0},{8,2},{10,4},{12,6},{14,8},{1,11},{3,13... | collective-permute-start | bytes 196616 | tf_op jit(solution)/shard_map/ppermute | solution.py:147
  10.4 1.2 %collective-permute-start.12 = (bf16[64,512]{1,0:T(8,128)(2,1)S(1)}, bf16[64,512]{1,0:T(8,128)(2,1)S(1)}, u32[]{:S(2)}, u32[]{:S(2)}) collective-permute-start(bf16[64,512]{1,0:T(8,128)(2,1)S(1)} %get-tuple-element.31), channel_id=1, source_target_pairs={{0,12},{2,14},{4,0},{6,2},{8,4},{10,6},{12,8},{14,10},{1,13},{3,15... | collective-permute-start | bytes 196616 | tf_op jit(solution)/shard_map/ppermute | solution.py:147
  11.6 0.0 collective-permute-done.8.refs_2_
  11.6 1.4 %collective-permute-start.13 = (bf16[64,512]{1,0:T(8,128)(2,1)S(1)}, bf16[64,512]{1,0:T(8,128)(2,1)S(1)}, u32[]{:S(2)}, u32[]{:S(2)}) collective-permute-start(bf16[64,512]{1,0:T(8,128)(2,1)S(1)} %get-tuple-element.32), channel_id=1, source_target_pairs={{0,14},{2,0},{4,2},{6,4},{8,6},{10,8},{12,10},{14,12},{1,15},{3,1}... | collective-permute-start | bytes 196616 | tf_op jit(solution)/shard_map/ppermute | solution.py:147
  13.0 0.8 constant_dynamic-update-slice_fusion.1
  13.8 0.0 collective-permute-done.9.refs_3_
  13.8 3.1 %collective-permute-done.10.refs_4_ = bf16[64,512]{1,0:T(8,128)(2,1)S(1)} collective-permute-done((bf16[64,512]{1,0:T(8,128)(2,1)S(1)}, bf16[64,512]{1,0:T(8,128)(2,1)S(1)}, u32[]{:S(2)}, u32[]{:S(2)}) %collective-permute-start.10) | collective-permute-done | bytes 65568 | tf_op jit(solution)/shard_map/ppermute | solution.py:147
  16.9 2.4 %collective-permute-done.12.refs_6_ = bf16[64,512]{1,0:T(8,128)(2,1)S(1)} collective-permute-done((bf16[64,512]{1,0:T(8,128)(2,1)S(1)}, bf16[64,512]{1,0:T(8,128)(2,1)S(1)}, u32[]{:S(2)}, u32[]{:S(2)}) %collective-permute-start.12) | collective-permute-done | bytes 65568 | tf_op jit(solution)/shard_map/ppermute | solution.py:147
  19.2 1.8 %collective-permute-done.13.refs_7_ = bf16[64,512]{1,0:T(8,128)(2,1)S(1)} collective-permute-done((bf16[64,512]{1,0:T(8,128)(2,1)S(1)}, bf16[64,512]{1,0:T(8,128)(2,1)S(1)}, u32[]{:S(2)}, u32[]{:S(2)}) %collective-permute-start.13) | collective-permute-done | bytes 65568 | tf_op jit(solution)/shard_map/ppermute | solution.py:147
  21.0 0.7 copy-done.3
  21.6 0.9 compact.1.own
  22.5 0.8 collective-permute-start.14
  23.3 0.8 constant_dynamic-update-slice_fusion.refs_0_
  24.0 1.4 %collective-permute-start.1 = (bf16[64,512]{1,0:T(8,128)(2,1)S(1)}, bf16[64,512]{1,0:T(8,128)(2,1)S(1)}, u32[]{:S(2)}, u32[]{:S(2)}) collective-permute-start(bf16[64,512]{1,0:T(8,128)(2,1)S(1)} %constant_dynamic-update-slice_fusion.refs_0_), channel_id=1, source_target_pairs={{0,4},{2,6},{4,8},{6,10},{8,12},{10,14},{12,0},{14,2},{1,5},{3,7},... | collective-permute-start | bytes 196616 | tf_op jit(solution)/shard_map/ppermute | solution.py:147
  25.5 1.6 %collective-permute-start.2 = (bf16[64,512]{1,0:T(8,128)(2,1)S(1)}, bf16[64,512]{1,0:T(8,128)(2,1)S(1)}, u32[]{:S(2)}, u32[]{:S(2)}) collective-permute-start(bf16[64,512]{1,0:T(8,128)(2,1)S(1)} %constant_dynamic-update-slice_fusion.refs_0_), channel_id=1, source_target_pairs={{0,6},{2,8},{4,10},{6,12},{8,14},{10,0},{12,2},{14,4},{1,7},{3,9},... | collective-permute-start | bytes 196616 | tf_op jit(solution)/shard_map/ppermute | solution.py:147
  27.1 1.9 %collective-permute-start.3 = (bf16[64,512]{1,0:T(8,128)(2,1)S(1)}, bf16[64,512]{1,0:T(8,128)(2,1)S(1)}, u32[]{:S(2)}, u32[]{:S(2)}) collective-permute-start(bf16[64,512]{1,0:T(8,128)(2,1)S(1)} %constant_dynamic-update-slice_fusion.refs_0_), channel_id=1, source_target_pairs={{0,8},{2,10},{4,12},{6,14},{8,0},{10,2},{12,4},{14,6},{1,9},{3,11}... | collective-permute-start | bytes 196616 | tf_op jit(solution)/shard_map/ppermute | solution.py:147
  29.0 0.5 collective-permute-start.4
  29.5 1.7 %collective-permute-start.5 = (bf16[64,512]{1,0:T(8,128)(2,1)S(1)}, bf16[64,512]{1,0:T(8,128)(2,1)S(1)}, u32[]{:S(2)}, u32[]{:S(2)}) collective-permute-start(bf16[64,512]{1,0:T(8,128)(2,1)S(1)} %constant_dynamic-update-slice_fusion.refs_0_), channel_id=1, source_target_pairs={{0,12},{2,14},{4,0},{6,2},{8,4},{10,6},{12,8},{14,10},{1,13},{3,15... | collective-permute-start | bytes 196616 | tf_op jit(solution)/shard_map/ppermute | solution.py:147
  31.2 0.8 collective-permute-start.6
  31.9 3.5 %collective-permute-done.3.refs_4_ = bf16[64,512]{1,0:T(8,128)(2,1)S(1)} collective-permute-done((bf16[64,512]{1,0:T(8,128)(2,1)S(1)}, bf16[64,512]{1,0:T(8,128)(2,1)S(1)}, u32[]{:S(2)}, u32[]{:S(2)}) %collective-permute-start.3) | collective-permute-done | bytes 65568 | tf_op jit(solution)/shard_map/ppermute | solution.py:147
  35.4 1.9 %collective-permute-done.5.refs_6_ = bf16[64,512]{1,0:T(8,128)(2,1)S(1)} collective-permute-done((bf16[64,512]{1,0:T(8,128)(2,1)S(1)}, bf16[64,512]{1,0:T(8,128)(2,1)S(1)}, u32[]{:S(2)}, u32[]{:S(2)}) %collective-permute-start.5) | collective-permute-done | bytes 65568 | tf_op jit(solution)/shard_map/ppermute | solution.py:147
  37.3 1.3 %collective-permute-done.6.refs_7_ = bf16[64,512]{1,0:T(8,128)(2,1)S(1)} collective-permute-done((bf16[64,512]{1,0:T(8,128)(2,1)S(1)}, bf16[64,512]{1,0:T(8,128)(2,1)S(1)}, u32[]{:S(2)}, u32[]{:S(2)}) %collective-permute-start.6) | collective-permute-done | bytes 65568 | tf_op jit(solution)/shard_map/ppermute | solution.py:147
  38.6 0.9 %copy-done.4 = bf16[64,2048]{1,0:T(8,128)(2,1)S(1)} copy-done((bf16[64,2048]{1,0:T(8,128)(2,1)S(1)}, bf16[64,2048]{1,0:T(8,128)(2,1)}, u32[]{:S(2)}) %copy-start.4) | copy-done | bytes 262168
  39.5 5.6 %attention.1 = (f32[64,2048]{1,0:T(8,128)}, f32[1,512]{1,0:T(1,128)S(1)}) custom-call(s32[2]{0:T(128)S(1)} %pad_add_fusion.place, bf16[64,2048]{1,0:T(8,128)(2,1)S(1)} %copy-done.4, bf16[64,512]{1,0:T(8,128)(2,1)S(1)} %constant_dynamic-update-slice_fusion.refs_0_, bf16[64,512]{1,0:T(8,128)(2,1)S(1)} %collective-permute-done.refs_1_, ...), custom_call_target="tpu_custom_call" | custom-call | flops 268435456 | bytes 786432 | tf_op jit(solution)/shard_map/attention/pallas_call | solution.py:166
  45.2 2.1 %collective-permute-start.15 = (f32[1,512]{1,0:T(1,128)S(1)}, f32[1,512]{1,0:T(1,128)S(1)}, u32[]{:S(2)}, u32[]{:S(2)}) collective-permute-start(f32[1,512]{1,0:T(1,128)S(1)} %get-tuple-element.33.columns), channel_id=1, source_target_pairs={{0,1},{1,0},{2,3},{3,2},{4,5},{5,4},{6,7},{7,6},{8,9},{9,8},{10,11... | collective-permute-start | bytes 6152 | tf_op jit(solution)/shard_map/ppermute | solution.py:150
  47.3 0.8 collective-permute-done.15.columns_other
  48.1 4.0 %project.1 = (f32[32,2560]{1,0:T(8,128)S(1)}, f32[1,64]{1,0:T(1,128)S(1)}, bf16[32,2688]{1,0:T(8,128)(2,1)S(1)}, bf16[32,2688]{1,0:T(8,128)(2,1)S(1)}, bf16[32,2...) custom-call(s32[2]{0:T(128)S(1)} %pad_add_fusion.place, ...), custom_call_target="tpu_custom_call" | custom-call | flops 1342177280 | bytes 6553600 | tf_op jit(solution)/shard_map/project/pallas_call | solution.py:190
  52.2 0.1 collective-permute-start.16
  52.2 3.4 %collective-permute-start.17 = (bf16[32,2688]{1,0:T(8,128)(2,1)S(1)}, bf16[32,2688]{1,0:T(8,128)(2,1)S(1)}, u32[]{:S(2)}, u32[]{:S(2)}) collective-permute-start(bf16[32,2688]{1,0:T(8,128)(2,1)S(1)} %get-tuple-element.37), channel_id=1, source_target_pairs={{0,4},{2,6},{4,8},{6,10},{8,12},{10,14},{12,0},{14,2},{1,5},{3,7},... | collective-permute-start | bytes 516104 | tf_op jit(solution)/shard_map/ppermute | solution.py:147
  55.6 1.8 %collective-permute-start.19 = (bf16[32,2688]{1,0:T(8,128)(2,1)S(1)}, bf16[32,2688]{1,0:T(8,128)(2,1)S(1)}, u32[]{:S(2)}, u32[]{:S(2)}) collective-permute-start(bf16[32,2688]{1,0:T(8,128)(2,1)S(1)} %get-tuple-element.39), channel_id=1, source_target_pairs={{0,8},{2,10},{4,12},{6,14},{8,0},{10,2},{12,4},{14,6},{1,9},{3,11}... | collective-permute-start | bytes 516104 | tf_op jit(solution)/shard_map/ppermute | solution.py:147
  57.4 0.6 collective-permute-start.20
  58.0 2.1 %collective-permute-start.21 = (bf16[32,2688]{1,0:T(8,128)(2,1)S(1)}, bf16[32,2688]{1,0:T(8,128)(2,1)S(1)}, u32[]{:S(2)}, u32[]{:S(2)}) collective-permute-start(bf16[32,2688]{1,0:T(8,128)(2,1)S(1)} %get-tuple-element.41), channel_id=1, source_target_pairs={{0,12},{2,14},{4,0},{6,2},{8,4},{10,6},{12,8},{14,10},{1,13},{3,15... | collective-permute-start | bytes 516104 | tf_op jit(solution)/shard_map/ppermute | solution.py:147
  60.1 0.0 collective-permute-done.17.refs_1_
  60.1 1.1 %collective-permute-start.22 = (bf16[32,2688]{1,0:T(8,128)(2,1)S(1)}, bf16[32,2688]{1,0:T(8,128)(2,1)S(1)}, u32[]{:S(2)}, u32[]{:S(2)}) collective-permute-start(bf16[32,2688]{1,0:T(8,128)(2,1)S(1)} %get-tuple-element.42), channel_id=1, source_target_pairs={{0,14},{2,0},{4,2},{6,4},{8,6},{10,8},{12,10},{14,12},{1,15},{3,1}... | collective-permute-start | bytes 516104 | tf_op jit(solution)/shard_map/ppermute | solution.py:147
  61.2 16.6 %collective-permute-done.18.refs_2_ = bf16[32,2688]{1,0:T(8,128)(2,1)S(1)} collective-permute-done((bf16[32,2688]{1,0:T(8,128)(2,1)S(1)}, bf16[32,2688]{1,0:T(8,128)(2,1)S(1)}, u32[]{:S(2)}, u32[]{:S(2)}) %collective-permute-start.18) | collective-permute-done | bytes 172064 | tf_op jit(solution)/shard_map/ppermute | solution.py:147
  77.8 3.7 %collective-permute-done.19.refs_3_ = bf16[32,2688]{1,0:T(8,128)(2,1)S(1)} collective-permute-done((bf16[32,2688]{1,0:T(8,128)(2,1)S(1)}, bf16[32,2688]{1,0:T(8,128)(2,1)S(1)}, u32[]{:S(2)}, u32[]{:S(2)}) %collective-permute-start.19) | collective-permute-done | bytes 172064 | tf_op jit(solution)/shard_map/ppermute | solution.py:147
  81.5 3.9 %collective-permute-done.21.refs_5_ = bf16[32,2688]{1,0:T(8,128)(2,1)S(1)} collective-permute-done((bf16[32,2688]{1,0:T(8,128)(2,1)S(1)}, bf16[32,2688]{1,0:T(8,128)(2,1)S(1)}, u32[]{:S(2)}, u32[]{:S(2)}) %collective-permute-start.21) | collective-permute-done | bytes 172064 | tf_op jit(solution)/shard_map/ppermute | solution.py:147
  85.4 0.7 collective-permute-done.22.refs_6_
  86.0 1.0 %finish.1 = (f32[32,2560]{1,0:T(8,128)}, f32[1,64]{1,0:T(1,128)}) custom-call(f32[32,2560]{1,0:T(8,128)S(1)} %get-tuple-element.34.own, f32[1,64]{1,0:T(1,128)S(1)} %get-tuple-element.35.own_columns, f32[1,2560]{1,0:T(1,128)S(1)} %reshape.20.bias, bf16[32,2688]{1,0:T(8,128)(2,1)S(1)} %collective-permute-done.16.refs_0_, ...), custom_call_target="tpu_custom_call" | custom-call | flops 655360 | bytes 1310720 | tf_op jit(solution)/shard_map/finish/pallas_call | solution.py:204
  (19 shorter events, 0.0 us)
Async XLA Ops:
  0.6 60.5 %copy-start.5 = (f32[2560]{0:T(1024)S(1)}, f32[2560]{0:T(1024)}, u32[]{:S(2)}) copy-start(f32[2560]{0:T(1024)} %param.17) | copy-start | bytes 30724
  0.7 1.2 %copy-start = (bf16[64,8192]{1,0:T(8,128)(2,1)S(1)}, bf16[64,8192]{1,0:T(8,128)(2,1)}, u32[]{:S(2)}) copy-start(bf16[64,8192]{1,0:T(8,128)(2,1)} %hidden.1) | copy-start | bytes 3145732
  1.9 0.8 copy-start.1
  2.7 0.7 copy-start.2
  4.5 5.9 %collective-permute-start.7 = (bf16[64,512]{1,0:T(8,128)(2,1)S(1)}, bf16[64,512]{1,0:T(8,128)(2,1)S(1)}, u32[]{:S(2)}, u32[]{:S(2)}) collective-permute-start(bf16[64,512]{1,0:T(8,128)(2,1)S(1)} %get-tuple-element.26), channel_id=1, source_target_pairs={{0,2},{2,4},{4,6},{6,8},{8,10},{10,12},{12,14},{14,0},{1,3},{3,5},... | collective-permute-start | bytes 196616 | tf_op jit(solution)/shard_map/ppermute | solution.py:147
  5.8 5.9 %collective-permute-start.8 = (bf16[64,512]{1,0:T(8,128)(2,1)S(1)}, bf16[64,512]{1,0:T(8,128)(2,1)S(1)}, u32[]{:S(2)}, u32[]{:S(2)}) collective-permute-start(bf16[64,512]{1,0:T(8,128)(2,1)S(1)} %get-tuple-element.27), channel_id=1, source_target_pairs={{0,4},{2,6},{4,8},{6,10},{8,12},{10,14},{12,0},{14,2},{1,5},{3,7},... | collective-permute-start | bytes 196616 | tf_op jit(solution)/shard_map/ppermute | solution.py:147
  7.1 6.7 %collective-permute-start.9 = (bf16[64,512]{1,0:T(8,128)(2,1)S(1)}, bf16[64,512]{1,0:T(8,128)(2,1)S(1)}, u32[]{:S(2)}, u32[]{:S(2)}) collective-permute-start(bf16[64,512]{1,0:T(8,128)(2,1)S(1)} %get-tuple-element.28), channel_id=1, source_target_pairs={{0,6},{2,8},{4,10},{6,12},{8,14},{10,0},{12,2},{14,4},{1,7},{3,9},... | collective-permute-start | bytes 196616 | tf_op jit(solution)/shard_map/ppermute | solution.py:147
  8.0 8.8 %collective-permute-start.10 = (bf16[64,512]{1,0:T(8,128)(2,1)S(1)}, bf16[64,512]{1,0:T(8,128)(2,1)S(1)}, u32[]{:S(2)}, u32[]{:S(2)}) collective-permute-start(bf16[64,512]{1,0:T(8,128)(2,1)S(1)} %get-tuple-element.29), channel_id=1, source_target_pairs={{0,8},{2,10},{4,12},{6,14},{8,0},{10,2},{12,4},{14,6},{1,9},{3,11}... | collective-permute-start | bytes 196616 | tf_op jit(solution)/shard_map/ppermute | solution.py:147
  9.4 7.5 %collective-permute-start.11 = (bf16[64,512]{1,0:T(8,128)(2,1)S(1)}, bf16[64,512]{1,0:T(8,128)(2,1)S(1)}, u32[]{:S(2)}, u32[]{:S(2)}) collective-permute-start(bf16[64,512]{1,0:T(8,128)(2,1)S(1)} %get-tuple-element.30), channel_id=1, source_target_pairs={{0,10},{2,12},{4,14},{6,0},{8,2},{10,4},{12,6},{14,8},{1,11},{3,13... | collective-permute-start | bytes 196616 | tf_op jit(solution)/shard_map/ppermute | solution.py:147
  10.4 8.8 %collective-permute-start.12 = (bf16[64,512]{1,0:T(8,128)(2,1)S(1)}, bf16[64,512]{1,0:T(8,128)(2,1)S(1)}, u32[]{:S(2)}, u32[]{:S(2)}) collective-permute-start(bf16[64,512]{1,0:T(8,128)(2,1)S(1)} %get-tuple-element.31), channel_id=1, source_target_pairs={{0,12},{2,14},{4,0},{6,2},{8,4},{10,6},{12,8},{14,10},{1,13},{3,15... | collective-permute-start | bytes 196616 | tf_op jit(solution)/shard_map/ppermute | solution.py:147
  11.6 9.4 %collective-permute-start.13 = (bf16[64,512]{1,0:T(8,128)(2,1)S(1)}, bf16[64,512]{1,0:T(8,128)(2,1)S(1)}, u32[]{:S(2)}, u32[]{:S(2)}) collective-permute-start(bf16[64,512]{1,0:T(8,128)(2,1)S(1)} %get-tuple-element.32), channel_id=1, source_target_pairs={{0,14},{2,0},{4,2},{6,4},{8,6},{10,8},{12,10},{14,12},{1,15},{3,1}... | collective-permute-start | bytes 196616 | tf_op jit(solution)/shard_map/ppermute | solution.py:147
  21.0 0.7 copy-start.3
  22.5 25.6 %collective-permute-start.14 = (bf16[256,512]{1,0:T(8,128)(2,1)S(1)}, bf16[256,512]{1,0:T(8,128)(2,1)S(1)}, u32[]{:S(2)}, u32[]{:S(2)}) collective-permute-start(bf16[256,512]{1,0:T(8,128)(2,1)S(1)} %compact.1.own), channel_id=1, source_target_pairs={{0,1},{1,0},{2,3},{3,2},{4,5},{5,4},{6,7},{7,6},{8,9},{9,8},{10,11... | collective-permute-start | bytes 786440 | tf_op jit(solution)/shard_map/ppermute | solution.py:150
  24.0 5.0 %collective-permute-start = (bf16[64,512]{1,0:T(8,128)(2,1)S(1)}, bf16[64,512]{1,0:T(8,128)(2,1)S(1)}, u32[]{:S(2)}, u32[]{:S(2)}) collective-permute-start(bf16[64,512]{1,0:T(8,128)(2,1)S(1)} %constant_dynamic-update-slice_fusion.refs_0_), channel_id=1, source_target_pairs={{0,2},{2,4},{4,6},{6,8},{8,10},{10,12},{12,14},{14,0},{1,3},{3,5},... | collective-permute-start | bytes 196616 | tf_op jit(solution)/shard_map/ppermute | solution.py:147
  24.0 5.5 %collective-permute-start.1 = (bf16[64,512]{1,0:T(8,128)(2,1)S(1)}, bf16[64,512]{1,0:T(8,128)(2,1)S(1)}, u32[]{:S(2)}, u32[]{:S(2)}) collective-permute-start(bf16[64,512]{1,0:T(8,128)(2,1)S(1)} %constant_dynamic-update-slice_fusion.refs_0_), channel_id=1, source_target_pairs={{0,4},{2,6},{4,8},{6,10},{8,12},{10,14},{12,0},{14,2},{1,5},{3,7},... | collective-permute-start | bytes 196616 | tf_op jit(solution)/shard_map/ppermute | solution.py:147
  25.5 5.7 %collective-permute-start.2 = (bf16[64,512]{1,0:T(8,128)(2,1)S(1)}, bf16[64,512]{1,0:T(8,128)(2,1)S(1)}, u32[]{:S(2)}, u32[]{:S(2)}) collective-permute-start(bf16[64,512]{1,0:T(8,128)(2,1)S(1)} %constant_dynamic-update-slice_fusion.refs_0_), channel_id=1, source_target_pairs={{0,6},{2,8},{4,10},{6,12},{8,14},{10,0},{12,2},{14,4},{1,7},{3,9},... | collective-permute-start | bytes 196616 | tf_op jit(solution)/shard_map/ppermute | solution.py:147
  27.1 8.3 %collective-permute-start.3 = (bf16[64,512]{1,0:T(8,128)(2,1)S(1)}, bf16[64,512]{1,0:T(8,128)(2,1)S(1)}, u32[]{:S(2)}, u32[]{:S(2)}) collective-permute-start(bf16[64,512]{1,0:T(8,128)(2,1)S(1)} %constant_dynamic-update-slice_fusion.refs_0_), channel_id=1, source_target_pairs={{0,8},{2,10},{4,12},{6,14},{8,0},{10,2},{12,4},{14,6},{1,9},{3,11}... | collective-permute-start | bytes 196616 | tf_op jit(solution)/shard_map/ppermute | solution.py:147
  29.0 6.4 %collective-permute-start.4 = (bf16[64,512]{1,0:T(8,128)(2,1)S(1)}, bf16[64,512]{1,0:T(8,128)(2,1)S(1)}, u32[]{:S(2)}, u32[]{:S(2)}) collective-permute-start(bf16[64,512]{1,0:T(8,128)(2,1)S(1)} %constant_dynamic-update-slice_fusion.refs_0_), channel_id=1, source_target_pairs={{0,10},{2,12},{4,14},{6,0},{8,2},{10,4},{12,6},{14,8},{1,11},{3,13... | collective-permute-start | bytes 196616 | tf_op jit(solution)/shard_map/ppermute | solution.py:147
  29.5 7.8 %collective-permute-start.5 = (bf16[64,512]{1,0:T(8,128)(2,1)S(1)}, bf16[64,512]{1,0:T(8,128)(2,1)S(1)}, u32[]{:S(2)}, u32[]{:S(2)}) collective-permute-start(bf16[64,512]{1,0:T(8,128)(2,1)S(1)} %constant_dynamic-update-slice_fusion.refs_0_), channel_id=1, source_target_pairs={{0,12},{2,14},{4,0},{6,2},{8,4},{10,6},{12,8},{14,10},{1,13},{3,15... | collective-permute-start | bytes 196616 | tf_op jit(solution)/shard_map/ppermute | solution.py:147
  31.2 7.4 %collective-permute-start.6 = (bf16[64,512]{1,0:T(8,128)(2,1)S(1)}, bf16[64,512]{1,0:T(8,128)(2,1)S(1)}, u32[]{:S(2)}, u32[]{:S(2)}) collective-permute-start(bf16[64,512]{1,0:T(8,128)(2,1)S(1)} %constant_dynamic-update-slice_fusion.refs_0_), channel_id=1, source_target_pairs={{0,14},{2,0},{4,2},{6,4},{8,6},{10,8},{12,10},{14,12},{1,15},{3,1}... | collective-permute-start | bytes 196616 | tf_op jit(solution)/shard_map/ppermute | solution.py:147
  38.6 1.0 %copy-start.4 = (bf16[64,2048]{1,0:T(8,128)(2,1)S(1)}, bf16[64,2048]{1,0:T(8,128)(2,1)}, u32[]{:S(2)}) copy-start(bf16[64,2048]{1,0:T(8,128)(2,1)} %queries.1) | copy-start | bytes 786436
  45.2 3.0 %collective-permute-start.15 = (f32[1,512]{1,0:T(1,128)S(1)}, f32[1,512]{1,0:T(1,128)S(1)}, u32[]{:S(2)}, u32[]{:S(2)}) collective-permute-start(f32[1,512]{1,0:T(1,128)S(1)} %get-tuple-element.33.columns), channel_id=1, source_target_pairs={{0,1},{1,0},{2,3},{3,2},{4,5},{5,4},{6,7},{7,6},{8,9},{9,8},{10,11... | collective-permute-start | bytes 6152 | tf_op jit(solution)/shard_map/ppermute | solution.py:150
  52.2 5.8 %collective-permute-start.16 = (bf16[32,2688]{1,0:T(8,128)(2,1)S(1)}, bf16[32,2688]{1,0:T(8,128)(2,1)S(1)}, u32[]{:S(2)}, u32[]{:S(2)}) collective-permute-start(bf16[32,2688]{1,0:T(8,128)(2,1)S(1)} %get-tuple-element.36), channel_id=1, source_target_pairs={{0,2},{2,4},{4,6},{6,8},{8,10},{10,12},{12,14},{14,0},{1,3},{3,5},... | collective-permute-start | bytes 516104 | tf_op jit(solution)/shard_map/ppermute | solution.py:147
  52.2 7.8 %collective-permute-start.17 = (bf16[32,2688]{1,0:T(8,128)(2,1)S(1)}, bf16[32,2688]{1,0:T(8,128)(2,1)S(1)}, u32[]{:S(2)}, u32[]{:S(2)}) collective-permute-start(bf16[32,2688]{1,0:T(8,128)(2,1)S(1)} %get-tuple-element.37), channel_id=1, source_target_pairs={{0,4},{2,6},{4,8},{6,10},{8,12},{10,14},{12,0},{14,2},{1,5},{3,7},... | collective-permute-start | bytes 516104 | tf_op jit(solution)/shard_map/ppermute | solution.py:147
  55.6 22.2 %collective-permute-start.18 = (bf16[32,2688]{1,0:T(8,128)(2,1)S(1)}, bf16[32,2688]{1,0:T(8,128)(2,1)S(1)}, u32[]{:S(2)}, u32[]{:S(2)}) collective-permute-start(bf16[32,2688]{1,0:T(8,128)(2,1)S(1)} %get-tuple-element.38), channel_id=1, source_target_pairs={{0,6},{2,8},{4,10},{6,12},{8,14},{10,0},{12,2},{14,4},{1,7},{3,9},... | collective-permute-start | bytes 516104 | tf_op jit(solution)/shard_map/ppermute | solution.py:147
  55.6 25.8 %collective-permute-start.19 = (bf16[32,2688]{1,0:T(8,128)(2,1)S(1)}, bf16[32,2688]{1,0:T(8,128)(2,1)S(1)}, u32[]{:S(2)}, u32[]{:S(2)}) collective-permute-start(bf16[32,2688]{1,0:T(8,128)(2,1)S(1)} %get-tuple-element.39), channel_id=1, source_target_pairs={{0,8},{2,10},{4,12},{6,14},{8,0},{10,2},{12,4},{14,6},{1,9},{3,11}... | collective-permute-start | bytes 516104 | tf_op jit(solution)/shard_map/ppermute | solution.py:147
  57.4 24.0 %collective-permute-start.20 = (bf16[32,2688]{1,0:T(8,128)(2,1)S(1)}, bf16[32,2688]{1,0:T(8,128)(2,1)S(1)}, u32[]{:S(2)}, u32[]{:S(2)}) collective-permute-start(bf16[32,2688]{1,0:T(8,128)(2,1)S(1)} %get-tuple-element.40), channel_id=1, source_target_pairs={{0,10},{2,12},{4,14},{6,0},{8,2},{10,4},{12,6},{14,8},{1,11},{3,13... | collective-permute-start | bytes 516104 | tf_op jit(solution)/shard_map/ppermute | solution.py:147
  58.0 27.4 %collective-permute-start.21 = (bf16[32,2688]{1,0:T(8,128)(2,1)S(1)}, bf16[32,2688]{1,0:T(8,128)(2,1)S(1)}, u32[]{:S(2)}, u32[]{:S(2)}) collective-permute-start(bf16[32,2688]{1,0:T(8,128)(2,1)S(1)} %get-tuple-element.41), channel_id=1, source_target_pairs={{0,12},{2,14},{4,0},{6,2},{8,4},{10,6},{12,8},{14,10},{1,13},{3,15... | collective-permute-start | bytes 516104 | tf_op jit(solution)/shard_map/ppermute | solution.py:147
  60.1 26.0 %collective-permute-start.22 = (bf16[32,2688]{1,0:T(8,128)(2,1)S(1)}, bf16[32,2688]{1,0:T(8,128)(2,1)S(1)}, u32[]{:S(2)}, u32[]{:S(2)}) collective-permute-start(bf16[32,2688]{1,0:T(8,128)(2,1)S(1)} %get-tuple-element.42), channel_id=1, source_target_pairs={{0,14},{2,0},{4,2},{6,4},{8,6},{10,8},{12,10},{14,12},{1,15},{3,1}... | collective-permute-start | bytes 516104 | tf_op jit(solution)/shard_map/ppermute | solution.py:147

commit v2 on v1

v2 whole, which is shorter than its diff:
```python
import functools

import jax
import jax.numpy as jnp
from jax import lax
from jax.experimental import pallas as pl
from jax.experimental.pallas import tpu as pltpu
from jax.sharding import PartitionSpec as P

HEAD_SIZE = 128
QUERY_HEADS = 32
CHUNKS = 2
VMEM = pl.BlockSpec(memory_space=pltpu.VMEM)
SMEM = pl.BlockSpec(memory_space=pltpu.SMEM)
ANY = pl.BlockSpec(memory_space=pl.ANY)
PARAMS = pltpu.CompilerParams(vmem_limit_bytes=16 * 1024 * 1024)


def norm_select_kernel(n, place, hidden_in, gain_in, kept_in, keys_in, values_in, pair, *refs):
    outs, (hidden, gain, kept, sems) = refs[:n], refs[n:]
    rows, width = hidden.shape
    block = width // n
    half = block // 2
    pieces = 4
    piece = width // pieces
    loads = [
        pltpu.make_async_copy(
            hidden_in.at[:, i * piece : (i + 1) * piece], hidden.at[:, i * piece : (i + 1) * piece], sems.at[i]
        )
        for i in range(pieces)
    ]
    key_width = keys_in.shape[1]
    loads += [
        pltpu.make_async_copy(gain_in, gain, sems.at[pieces]),
        pltpu.make_async_copy(kept_in, kept, sems.at[pieces + 1]),
        pltpu.make_async_copy(keys_in, pair.at[:, :key_width], sems.at[pieces + 2]),
        pltpu.make_async_copy(values_in, pair.at[:, key_width:], sems.at[pieces + 3]),
    ]
    for load in loads:
        load.start()
    s, t = place[0], place[1]
    step = min(piece, 1024)
    total = jnp.zeros((rows, step), jnp.float32)
    for i in range(pieces):
        loads[i].wait()
        for j in range(i * piece, (i + 1) * piece, step):
            part = hidden[:, j : j + step].astype(jnp.float32)
            total += part * part
    scale = lax.rsqrt(jnp.sum(total, axis=1, keepdims=True) / width + 1e-06)
    for load in loads[pieces:]:
        load.wait()
    selector = (kept[...] == lax.broadcasted_iota(jnp.int32, (rows, rows), 0)).astype(jnp.bfloat16)
    for k in range(n):
        start = pl.multiple_of(lax.bitwise_xor(s, k) * block + t * half, half)
        columns = pl.ds(start, half)
        normed = (hidden[:, columns].astype(jnp.float32) * scale * gain[:, columns]).astype(jnp.bfloat16)
        outs[k][...] = lax.dot_general(
            selector, normed, (((0,), (0,)), ((), ())), preferred_element_type=jnp.float32
        ).astype(jnp.bfloat16)


def attention_kernel(n, kv_heads, order, place, queries, held, context, columns):
    rows = queries.shape[0]
    group = queries.shape[1] // (HEAD_SIZE * kv_heads)
    s = place[0]
    keys_total = n * rows
    column = lax.broadcasted_iota(jnp.int32, (1, keys_total), 1)
    position = column
    for at, k in enumerate(order):
        inside = (column >= at * rows) & (column < (at + 1) * rows)
        position = jnp.where(inside, column + (lax.bitwise_xor(s, k) - s - at) * rows, position)
    allowed = position <= lax.broadcasted_iota(jnp.int32, (rows, keys_total), 0)
    sums = jnp.zeros((1, keys_total), jnp.float32)
    for g in range(kv_heads):
        key = held[:, g * HEAD_SIZE : (g + 1) * HEAD_SIZE]
        value = held[:, (kv_heads + g) * HEAD_SIZE : (kv_heads + g + 1) * HEAD_SIZE]
        for h in range(g * group, (g + 1) * group):
            lanes = slice(h * HEAD_SIZE, (h + 1) * HEAD_SIZE)
            scores = lax.dot_general(
                queries[:, lanes], key, (((1,), (1,)), ((), ())), preferred_element_type=jnp.float32
            ) * HEAD_SIZE ** (-0.5)
            scores = jnp.where(allowed, scores, -1e30)
            row_max = jnp.max(scores, axis=1, keepdims=True)
            weights = jnp.where(allowed, jnp.exp(scores - row_max), 0.0)
            inverse = 1.0 / jnp.sum(weights, axis=1, keepdims=True)
            mixed = jnp.dot(weights.astype(jnp.bfloat16), value, preferred_element_type=jnp.float32)
            context[:, lanes] = mixed * inverse
            sums += jnp.sum(weights * inverse, axis=0, keepdims=True)
    for at, k in enumerate(order):
        columns[k : k + 1, :] = sums[:, at * rows : (at + 1) * rows]


def compact_kernel(n, owners, place, counts, *refs):
    blocks, out = refs[:n], refs[n]
    rows = blocks[0].shape[0]
    survivors = out.shape[0]
    lines = survivors // n
    s = place[0]
    slot_all = lax.broadcasted_iota(jnp.int32, (1, n * rows), 1)
    target = jnp.full((1, n * rows), -1, jnp.int32)
    for k in range(n):
        source = lax.bitwise_xor(s, k)
        begin = jnp.int32(0)
        for i in range(n):
            begin += jnp.where(i < source, counts[i], 0)
        slot = slot_all - k * rows
        inside = (slot >= 0) & (slot < counts[source])
        target = jnp.where(inside, begin + slot, target)
    line = lax.broadcasted_iota(jnp.int32, (lines, n * rows), 0)
    received = jnp.concatenate([b[...] for b in blocks], axis=0)
    pick = jnp.concatenate(
        [(line + lax.bitwise_xor(s, k) * lines == target).astype(jnp.float32) for k in owners], axis=0
    ).astype(jnp.bfloat16)
    out[...] = jnp.dot(pick, received, preferred_element_type=jnp.float32).astype(jnp.bfloat16)


def project_kernel(place, own, other, matrix, *outs):
    survivors, half = own.shape
    near = survivors // 2
    first = place[1] == 0
    low = jnp.where(first, own[...], other[...])
    high = jnp.where(first, other[...], own[...])
    features = jnp.concatenate([low, high], axis=1)
    for c in range(CHUNKS):
        width = outs[2 * c].shape[1]
        tile = width // 2 if width % 256 == 0 else width
        for j in range(0, width, tile):
            lanes = slice(c * width + j, c * width + j + tile)
            part = jnp.dot(features, matrix[:, lanes], preferred_element_type=jnp.float32)
            outs[2 * c][:, j : j + tile] = part[:near]
            outs[2 * c + 1][:, j : j + tile] = part[near:].astype(jnp.bfloat16)


def pair_kernel(kept, received, own, *outs):
    lines = own.shape[0]
    own[...] = kept[:lines] + received[:lines].astype(jnp.float32)
    for i, out in enumerate(outs):
        at = slice((i + 1) * lines, (i + 2) * lines)
        out[...] = (kept[at] + received[at].astype(jnp.float32)).astype(jnp.bfloat16)


def finish_kernel(bias, *refs):
    *parts, out = refs
    per_chunk = len(parts) // CHUNKS
    width = parts[0].shape[1]
    for c in range(CHUNKS):
        own, *received = parts[c * per_chunk : (c + 1) * per_chunk]
        total = own[...]
        for r in received:
            total += r[...].astype(jnp.float32)
        lanes = slice(c * width, (c + 1) * width)
        out[:, lanes] = total + bias[:, lanes]


def shards(queries, keys, values, hidden, norm_gain, retained_lists, counts, affine_matrix, affine_offset_vector):
    n = lax.axis_size("seq")
    rows, model = hidden.shape
    kv_heads = keys.shape[1] // HEAD_SIZE
    half = affine_matrix.shape[0] // 2
    width = affine_matrix.shape[1]
    survivors = n * rows // 2
    lines = survivors // n
    chunk = width // CHUNKS
    s, t = lax.axis_index("seq"), lax.axis_index("ten")
    place = jnp.stack([s, t]).astype(jnp.int32)
    f32, bf16 = jnp.float32, jnp.bfloat16
    shape = jax.ShapeDtypeStruct

    def trade(x, k):
        return lax.ppermute(x, "seq", [(i, i ^ k) for i in range(n)])

    def swap(x):
        return lax.ppermute(x, "ten", [(0, 1), (1, 0)])

    def cost(flops, size):
        return pl.CostEstimate(flops=flops, bytes_accessed=size, transcendentals=0)

    pair, *chosen = pl.pallas_call(
        functools.partial(norm_select_kernel, n),
        out_shape=[shape((rows, 2 * keys.shape[1]), bf16)] + [shape((rows, half), bf16)] * n,
        in_specs=[SMEM] + [ANY] * 5,
        out_specs=[VMEM] * (n + 1),
        scratch_shapes=[
            pltpu.VMEM((rows, model), bf16),
            pltpu.VMEM((1, model), f32),
            pltpu.VMEM((1, rows), jnp.int32),
            pltpu.SemaphoreType.DMA((8,)),
        ],
        compiler_params=PARAMS,
        cost_estimate=cost(4 * rows * model, 3 * rows * model),
        name="norm_select",
    )(place, hidden, norm_gain.reshape(1, model), retained_lists.reshape(1, rows), keys, values)
    received = [chosen[0]] + [trade(chosen[k], k) for k in range(1, n)]

    masks = [1 << i for i in range(1, n.bit_length() - 1)] + [1]
    held, order = pair, [0]
    for mask in masks:
        held = jnp.concatenate([held, trade(held, mask)], axis=0)
        order = order + [k ^ mask for k in order]
    context, columns = pl.pallas_call(
        functools.partial(attention_kernel, n, kv_heads, order),
        out_shape=[shape(queries.shape, f32), shape((n, rows), f32)],
        in_specs=[SMEM, VMEM, VMEM],
        out_specs=[VMEM] * 2,
        compiler_params=PARAMS,
        cost_estimate=cost(4 * rows * n * rows * queries.shape[1], 6 * rows * queries.shape[1]),
        name="attention",
    )(place, queries, held)
    mask = n // 2
    while mask:
        columns = columns[:mask] + trade(columns[mask:], mask)
        mask //= 2
    scores = (columns + swap(columns)).reshape(rows) / QUERY_HEADS

    owners = list(range(0, n, 2)) + list(range(1, n, 2))
    own = pl.pallas_call(
        functools.partial(compact_kernel, n, owners),
        out_shape=shape((survivors, half), bf16),
        in_specs=[SMEM, SMEM] + [VMEM] * n,
        out_specs=VMEM,
        compiler_params=PARAMS,
        cost_estimate=cost(2 * survivors * n * rows * half, 4 * n * rows * half),
        name="compact",
    )(place, counts, *received)
    other = swap(own)

    partial_sums = pl.pallas_call(
        project_kernel,
        out_shape=[shape((survivors // 2, chunk), f32), shape((survivors // 2, chunk), bf16)] * CHUNKS,
        in_specs=[SMEM] + [VMEM] * 3,
        out_specs=[VMEM] * (2 * CHUNKS),
        compiler_params=PARAMS,
        cost_estimate=cost(4 * survivors * half * width, 4 * half * width + 6 * survivors * width),
        name="project",
    )(place, own, other, affine_matrix)

    parts = []
    for c in range(CHUNKS):
        mine, *sent = pl.pallas_call(
            pair_kernel,
            out_shape=[shape((lines, chunk), f32)] + [shape((lines, chunk), bf16)] * (n // 2 - 1),
            in_specs=[VMEM] * 2,
            out_specs=[VMEM] * (n // 2),
            compiler_params=PARAMS,
            cost_estimate=cost(survivors * chunk, 3 * survivors * chunk),
            name="pair_sum",
        )(partial_sums[2 * c], trade(partial_sums[2 * c + 1], 1))
        parts += [mine] + [trade(sent[i], 2 * (i + 1)) for i in range(n // 2 - 1)]

    triples = pl.pallas_call(
        finish_kernel,
        out_shape=shape((lines, width), f32),
        in_specs=[VMEM] * (len(parts) + 1),
        out_specs=VMEM,
        compiler_params=PARAMS,
        cost_estimate=cost(n * lines * width, 2 * n * lines * width),
        name="finish",
    )(affine_offset_vector.reshape(1, width), *parts)
    return (context, scores, triples)


def solution(mesh):
    in_specs = (
        P(("grp", "seq"), "ten"),
        P(("grp", "seq"), "ten"),
        P(("grp", "seq"), "ten"),
        P(("grp", "seq"), None),
        P(),
        P(("grp", "seq")),
        P("grp"),
        P("seq", "ten"),
        P("ten"),
    )
    out_specs = (P(("grp", "seq"), "ten"), P(("grp", "seq")), P(("grp", "seq"), "ten"))
    return jax.shard_map(shards, mesh=mesh, in_specs=in_specs, out_specs=out_specs, check_vma=False)
```

time: 87.5 us -> 88.7 us (1.014)
  the two profiles are of different devices: /device:TPU:13 before, /device:TPU:0 now
where the time goes in v2:
time: 88.7 us; the launch traced here: 88.3 us
  starting transfers between devices  36 us (41%)
  waiting for transfers between devices  31.4 us (35%)
  Pallas kernels  11.2 us (13%)
  local copies, waits for them, and re-layouts  8.27 us (9%)
    ppermute x21, starting transfers between devices, trade(): return lax.ppermute(x, 'seq', [(i, i ^ k) for i in range(n)])  35.9 us
    ppermute x21, waiting for transfers between devices, trade(): return lax.ppermute(x, 'seq', [(i, i ^ k) for i in range(n)])  31.4 us
    unnamed x18, local copies, waits for them, and re-layouts  8.24 us
    pallas_call x1, Pallas kernels, shards(): pl.pallas_call(functools.partial(attention_kernel, n, kv_heads, order), o...  5.58 us
    pallas_call x1, Pallas kernels, shards(): pl.pallas_call(project_kernel, out_shape=[shape((survivors // 2, chunk),...  2.38 us
  transfers between devices with their start and end apart: 23, of which 11 were waited for; matrix products, arithmetic and copies ran while one was open for 1% of the time, Pallas kernels for 10%

profile of v2, /device:TPU:0, one launch (start us, length us, event | category | flops | bytes accessed | tf_op | source)
XLA Modules:
  0.0 88.3 jit_solution(13961998100008083124)
XLA Ops:
  0.6 0.1 pad_add_fusion.place
  0.7 1.2 %copy-done.1 = bf16[64,8192]{1,0:T(8,128)(2,1)S(1)} copy-done((bf16[64,8192]{1,0:T(8,128)(2,1)S(1)}, bf16[64,8192]{1,0:T(8,128)(2,1)}, u32[]{:S(2)}) %copy-start.1) | copy-done | bytes 1048600
  1.9 0.8 copy-done.2
  2.7 0.8 copy-done.3
  3.5 0.8 copy-done.4
  4.2 0.7 copy-done.5
  4.9 1.4 %norm_select.1 = (bf16[64,512]{1,0:T(8,128)(2,1)S(1)}, bf16[64,512]{1,0:T(8,128)(2,1)S(1)}, bf16[64,512]{1,0:T(8,128)(2,1)S(1)}, bf16[64,512]{1,0:T(8,128)(2,1)S...) custom-call(s32[2]{0:T(128)S(1)} %pad_add_fusion.place, ...), custom_call_target="tpu_custom_call" | custom-call | flops 2097152 | bytes 1572864 | tf_op jit(solution)/shard_map/norm_select/pallas_call | solution.py:178
  6.3 3.1 %collective-permute-start = (bf16[64,512]{1,0:T(8,128)(2,1)S(1)}, bf16[64,512]{1,0:T(8,128)(2,1)S(1)}, u32[]{:S(2)}, u32[]{:S(2)}) collective-permute-start(bf16[64,512]{1,0:T(8,128)(2,1)S(1)} %get-tuple-element.26), channel_id=1, source_target_pairs={{0,4},{2,6},{4,0},{6,2},{8,12},{10,14},{12,8},{14,10},{1,5},{3,7},... | collective-permute-start | bytes 196616 | tf_op jit(solution)/shard_map/ppermute | solution.py:170
  9.4 2.2 %collective-permute-done = bf16[64,512]{1,0:T(8,128)(2,1)S(1)} collective-permute-done((bf16[64,512]{1,0:T(8,128)(2,1)S(1)}, bf16[64,512]{1,0:T(8,128)(2,1)S(1)}, u32[]{:S(2)}, u32[]{:S(2)}) %collective-permute-start) | collective-permute-done | bytes 65568 | tf_op jit(solution)/shard_map/ppermute | solution.py:170
  11.6 3.1 %collective-permute-start.1 = (bf16[128,512]{1,0:T(8,128)(2,1)S(1)}, bf16[128,512]{1,0:T(8,128)(2,1)S(1)}, u32[]{:S(2)}, u32[]{:S(2)}) collective-permute-start(bf16[128,512]{1,0:T(8,128)(2,1)S(1)} %pad_maximum_fusion.2), channel_id=1, source_target_pairs={{0,8},{2,10},{4,12},{6,14},{8,0},{10,2},{12,4},{14,6},{1,9},{3,11}... | collective-permute-start | bytes 393224 | tf_op jit(solution)/shard_map/ppermute | solution.py:170
  14.7 5.2 %collective-permute-done.1 = bf16[128,512]{1,0:T(8,128)(2,1)S(1)} collective-permute-done((bf16[128,512]{1,0:T(8,128)(2,1)S(1)}, bf16[128,512]{1,0:T(8,128)(2,1)S(1)}, u32[]{:S(2)}, u32[]{:S(2)}) %collective-permute-start.1) | collective-permute-done | bytes 131104 | tf_op jit(solution)/shard_map/ppermute | solution.py:170
  19.9 1.6 %collective-permute-start.2 = (bf16[256,512]{1,0:T(8,128)(2,1)S(1)}, bf16[256,512]{1,0:T(8,128)(2,1)S(1)}, u32[]{:S(2)}, u32[]{:S(2)}) collective-permute-start(bf16[256,512]{1,0:T(8,128)(2,1)S(1)} %pad_maximum_fusion.1), channel_id=1, source_target_pairs={{0,2},{2,0},{4,6},{6,4},{8,10},{10,8},{12,14},{14,12},{1,3},{3,1},... | collective-permute-start | bytes 786440 | tf_op jit(solution)/shard_map/ppermute | solution.py:170
  21.5 0.7 collective-permute-start.10
  22.3 2.1 %collective-permute-start.11 = (bf16[64,512]{1,0:T(8,128)(2,1)S(1)}, bf16[64,512]{1,0:T(8,128)(2,1)S(1)}, u32[]{:S(2)}, u32[]{:S(2)}) collective-permute-start(bf16[64,512]{1,0:T(8,128)(2,1)S(1)} %get-tuple-element.34), channel_id=1, source_target_pairs={{0,10},{2,8},{4,14},{6,12},{8,2},{10,0},{12,6},{14,4},{1,11},{3,9}... | collective-permute-start | bytes 196616 | tf_op jit(solution)/shard_map/ppermute | solution.py:170
  24.4 3.8 %collective-permute-start.12 = (bf16[64,512]{1,0:T(8,128)(2,1)S(1)}, bf16[64,512]{1,0:T(8,128)(2,1)S(1)}, u32[]{:S(2)}, u32[]{:S(2)}) collective-permute-start(bf16[64,512]{1,0:T(8,128)(2,1)S(1)} %get-tuple-element.35), channel_id=1, source_target_pairs={{0,12},{2,14},{4,8},{6,10},{8,4},{10,6},{12,0},{14,2},{1,13},{3,15... | collective-permute-start | bytes 196616 | tf_op jit(solution)/shard_map/ppermute | solution.py:170
  28.2 1.4 %collective-permute-start.13 = (bf16[64,512]{1,0:T(8,128)(2,1)S(1)}, bf16[64,512]{1,0:T(8,128)(2,1)S(1)}, u32[]{:S(2)}, u32[]{:S(2)}) collective-permute-start(bf16[64,512]{1,0:T(8,128)(2,1)S(1)} %get-tuple-element.36), channel_id=1, source_target_pairs={{0,14},{2,12},{4,10},{6,8},{8,6},{10,4},{12,2},{14,0},{1,15},{3,13... | collective-permute-start | bytes 196616 | tf_op jit(solution)/shard_map/ppermute | solution.py:170
  29.6 0.6 collective-permute-start.7
  30.1 0.3 collective-permute-done.11.refs_5_
  30.5 2.6 %collective-permute-start.8 = (bf16[64,512]{1,0:T(8,128)(2,1)S(1)}, bf16[64,512]{1,0:T(8,128)(2,1)S(1)}, u32[]{:S(2)}, u32[]{:S(2)}) collective-permute-start(bf16[64,512]{1,0:T(8,128)(2,1)S(1)} %get-tuple-element.31), channel_id=1, source_target_pairs={{0,4},{2,6},{4,0},{6,2},{8,12},{10,14},{12,8},{14,10},{1,5},{3,7},... | collective-permute-start | bytes 196616 | tf_op jit(solution)/shard_map/ppermute | solution.py:170
  33.1 2.8 %collective-permute-start.9 = (bf16[64,512]{1,0:T(8,128)(2,1)S(1)}, bf16[64,512]{1,0:T(8,128)(2,1)S(1)}, u32[]{:S(2)}, u32[]{:S(2)}) collective-permute-start(bf16[64,512]{1,0:T(8,128)(2,1)S(1)} %get-tuple-element.32), channel_id=1, source_target_pairs={{0,6},{2,4},{4,2},{6,0},{8,14},{10,12},{12,10},{14,8},{1,7},{3,5},... | collective-permute-start | bytes 196616 | tf_op jit(solution)/shard_map/ppermute | solution.py:170
  35.9 0.1 collective-permute-done.8.refs_2_
  36.1 2.8 %collective-permute-done.9.refs_3_ = bf16[64,512]{1,0:T(8,128)(2,1)S(1)} collective-permute-done((bf16[64,512]{1,0:T(8,128)(2,1)S(1)}, bf16[64,512]{1,0:T(8,128)(2,1)S(1)}, u32[]{:S(2)}, u32[]{:S(2)}) %collective-permute-start.9) | collective-permute-done | bytes 65568 | tf_op jit(solution)/shard_map/ppermute | solution.py:170
  38.9 0.7 copy-done.6
  39.5 0.9 compact.1.own
  40.5 0.9 %copy-done.7 = bf16[64,2048]{1,0:T(8,128)(2,1)S(1)} copy-done((bf16[64,2048]{1,0:T(8,128)(2,1)S(1)}, bf16[64,2048]{1,0:T(8,128)(2,1)}, u32[]{:S(2)}) %copy-start.7) | copy-done | bytes 262168
  41.5 5.6 %attention.1 = (f32[64,2048]{1,0:T(8,128)}, f32[8,64]{1,0:T(8,128)S(1)}) custom-call(s32[2]{0:T(128)S(1)} %pad_add_fusion.place, bf16[64,2048]{1,0:T(8,128)(2,1)S(1)} %copy-done.7, bf16[512,512]{1,0:T(8,128)(2,1)S(1)} %pad_maximum_fusion.held), custom_call_target="tpu_custom_call" | custom-call | flops 268435456 | bytes 786432 | tf_op jit(solution)/shard_map/attention/pallas_call | solution.py:200
  47.1 1.9 %collective-permute-start.3 = (f32[4,64]{1,0:T(4,128)S(1)}, f32[4,64]{1,0:T(4,128)S(1)}, u32[]{:S(2)}, u32[]{:S(2)}) collective-permute-start(f32[4,64]{1,0:T(4,128)S(1)} %slice.19), channel_id=1, source_target_pairs={{0,8},{2,10},{4,12},{6,14},{8,0},{10,2},{12,4},{14,6},{1,9},{3,11}... | collective-permute-start | bytes 3080 | tf_op jit(solution)/shard_map/ppermute | solution.py:170
  48.9 2.5 %copy-done = bf16[1024,2560]{1,0:T(8,128)(2,1)S(1)} copy-done((bf16[1024,2560]{1,0:T(8,128)(2,1)S(1)}, bf16[1024,2560]{1,0:T(8,128)(2,1)}, u32[]{:S(2)}) %copy-start) | copy-done | bytes 5242904
  51.4 2.4 %project.1 = (f32[128,1280]{1,0:T(8,128)S(1)}, bf16[128,1280]{1,0:T(8,128)(2,1)S(1)}, f32[128,1280]{1,0:T(8,128)S(1)}, bf16[128,1280]{1,0:T(8,128)(2,1)S(1)}) custom-call(s32[2]{0:T(128)S(1)} %pad_add_fusion.place, bf16[256,512]{1,0:T(8,128)(2,1)S(1)} %compact.1.own, bf16[256,512]{1,0:T(8,128)(2,1)S(1)} %collective-permute-done.14.other, ...), custom_call_target="tpu_custom_call" | custom-call | flops 1342177280 | bytes 9175040 | tf_op jit(solution)/shard_map/project/pallas_call | solution.py:227
  53.8 1.8 %collective-permute-start.19 = (bf16[128,1280]{1,0:T(8,128)(2,1)S(1)}, bf16[128,1280]{1,0:T(8,128)(2,1)S(1)}, u32[]{:S(2)}, u32[]{:S(2)}) collective-permute-start(bf16[128,1280]{1,0:T(8,128)(2,1)S(1)} %get-tuple-element.44), channel_id=1, source_target_pairs={{0,2},{2,0},{4,6},{6,4},{8,10},{10,8},{12,14},{14,12},{1,3},{3,1},... | collective-permute-start | bytes 983048 | tf_op jit(solution)/shard_map/ppermute | solution.py:170
  55.5 0.1 collective-permute-start.4
  55.7 1.3 %collective-permute-start.15 = (bf16[128,1280]{1,0:T(8,128)(2,1)S(1)}, bf16[128,1280]{1,0:T(8,128)(2,1)S(1)}, u32[]{:S(2)}, u32[]{:S(2)}) collective-permute-start(bf16[128,1280]{1,0:T(8,128)(2,1)S(1)} %get-tuple-element.38), channel_id=1, source_target_pairs={{0,2},{2,0},{4,6},{6,4},{8,10},{10,8},{12,14},{14,12},{1,3},{3,1},... | collective-permute-start | bytes 983048 | tf_op jit(solution)/shard_map/ppermute | solution.py:170
  57.0 2.2 %collective-permute-done.4 = f32[2,64]{1,0:T(2,128)S(1)} collective-permute-done((f32[2,64]{1,0:T(2,128)S(1)}, f32[2,64]{1,0:T(2,128)S(1)}, u32[]{:S(2)}, u32[]{:S(2)}) %collective-permute-start.4) | collective-permute-done | bytes 544 | tf_op jit(solution)/shard_map/ppermute | solution.py:170
  59.2 0.3 collective-permute-start.5
  59.5 4.9 %collective-permute-done.19.received = bf16[128,1280]{1,0:T(8,128)(2,1)S(1)} collective-permute-done((bf16[128,1280]{1,0:T(8,128)(2,1)S(1)}, bf16[128,1280]{1,0:T(8,128)(2,1)S(1)}, u32[]{:S(2)}, u32[]{:S(2)}) %collective-permute-start.19) | collective-permute-done | bytes 327712 | tf_op jit(solution)/shard_map/ppermute | solution.py:170
  64.4 0.1 pair_sum.3
  64.5 1.0 %collective-permute-start.20 = (bf16[32,1280]{1,0:T(8,128)(2,1)S(1)}, bf16[32,1280]{1,0:T(8,128)(2,1)S(1)}, u32[]{:S(2)}, u32[]{:S(2)}) collective-permute-start(bf16[32,1280]{1,0:T(8,128)(2,1)S(1)} %get-tuple-element.46), channel_id=1, source_target_pairs={{0,4},{2,6},{4,0},{6,2},{8,12},{10,14},{12,8},{14,10},{1,5},{3,7},... | collective-permute-start | bytes 245768 | tf_op jit(solution)/shard_map/ppermute | solution.py:170
  65.5 5.3 %collective-permute-done.5 = f32[1,64]{1,0:T(1,128)S(1)} collective-permute-done((f32[1,64]{1,0:T(1,128)S(1)}, f32[1,64]{1,0:T(1,128)S(1)}, u32[]{:S(2)}, u32[]{:S(2)}) %collective-permute-start.5) | collective-permute-done | bytes 288 | tf_op jit(solution)/shard_map/ppermute | solution.py:170
  70.8 1.1 %collective-permute-start.21 = (bf16[32,1280]{1,0:T(8,128)(2,1)S(1)}, bf16[32,1280]{1,0:T(8,128)(2,1)S(1)}, u32[]{:S(2)}, u32[]{:S(2)}) collective-permute-start(bf16[32,1280]{1,0:T(8,128)(2,1)S(1)} %get-tuple-element.47), channel_id=1, source_target_pairs={{0,8},{2,10},{4,12},{6,14},{8,0},{10,2},{12,4},{14,6},{1,9},{3,11}... | collective-permute-start | bytes 245768 | tf_op jit(solution)/shard_map/ppermute | solution.py:170
  71.8 2.2 %collective-permute-start.22 = (bf16[32,1280]{1,0:T(8,128)(2,1)S(1)}, bf16[32,1280]{1,0:T(8,128)(2,1)S(1)}, u32[]{:S(2)}, u32[]{:S(2)}) collective-permute-start(bf16[32,1280]{1,0:T(8,128)(2,1)S(1)} %get-tuple-element.48), channel_id=1, source_target_pairs={{0,12},{2,14},{4,8},{6,10},{8,4},{10,6},{12,0},{14,2},{1,13},{3,15... | collective-permute-start | bytes 245768 | tf_op jit(solution)/shard_map/ppermute | solution.py:170
  74.1 0.3 collective-permute-start.16
  74.4 2.0 %collective-permute-start.17 = (bf16[32,1280]{1,0:T(8,128)(2,1)S(1)}, bf16[32,1280]{1,0:T(8,128)(2,1)S(1)}, u32[]{:S(2)}, u32[]{:S(2)}) collective-permute-start(bf16[32,1280]{1,0:T(8,128)(2,1)S(1)} %get-tuple-element.41), channel_id=1, source_target_pairs={{0,8},{2,10},{4,12},{6,14},{8,0},{10,2},{12,4},{14,6},{1,9},{3,11}... | collective-permute-start | bytes 245768 | tf_op jit(solution)/shard_map/ppermute | solution.py:170
  76.3 2.2 %collective-permute-start.18 = (bf16[32,1280]{1,0:T(8,128)(2,1)S(1)}, bf16[32,1280]{1,0:T(8,128)(2,1)S(1)}, u32[]{:S(2)}, u32[]{:S(2)}) collective-permute-start(bf16[32,1280]{1,0:T(8,128)(2,1)S(1)} %get-tuple-element.42), channel_id=1, source_target_pairs={{0,12},{2,14},{4,8},{6,10},{8,4},{10,6},{12,0},{14,2},{1,13},{3,15... | collective-permute-start | bytes 245768 | tf_op jit(solution)/shard_map/ppermute | solution.py:170
  78.6 0.5 multiply_bitcast_fusion
  79.1 1.7 %collective-permute-done.21.refs_6_ = bf16[32,1280]{1,0:T(8,128)(2,1)S(1)} collective-permute-done((bf16[32,1280]{1,0:T(8,128)(2,1)S(1)}, bf16[32,1280]{1,0:T(8,128)(2,1)S(1)}, u32[]{:S(2)}, u32[]{:S(2)}) %collective-permute-start.21) | collective-permute-done | bytes 81952 | tf_op jit(solution)/shard_map/ppermute | solution.py:170
  80.8 0.6 collective-permute-done.16.refs_1_
  81.5 6.0 %collective-permute-done.17.refs_2_ = bf16[32,1280]{1,0:T(8,128)(2,1)S(1)} collective-permute-done((bf16[32,1280]{1,0:T(8,128)(2,1)S(1)}, bf16[32,1280]{1,0:T(8,128)(2,1)S(1)}, u32[]{:S(2)}, u32[]{:S(2)}) %collective-permute-start.17) | collective-permute-done | bytes 81952 | tf_op jit(solution)/shard_map/ppermute | solution.py:170
  87.5 0.8 finish.1
  (35 shorter events, 0.3 us)
Async XLA Ops:
  0.7 1.2 %copy-start.1 = (bf16[64,8192]{1,0:T(8,128)(2,1)S(1)}, bf16[64,8192]{1,0:T(8,128)(2,1)}, u32[]{:S(2)}) copy-start(bf16[64,8192]{1,0:T(8,128)(2,1)} %hidden_in.1) | copy-start | bytes 3145732
  1.9 0.8 copy-start.2
  2.7 0.8 copy-start.3
  3.5 0.8 copy-start.4
  4.2 0.7 copy-start.5
  4.9 50.8 %copy-start.8 = (f32[2560]{0:T(1024)S(1)}, f32[2560]{0:T(1024)}, u32[]{:S(2)}) copy-start(f32[2560]{0:T(1024)} %param.17) | copy-start | bytes 30724
  6.3 5.3 %collective-permute-start = (bf16[64,512]{1,0:T(8,128)(2,1)S(1)}, bf16[64,512]{1,0:T(8,128)(2,1)S(1)}, u32[]{:S(2)}, u32[]{:S(2)}) collective-permute-start(bf16[64,512]{1,0:T(8,128)(2,1)S(1)} %get-tuple-element.26), channel_id=1, source_target_pairs={{0,4},{2,6},{4,0},{6,2},{8,12},{10,14},{12,8},{14,10},{1,5},{3,7},... | collective-permute-start | bytes 196616 | tf_op jit(solution)/shard_map/ppermute | solution.py:170
  11.6 8.3 %collective-permute-start.1 = (bf16[128,512]{1,0:T(8,128)(2,1)S(1)}, bf16[128,512]{1,0:T(8,128)(2,1)S(1)}, u32[]{:S(2)}, u32[]{:S(2)}) collective-permute-start(bf16[128,512]{1,0:T(8,128)(2,1)S(1)} %pad_maximum_fusion.2), channel_id=1, source_target_pairs={{0,8},{2,10},{4,12},{6,14},{8,0},{10,2},{12,4},{14,6},{1,9},{3,11}... | collective-permute-start | bytes 393224 | tf_op jit(solution)/shard_map/ppermute | solution.py:170
  19.9 20.5 %collective-permute-start.2 = (bf16[256,512]{1,0:T(8,128)(2,1)S(1)}, bf16[256,512]{1,0:T(8,128)(2,1)S(1)}, u32[]{:S(2)}, u32[]{:S(2)}) collective-permute-start(bf16[256,512]{1,0:T(8,128)(2,1)S(1)} %pad_maximum_fusion.1), channel_id=1, source_target_pairs={{0,2},{2,0},{4,6},{6,4},{8,10},{10,8},{12,14},{14,12},{1,3},{3,1},... | collective-permute-start | bytes 786440 | tf_op jit(solution)/shard_map/ppermute | solution.py:170
  21.5 8.0 %collective-permute-start.10 = (bf16[64,512]{1,0:T(8,128)(2,1)S(1)}, bf16[64,512]{1,0:T(8,128)(2,1)S(1)}, u32[]{:S(2)}, u32[]{:S(2)}) collective-permute-start(bf16[64,512]{1,0:T(8,128)(2,1)S(1)} %get-tuple-element.33), channel_id=1, source_target_pairs={{0,8},{2,10},{4,12},{6,14},{8,0},{10,2},{12,4},{14,6},{1,9},{3,11}... | collective-permute-start | bytes 196616 | tf_op jit(solution)/shard_map/ppermute | solution.py:170
  22.3 8.2 %collective-permute-start.11 = (bf16[64,512]{1,0:T(8,128)(2,1)S(1)}, bf16[64,512]{1,0:T(8,128)(2,1)S(1)}, u32[]{:S(2)}, u32[]{:S(2)}) collective-permute-start(bf16[64,512]{1,0:T(8,128)(2,1)S(1)} %get-tuple-element.34), channel_id=1, source_target_pairs={{0,10},{2,8},{4,14},{6,12},{8,2},{10,0},{12,6},{14,4},{1,11},{3,9}... | collective-permute-start | bytes 196616 | tf_op jit(solution)/shard_map/ppermute | solution.py:170
  24.4 8.8 %collective-permute-start.12 = (bf16[64,512]{1,0:T(8,128)(2,1)S(1)}, bf16[64,512]{1,0:T(8,128)(2,1)S(1)}, u32[]{:S(2)}, u32[]{:S(2)}) collective-permute-start(bf16[64,512]{1,0:T(8,128)(2,1)S(1)} %get-tuple-element.35), channel_id=1, source_target_pairs={{0,12},{2,14},{4,8},{6,10},{8,4},{10,6},{12,0},{14,2},{1,13},{3,15... | collective-permute-start | bytes 196616 | tf_op jit(solution)/shard_map/ppermute | solution.py:170
  28.2 7.7 %collective-permute-start.13 = (bf16[64,512]{1,0:T(8,128)(2,1)S(1)}, bf16[64,512]{1,0:T(8,128)(2,1)S(1)}, u32[]{:S(2)}, u32[]{:S(2)}) collective-permute-start(bf16[64,512]{1,0:T(8,128)(2,1)S(1)} %get-tuple-element.36), channel_id=1, source_target_pairs={{0,14},{2,12},{4,10},{6,8},{8,6},{10,4},{12,2},{14,0},{1,15},{3,13... | collective-permute-start | bytes 196616 | tf_op jit(solution)/shard_map/ppermute | solution.py:170
  29.6 6.4 %collective-permute-start.7 = (bf16[64,512]{1,0:T(8,128)(2,1)S(1)}, bf16[64,512]{1,0:T(8,128)(2,1)S(1)}, u32[]{:S(2)}, u32[]{:S(2)}) collective-permute-start(bf16[64,512]{1,0:T(8,128)(2,1)S(1)} %get-tuple-element.30), channel_id=1, source_target_pairs={{0,2},{2,0},{4,6},{6,4},{8,10},{10,8},{12,14},{14,12},{1,3},{3,1},... | collective-permute-start | bytes 196616 | tf_op jit(solution)/shard_map/ppermute | solution.py:170
  30.5 5.6 %collective-permute-start.8 = (bf16[64,512]{1,0:T(8,128)(2,1)S(1)}, bf16[64,512]{1,0:T(8,128)(2,1)S(1)}, u32[]{:S(2)}, u32[]{:S(2)}) collective-permute-start(bf16[64,512]{1,0:T(8,128)(2,1)S(1)} %get-tuple-element.31), channel_id=1, source_target_pairs={{0,4},{2,6},{4,0},{6,2},{8,12},{10,14},{12,8},{14,10},{1,5},{3,7},... | collective-permute-start | bytes 196616 | tf_op jit(solution)/shard_map/ppermute | solution.py:170
  33.1 5.7 %collective-permute-start.9 = (bf16[64,512]{1,0:T(8,128)(2,1)S(1)}, bf16[64,512]{1,0:T(8,128)(2,1)S(1)}, u32[]{:S(2)}, u32[]{:S(2)}) collective-permute-start(bf16[64,512]{1,0:T(8,128)(2,1)S(1)} %get-tuple-element.32), channel_id=1, source_target_pairs={{0,6},{2,4},{4,2},{6,0},{8,14},{10,12},{12,10},{14,8},{1,7},{3,5},... | collective-permute-start | bytes 196616 | tf_op jit(solution)/shard_map/ppermute | solution.py:170
  38.9 0.7 copy-start.6
  40.4 8.5 %collective-permute-start.14 = (bf16[256,512]{1,0:T(8,128)(2,1)S(1)}, bf16[256,512]{1,0:T(8,128)(2,1)S(1)}, u32[]{:S(2)}, u32[]{:S(2)}) collective-permute-start(bf16[256,512]{1,0:T(8,128)(2,1)S(1)} %compact.1.own), channel_id=1, source_target_pairs={{0,1},{1,0},{2,3},{3,2},{4,5},{5,4},{6,7},{7,6},{8,9},{9,8},{10,11... | collective-permute-start | bytes 786440 | tf_op jit(solution)/shard_map/ppermute | solution.py:173
  40.5 1.0 %copy-start.7 = (bf16[64,2048]{1,0:T(8,128)(2,1)S(1)}, bf16[64,2048]{1,0:T(8,128)(2,1)}, u32[]{:S(2)}) copy-start(bf16[64,2048]{1,0:T(8,128)(2,1)} %queries.1) | copy-start | bytes 786436
  47.1 8.5 %collective-permute-start.3 = (f32[4,64]{1,0:T(4,128)S(1)}, f32[4,64]{1,0:T(4,128)S(1)}, u32[]{:S(2)}, u32[]{:S(2)}) collective-permute-start(f32[4,64]{1,0:T(4,128)S(1)} %slice.19), channel_id=1, source_target_pairs={{0,8},{2,10},{4,12},{6,14},{8,0},{10,2},{12,4},{14,6},{1,9},{3,11}... | collective-permute-start | bytes 3080 | tf_op jit(solution)/shard_map/ppermute | solution.py:170
  48.9 2.5 %copy-start = (bf16[1024,2560]{1,0:T(8,128)(2,1)S(1)}, bf16[1024,2560]{1,0:T(8,128)(2,1)}, u32[]{:S(2)}) copy-start(bf16[1024,2560]{1,0:T(8,128)(2,1)} %matrix.1) | copy-start | bytes 15728644
  53.8 10.6 %collective-permute-start.19 = (bf16[128,1280]{1,0:T(8,128)(2,1)S(1)}, bf16[128,1280]{1,0:T(8,128)(2,1)S(1)}, u32[]{:S(2)}, u32[]{:S(2)}) collective-permute-start(bf16[128,1280]{1,0:T(8,128)(2,1)S(1)} %get-tuple-element.44), channel_id=1, source_target_pairs={{0,2},{2,0},{4,6},{6,4},{8,10},{10,8},{12,14},{14,12},{1,3},{3,1},... | collective-permute-start | bytes 983048 | tf_op jit(solution)/shard_map/ppermute | solution.py:170
  55.5 3.6 %collective-permute-start.4 = (f32[2,64]{1,0:T(2,128)S(1)}, f32[2,64]{1,0:T(2,128)S(1)}, u32[]{:S(2)}, u32[]{:S(2)}) collective-permute-start(f32[2,64]{1,0:T(2,128)S(1)} %slice.21), channel_id=1, source_target_pairs={{0,4},{2,6},{4,0},{6,2},{8,12},{10,14},{12,8},{14,10},{1,5},{3,7},... | collective-permute-start | bytes 1544 | tf_op jit(solution)/shard_map/ppermute | solution.py:170
  55.7 18.4 %collective-permute-start.15 = (bf16[128,1280]{1,0:T(8,128)(2,1)S(1)}, bf16[128,1280]{1,0:T(8,128)(2,1)S(1)}, u32[]{:S(2)}, u32[]{:S(2)}) collective-permute-start(bf16[128,1280]{1,0:T(8,128)(2,1)S(1)} %get-tuple-element.38), channel_id=1, source_target_pairs={{0,2},{2,0},{4,6},{6,4},{8,10},{10,8},{12,14},{14,12},{1,3},{3,1},... | collective-permute-start | bytes 983048 | tf_op jit(solution)/shard_map/ppermute | solution.py:170
  59.2 11.6 %collective-permute-start.5 = (f32[1,64]{1,0:T(1,128)S(1)}, f32[1,64]{1,0:T(1,128)S(1)}, u32[]{:S(2)}, u32[]{:S(2)}) collective-permute-start(f32[1,64]{1,0:T(1,128)S(1)} %slice.23), channel_id=1, source_target_pairs={{0,2},{2,0},{4,6},{6,4},{8,10},{10,8},{12,14},{14,12},{1,3},{3,1},... | collective-permute-start | bytes 776 | tf_op jit(solution)/shard_map/ppermute | solution.py:170
  64.5 11.9 %collective-permute-start.20 = (bf16[32,1280]{1,0:T(8,128)(2,1)S(1)}, bf16[32,1280]{1,0:T(8,128)(2,1)S(1)}, u32[]{:S(2)}, u32[]{:S(2)}) collective-permute-start(bf16[32,1280]{1,0:T(8,128)(2,1)S(1)} %get-tuple-element.46), channel_id=1, source_target_pairs={{0,4},{2,6},{4,0},{6,2},{8,12},{10,14},{12,8},{14,10},{1,5},{3,7},... | collective-permute-start | bytes 245768 | tf_op jit(solution)/shard_map/ppermute | solution.py:170
  70.8 3.6 %collective-permute-start.6 = (f32[1,64]{1,0:T(1,128)S(1)}, f32[1,64]{1,0:T(1,128)S(1)}, u32[]{:S(2)}, u32[]{:S(2)}) collective-permute-start(f32[1,64]{1,0:T(1,128)S(1)} %slice_add_fusion.2), channel_id=1, source_target_pairs={{0,1},{1,0},{2,3},{3,2},{4,5},{5,4},{6,7},{7,6},{8,9},{9,8},{10,11... | collective-permute-start | bytes 776 | tf_op jit(solution)/shard_map/ppermute | solution.py:173
  70.8 10.1 %collective-permute-start.21 = (bf16[32,1280]{1,0:T(8,128)(2,1)S(1)}, bf16[32,1280]{1,0:T(8,128)(2,1)S(1)}, u32[]{:S(2)}, u32[]{:S(2)}) collective-permute-start(bf16[32,1280]{1,0:T(8,128)(2,1)S(1)} %get-tuple-element.47), channel_id=1, source_target_pairs={{0,8},{2,10},{4,12},{6,14},{8,0},{10,2},{12,4},{14,6},{1,9},{3,11}... | collective-permute-start | bytes 245768 | tf_op jit(solution)/shard_map/ppermute | solution.py:170
  71.8 9.0 %collective-permute-start.22 = (bf16[32,1280]{1,0:T(8,128)(2,1)S(1)}, bf16[32,1280]{1,0:T(8,128)(2,1)S(1)}, u32[]{:S(2)}, u32[]{:S(2)}) collective-permute-start(bf16[32,1280]{1,0:T(8,128)(2,1)S(1)} %get-tuple-element.48), channel_id=1, source_target_pairs={{0,12},{2,14},{4,8},{6,10},{8,4},{10,6},{12,0},{14,2},{1,13},{3,15... | collective-permute-start | bytes 245768 | tf_op jit(solution)/shard_map/ppermute | solution.py:170
  74.1 7.3 %collective-permute-start.16 = (bf16[32,1280]{1,0:T(8,128)(2,1)S(1)}, bf16[32,1280]{1,0:T(8,128)(2,1)S(1)}, u32[]{:S(2)}, u32[]{:S(2)}) collective-permute-start(bf16[32,1280]{1,0:T(8,128)(2,1)S(1)} %get-tuple-element.40), channel_id=1, source_target_pairs={{0,4},{2,6},{4,0},{6,2},{8,12},{10,14},{12,8},{14,10},{1,5},{3,7},... | collective-permute-start | bytes 245768 | tf_op jit(solution)/shard_map/ppermute | solution.py:170
  74.4 13.1 %collective-permute-start.17 = (bf16[32,1280]{1,0:T(8,128)(2,1)S(1)}, bf16[32,1280]{1,0:T(8,128)(2,1)S(1)}, u32[]{:S(2)}, u32[]{:S(2)}) collective-permute-start(bf16[32,1280]{1,0:T(8,128)(2,1)S(1)} %get-tuple-element.41), channel_id=1, source_target_pairs={{0,8},{2,10},{4,12},{6,14},{8,0},{10,2},{12,4},{14,6},{1,9},{3,11}... | collective-permute-start | bytes 245768 | tf_op jit(solution)/shard_map/ppermute | solution.py:170
  76.3 11.1 %collective-permute-start.18 = (bf16[32,1280]{1,0:T(8,128)(2,1)S(1)}, bf16[32,1280]{1,0:T(8,128)(2,1)S(1)}, u32[]{:S(2)}, u32[]{:S(2)}) collective-permute-start(bf16[32,1280]{1,0:T(8,128)(2,1)S(1)} %get-tuple-element.42), channel_id=1, source_target_pairs={{0,12},{2,14},{4,8},{6,10},{8,4},{10,6},{12,0},{14,2},{1,13},{3,15... | collective-permute-start | bytes 245768 | tf_op jit(solution)/shard_map/ppermute | solution.py:170

commit v3 on v2

v3 whole, which is shorter than its diff:
```python
import functools
import math

import jax
import jax.numpy as jnp
from jax import lax
from jax.experimental import pallas as pl
from jax.experimental.pallas import tpu as pltpu
from jax.sharding import PartitionSpec as P

HEAD_SIZE = 128
QUERY_HEADS = 32
VMEM = pl.BlockSpec(memory_space=pltpu.VMEM)
ANY = pl.BlockSpec(memory_space=pl.ANY)
MIB = 1024 * 1024


def call(body, name, inputs, outputs, flops, limit=16, in_specs=None, scratch=(), remote=0):
    inputs = [pltpu.with_memory_space_constraint(x, pltpu.HBM) if i < remote else x for i, x in enumerate(inputs)]
    size = sum(math.prod(x.shape) * x.dtype.itemsize for x in list(inputs) + list(outputs))
    return pl.pallas_call(
        body,
        out_shape=list(outputs),
        in_specs=in_specs or [VMEM] * len(inputs),
        out_specs=[VMEM] * len(outputs),
        scratch_shapes=list(scratch),
        compiler_params=pltpu.CompilerParams(vmem_limit_bytes=limit * MIB),
        cost_estimate=pl.CostEstimate(flops=flops, bytes_accessed=size, transcendentals=0),
        name=name,
    )(*inputs)


def norm_select_kernel(n, hidden_in, gain_in, kept_in, keys_in, values_in, pair, *refs):
    outs, (hidden, gain, kept, sems) = refs[:n], refs[n:]
    rows, width = hidden.shape
    block = width // n
    half = block // 2
    pieces = 4
    piece = width // pieces
    key_width = keys_in.shape[1]
    loads = [
        pltpu.make_async_copy(
            hidden_in.at[:, i * piece : (i + 1) * piece], hidden.at[:, i * piece : (i + 1) * piece], sems.at[i]
        )
        for i in range(pieces)
    ]
    loads += [
        pltpu.make_async_copy(gain_in, gain, sems.at[pieces]),
        pltpu.make_async_copy(kept_in, kept, sems.at[pieces + 1]),
        pltpu.make_async_copy(keys_in, pair.at[:, :key_width], sems.at[pieces + 2]),
        pltpu.make_async_copy(values_in, pair.at[:, key_width:], sems.at[pieces + 3]),
    ]
    for load in loads:
        load.start()
    s, t = lax.axis_index("seq"), lax.axis_index("ten")
    step = min(piece, 1024)
    total = jnp.zeros((rows, step), jnp.float32)
    for i in range(pieces):
        loads[i].wait()
        for j in range(i * piece, (i + 1) * piece, step):
            part = hidden[:, j : j + step].astype(jnp.float32)
            total += part * part
    scale = lax.rsqrt(jnp.sum(total, axis=1, keepdims=True) / width + 1e-06)
    for load in loads[pieces:]:
        load.wait()
    selector = (kept[...] == lax.broadcasted_iota(jnp.int32, (rows, rows), 0)).astype(jnp.bfloat16)
    for k in range(n):
        start = pl.multiple_of(lax.bitwise_xor(s, k) * block + t * half, half)
        columns = pl.ds(start, half)
        normed = (hidden[:, columns].astype(jnp.float32) * scale * gain[:, columns]).astype(jnp.bfloat16)
        outs[k][...] = lax.dot_general(
            selector, normed, (((0,), (0,)), ((), ())), preferred_element_type=jnp.float32
        ).astype(jnp.bfloat16)


def stage_kernel(n, counts_in, matrix_in, queries_in, pair, pair_other, *refs):
    matrix, queries, held, target, counts, sems = refs[n // 2 :]
    loads = [
        pltpu.make_async_copy(counts_in, counts, sems.at[0]),
        pltpu.make_async_copy(matrix_in, matrix, sems.at[1]),
        pltpu.make_async_copy(queries_in, queries, sems.at[2]),
    ]
    for load in loads:
        load.start()
    rows = pair.shape[0]
    held[:rows] = pair[...]
    held[rows:] = pair_other[...]
    s = lax.axis_index("seq")
    loads[0].wait()
    slot_all = lax.broadcasted_iota(jnp.int32, (1, n * rows), 1)
    found = jnp.full((1, n * rows), -1, jnp.int32)
    for k in range(n):
        source = lax.bitwise_xor(s, k)
        begin = jnp.int32(0)
        for i in range(n):
            begin += jnp.where(i < source, counts[i], 0)
        slot = slot_all - k * rows
        inside = (slot >= 0) & (slot < counts[source])
        found = jnp.where(inside, begin + slot, found)
    target[...] = found
    for load in loads[1:]:
        load.wait()


def compact_kernel(n, owners, target, *refs):
    blocks, out = refs[:n], refs[n]
    lines = out.shape[0] // n
    s = lax.axis_index("seq")
    received = jnp.concatenate([b[...] for b in blocks], axis=0)
    line = lax.broadcasted_iota(jnp.int32, (lines, received.shape[0]), 0)
    pick = jnp.concatenate(
        [(line + lax.bitwise_xor(s, k) * lines == target[...]).astype(jnp.float32) for k in owners], axis=0
    ).astype(jnp.bfloat16)
    out[...] = jnp.dot(pick, received, preferred_element_type=jnp.float32).astype(jnp.bfloat16)


def project_kernel(first, own, other, matrix, near, far):
    survivors, half = own.shape
    lines = survivors // 2
    width = near.shape[1]
    t = lax.axis_index("ten")
    mine = pl.ds(pl.multiple_of(t * half, half), half)
    others = pl.ds(pl.multiple_of((1 - t) * half, half), half)
    tile = width // 2 if width % 256 == 0 else width
    for j in range(0, width, tile):
        lanes = slice(first + j, first + j + tile)
        part = jnp.dot(own[...], matrix[mine, lanes], preferred_element_type=jnp.float32)
        part += jnp.dot(other[...], matrix[others, lanes], preferred_element_type=jnp.float32)
        near[:, j : j + tile] = part[:lines]
        far[:, j : j + tile] = part[lines:].astype(jnp.bfloat16)


def pair_sum_kernel(kept, received, next_in, after, own, next_out, *outs):
    lines = own.shape[0]
    own[...] = kept[:lines] + received[:lines].astype(jnp.float32)
    for i, out in enumerate(outs):
        at = slice((i + 1) * lines, (i + 2) * lines)
        out[...] = (kept[at] + received[at].astype(jnp.float32)).astype(jnp.bfloat16)
    next_out[...] = next_in[...]


def total_of(own, received):
    total = own[...]
    for r in received:
        total += r[...].astype(jnp.float32)
    return total


def pair_sum_last_kernel(n, kept, received, columns, columns_other, *refs):
    chunk_parts, (done, own, own_columns, *outs) = refs[: n // 2], refs[n // 2 :]
    lines, width = own.shape
    done[...] = total_of(chunk_parts[0], chunk_parts[1:])
    rows = columns.shape[1]
    own[...] = kept[:lines] + received[:lines].astype(jnp.float32)
    own_columns[...] = columns[:1] + columns_other[:1]
    for i, out in enumerate(outs):
        at = slice((i + 1) * lines, (i + 2) * lines)
        out[:, :width] = (kept[at] + received[at].astype(jnp.float32)).astype(jnp.bfloat16)
        total = columns[i + 1 : i + 2] + columns_other[i + 1 : i + 2]
        head = total.astype(jnp.bfloat16).astype(jnp.float32)
        extra = jnp.concatenate([head, total - head], axis=1).astype(jnp.bfloat16)
        out[:, width:] = jnp.broadcast_to(extra, (lines, 2 * rows))


def attention_kernel(n, kv_heads, order, owners, queries, held_a, held_b, after, context, columns):
    rows = queries.shape[0]
    group = queries.shape[1] // (HEAD_SIZE * kv_heads)
    s = lax.axis_index("seq")
    keys_total = n * rows
    column = lax.broadcasted_iota(jnp.int32, (1, keys_total), 1)
    position = column
    for at, k in enumerate(order):
        inside = (column >= at * rows) & (column < (at + 1) * rows)
        position = jnp.where(inside, column + (lax.bitwise_xor(s, k) - s - at) * rows, position)
    row = lax.rem(lax.broadcasted_iota(jnp.int32, (group * rows, keys_total), 0), rows)
    allowed = position <= row
    sums = jnp.zeros((1, keys_total), jnp.float32)
    for g in range(kv_heads):
        key_lanes = slice(g * HEAD_SIZE, (g + 1) * HEAD_SIZE)
        value_lanes = slice((kv_heads + g) * HEAD_SIZE, (kv_heads + g + 1) * HEAD_SIZE)
        key = jnp.concatenate([held_a[:, key_lanes], held_b[:, key_lanes]], axis=0)
        value = jnp.concatenate([held_a[:, value_lanes], held_b[:, value_lanes]], axis=0)
        heads = range(g * group, (g + 1) * group)
        stacked = jnp.concatenate([queries[:, h * HEAD_SIZE : (h + 1) * HEAD_SIZE] for h in heads], axis=0)
        scores = lax.dot_general(
            stacked, key, (((1,), (1,)), ((), ())), preferred_element_type=jnp.float32
        ) * HEAD_SIZE ** (-0.5)
        scores = jnp.where(allowed, scores, -1e30)
        weights = jnp.exp(scores - jnp.max(scores, axis=1, keepdims=True))
        inverse = 1.0 / jnp.sum(weights, axis=1, keepdims=True)
        mixed = jnp.dot(weights.astype(jnp.bfloat16), value, preferred_element_type=jnp.float32) * inverse
        for i, h in enumerate(heads):
            context[:, h * HEAD_SIZE : (h + 1) * HEAD_SIZE] = mixed[i * rows : (i + 1) * rows]
        sums += jnp.sum(weights * inverse, axis=0, keepdims=True)
    for at, k in enumerate(order):
        i = owners.index(k)
        columns[i : i + 1, :] = sums[:, at * rows : (at + 1) * rows]


def finish_kernel(bias, done, own_columns, own, *refs):
    *received, out, scores = refs
    width = own.shape[1]
    rows = own_columns.shape[1]
    out[:, :width] = done[...] + bias[:, :width]
    out[:, width:] = total_of(own, [r.at[:, :width] for r in received]) + bias[:, width:]
    sums = own_columns[...]
    for r in received:
        extra = r[:16, width:].astype(jnp.float32)
        sums += extra[:1, :rows] + extra[:1, rows:]
    scores[...] = sums / QUERY_HEADS


def shards(queries, keys, values, hidden, norm_gain, retained_lists, counts, affine_matrix, affine_offset_vector):
    n = lax.axis_size("seq")
    rows, model = hidden.shape
    kv_heads = keys.shape[1] // HEAD_SIZE
    half = affine_matrix.shape[0] // 2
    width = affine_matrix.shape[1]
    survivors = n * rows // 2
    lines = survivors // n
    chunk = width // 2
    near = survivors // 2
    owners = list(range(0, n, 2)) + list(range(1, n, 2))
    f32, bf16, i32 = jnp.float32, jnp.bfloat16, jnp.int32
    shape = jax.ShapeDtypeStruct
    dma = pltpu.SemaphoreType.DMA

    def trade(x, k):
        return lax.ppermute(x, "seq", [(i, i ^ k) for i in range(n)])

    def swap(x):
        return lax.ppermute(x, "ten", [(0, 1), (1, 0)])

    pair, *chosen = call(
        functools.partial(norm_select_kernel, n),
        "norm_select",
        (hidden, norm_gain.reshape(1, model), retained_lists.reshape(1, rows), keys, values),
        [shape((rows, 2 * keys.shape[1]), bf16)] + [shape((rows, half), bf16)] * n,
        4 * rows * model,
        limit=16,
        in_specs=[ANY] * 5,
        remote=5,
        scratch=[pltpu.VMEM((rows, model), bf16), pltpu.VMEM((1, model), f32), pltpu.VMEM((1, rows), i32), dma((8,))],
    )
    pair_other = trade(pair, 1)
    received = [chosen[0]] + [trade(chosen[k], k) for k in range(1, n)]

    matrix, queries, held, target = call(
        functools.partial(stage_kernel, n),
        "stage",
        (counts, affine_matrix, queries, pair, pair_other, *received[n // 2 :]),
        [shape(affine_matrix.shape, bf16), shape(queries.shape, bf16), shape((2 * rows, pair.shape[1]), bf16), shape((1, n * rows), i32)],
        0,
        limit=16,
        in_specs=[ANY] * 3 + [VMEM] * 2 + [ANY] * (n // 2),
        remote=3,
        scratch=[pltpu.SMEM(counts.shape, i32), dma((3,))],
    )
    order = [0, 1]
    mask = n // 2
    held_other = trade(held, mask)
    order = order + [k ^ mask for k in order]
    while mask > 2:
        mask //= 2
        held = jnp.concatenate([held, held_other], axis=0)
        held_other = trade(held, mask)
        order = order + [k ^ mask for k in order]

    (own,) = call(
        functools.partial(compact_kernel, n, owners),
        "compact",
        (target, *received),
        [shape((survivors, half), bf16)],
        2 * survivors * n * rows * half,
    )
    other = swap(own)

    products = [
        call(
            functools.partial(project_kernel, c * chunk),
            "project",
            (own, other, matrix),
            [shape((near, chunk), f32), shape((near, chunk), bf16)],
            4 * survivors * half * chunk,
        )
        for c in range(2)
    ]
    context, columns = call(
        functools.partial(attention_kernel, n, kv_heads, order, owners),
        "attention",
        (queries, held, held_other, products[1][1]),
        [shape(queries.shape, f32), shape((n, rows), f32)],
        4 * rows * n * rows * queries.shape[1],
        limit=32,
        in_specs=[VMEM] * 3 + [ANY],
    )
    first, far, *sent = call(
        pair_sum_kernel,
        "pair_sum",
        (products[0][0], trade(products[0][1], 1), products[1][1], columns),
        [shape((lines, chunk), f32), shape((near, chunk), bf16)] + [shape((lines, chunk), bf16)] * (n // 2 - 1),
        near * chunk,
        in_specs=[VMEM] * 3 + [ANY],
    )
    parts = [first] + [trade(x, 2 * (i + 1)) for i, x in enumerate(sent)]
    far = trade(far, 1)

    columns = columns + swap(columns)
    done, last, own_columns, *sent = call(
        functools.partial(pair_sum_last_kernel, n),
        "pair_sum_last",
        (products[1][0], far, columns[: n // 2], trade(columns[n // 2 :], 1), *parts),
        [shape((lines, chunk), f32), shape((lines, chunk), f32), shape((1, rows), f32)] + [shape((lines, chunk + 2 * rows), bf16)] * (n // 2 - 1),
        near * chunk,
    )
    parts = [last] + [trade(x, 2 * (i + 1)) for i, x in enumerate(sent)]

    triples, scores = call(
        finish_kernel,
        "finish",
        (affine_offset_vector.reshape(1, width), done, own_columns, *parts),
        [shape((lines, width), f32), shape((1, rows), f32)],
        n * lines * width,
    )
    return (context, scores.reshape(rows), triples)


def solution(mesh):
    in_specs = (
        P(("grp", "seq"), "ten"),
        P(("grp", "seq"), "ten"),
        P(("grp", "seq"), "ten"),
        P(("grp", "seq"), None),
        P(),
        P(("grp", "seq")),
        P("grp"),
        P("seq", "ten"),
        P("ten"),
    )
    out_specs = (P(("grp", "seq"), "ten"), P(("grp", "seq")), P(("grp", "seq"), "ten"))
    return jax.shard_map(shards, mesh=mesh, in_specs=in_specs, out_specs=out_specs, check_vma=False)
```

time: 88.7 us -> 67.4 us (0.76)
  local copies, waits for them, and re-layouts: 8.27 us -> 0.04 us
  starting transfers between devices: 36 us -> 28.4 us
  waiting for transfers between devices: 31.4 us -> 28.5 us
  Pallas kernels: 11.2 us -> 9.55 us
    unnamed x18 -> x3, local copies, waits for them, and re-layouts: 8.24 us -> 0.02 us
    ppermute x21 -> x19, starting transfers between devices: 35.9 us -> 28.3 us  [trade(): return lax.ppermute(x, 'seq', [(i, i ^ k) for i in range(n)])]
    ppermute x21 -> x19, waiting for transfers between devices: 31.4 us -> 27.4 us  [trade(): return lax.ppermute(x, 'seq', [(i, i ^ k) for i in range(n)])]
    pallas_call x7 -> x9, Pallas kernels: 11.2 us -> 9.55 us  [call(): pl.pallas_call(body, out_shape=list(outputs), in_specs=in_specs or [VMEM]...]
    ppermute x2, waiting for transfers between devices: 0.01 us -> 1.17 us  [swap(): return lax.ppermute(x, 'ten', [(0, 1), (1, 0)])]
  transfers between devices with their start and end apart: 23 -> 21, of which waited for: 11 -> 10; matrix products, arithmetic and copies ran while one was open for 1% -> 0% of each run, Pallas kernels for 10% -> 10%
where the time goes in v3:
time: 67.4 us; the launch traced here: 67.3 us
  waiting for transfers between devices  28.5 us (42%)
  starting transfers between devices  28.4 us (42%)
  Pallas kernels  9.55 us (14%)
  between operations  0.76 us (1%)
    ppermute x19, starting transfers between devices, trade(): return lax.ppermute(x, 'seq', [(i, i ^ k) for i in range(n)])  28.3 us
    ppermute x19, waiting for transfers between devices, trade(): return lax.ppermute(x, 'seq', [(i, i ^ k) for i in range(n)])  27.4 us
    pallas_call x9, Pallas kernels, call(): pl.pallas_call(body, out_shape=list(outputs), in_specs=in_specs or [VMEM]...  9.55 us
  transfers between devices with their start and end apart: 21, of which 10 were waited for; matrix products, arithmetic and copies ran while one was open for 0% of the time, Pallas kernels for 10%

profile of v3, /device:TPU:0, one launch (start us, length us, event | category | flops | bytes accessed | tf_op | source)
XLA Modules:
  0.0 67.3 jit_solution(3973360584843828824)
XLA Ops:
  0.6 1.7 %norm_select.1 = (bf16[64,512]{1,0:T(8,128)(2,1)S(1)}, bf16[64,512]{1,0:T(8,128)(2,1)S(1)}, bf16[64,512]{1,0:T(8,128)(2,1)S(1)}, bf16[64,512]{1,0:T(8,128)(2,1)S...) custom-call(bf16[64,8192]{1,0:T(8,128)(2,1)} %hidden_in.1, ...), custom_call_target="tpu_custom_call" | custom-call | flops 2097152 | bytes 1736960 | tf_op jit(solution)/shard_map/norm_select/pallas_call | solution.py:21
  2.4 3.0 %collective-permute-start = (bf16[64,512]{1,0:T(8,128)(2,1)S(1)}, bf16[64,512]{1,0:T(8,128)(2,1)S(1)}, u32[]{:S(2)}, u32[]{:S(2)}) collective-permute-start(bf16[64,512]{1,0:T(8,128)(2,1)S(1)} %get-tuple-element.35.pair), channel_id=1, source_target_pairs={{0,2},{2,0},{4,6},{6,4},{8,10},{10,8},{12,14},{14,12},{1,3},{3,1},... | collective-permute-start | bytes 196616 | tf_op jit(solution)/shard_map/ppermute | solution.py:229
  5.4 2.6 %collective-permute-start.1 = (bf16[64,512]{1,0:T(8,128)(2,1)S(1)}, bf16[64,512]{1,0:T(8,128)(2,1)S(1)}, u32[]{:S(2)}, u32[]{:S(2)}) collective-permute-start(bf16[64,512]{1,0:T(8,128)(2,1)S(1)} %get-tuple-element.36), channel_id=1, source_target_pairs={{0,8},{2,10},{4,12},{6,14},{8,0},{10,2},{12,4},{14,6},{1,9},{3,11}... | collective-permute-start | bytes 196616 | tf_op jit(solution)/shard_map/ppermute | solution.py:229
  8.0 0.0 collective-permute-start.2
  8.0 3.9 %collective-permute-start.3 = (bf16[64,512]{1,0:T(8,128)(2,1)S(1)}, bf16[64,512]{1,0:T(8,128)(2,1)S(1)}, u32[]{:S(2)}, u32[]{:S(2)}) collective-permute-start(bf16[64,512]{1,0:T(8,128)(2,1)S(1)} %get-tuple-element.38), channel_id=1, source_target_pairs={{0,12},{2,14},{4,8},{6,10},{8,4},{10,6},{12,0},{14,2},{1,13},{3,15... | collective-permute-start | bytes 196616 | tf_op jit(solution)/shard_map/ppermute | solution.py:229
  11.9 1.2 %collective-permute-start.4 = (bf16[64,512]{1,0:T(8,128)(2,1)S(1)}, bf16[64,512]{1,0:T(8,128)(2,1)S(1)}, u32[]{:S(2)}, u32[]{:S(2)}) collective-permute-start(bf16[64,512]{1,0:T(8,128)(2,1)S(1)} %get-tuple-element.39), channel_id=1, source_target_pairs={{0,14},{2,12},{4,10},{6,8},{8,6},{10,4},{12,2},{14,0},{1,15},{3,13... | collective-permute-start | bytes 196616 | tf_op jit(solution)/shard_map/ppermute | solution.py:229
  13.1 0.0 collective-permute-done.pair_other
  13.1 0.3 collective-permute-start.7
  13.4 0.0 collective-permute-done.1.refs_0_.refs_4_
  13.4 2.1 %collective-permute-start.8 = (bf16[64,512]{1,0:T(8,128)(2,1)S(1)}, bf16[64,512]{1,0:T(8,128)(2,1)S(1)}, u32[]{:S(2)}, u32[]{:S(2)}) collective-permute-start(bf16[64,512]{1,0:T(8,128)(2,1)S(1)} %get-tuple-element.45), channel_id=1, source_target_pairs={{0,4},{2,6},{4,0},{6,2},{8,12},{10,14},{12,8},{14,10},{1,5},{3,7},... | collective-permute-start | bytes 196616 | tf_op jit(solution)/shard_map/ppermute | solution.py:229
  15.5 2.3 %collective-permute-done.2.refs_1_.refs_5_ = bf16[64,512]{1,0:T(8,128)(2,1)S(1)} collective-permute-done((bf16[64,512]{1,0:T(8,128)(2,1)S(1)}, bf16[64,512]{1,0:T(8,128)(2,1)S(1)}, u32[]{:S(2)}, u32[]{:S(2)}) %collective-permute-start.2) | collective-permute-done | bytes 65568 | tf_op jit(solution)/shard_map/ppermute | solution.py:229
  17.8 0.0 collective-permute-start.9
  17.8 0.0 collective-permute-done.3.refs_2_.refs_6_
  17.8 1.2 %collective-permute-done.4.refs_3_.refs_7_ = bf16[64,512]{1,0:T(8,128)(2,1)S(1)} collective-permute-done((bf16[64,512]{1,0:T(8,128)(2,1)S(1)}, bf16[64,512]{1,0:T(8,128)(2,1)S(1)}, u32[]{:S(2)}, u32[]{:S(2)}) %collective-permute-start.4) | collective-permute-done | bytes 65568 | tf_op jit(solution)/shard_map/ppermute | solution.py:229
  19.0 2.5 %stage.1 = (bf16[1024,2560]{1,0:T(8,128)(2,1)S(1)}, bf16[64,2048]{1,0:T(8,128)(2,1)S(1)}, bf16[128,512]{1,0:T(8,128)(2,1)S(1)}, s32[1,512]{1,0:T(1,128)S(1)}) custom-call(s32[8]{0:T(128)} %counts_in.1, bf16[1024,2560]{1,0:T(8,128)(2,1)} %matrix_in.1, bf16[64,2048]{1,0:T(8,128)(2,1)} %queries_in.1, bf16[64,512]{1,0:T(8,128)(2,1)S(1)} %get-tuple-element.35.pair, ...), custom_call_target="tpu_custom_call" | custom-call | bytes 11536416 | tf_op jit(solution)/shard_map/stage/pallas_call | solution.py:21
  21.5 0.0 collective-permute-done.7.refs_1_
  21.5 0.0 collective-permute-done.8.refs_2_
  21.5 1.4 %collective-permute-done.9.refs_3_ = bf16[64,512]{1,0:T(8,128)(2,1)S(1)} collective-permute-done((bf16[64,512]{1,0:T(8,128)(2,1)S(1)}, bf16[64,512]{1,0:T(8,128)(2,1)S(1)}, u32[]{:S(2)}, u32[]{:S(2)}) %collective-permute-start.9) | collective-permute-done | bytes 65568 | tf_op jit(solution)/shard_map/ppermute | solution.py:229
  22.9 0.3 compact.1.own
  23.2 0.1 collective-permute-start.10
  23.3 1.9 %collective-permute-start.5 = (bf16[128,512]{1,0:T(8,128)(2,1)S(1)}, bf16[128,512]{1,0:T(8,128)(2,1)S(1)}, u32[]{:S(2)}, u32[]{:S(2)}) collective-permute-start(bf16[128,512]{1,0:T(8,128)(2,1)S(1)} %get-tuple-element.41), channel_id=1, source_target_pairs={{0,8},{2,10},{4,12},{6,14},{8,0},{10,2},{12,4},{14,6},{1,9},{3,11}... | collective-permute-start | bytes 393224 | tf_op jit(solution)/shard_map/ppermute | solution.py:229
  25.3 0.0 collective-permute-done.10.other
  25.3 1.0 %project.3 = (f32[128,1280]{1,0:T(8,128)S(1)}, bf16[128,1280]{1,0:T(8,128)(2,1)S(1)}) custom-call(bf16[256,512]{1,0:T(8,128)(2,1)S(1)} %compact.1.own, bf16[256,512]{1,0:T(8,128)(2,1)S(1)} %collective-permute-done.10.other, bf16[1024,2560]{1,0:T(8,128)(2,1)S(1)} %get-tuple-element.47.matrix), custom_call_target="tpu_custom_call" | custom-call | flops 671088640 | bytes 6750208 | tf_op jit(solution)/shard_map/project/pallas_call | solution.py:21
  26.3 0.0 copy-start
  26.3 2.3 %collective-permute-start.11 = (bf16[128,1280]{1,0:T(8,128)(2,1)S(1)}, bf16[128,1280]{1,0:T(8,128)(2,1)S(1)}, u32[]{:S(2)}, u32[]{:S(2)}) collective-permute-start(bf16[128,1280]{1,0:T(8,128)(2,1)S(1)} %get-tuple-element.52), channel_id=1, source_target_pairs={{0,2},{2,0},{4,6},{6,4},{8,10},{10,8},{12,14},{14,12},{1,3},{3,1},... | collective-permute-start | bytes 983048 | tf_op jit(solution)/shard_map/ppermute | solution.py:229
  28.6 4.4 %collective-permute-done.5 = bf16[128,512]{1,0:T(8,128)(2,1)S(1)} collective-permute-done((bf16[128,512]{1,0:T(8,128)(2,1)S(1)}, bf16[128,512]{1,0:T(8,128)(2,1)S(1)}, u32[]{:S(2)}, u32[]{:S(2)}) %collective-permute-start.5) | collective-permute-done | bytes 131104 | tf_op jit(solution)/shard_map/ppermute | solution.py:229
  33.0 0.1 collective-permute-start.6
  33.0 1.0 %project.2 = (f32[128,1280]{1,0:T(8,128)S(1)}, bf16[128,1280]{1,0:T(8,128)(2,1)S(1)}) custom-call(bf16[256,512]{1,0:T(8,128)(2,1)S(1)} %compact.1.own, bf16[256,512]{1,0:T(8,128)(2,1)S(1)} %collective-permute-done.10.other, bf16[1024,2560]{1,0:T(8,128)(2,1)S(1)} %get-tuple-element.47.matrix), custom_call_target="tpu_custom_call" | custom-call | flops 671088640 | bytes 6750208 | tf_op jit(solution)/shard_map/project/pallas_call | solution.py:21
  34.0 7.0 %collective-permute-done.6.held_b = bf16[256,512]{1,0:T(8,128)(2,1)S(1)} collective-permute-done((bf16[256,512]{1,0:T(8,128)(2,1)S(1)}, bf16[256,512]{1,0:T(8,128)(2,1)S(1)}, u32[]{:S(2)}, u32[]{:S(2)}) %collective-permute-start.6) | collective-permute-done | bytes 262176 | tf_op jit(solution)/shard_map/ppermute | solution.py:229
  41.0 2.0 %attention.1 = (f32[64,2048]{1,0:T(8,128)}, f32[8,64]{1,0:T(8,128)S(1)}) custom-call(bf16[64,2048]{1,0:T(8,128)(2,1)S(1)} %get-tuple-element.40.queries, bf16[256,512]{1,0:T(8,128)(2,1)S(1)} %constant_dynamic-update-slice_fusion.held_a, bf16[256,512]{1,0:T(8,128)(2,1)S(1)} %collective-permute-done.6.held_b, bf16[128,1280]{1,0:T(8,128)(2,1)S(1)} %get-tuple-element.48.after.next_in), custom_call_target="tpu_custom_call" | custom-call | flops 268435456 | bytes 1640448 | tf_op jit(solution)/shard_map/attention/pallas_call | solution.py:21
  43.0 0.0 collective-permute-done.11.received
  43.0 0.1 pair_sum.1
  43.1 1.6 %collective-permute-start.12 = (bf16[128,1280]{1,0:T(8,128)(2,1)S(1)}, bf16[128,1280]{1,0:T(8,128)(2,1)S(1)}, u32[]{:S(2)}, u32[]{:S(2)}) collective-permute-start(bf16[128,1280]{1,0:T(8,128)(2,1)S(1)} %get-tuple-element.54), channel_id=1, source_target_pairs={{0,2},{2,0},{4,6},{6,4},{8,10},{10,8},{12,14},{14,12},{1,3},{3,1},... | collective-permute-start | bytes 983048 | tf_op jit(solution)/shard_map/ppermute | solution.py:229
  44.7 0.0 collective-permute-start.13
  44.7 1.2 %collective-permute-done.13 = f32[8,64]{1,0:T(8,128)S(1)} collective-permute-done((f32[8,64]{1,0:T(8,128)S(1)}, f32[8,64]{1,0:T(8,128)S(1)}, u32[]{:S(2)}, u32[]{:S(2)}) %collective-permute-start.13) | collective-permute-done | bytes 2080 | tf_op jit(solution)/shard_map/ppermute | solution.py:232
  45.9 0.3 collective-permute-start.15
  46.2 2.8 %collective-permute-start.16 = (bf16[32,1280]{1,0:T(8,128)(2,1)S(1)}, bf16[32,1280]{1,0:T(8,128)(2,1)S(1)}, u32[]{:S(2)}, u32[]{:S(2)}) collective-permute-start(bf16[32,1280]{1,0:T(8,128)(2,1)S(1)} %get-tuple-element.57), channel_id=1, source_target_pairs={{0,8},{2,10},{4,12},{6,14},{8,0},{10,2},{12,4},{14,6},{1,9},{3,11}... | collective-permute-start | bytes 245768 | tf_op jit(solution)/shard_map/ppermute | solution.py:229
  49.0 1.3 %collective-permute-start.17 = (bf16[32,1280]{1,0:T(8,128)(2,1)S(1)}, bf16[32,1280]{1,0:T(8,128)(2,1)S(1)}, u32[]{:S(2)}, u32[]{:S(2)}) collective-permute-start(bf16[32,1280]{1,0:T(8,128)(2,1)S(1)} %get-tuple-element.58), channel_id=1, source_target_pairs={{0,12},{2,14},{4,8},{6,10},{8,4},{10,6},{12,0},{14,2},{1,13},{3,15... | collective-permute-start | bytes 245768 | tf_op jit(solution)/shard_map/ppermute | solution.py:229
  50.3 0.5 collective-permute-start.14
  50.8 3.1 %collective-permute-done.14.columns_other = f32[4,64]{1,0:T(4,128)S(1)} collective-permute-done((f32[4,64]{1,0:T(4,128)S(1)}, f32[4,64]{1,0:T(4,128)S(1)}, u32[]{:S(2)}, u32[]{:S(2)}) %collective-permute-start.14) | collective-permute-done | bytes 1056 | tf_op jit(solution)/shard_map/ppermute | solution.py:229
  53.9 1.8 %collective-permute-done.16.refs_2_ = bf16[32,1280]{1,0:T(8,128)(2,1)S(1)} collective-permute-done((bf16[32,1280]{1,0:T(8,128)(2,1)S(1)}, bf16[32,1280]{1,0:T(8,128)(2,1)S(1)}, u32[]{:S(2)}, u32[]{:S(2)}) %collective-permute-start.16) | collective-permute-done | bytes 81952 | tf_op jit(solution)/shard_map/ppermute | solution.py:229
  55.7 0.1 pair_sum_last.1
  55.9 1.7 %collective-permute-start.18 = (bf16[32,1408]{1,0:T(8,128)(2,1)S(1)}, bf16[32,1408]{1,0:T(8,128)(2,1)S(1)}, u32[]{:S(2)}, u32[]{:S(2)}) collective-permute-start(bf16[32,1408]{1,0:T(8,128)(2,1)S(1)} %get-tuple-element.62), channel_id=1, source_target_pairs={{0,4},{2,6},{4,0},{6,2},{8,12},{10,14},{12,8},{14,10},{1,5},{3,7},... | collective-permute-start | bytes 270344 | tf_op jit(solution)/shard_map/ppermute | solution.py:229
  57.6 1.4 %collective-permute-start.19 = (bf16[32,1408]{1,0:T(8,128)(2,1)S(1)}, bf16[32,1408]{1,0:T(8,128)(2,1)S(1)}, u32[]{:S(2)}, u32[]{:S(2)}) collective-permute-start(bf16[32,1408]{1,0:T(8,128)(2,1)S(1)} %get-tuple-element.63), channel_id=1, source_target_pairs={{0,8},{2,10},{4,12},{6,14},{8,0},{10,2},{12,4},{14,6},{1,9},{3,11}... | collective-permute-start | bytes 270344 | tf_op jit(solution)/shard_map/ppermute | solution.py:229
  59.0 1.3 %collective-permute-start.20 = (bf16[32,1408]{1,0:T(8,128)(2,1)S(1)}, bf16[32,1408]{1,0:T(8,128)(2,1)S(1)}, u32[]{:S(2)}, u32[]{:S(2)}) collective-permute-start(bf16[32,1408]{1,0:T(8,128)(2,1)S(1)} %get-tuple-element.64), channel_id=1, source_target_pairs={{0,12},{2,14},{4,8},{6,10},{8,4},{10,6},{12,0},{14,2},{1,13},{3,15... | collective-permute-start | bytes 270344 | tf_op jit(solution)/shard_map/ppermute | solution.py:229
  60.3 0.3 collective-permute-done.18.refs_0_
  60.6 5.9 %collective-permute-done.19.refs_1_ = bf16[32,1408]{1,0:T(8,128)(2,1)S(1)} collective-permute-done((bf16[32,1408]{1,0:T(8,128)(2,1)S(1)}, bf16[32,1408]{1,0:T(8,128)(2,1)S(1)}, u32[]{:S(2)}, u32[]{:S(2)}) %collective-permute-start.19) | collective-permute-done | bytes 90144 | tf_op jit(solution)/shard_map/ppermute | solution.py:229
  66.5 0.8 %finish.1 = (f32[32,2560]{1,0:T(8,128)}, f32[1,64]{1,0:T(1,128)}) custom-call(f32[1,2560]{1,0:T(1,128)S(1)} %reshape.20.bias, f32[32,1280]{1,0:T(8,128)S(1)} %get-tuple-element.59.done, f32[1,64]{1,0:T(1,128)S(1)} %get-tuple-element.60.own_columns, f32[32,1280]{1,0:T(8,128)S(1)} %get-tuple-element.61.own, ...), custom_call_target="tpu_custom_call" | custom-call | flops 655360 | bytes 936448 | tf_op jit(solution)/shard_map/finish/pallas_call | solution.py:21
  (10 shorter events, 0.0 us)
Async XLA Ops:
  2.4 10.7 %collective-permute-start = (bf16[64,512]{1,0:T(8,128)(2,1)S(1)}, bf16[64,512]{1,0:T(8,128)(2,1)S(1)}, u32[]{:S(2)}, u32[]{:S(2)}) collective-permute-start(bf16[64,512]{1,0:T(8,128)(2,1)S(1)} %get-tuple-element.35.pair), channel_id=1, source_target_pairs={{0,2},{2,0},{4,6},{6,4},{8,10},{10,8},{12,14},{14,12},{1,3},{3,1},... | collective-permute-start | bytes 196616 | tf_op jit(solution)/shard_map/ppermute | solution.py:229
  5.4 8.0 %collective-permute-start.1 = (bf16[64,512]{1,0:T(8,128)(2,1)S(1)}, bf16[64,512]{1,0:T(8,128)(2,1)S(1)}, u32[]{:S(2)}, u32[]{:S(2)}) collective-permute-start(bf16[64,512]{1,0:T(8,128)(2,1)S(1)} %get-tuple-element.36), channel_id=1, source_target_pairs={{0,8},{2,10},{4,12},{6,14},{8,0},{10,2},{12,4},{14,6},{1,9},{3,11}... | collective-permute-start | bytes 196616 | tf_op jit(solution)/shard_map/ppermute | solution.py:229
  8.0 9.8 %collective-permute-start.2 = (bf16[64,512]{1,0:T(8,128)(2,1)S(1)}, bf16[64,512]{1,0:T(8,128)(2,1)S(1)}, u32[]{:S(2)}, u32[]{:S(2)}) collective-permute-start(bf16[64,512]{1,0:T(8,128)(2,1)S(1)} %get-tuple-element.37), channel_id=1, source_target_pairs={{0,10},{2,8},{4,14},{6,12},{8,2},{10,0},{12,6},{14,4},{1,11},{3,9}... | collective-permute-start | bytes 196616 | tf_op jit(solution)/shard_map/ppermute | solution.py:229
  8.0 9.8 %collective-permute-start.3 = (bf16[64,512]{1,0:T(8,128)(2,1)S(1)}, bf16[64,512]{1,0:T(8,128)(2,1)S(1)}, u32[]{:S(2)}, u32[]{:S(2)}) collective-permute-start(bf16[64,512]{1,0:T(8,128)(2,1)S(1)} %get-tuple-element.38), channel_id=1, source_target_pairs={{0,12},{2,14},{4,8},{6,10},{8,4},{10,6},{12,0},{14,2},{1,13},{3,15... | collective-permute-start | bytes 196616 | tf_op jit(solution)/shard_map/ppermute | solution.py:229
  11.9 7.1 %collective-permute-start.4 = (bf16[64,512]{1,0:T(8,128)(2,1)S(1)}, bf16[64,512]{1,0:T(8,128)(2,1)S(1)}, u32[]{:S(2)}, u32[]{:S(2)}) collective-permute-start(bf16[64,512]{1,0:T(8,128)(2,1)S(1)} %get-tuple-element.39), channel_id=1, source_target_pairs={{0,14},{2,12},{4,10},{6,8},{8,6},{10,4},{12,2},{14,0},{1,15},{3,13... | collective-permute-start | bytes 196616 | tf_op jit(solution)/shard_map/ppermute | solution.py:229
  13.1 8.4 %collective-permute-start.7 = (bf16[64,512]{1,0:T(8,128)(2,1)S(1)}, bf16[64,512]{1,0:T(8,128)(2,1)S(1)}, u32[]{:S(2)}, u32[]{:S(2)}) collective-permute-start(bf16[64,512]{1,0:T(8,128)(2,1)S(1)} %get-tuple-element.44), channel_id=1, source_target_pairs={{0,2},{2,0},{4,6},{6,4},{8,10},{10,8},{12,14},{14,12},{1,3},{3,1},... | collective-permute-start | bytes 196616 | tf_op jit(solution)/shard_map/ppermute | solution.py:229
  13.4 8.1 %collective-permute-start.8 = (bf16[64,512]{1,0:T(8,128)(2,1)S(1)}, bf16[64,512]{1,0:T(8,128)(2,1)S(1)}, u32[]{:S(2)}, u32[]{:S(2)}) collective-permute-start(bf16[64,512]{1,0:T(8,128)(2,1)S(1)} %get-tuple-element.45), channel_id=1, source_target_pairs={{0,4},{2,6},{4,0},{6,2},{8,12},{10,14},{12,8},{14,10},{1,5},{3,7},... | collective-permute-start | bytes 196616 | tf_op jit(solution)/shard_map/ppermute | solution.py:229
  17.8 5.2 %collective-permute-start.9 = (bf16[64,512]{1,0:T(8,128)(2,1)S(1)}, bf16[64,512]{1,0:T(8,128)(2,1)S(1)}, u32[]{:S(2)}, u32[]{:S(2)}) collective-permute-start(bf16[64,512]{1,0:T(8,128)(2,1)S(1)} %get-tuple-element.46), channel_id=1, source_target_pairs={{0,6},{2,4},{4,2},{6,0},{8,14},{10,12},{12,10},{14,8},{1,7},{3,5},... | collective-permute-start | bytes 196616 | tf_op jit(solution)/shard_map/ppermute | solution.py:229
  23.2 2.0 %collective-permute-start.10 = (bf16[256,512]{1,0:T(8,128)(2,1)S(1)}, bf16[256,512]{1,0:T(8,128)(2,1)S(1)}, u32[]{:S(2)}, u32[]{:S(2)}) collective-permute-start(bf16[256,512]{1,0:T(8,128)(2,1)S(1)} %compact.1.own), channel_id=1, source_target_pairs={{0,1},{1,0},{2,3},{3,2},{4,5},{5,4},{6,7},{7,6},{8,9},{9,8},{10,11... | collective-permute-start | bytes 786440 | tf_op jit(solution)/shard_map/ppermute | solution.py:232
  23.3 9.6 %collective-permute-start.5 = (bf16[128,512]{1,0:T(8,128)(2,1)S(1)}, bf16[128,512]{1,0:T(8,128)(2,1)S(1)}, u32[]{:S(2)}, u32[]{:S(2)}) collective-permute-start(bf16[128,512]{1,0:T(8,128)(2,1)S(1)} %get-tuple-element.41), channel_id=1, source_target_pairs={{0,8},{2,10},{4,12},{6,14},{8,0},{10,2},{12,4},{14,6},{1,9},{3,11}... | collective-permute-start | bytes 393224 | tf_op jit(solution)/shard_map/ppermute | solution.py:229
  26.3 34.0 %copy-start = (f32[2560]{0:T(1024)S(1)}, f32[2560]{0:T(1024)}, u32[]{:S(2)}) copy-start(f32[2560]{0:T(1024)} %param.17) | copy-start | bytes 30724
  26.3 16.7 %collective-permute-start.11 = (bf16[128,1280]{1,0:T(8,128)(2,1)S(1)}, bf16[128,1280]{1,0:T(8,128)(2,1)S(1)}, u32[]{:S(2)}, u32[]{:S(2)}) collective-permute-start(bf16[128,1280]{1,0:T(8,128)(2,1)S(1)} %get-tuple-element.52), channel_id=1, source_target_pairs={{0,2},{2,0},{4,6},{6,4},{8,10},{10,8},{12,14},{14,12},{1,3},{3,1},... | collective-permute-start | bytes 983048 | tf_op jit(solution)/shard_map/ppermute | solution.py:229
  33.0 8.1 %collective-permute-start.6 = (bf16[256,512]{1,0:T(8,128)(2,1)S(1)}, bf16[256,512]{1,0:T(8,128)(2,1)S(1)}, u32[]{:S(2)}, u32[]{:S(2)}) collective-permute-start(bf16[256,512]{1,0:T(8,128)(2,1)S(1)} %constant_dynamic-update-slice_fusion.held_a), channel_id=1, source_target_pairs={{0,4},{2,6},{4,0},{6,2},{8,12},{10,14},{12,8},{14,10},{1,5},{3,7},... | collective-permute-start | bytes 786440 | tf_op jit(solution)/shard_map/ppermute | solution.py:229
  43.1 12.6 %collective-permute-start.12 = (bf16[128,1280]{1,0:T(8,128)(2,1)S(1)}, bf16[128,1280]{1,0:T(8,128)(2,1)S(1)}, u32[]{:S(2)}, u32[]{:S(2)}) collective-permute-start(bf16[128,1280]{1,0:T(8,128)(2,1)S(1)} %get-tuple-element.54), channel_id=1, source_target_pairs={{0,2},{2,0},{4,6},{6,4},{8,10},{10,8},{12,14},{14,12},{1,3},{3,1},... | collective-permute-start | bytes 983048 | tf_op jit(solution)/shard_map/ppermute | solution.py:229
  44.7 1.2 %collective-permute-start.13 = (f32[8,64]{1,0:T(8,128)S(1)}, f32[8,64]{1,0:T(8,128)S(1)}, u32[]{:S(2)}, u32[]{:S(2)}) collective-permute-start(f32[8,64]{1,0:T(8,128)S(1)} %get-tuple-element.53.after), channel_id=1, source_target_pairs={{0,1},{1,0},{2,3},{3,2},{4,5},{5,4},{6,7},{7,6},{8,9},{9,8},{10,11... | collective-permute-start | bytes 6152 | tf_op jit(solution)/shard_map/ppermute | solution.py:232
  45.9 8.0 %collective-permute-start.15 = (bf16[32,1280]{1,0:T(8,128)(2,1)S(1)}, bf16[32,1280]{1,0:T(8,128)(2,1)S(1)}, u32[]{:S(2)}, u32[]{:S(2)}) collective-permute-start(bf16[32,1280]{1,0:T(8,128)(2,1)S(1)} %get-tuple-element.56), channel_id=1, source_target_pairs={{0,4},{2,6},{4,0},{6,2},{8,12},{10,14},{12,8},{14,10},{1,5},{3,7},... | collective-permute-start | bytes 245768 | tf_op jit(solution)/shard_map/ppermute | solution.py:229
  46.2 9.5 %collective-permute-start.16 = (bf16[32,1280]{1,0:T(8,128)(2,1)S(1)}, bf16[32,1280]{1,0:T(8,128)(2,1)S(1)}, u32[]{:S(2)}, u32[]{:S(2)}) collective-permute-start(bf16[32,1280]{1,0:T(8,128)(2,1)S(1)} %get-tuple-element.57), channel_id=1, source_target_pairs={{0,8},{2,10},{4,12},{6,14},{8,0},{10,2},{12,4},{14,6},{1,9},{3,11}... | collective-permute-start | bytes 245768 | tf_op jit(solution)/shard_map/ppermute | solution.py:229
  49.0 6.8 %collective-permute-start.17 = (bf16[32,1280]{1,0:T(8,128)(2,1)S(1)}, bf16[32,1280]{1,0:T(8,128)(2,1)S(1)}, u32[]{:S(2)}, u32[]{:S(2)}) collective-permute-start(bf16[32,1280]{1,0:T(8,128)(2,1)S(1)} %get-tuple-element.58), channel_id=1, source_target_pairs={{0,12},{2,14},{4,8},{6,10},{8,4},{10,6},{12,0},{14,2},{1,13},{3,15... | collective-permute-start | bytes 245768 | tf_op jit(solution)/shard_map/ppermute | solution.py:229
  50.3 3.6 %collective-permute-start.14 = (f32[4,64]{1,0:T(4,128)S(1)}, f32[4,64]{1,0:T(4,128)S(1)}, u32[]{:S(2)}, u32[]{:S(2)}) collective-permute-start(f32[4,64]{1,0:T(4,128)S(1)} %get-tuple-element.67), channel_id=1, source_target_pairs={{0,2},{2,0},{4,6},{6,4},{8,10},{10,8},{12,14},{14,12},{1,3},{3,1},... | collective-permute-start | bytes 3080 | tf_op jit(solution)/shard_map/ppermute | solution.py:229
  55.9 4.8 %collective-permute-start.18 = (bf16[32,1408]{1,0:T(8,128)(2,1)S(1)}, bf16[32,1408]{1,0:T(8,128)(2,1)S(1)}, u32[]{:S(2)}, u32[]{:S(2)}) collective-permute-start(bf16[32,1408]{1,0:T(8,128)(2,1)S(1)} %get-tuple-element.62), channel_id=1, source_target_pairs={{0,4},{2,6},{4,0},{6,2},{8,12},{10,14},{12,8},{14,10},{1,5},{3,7},... | collective-permute-start | bytes 270344 | tf_op jit(solution)/shard_map/ppermute | solution.py:229
  57.6 8.9 %collective-permute-start.19 = (bf16[32,1408]{1,0:T(8,128)(2,1)S(1)}, bf16[32,1408]{1,0:T(8,128)(2,1)S(1)}, u32[]{:S(2)}, u32[]{:S(2)}) collective-permute-start(bf16[32,1408]{1,0:T(8,128)(2,1)S(1)} %get-tuple-element.63), channel_id=1, source_target_pairs={{0,8},{2,10},{4,12},{6,14},{8,0},{10,2},{12,4},{14,6},{1,9},{3,11}... | collective-permute-start | bytes 270344 | tf_op jit(solution)/shard_map/ppermute | solution.py:229
  59.0 7.5 %collective-permute-start.20 = (bf16[32,1408]{1,0:T(8,128)(2,1)S(1)}, bf16[32,1408]{1,0:T(8,128)(2,1)S(1)}, u32[]{:S(2)}, u32[]{:S(2)}) collective-permute-start(bf16[32,1408]{1,0:T(8,128)(2,1)S(1)} %get-tuple-element.64), channel_id=1, source_target_pairs={{0,12},{2,14},{4,8},{6,10},{8,4},{10,6},{12,0},{14,2},{1,13},{3,15... | collective-permute-start | bytes 270344 | tf_op jit(solution)/shard_map/ppermute | solution.py:229

commit v4 on v3

--- a/solution.py
+++ b/solution.py
@@ -30,8 +30,7 @@
     )(*inputs)
 
 
-def norm_select_kernel(n, hidden_in, gain_in, kept_in, keys_in, values_in, pair, *refs):
-    outs, (hidden, gain, kept, sems) = refs[:n], refs[n:]
+def norm_select_kernel(n, hidden_in, gain_in, kept_in, keys_in, values_in, pair, out, hidden, gain, kept, sems):
     rows, width = hidden.shape
     block = width // n
     half = block // 2
@@ -52,7 +51,7 @@
     ]
     for load in loads:
         load.start()
-    s, t = lax.axis_index("seq"), lax.axis_index("ten")
+    t = lax.axis_index("ten")
     step = min(piece, 1024)
     total = jnp.zeros((rows, step), jnp.float32)
     for i in range(pieces):
@@ -65,16 +64,15 @@
         load.wait()
     selector = (kept[...] == lax.broadcasted_iota(jnp.int32, (rows, rows), 0)).astype(jnp.bfloat16)
     for k in range(n):
-        start = pl.multiple_of(lax.bitwise_xor(s, k) * block + t * half, half)
+        start = pl.multiple_of(k * block + t * half, half)
         columns = pl.ds(start, half)
         normed = (hidden[:, columns].astype(jnp.float32) * scale * gain[:, columns]).astype(jnp.bfloat16)
-        outs[k][...] = lax.dot_general(
+        out[k * rows : (k + 1) * rows] = lax.dot_general(
             selector, normed, (((0,), (0,)), ((), ())), preferred_element_type=jnp.float32
         ).astype(jnp.bfloat16)
 
 
-def stage_kernel(n, counts_in, matrix_in, queries_in, pair, pair_other, *refs):
-    matrix, queries, held, target, counts, sems = refs[n // 2 :]
+def stage_kernel(n, counts_in, matrix_in, queries_in, after, matrix, queries, target, counts, sems):
     loads = [
         pltpu.make_async_copy(counts_in, counts, sems.at[0]),
         pltpu.make_async_copy(matrix_in, matrix, sems.at[1]),
@@ -82,36 +80,31 @@
     ]
     for load in loads:
         load.start()
-    rows = pair.shape[0]
-    held[:rows] = pair[...]
-    held[rows:] = pair_other[...]
-    s = lax.axis_index("seq")
+    total = target.shape[1]
+    rows = total // n
     loads[0].wait()
-    slot_all = lax.broadcasted_iota(jnp.int32, (1, n * rows), 1)
-    found = jnp.full((1, n * rows), -1, jnp.int32)
-    for k in range(n):
-        source = lax.bitwise_xor(s, k)
-        begin = jnp.int32(0)
-        for i in range(n):
-            begin += jnp.where(i < source, counts[i], 0)
-        slot = slot_all - k * rows
+    slot_all = lax.broadcasted_iota(jnp.int32, (1, total), 1)
+    found = jnp.full((1, total), -1, jnp.int32)
+    begin = jnp.int32(0)
+    for source in range(n):
+        slot = slot_all - source * rows
         inside = (slot >= 0) & (slot < counts[source])
         found = jnp.where(inside, begin + slot, found)
+        begin += counts[source]
     target[...] = found
     for load in loads[1:]:
         load.wait()
 
 
-def compact_kernel(n, owners, target, *refs):
-    blocks, out = refs[:n], refs[n]
+def compact_kernel(n, target, received, out):
     lines = out.shape[0] // n
-    s = lax.axis_index("seq")
-    received = jnp.concatenate([b[...] for b in blocks], axis=0)
+    parity = lax.rem(lax.axis_index("seq"), 2)
     line = lax.broadcasted_iota(jnp.int32, (lines, received.shape[0]), 0)
+    owners = [2 * p + parity for p in range(n // 2)] + [2 * p + 1 - parity for p in range(n // 2)]
     pick = jnp.concatenate(
-        [(line + lax.bitwise_xor(s, k) * lines == target[...]).astype(jnp.float32) for k in owners], axis=0
+        [(line + owner * lines == target[...]).astype(jnp.float32) for owner in owners], axis=0
     ).astype(jnp.bfloat16)
-    out[...] = jnp.dot(pick, received, preferred_element_type=jnp.float32).astype(jnp.bfloat16)
+    out[...] = jnp.dot(pick, received[...], preferred_element_type=jnp.float32).astype(jnp.bfloat16)
 
 
 def project_kernel(first, own, other, matrix, near, far):
@@ -130,36 +123,43 @@
         far[:, j : j + tile] = part[lines:].astype(jnp.bfloat16)
 
 
-def pair_sum_kernel(kept, received, next_in, after, own, next_out, *outs):
+def own_rows(lines):
+    place = lax.div(lax.axis_index("seq"), 2)
+    return pl.ds(pl.multiple_of(place * lines, lines), lines)
+
+
+def pair_sum_kernel(kept, received, next_in, after, own, next_out, out):
+    mine = own_rows(own.shape[0])
+    own[...] = kept[mine] + received[mine].astype(jnp.float32)
+    out[...] = (kept[...] + received[...].astype(jnp.float32)).astype(jnp.bfloat16)
+    next_out[...] = next_in[...]
+
+
+def total_of(own, received, width):
     lines = own.shape[0]
-    own[...] = kept[:lines] + received[:lines].astype(jnp.float32)
-    for i, out in enumerate(outs):
-        at = slice((i + 1) * lines, (i + 2) * lines)
-        out[...] = (kept[at] + received[at].astype(jnp.float32)).astype(jnp.bfloat16)
-    next_out[...] = next_in[...]
-
-
-def total_of(own, received):
+    place = lax.div(lax.axis_index("seq"), 2)
     total = own[...]
-    for r in received:
-        total += r[...].astype(jnp.float32)
+    for p in range(received.shape[0] // lines):
+        block = received[p * lines : (p + 1) * lines, :width].astype(jnp.float32)
+        total += jnp.where(place == p, 0.0, block)
     return total
 
 
-def pair_sum_last_kernel(n, kept, received, columns, columns_other, *refs):
-    chunk_parts, (done, own, own_columns, *outs) = refs[: n // 2], refs[n // 2 :]
+def pair_sum_last_kernel(kept, received, columns, columns_other, first, arrived, done, own, own_columns, out):
     lines, width = own.shape
-    done[...] = total_of(chunk_parts[0], chunk_parts[1:])
     rows = columns.shape[1]
-    own[...] = kept[:lines] + received[:lines].astype(jnp.float32)
+    place = lax.div(lax.axis_index("seq"), 2)
+    done[...] = total_of(first, arrived, width)
+    mine = own_rows(lines)
+    own[...] = kept[mine] + received[mine].astype(jnp.float32)
     own_columns[...] = columns[:1] + columns_other[:1]
-    for i, out in enumerate(outs):
-        at = slice((i + 1) * lines, (i + 2) * lines)
-        out[:, :width] = (kept[at] + received[at].astype(jnp.float32)).astype(jnp.bfloat16)
-        total = columns[i + 1 : i + 2] + columns_other[i + 1 : i + 2]
+    out[:, :width] = (kept[...] + received[...].astype(jnp.float32)).astype(jnp.bfloat16)
+    for p in range(kept.shape[0] // lines):
+        at = pl.ds(lax.bitwise_xor(place, p), 1)
+        total = columns[at] + columns_other[at]
         head = total.astype(jnp.bfloat16).astype(jnp.float32)
         extra = jnp.concatenate([head, total - head], axis=1).astype(jnp.bfloat16)
-        out[:, width:] = jnp.broadcast_to(extra, (lines, 2 * rows))
+        out[p * lines : (p + 1) * lines, width:] = jnp.broadcast_to(extra, (lines, 2 * rows))
 
 
 def attention_kernel(n, kv_heads, order, owners, queries, held_a, held_b, after, context, columns):
@@ -197,16 +197,16 @@
         columns[i : i + 1, :] = sums[:, at * rows : (at + 1) * rows]
 
 
-def finish_kernel(bias, done, own_columns, own, *refs):
-    *received, out, scores = refs
-    width = own.shape[1]
+def finish_kernel(bias, done, own_columns, own, arrived, out, scores):
+    lines, width = own.shape
     rows = own_columns.shape[1]
     out[:, :width] = done[...] + bias[:, :width]
-    out[:, width:] = total_of(own, [r.at[:, :width] for r in received]) + bias[:, width:]
+    out[:, width:] = total_of(own, arrived, width) + bias[:, width:]
+    place = lax.div(lax.axis_index("seq"), 2)
     sums = own_columns[...]
-    for r in received:
-        extra = r[:16, width:].astype(jnp.float32)
-        sums += extra[:1, :rows] + extra[:1, rows:]
+    for p in range(arrived.shape[0] // lines):
+        extra = arrived[p * lines : p * lines + 16, width:].astype(jnp.float32)
+        sums += jnp.where(place == p, 0.0, extra[:1, :rows] + extra[:1, rows:])
     scores[...] = sums / QUERY_HEADS
 
 
@@ -228,14 +228,18 @@
     def trade(x, k):
         return lax.ppermute(x, "seq", [(i, i ^ k) for i in range(n)])
 
+    def spread(x):
+        groups = [[2 * p + parity for p in range(n // 2)] for parity in range(2)]
+        return lax.all_to_all(x, "seq", 0, 0, axis_index_groups=groups, tiled=True)
+
     def swap(x):
         return lax.ppermute(x, "ten", [(0, 1), (1, 0)])
 
-    pair, *chosen = call(
+    pair, chosen = call(
         functools.partial(norm_select_kernel, n),
         "norm_select",
         (hidden, norm_gain.reshape(1, model), retained_lists.reshape(1, rows), keys, values),
-        [shape((rows, 2 * keys.shape[1]), bf16)] + [shape((rows, half), bf16)] * n,
+        [shape((rows, 2 * keys.shape[1]), bf16), shape((n * rows, half), bf16)],
         4 * rows * model,
         limit=16,
         in_specs=[ANY] * 5,
@@ -243,20 +247,19 @@
         scratch=[pltpu.VMEM((rows, model), bf16), pltpu.VMEM((1, model), f32), pltpu.VMEM((1, rows), i32), dma((8,))],
     )
     pair_other = trade(pair, 1)
-    received = [chosen[0]] + [trade(chosen[k], k) for k in range(1, n)]
-
-    matrix, queries, held, target = call(
+    received = lax.all_to_all(chosen, "seq", 0, 0, tiled=True)
+
+    matrix, queries, target = call(
         functools.partial(stage_kernel, n),
         "stage",
-        (counts, affine_matrix, queries, pair, pair_other, *received[n // 2 :]),
-        [shape(affine_matrix.shape, bf16), shape(queries.shape, bf16), shape((2 * rows, pair.shape[1]), bf16), shape((1, n * rows), i32)],
+        (counts, affine_matrix, queries, pair_other),
+        [shape(affine_matrix.shape, bf16), shape(queries.shape, bf16), shape((1, n * rows), i32)],
         0,
-        limit=16,
-        in_specs=[ANY] * 3 + [VMEM] * 2 + [ANY] * (n // 2),
+        in_specs=[ANY] * 4,
         remote=3,
         scratch=[pltpu.SMEM(counts.shape, i32), dma((3,))],
     )
-    order = [0, 1]
+    held, order = jnp.concatenate([pair, pair_other], axis=0), [0, 1]
     mask = n // 2
     held_other = trade(held, mask)
     order = order + [k ^ mask for k in order]
@@ -267,9 +270,9 @@
         order = order + [k ^ mask for k in order]
 
     (own,) = call(
-        functools.partial(compact_kernel, n, owners),
+        functools.partial(compact_kernel, n),
         "compact",
-        (target, *received),
+        (target, received),
         [shape((survivors, half), bf16)],
         2 * survivors * n * rows * half,
     )
@@ -294,31 +297,30 @@
         limit=32,
         in_specs=[VMEM] * 3 + [ANY],
     )
-    first, far, *sent = call(
+    first, far, sent = call(
         pair_sum_kernel,
         "pair_sum",
         (products[0][0], trade(products[0][1], 1), products[1][1], columns),
-        [shape((lines, chunk), f32), shape((near, chunk), bf16)] + [shape((lines, chunk), bf16)] * (n // 2 - 1),
+        [shape((lines, chunk), f32), shape((near, chunk), bf16), shape((near, chunk), bf16)],
         near * chunk,
         in_specs=[VMEM] * 3 + [ANY],
     )
-    parts = [first] + [trade(x, 2 * (i + 1)) for i, x in enumerate(sent)]
+    arrived = spread(sent)
     far = trade(far, 1)
 
     columns = columns + swap(columns)
-    done, last, own_columns, *sent = call(
-        functools.partial(pair_sum_last_kernel, n),
+    done, last, own_columns, sent = call(
+        pair_sum_last_kernel,
         "pair_sum_last",
-        (products[1][0], far, columns[: n // 2], trade(columns[n // 2 :], 1), *parts),
-        [shape((lines, chunk), f32), shape((lines, chunk), f32), shape((1, rows), f32)] + [shape((lines, chunk + 2 * rows), bf16)] * (n // 2 - 1),
+        (products[1][0], far, columns[: n // 2], trade(columns[n // 2 :], 1), first, arrived),
+        [shape((lines, chunk), f32), shape((lines, chunk), f32), shape((1, rows), f32), shape((near, chunk + 2 * rows), bf16)],
         near * chunk,
     )
-    parts = [last] + [trade(x, 2 * (i + 1)) for i, x in enumerate(sent)]
 
     triples, scores = call(
         finish_kernel,
         "finish",
-        (affine_offset_vector.reshape(1, width), done, own_columns, *parts),
+        (affine_offset_vector.reshape(1, width), done, own_columns, last, spread(sent)),
         [shape((lines, width), f32), shape((1, rows), f32)],
         n * lines * width,
     )

time: 67.4 us -> 74 us (1.098)
  starting transfers between devices: 28.4 us -> 20.5 us
  waiting for transfers between devices: 28.5 us -> 35.6 us
  local copies, waits for them, and re-layouts: 0.04 us -> 4.87 us
  Pallas kernels: 9.55 us -> 11.9 us
    ppermute x19 -> x6, starting transfers between devices: 28.3 us -> 5.93 us  [trade(): return lax.ppermute(x, 'seq', [(i, i ^ k) for i in range(n)])]
    all_to_all x0 -> x3, starting transfers between devices: none -> 14.5 us  [the longest x1 7.3 us: shards(): received = lax.all_to_all(chosen, 'seq', 0, 0, tiled=True)]
    all_to_all x0 -> x3, waiting for transfers between devices: none -> 12.1 us  [the longest x2 9.96 us: spread(): return lax.all_to_all(x, 'seq', 0, 0, axis_index_groups=groups, tiled=True)]
    ppermute x19 -> x6, waiting for transfers between devices: 27.4 us -> 21 us  [trade(): return lax.ppermute(x, 'seq', [(i, i ^ k) for i in range(n)])]
    unnamed x3 -> x8, local copies, waits for them, and re-layouts: 0.02 us -> 4.85 us
    pallas_call x9, Pallas kernels: 9.55 us -> 11.9 us  [call(): pl.pallas_call(body, out_shape=list(outputs), in_specs=in_specs or [VMEM]...]
    ppermute x2, waiting for transfers between devices: 1.17 us -> 2.43 us  [swap(): return lax.ppermute(x, 'ten', [(0, 1), (1, 0)])]
  transfers between devices with their start and end apart: 21 -> 11, of which waited for: 10 -> 9; matrix products, arithmetic and copies ran while one was open for 0% -> 0% of each run, Pallas kernels for 10% -> 9%
where the time goes in v4:
time: 74 us; the launch traced here: 73.6 us
  waiting for transfers between devices  35.6 us (48%)
  starting transfers between devices  20.5 us (28%)
  Pallas kernels  11.9 us (16%)
  local copies, waits for them, and re-layouts  4.87 us (7%)
  between operations  0.74 us (1%)
    ppermute x6, waiting for transfers between devices, trade(): return lax.ppermute(x, 'seq', [(i, i ^ k) for i in range(n)])  21 us
    pallas_call x9, Pallas kernels, call(): pl.pallas_call(body, out_shape=list(outputs), in_specs=in_specs or [VMEM]...  11.9 us
    all_to_all x2, waiting for transfers between devices, spread(): return lax.all_to_all(x, 'seq', 0, 0, axis_index_groups=groups, tiled=True)  9.96 us
    all_to_all x1, starting transfers between devices, shards(): received = lax.all_to_all(chosen, 'seq', 0, 0, tiled=True)  7.3 us
    all_to_all x2, starting transfers between devices, spread(): return lax.all_to_all(x, 'seq', 0, 0, axis_index_groups=groups, tiled=True)  7.21 us
    ppermute x6, starting transfers between devices, trade(): return lax.ppermute(x, 'seq', [(i, i ^ k) for i in range(n)])  5.93 us
    unnamed x8, local copies, waits for them, and re-layouts  4.85 us
    ppermute x2, waiting for transfers between devices, swap(): return lax.ppermute(x, 'ten', [(0, 1), (1, 0)])  2.43 us
  transfers between devices with their start and end apart: 11, of which 9 were waited for; matrix products, arithmetic and copies ran while one was open for 0% of the time, Pallas kernels for 9%

profile of v4, /device:TPU:0, one launch (start us, length us, event | category | flops | bytes accessed | tf_op | source)
XLA Modules:
  0.0 73.6 jit_solution(11477402095747145705)
XLA Ops:
  0.6 2.5 %norm_select.1 = (bf16[64,512]{1,0:T(8,128)(2,1)S(1)}, bf16[512,512]{1,0:T(8,128)(2,1)}) custom-call(bf16[64,8192]{1,0:T(8,128)(2,1)} %hidden_in.1, f32[1,8192]{1,0:T(1,128)} %bitcast.12, s32[1,64]{1,0:T(1,128)} %bitcast.13, bf16[64,256]{1,0:T(8,128)(2,1)} %keys_in.1, bf16[64,256]{1,0:T(8,128)(2,1)} %values_in.1), custom_call_target="tpu_custom_call" | custom-call | flops 2097152 | bytes 1736960 | tf_op jit(solution)/shard_map/norm_select/pallas_call | solution.py:21
  3.2 7.3 %all-to-all-start = ((bf16[8,64,512]{2,1,0:T(8,128)(2,1)}), bf16[8,64,512]{2,1,0:T(8,128)(2,1)S(1)}, u32[]{:S(2)}, u32[]{:S(2)}) async-start(bf16[8,64,512]{2,1,0:T(8,128)(2,1)} %bitcast.2), calls=%async_computation | async-start | bytes 1048576 | tf_op jit(solution)/shard_map/all_to_all | solution.py:250
  10.5 2.0 %collective-permute-start = (bf16[64,512]{1,0:T(8,128)(2,1)S(1)}, bf16[64,512]{1,0:T(8,128)(2,1)S(1)}, u32[]{:S(2)}, u32[]{:S(2)}) collective-permute-start(bf16[64,512]{1,0:T(8,128)(2,1)S(1)} %get-tuple-element.23), channel_id=1, source_target_pairs={{0,2},{2,0},{4,6},{6,4},{8,10},{10,8},{12,14},{14,12},{1,3},{3,1},... | collective-permute-start | bytes 196616 | tf_op jit(solution)/shard_map/ppermute | solution.py:229
  12.5 5.4 %collective-permute-done.after = bf16[64,512]{1,0:T(8,128)(2,1)S(1)} collective-permute-done((bf16[64,512]{1,0:T(8,128)(2,1)S(1)}, bf16[64,512]{1,0:T(8,128)(2,1)S(1)}, u32[]{:S(2)}, u32[]{:S(2)}) %collective-permute-start) | collective-permute-done | bytes 65568 | tf_op jit(solution)/shard_map/ppermute | solution.py:229
  17.9 2.5 %stage.1 = (bf16[1024,2560]{1,0:T(8,128)(2,1)S(1)}, bf16[64,2048]{1,0:T(8,128)(2,1)S(1)}, s32[1,512]{1,0:T(1,128)S(1)}) custom-call(s32[8]{0:T(128)} %counts_in.1, bf16[1024,2560]{1,0:T(8,128)(2,1)} %matrix_in.1, bf16[64,2048]{1,0:T(8,128)(2,1)} %queries_in.1, bf16[64,512]{1,0:T(8,128)(2,1)S(1)} %collective-permute-done.after), custom_call_target="tpu_custom_call" | custom-call | bytes 11077664 | tf_op jit(solution)/shard_map/stage/pallas_call | solution.py:21
  20.4 0.0 copy-start
  20.5 2.3 %copy-done = bf16[1024,2560]{1,0:T(8,128)(2,1)} copy-done((bf16[1024,2560]{1,0:T(8,128)(2,1)}, bf16[1024,2560]{1,0:T(8,128)(2,1)S(1)}, u32[]{:S(2)}) %copy-start) | copy-done | bytes 5242904
  22.8 2.2 %all-to-all-done = bf16[8,64,512]{2,1,0:T(8,128)(2,1)S(1)} async-done(((bf16[8,64,512]{2,1,0:T(8,128)(2,1)}), bf16[8,64,512]{2,1,0:T(8,128)(2,1)S(1)}, u32[]{:S(2)}, u32[]{:S(2)}) %all-to-all-start) | async-done | bytes 524320 | tf_op jit(solution)/shard_map/all_to_all | solution.py:250
  25.0 0.3 compact.1.own
  25.3 0.1 collective-permute-start.3
  25.4 0.2 collective-permute-start.1
  25.6 1.3 %collective-permute-done.3.other = bf16[256,512]{1,0:T(8,128)(2,1)S(1)} collective-permute-done((bf16[256,512]{1,0:T(8,128)(2,1)S(1)}, bf16[256,512]{1,0:T(8,128)(2,1)S(1)}, u32[]{:S(2)}, u32[]{:S(2)}) %collective-permute-start.3) | collective-permute-done | bytes 262176 | tf_op jit(solution)/shard_map/ppermute | solution.py:236
  26.9 0.0 copy-start.1
  26.9 2.5 %copy-done.1 = bf16[1024,2560]{1,0:T(8,128)(2,1)S(1)} copy-done((bf16[1024,2560]{1,0:T(8,128)(2,1)S(1)}, bf16[1024,2560]{1,0:T(8,128)(2,1)}, u32[]{:S(2)}) %copy-start.1) | copy-done | bytes 5242904
  29.4 1.0 %project.3 = (f32[128,1280]{1,0:T(8,128)S(1)}, bf16[128,1280]{1,0:T(8,128)(2,1)S(1)}) custom-call(bf16[256,512]{1,0:T(8,128)(2,1)S(1)} %compact.1.own, bf16[256,512]{1,0:T(8,128)(2,1)S(1)} %collective-permute-done.3.other, bf16[1024,2560]{1,0:T(8,128)(2,1)S(1)} %copy-done.1), custom_call_target="tpu_custom_call" | custom-call | flops 671088640 | bytes 6750208 | tf_op jit(solution)/shard_map/project/pallas_call | solution.py:21
  30.4 1.5 %collective-permute-start.4 = (bf16[128,1280]{1,0:T(8,128)(2,1)S(1)}, bf16[128,1280]{1,0:T(8,128)(2,1)S(1)}, u32[]{:S(2)}, u32[]{:S(2)}) collective-permute-start(bf16[128,1280]{1,0:T(8,128)(2,1)S(1)} %get-tuple-element.32), channel_id=1, source_target_pairs={{0,2},{2,0},{4,6},{6,4},{8,10},{10,8},{12,14},{14,12},{1,3},{3,1},... | collective-permute-start | bytes 983048 | tf_op jit(solution)/shard_map/ppermute | solution.py:229
  31.9 3.2 %collective-permute-done.1 = bf16[128,512]{1,0:T(8,128)(2,1)S(1)} collective-permute-done((bf16[128,512]{1,0:T(8,128)(2,1)S(1)}, bf16[128,512]{1,0:T(8,128)(2,1)S(1)}, u32[]{:S(2)}, u32[]{:S(2)}) %collective-permute-start.1) | collective-permute-done | bytes 131104 | tf_op jit(solution)/shard_map/ppermute | solution.py:229
  35.1 0.0 copy-start.2
  35.1 0.1 collective-permute-start.2
  35.1 1.0 %project.2 = (f32[128,1280]{1,0:T(8,128)S(1)}, bf16[128,1280]{1,0:T(8,128)(2,1)S(1)}) custom-call(bf16[256,512]{1,0:T(8,128)(2,1)S(1)} %compact.1.own, bf16[256,512]{1,0:T(8,128)(2,1)S(1)} %collective-permute-done.3.other, bf16[1024,2560]{1,0:T(8,128)(2,1)S(1)} %copy-done.1), custom_call_target="tpu_custom_call" | custom-call | flops 671088640 | bytes 6750208 | tf_op jit(solution)/shard_map/project/pallas_call | solution.py:21
  36.1 7.0 %collective-permute-done.2.held_b = bf16[256,512]{1,0:T(8,128)(2,1)S(1)} collective-permute-done((bf16[256,512]{1,0:T(8,128)(2,1)S(1)}, bf16[256,512]{1,0:T(8,128)(2,1)S(1)}, u32[]{:S(2)}, u32[]{:S(2)}) %collective-permute-start.2) | collective-permute-done | bytes 262176 | tf_op jit(solution)/shard_map/ppermute | solution.py:229
  43.2 2.0 %attention.1 = (f32[64,2048]{1,0:T(8,128)}, f32[8,64]{1,0:T(8,128)S(1)}) custom-call(bf16[64,2048]{1,0:T(8,128)(2,1)S(1)} %get-tuple-element.24.queries, bf16[256,512]{1,0:T(8,128)(2,1)S(1)} %constant_dynamic-update-slice_fusion.held_a, bf16[256,512]{1,0:T(8,128)(2,1)S(1)} %collective-permute-done.2.held_b, bf16[128,1280]{1,0:T(8,128)(2,1)S(1)} %get-tuple-element.28.after.next_in), custom_call_target="tpu_custom_call" | custom-call | flops 268435456 | bytes 1640448 | tf_op jit(solution)/shard_map/attention/pallas_call | solution.py:21
  45.2 0.0 collective-permute-done.4.received
  45.2 0.8 %pair_sum.1 = (f32[32,1280]{1,0:T(8,128)S(1)}, bf16[128,1280]{1,0:T(8,128)(2,1)S(1)}, bf16[128,1280]{1,0:T(8,128)(2,1)}) custom-call(f32[128,1280]{1,0:T(8,128)S(1)} %get-tuple-element.31.kept, bf16[128,1280]{1,0:T(8,128)(2,1)S(1)} %collective-permute-done.4.received, bf16[128,1280]{1,0:T(8,128)(2,1)S(1)} %get-tuple-element.28.after.next_in, ...), custom_call_target="tpu_custom_call" | custom-call | flops 163840 | bytes 2131968 | tf_op jit(solution)/shard_map/pair_sum/pallas_call | solution.py:21
  46.0 3.5 %all-to-all-start.1 = ((bf16[4,32,1280]{2,1,0:T(8,128)(2,1)}), bf16[4,32,1280]{2,1,0:T(8,128)(2,1)S(1)}, u32[]{:S(2)}, u32[]{:S(2)}) async-start(bf16[4,32,1280]{2,1,0:T(8,128)(2,1)} %bitcast.4), calls=%async_computation.1 | async-start | bytes 655360 | tf_op jit(solution)/shard_map/all_to_all | solution.py:233
  49.4 1.0 %collective-permute-start.5 = (bf16[128,1280]{1,0:T(8,128)(2,1)S(1)}, bf16[128,1280]{1,0:T(8,128)(2,1)S(1)}, u32[]{:S(2)}, u32[]{:S(2)}) collective-permute-start(bf16[128,1280]{1,0:T(8,128)(2,1)S(1)} %get-tuple-element.34), channel_id=1, source_target_pairs={{0,2},{2,0},{4,6},{6,4},{8,10},{10,8},{12,14},{14,12},{1,3},{3,1},... | collective-permute-start | bytes 983048 | tf_op jit(solution)/shard_map/ppermute | solution.py:229
  50.4 0.0 collective-permute-start.6
  50.4 1.2 %collective-permute-done.6 = f32[8,64]{1,0:T(8,128)S(1)} collective-permute-done((f32[8,64]{1,0:T(8,128)S(1)}, f32[8,64]{1,0:T(8,128)S(1)}, u32[]{:S(2)}, u32[]{:S(2)}) %collective-permute-start.6) | collective-permute-done | bytes 2080 | tf_op jit(solution)/shard_map/ppermute | solution.py:236
  51.6 1.1 %collective-permute-start.7 = (f32[4,64]{1,0:T(4,128)S(1)}, f32[4,64]{1,0:T(4,128)S(1)}, u32[]{:S(2)}, u32[]{:S(2)}) collective-permute-start(f32[4,64]{1,0:T(4,128)S(1)} %get-tuple-element.43), channel_id=1, source_target_pairs={{0,2},{2,0},{4,6},{6,4},{8,10},{10,8},{12,14},{14,12},{1,3},{3,1},... | collective-permute-start | bytes 3080 | tf_op jit(solution)/shard_map/ppermute | solution.py:229
  52.7 5.4 %collective-permute-done.7.columns_other = f32[4,64]{1,0:T(4,128)S(1)} collective-permute-done((f32[4,64]{1,0:T(4,128)S(1)}, f32[4,64]{1,0:T(4,128)S(1)}, u32[]{:S(2)}, u32[]{:S(2)}) %collective-permute-start.7) | collective-permute-done | bytes 1056 | tf_op jit(solution)/shard_map/ppermute | solution.py:229
  58.1 0.0 collective-permute-done.5.received
  58.1 1.0 %all-to-all-done.1 = bf16[4,32,1280]{2,1,0:T(8,128)(2,1)S(1)} async-done(((bf16[4,32,1280]{2,1,0:T(8,128)(2,1)}), bf16[4,32,1280]{2,1,0:T(8,128)(2,1)S(1)}, u32[]{:S(2)}, u32[]{:S(2)}) %all-to-all-start.1) | async-done | bytes 327712 | tf_op jit(solution)/shard_map/all_to_all | solution.py:233
  59.1 0.9 %pair_sum_last.1 = (f32[32,1280]{1,0:T(8,128)S(1)}, f32[32,1280]{1,0:T(8,128)S(1)}, f32[1,64]{1,0:T(1,128)S(1)}, bf16[128,1408]{1,0:T(8,128)(2,1)}) custom-call(f32[128,1280]{1,0:T(8,128)S(1)} %get-tuple-element.30.kept, bf16[128,1280]{1,0:T(8,128)(2,1)S(1)} %collective-permute-done.5.received, f32[4,64]{1,0:T(4,128)S(1)} %get-tuple-element.44.columns, ...), custom_call_target="tpu_custom_call" | custom-call | flops 163840 | bytes 2164992 | tf_op jit(solution)/shard_map/pair_sum_last/pallas_call | solution.py:21
  60.0 3.8 %all-to-all-start.2 = ((bf16[4,32,1408]{2,1,0:T(8,128)(2,1)}), bf16[4,32,1408]{2,1,0:T(8,128)(2,1)S(1)}, u32[]{:S(2)}, u32[]{:S(2)}) async-start(bf16[4,32,1408]{2,1,0:T(8,128)(2,1)} %bitcast.6), calls=%async_computation.2 | async-start | bytes 720896 | tf_op jit(solution)/shard_map/all_to_all | solution.py:233
  63.8 0.0 copy-done.2
  63.8 9.0 %all-to-all-done.2 = bf16[4,32,1408]{2,1,0:T(8,128)(2,1)S(1)} async-done(((bf16[4,32,1408]{2,1,0:T(8,128)(2,1)}), bf16[4,32,1408]{2,1,0:T(8,128)(2,1)S(1)}, u32[]{:S(2)}, u32[]{:S(2)}) %all-to-all-start.2) | async-done | bytes 360480 | tf_op jit(solution)/shard_map/all_to_all | solution.py:233
  72.8 0.8 %finish.1 = (f32[32,2560]{1,0:T(8,128)}, f32[1,64]{1,0:T(1,128)}) custom-call(f32[1,2560]{1,0:T(1,128)S(1)} %reshape.26.bias, f32[32,1280]{1,0:T(8,128)S(1)} %get-tuple-element.37.done, f32[1,64]{1,0:T(1,128)S(1)} %get-tuple-element.38.own_columns, f32[32,1280]{1,0:T(8,128)S(1)} %get-tuple-element.39.own, bf16[128,1408]{1,0:T(8,128)(2,1)S(1)} %bitcast.10), custom_call_target="tpu_custom_call" | custom-call | flops 655360 | bytes 1026560 | tf_op jit(solution)/shard_map/finish/pallas_call | solution.py:21
  (7 shorter events, 0.0 us)
Async XLA Ops:
  3.2 21.8 %all-to-all-start = ((bf16[8,64,512]{2,1,0:T(8,128)(2,1)}), bf16[8,64,512]{2,1,0:T(8,128)(2,1)S(1)}, u32[]{:S(2)}, u32[]{:S(2)}) async-start(bf16[8,64,512]{2,1,0:T(8,128)(2,1)} %bitcast.2), calls=%async_computation | async-start | bytes 1048576 | tf_op jit(solution)/shard_map/all_to_all | solution.py:250
  10.5 7.4 %collective-permute-start = (bf16[64,512]{1,0:T(8,128)(2,1)S(1)}, bf16[64,512]{1,0:T(8,128)(2,1)S(1)}, u32[]{:S(2)}, u32[]{:S(2)}) collective-permute-start(bf16[64,512]{1,0:T(8,128)(2,1)S(1)} %get-tuple-element.23), channel_id=1, source_target_pairs={{0,2},{2,0},{4,6},{6,4},{8,10},{10,8},{12,14},{14,12},{1,3},{3,1},... | collective-permute-start | bytes 196616 | tf_op jit(solution)/shard_map/ppermute | solution.py:229
  20.4 2.3 %copy-start = (bf16[1024,2560]{1,0:T(8,128)(2,1)}, bf16[1024,2560]{1,0:T(8,128)(2,1)S(1)}, u32[]{:S(2)}) copy-start(bf16[1024,2560]{1,0:T(8,128)(2,1)S(1)} %get-tuple-element.27.matrix) | copy-start | bytes 15728644
  25.3 1.6 %collective-permute-start.3 = (bf16[256,512]{1,0:T(8,128)(2,1)S(1)}, bf16[256,512]{1,0:T(8,128)(2,1)S(1)}, u32[]{:S(2)}, u32[]{:S(2)}) collective-permute-start(bf16[256,512]{1,0:T(8,128)(2,1)S(1)} %compact.1.own), channel_id=1, source_target_pairs={{0,1},{1,0},{2,3},{3,2},{4,5},{5,4},{6,7},{7,6},{8,9},{9,8},{10,11... | collective-permute-start | bytes 786440 | tf_op jit(solution)/shard_map/ppermute | solution.py:236
  25.4 9.7 %collective-permute-start.1 = (bf16[128,512]{1,0:T(8,128)(2,1)S(1)}, bf16[128,512]{1,0:T(8,128)(2,1)S(1)}, u32[]{:S(2)}, u32[]{:S(2)}) collective-permute-start(bf16[128,512]{1,0:T(8,128)(2,1)S(1)} %pad_maximum_fusion), channel_id=1, source_target_pairs={{0,8},{2,10},{4,12},{6,14},{8,0},{10,2},{12,4},{14,6},{1,9},{3,11}... | collective-permute-start | bytes 393224 | tf_op jit(solution)/shard_map/ppermute | solution.py:229
  26.9 2.5 %copy-start.1 = (bf16[1024,2560]{1,0:T(8,128)(2,1)S(1)}, bf16[1024,2560]{1,0:T(8,128)(2,1)}, u32[]{:S(2)}) copy-start(bf16[1024,2560]{1,0:T(8,128)(2,1)} %copy-done) | copy-start | bytes 15728644
  30.4 14.8 %collective-permute-start.4 = (bf16[128,1280]{1,0:T(8,128)(2,1)S(1)}, bf16[128,1280]{1,0:T(8,128)(2,1)S(1)}, u32[]{:S(2)}, u32[]{:S(2)}) collective-permute-start(bf16[128,1280]{1,0:T(8,128)(2,1)S(1)} %get-tuple-element.32), channel_id=1, source_target_pairs={{0,2},{2,0},{4,6},{6,4},{8,10},{10,8},{12,14},{14,12},{1,3},{3,1},... | collective-permute-start | bytes 983048 | tf_op jit(solution)/shard_map/ppermute | solution.py:229
  35.1 28.7 %copy-start.2 = (f32[2560]{0:T(1024)S(1)}, f32[2560]{0:T(1024)}, u32[]{:S(2)}) copy-start(f32[2560]{0:T(1024)} %param.17) | copy-start | bytes 30724
  35.1 8.1 %collective-permute-start.2 = (bf16[256,512]{1,0:T(8,128)(2,1)S(1)}, bf16[256,512]{1,0:T(8,128)(2,1)S(1)}, u32[]{:S(2)}, u32[]{:S(2)}) collective-permute-start(bf16[256,512]{1,0:T(8,128)(2,1)S(1)} %constant_dynamic-update-slice_fusion.held_a), channel_id=1, source_target_pairs={{0,4},{2,6},{4,0},{6,2},{8,12},{10,14},{12,8},{14,10},{1,5},{3,7},... | collective-permute-start | bytes 786440 | tf_op jit(solution)/shard_map/ppermute | solution.py:229
  46.0 13.1 %all-to-all-start.1 = ((bf16[4,32,1280]{2,1,0:T(8,128)(2,1)}), bf16[4,32,1280]{2,1,0:T(8,128)(2,1)S(1)}, u32[]{:S(2)}, u32[]{:S(2)}) async-start(bf16[4,32,1280]{2,1,0:T(8,128)(2,1)} %bitcast.4), calls=%async_computation.1 | async-start | bytes 655360 | tf_op jit(solution)/shard_map/all_to_all | solution.py:233
  49.4 8.7 %collective-permute-start.5 = (bf16[128,1280]{1,0:T(8,128)(2,1)S(1)}, bf16[128,1280]{1,0:T(8,128)(2,1)S(1)}, u32[]{:S(2)}, u32[]{:S(2)}) collective-permute-start(bf16[128,1280]{1,0:T(8,128)(2,1)S(1)} %get-tuple-element.34), channel_id=1, source_target_pairs={{0,2},{2,0},{4,6},{6,4},{8,10},{10,8},{12,14},{14,12},{1,3},{3,1},... | collective-permute-start | bytes 983048 | tf_op jit(solution)/shard_map/ppermute | solution.py:229
  50.4 1.2 %collective-permute-start.6 = (f32[8,64]{1,0:T(8,128)S(1)}, f32[8,64]{1,0:T(8,128)S(1)}, u32[]{:S(2)}, u32[]{:S(2)}) collective-permute-start(f32[8,64]{1,0:T(8,128)S(1)} %get-tuple-element.33.after), channel_id=1, source_target_pairs={{0,1},{1,0},{2,3},{3,2},{4,5},{5,4},{6,7},{7,6},{8,9},{9,8},{10,11... | collective-permute-start | bytes 6152 | tf_op jit(solution)/shard_map/ppermute | solution.py:236
  51.6 6.5 %collective-permute-start.7 = (f32[4,64]{1,0:T(4,128)S(1)}, f32[4,64]{1,0:T(4,128)S(1)}, u32[]{:S(2)}, u32[]{:S(2)}) collective-permute-start(f32[4,64]{1,0:T(4,128)S(1)} %get-tuple-element.43), channel_id=1, source_target_pairs={{0,2},{2,0},{4,6},{6,4},{8,10},{10,8},{12,14},{14,12},{1,3},{3,1},... | collective-permute-start | bytes 3080 | tf_op jit(solution)/shard_map/ppermute | solution.py:229
  60.0 12.8 %all-to-all-start.2 = ((bf16[4,32,1408]{2,1,0:T(8,128)(2,1)}), bf16[4,32,1408]{2,1,0:T(8,128)(2,1)S(1)}, u32[]{:S(2)}, u32[]{:S(2)}) async-start(bf16[4,32,1408]{2,1,0:T(8,128)(2,1)} %bitcast.6), calls=%async_computation.2 | async-start | bytes 720896 | tf_op jit(solution)/shard_map/all_to_all | solution.py:233

commit v5 on v3

--- a/solution.py
+++ b/solution.py
@@ -73,8 +73,8 @@
         ).astype(jnp.bfloat16)
 
 
-def stage_kernel(n, counts_in, matrix_in, queries_in, pair, pair_other, *refs):
-    matrix, queries, held, target, counts, sems = refs[n // 2 :]
+def stage_kernel(n, counts_in, matrix_in, queries_in, *refs):
+    matrix, queries, target, counts, sems = refs[-5:]
     loads = [
         pltpu.make_async_copy(counts_in, counts, sems.at[0]),
         pltpu.make_async_copy(matrix_in, matrix, sems.at[1]),
@@ -82,9 +82,7 @@
     ]
     for load in loads:
         load.start()
-    rows = pair.shape[0]
-    held[:rows] = pair[...]
-    held[rows:] = pair_other[...]
+    rows = target.shape[1] // n
     s = lax.axis_index("seq")
     loads[0].wait()
     slot_all = lax.broadcasted_iota(jnp.int32, (1, n * rows), 1)
@@ -102,21 +100,25 @@
         load.wait()
 
 
-def compact_kernel(n, owners, target, *refs):
+def compact_kernel(n, target, *refs):
     blocks, out = refs[:n], refs[n]
     lines = out.shape[0] // n
     s = lax.axis_index("seq")
     received = jnp.concatenate([b[...] for b in blocks], axis=0)
     line = lax.broadcasted_iota(jnp.int32, (lines, received.shape[0]), 0)
     pick = jnp.concatenate(
-        [(line + lax.bitwise_xor(s, k) * lines == target[...]).astype(jnp.float32) for k in owners], axis=0
+        [(line + lax.bitwise_xor(s, k) * lines == target[...]).astype(jnp.float32) for k in range(n)], axis=0
     ).astype(jnp.bfloat16)
     out[...] = jnp.dot(pick, received, preferred_element_type=jnp.float32).astype(jnp.bfloat16)
 
 
-def project_kernel(first, own, other, matrix, near, far):
+def halving_order(n, masks):
+    return sorted(range(n), key=lambda k: [k & mask for mask in masks])
+
+
+def project_kernel(first, order, own, other, matrix, near, far):
     survivors, half = own.shape
-    lines = survivors // 2
+    lines = survivors // len(order)
     width = near.shape[1]
     t = lax.axis_index("ten")
     mine = pl.ds(pl.multiple_of(t * half, half), half)
@@ -126,43 +128,37 @@
         lanes = slice(first + j, first + j + tile)
         part = jnp.dot(own[...], matrix[mine, lanes], preferred_element_type=jnp.float32)
         part += jnp.dot(other[...], matrix[others, lanes], preferred_element_type=jnp.float32)
-        near[:, j : j + tile] = part[:lines]
-        far[:, j : j + tile] = part[lines:].astype(jnp.bfloat16)
-
-
-def pair_sum_kernel(kept, received, next_in, after, own, next_out, *outs):
-    lines = own.shape[0]
-    own[...] = kept[:lines] + received[:lines].astype(jnp.float32)
-    for i, out in enumerate(outs):
-        at = slice((i + 1) * lines, (i + 2) * lines)
-        out[...] = (kept[at] + received[at].astype(jnp.float32)).astype(jnp.bfloat16)
-    next_out[...] = next_in[...]
-
-
-def total_of(own, received):
-    total = own[...]
-    for r in received:
-        total += r[...].astype(jnp.float32)
-    return total
-
-
-def pair_sum_last_kernel(n, kept, received, columns, columns_other, *refs):
-    chunk_parts, (done, own, own_columns, *outs) = refs[: n // 2], refs[n // 2 :]
-    lines, width = own.shape
-    done[...] = total_of(chunk_parts[0], chunk_parts[1:])
-    rows = columns.shape[1]
-    own[...] = kept[:lines] + received[:lines].astype(jnp.float32)
-    own_columns[...] = columns[:1] + columns_other[:1]
-    for i, out in enumerate(outs):
-        at = slice((i + 1) * lines, (i + 2) * lines)
-        out[:, :width] = (kept[at] + received[at].astype(jnp.float32)).astype(jnp.bfloat16)
-        total = columns[i + 1 : i + 2] + columns_other[i + 1 : i + 2]
-        head = total.astype(jnp.bfloat16).astype(jnp.float32)
-        extra = jnp.concatenate([head, total - head], axis=1).astype(jnp.bfloat16)
-        out[:, width:] = jnp.broadcast_to(extra, (lines, 2 * rows))
-
-
-def attention_kernel(n, kv_heads, order, owners, queries, held_a, held_b, after, context, columns):
+        for i, k in enumerate(order):
+            block = part[k * lines : (k + 1) * lines]
+            if i < len(order) // 2:
+                near[i * lines : (i + 1) * lines, j : j + tile] = block
+            else:
+                i -= len(order) // 2
+                far[i * lines : (i + 1) * lines, j : j + tile] = block.astype(jnp.bfloat16)
+
+
+def hop_sum_kernel(kept, received, columns_in, keep, sent, columns):
+    rows = keep.shape[0]
+    columns[...] = columns_in[...]
+    total = kept[...] + received[...].astype(jnp.float32)
+    keep[...] = total[:rows]
+    sent[...] = total[rows:].astype(jnp.bfloat16)
+
+
+def hop_sum_both_kernel(*refs):
+    *parts, columns_in, keep, sent, columns = refs
+    columns[...] = columns_in[...]
+    count = len(parts) // 2
+    rows = keep.shape[0]
+    width = keep.shape[1] // count
+    for c in range(count):
+        lanes = slice(c * width, (c + 1) * width)
+        total = parts[c][...] + parts[count + c][...].astype(jnp.float32)
+        keep[:, lanes] = total[:rows]
+        sent[:, lanes] = total[rows:].astype(jnp.bfloat16)
+
+
+def attention_kernel(n, kv_heads, order, masks, queries, held_a, held_b, after, context, columns):
     rows = queries.shape[0]
     group = queries.shape[1] // (HEAD_SIZE * kv_heads)
     s = lax.axis_index("seq")
@@ -193,21 +189,12 @@
             context[:, h * HEAD_SIZE : (h + 1) * HEAD_SIZE] = mixed[i * rows : (i + 1) * rows]
         sums += jnp.sum(weights * inverse, axis=0, keepdims=True)
     for at, k in enumerate(order):
-        i = owners.index(k)
+        i = halving_order(n, masks).index(k)
         columns[i : i + 1, :] = sums[:, at * rows : (at + 1) * rows]
 
 
-def finish_kernel(bias, done, own_columns, own, *refs):
-    *received, out, scores = refs
-    width = own.shape[1]
-    rows = own_columns.shape[1]
-    out[:, :width] = done[...] + bias[:, :width]
-    out[:, width:] = total_of(own, [r.at[:, :width] for r in received]) + bias[:, width:]
-    sums = own_columns[...]
-    for r in received:
-        extra = r[:16, width:].astype(jnp.float32)
-        sums += extra[:1, :rows] + extra[:1, rows:]
-    scores[...] = sums / QUERY_HEADS
+def finish_kernel(bias, kept, received, out):
+    out[...] = kept[...] + received[...].astype(jnp.float32) + bias[...]
 
 
 def shards(queries, keys, values, hidden, norm_gain, retained_lists, counts, affine_matrix, affine_offset_vector):
@@ -220,7 +207,6 @@
     lines = survivors // n
     chunk = width // 2
     near = survivors // 2
-    owners = list(range(0, n, 2)) + list(range(1, n, 2))
     f32, bf16, i32 = jnp.float32, jnp.bfloat16, jnp.int32
     shape = jax.ShapeDtypeStruct
     dma = pltpu.SemaphoreType.DMA
@@ -244,30 +230,27 @@
     )
     pair_other = trade(pair, 1)
     received = [chosen[0]] + [trade(chosen[k], k) for k in range(1, n)]
-
-    matrix, queries, held, target = call(
+    turns = [k for i in range(n // 2) for k in (n // 2 + i, i) if k]
+    matrix, queries, target = call(
         functools.partial(stage_kernel, n),
         "stage",
-        (counts, affine_matrix, queries, pair, pair_other, *received[n // 2 :]),
-        [shape(affine_matrix.shape, bf16), shape(queries.shape, bf16), shape((2 * rows, pair.shape[1]), bf16), shape((1, n * rows), i32)],
+        (counts, affine_matrix, queries, *[received[k] for k in turns[:5]]),
+        [shape(affine_matrix.shape, bf16), shape(queries.shape, bf16), shape((1, n * rows), i32)],
         0,
-        limit=16,
-        in_specs=[ANY] * 3 + [VMEM] * 2 + [ANY] * (n // 2),
+        in_specs=[ANY] * 8,
         remote=3,
         scratch=[pltpu.SMEM(counts.shape, i32), dma((3,))],
     )
-    order = [0, 1]
-    mask = n // 2
+    held, order, mask = jnp.concatenate([pair, pair_other], axis=0), [0, 1], 2
+    while mask < n // 2:
+        held = jnp.concatenate([held, trade(held, mask)], axis=0)
+        order = order + [k ^ mask for k in order]
+        mask *= 2
     held_other = trade(held, mask)
     order = order + [k ^ mask for k in order]
-    while mask > 2:
-        mask //= 2
-        held = jnp.concatenate([held, held_other], axis=0)
-        held_other = trade(held, mask)
-        order = order + [k ^ mask for k in order]
 
     (own,) = call(
-        functools.partial(compact_kernel, n, owners),
+        functools.partial(compact_kernel, n),
         "compact",
         (target, *received),
         [shape((survivors, half), bf16)],
@@ -275,9 +258,11 @@
     )
     other = swap(own)
 
+    rest = [1 << i for i in range(2, n.bit_length() - 1)]
+    masks = [[1, 2] + rest, [2, 1] + rest]
     products = [
         call(
-            functools.partial(project_kernel, c * chunk),
+            functools.partial(project_kernel, c * chunk, halving_order(n, masks[c])),
             "project",
             (own, other, matrix),
             [shape((near, chunk), f32), shape((near, chunk), bf16)],
@@ -286,7 +271,7 @@
         for c in range(2)
     ]
     context, columns = call(
-        functools.partial(attention_kernel, n, kv_heads, order, owners),
+        functools.partial(attention_kernel, n, kv_heads, order, masks[0]),
         "attention",
         (queries, held, held_other, products[1][1]),
         [shape(queries.shape, f32), shape((n, rows), f32)],
@@ -294,35 +279,44 @@
         limit=32,
         in_specs=[VMEM] * 3 + [ANY],
     )
-    first, far, *sent = call(
-        pair_sum_kernel,
-        "pair_sum",
-        (products[0][0], trade(products[0][1], 1), products[1][1], columns),
-        [shape((lines, chunk), f32), shape((near, chunk), bf16)] + [shape((lines, chunk), bf16)] * (n // 2 - 1),
-        near * chunk,
-        in_specs=[VMEM] * 3 + [ANY],
-    )
-    parts = [first] + [trade(x, 2 * (i + 1)) for i, x in enumerate(sent)]
-    far = trade(far, 1)
-
-    columns = columns + swap(columns)
-    done, last, own_columns, *sent = call(
-        functools.partial(pair_sum_last_kernel, n),
-        "pair_sum_last",
-        (products[1][0], far, columns[: n // 2], trade(columns[n // 2 :], 1), *parts),
-        [shape((lines, chunk), f32), shape((lines, chunk), f32), shape((1, rows), f32)] + [shape((lines, chunk + 2 * rows), bf16)] * (n // 2 - 1),
-        near * chunk,
-    )
-    parts = [last] + [trade(x, 2 * (i + 1)) for i, x in enumerate(sent)]
-
-    triples, scores = call(
+    kept = [product[0] for product in products]
+    arrived = [trade(product[1], masks[c][0]) for c, product in enumerate(products)]
+    def column_hop(columns, mask):
+        left = columns.shape[0] // 2
+        return columns[:left] + trade(columns[left:], mask)
+
+    lines_left = near // 2
+    for c in (1, 0):
+        keep, sent, columns = call(
+            hop_sum_kernel,
+            "hop_sum",
+            (kept[c], arrived[c], columns),
+            [shape((lines_left, chunk), f32), shape((lines_left, chunk), bf16), shape(columns.shape, f32)],
+            near * chunk,
+        )
+        kept[c], arrived[c] = keep, trade(sent, masks[c][1])
+    columns = column_hop(columns + swap(columns), masks[0][0])
+    for mask in rest:
+        lines_left //= 2
+        keep, sent, columns = call(
+            hop_sum_both_kernel,
+            "hop_sum_both",
+            (*kept, *arrived, columns),
+            [shape((lines_left, width), f32), shape((lines_left, width), bf16), shape(columns.shape, f32)],
+            lines_left * width,
+        )
+        kept, arrived = [keep], [trade(sent, mask)]
+    for mask in masks[0][1:]:
+        columns = column_hop(columns, mask)
+
+    (triples,) = call(
         finish_kernel,
         "finish",
-        (affine_offset_vector.reshape(1, width), done, own_columns, *parts),
-        [shape((lines, width), f32), shape((1, rows), f32)],
+        (affine_offset_vector.reshape(1, width), kept[0], arrived[0]),
+        [shape((lines, width), f32)],
         n * lines * width,
     )
-    return (context, scores.reshape(rows), triples)
+    return (context, columns.reshape(rows) / QUERY_HEADS, triples)
 
 
 def solution(mesh):

time: 67.4 us -> 69.5 us (1.031)
  waiting for transfers between devices: 28.5 us -> 31.7 us
  starting transfers between devices: 28.4 us -> 26.8 us
    ppermute x19 -> x18, waiting for transfers between devices: 27.4 us -> 29.4 us  [trade(): return lax.ppermute(x, 'seq', [(i, i ^ k) for i in range(n)])]
    ppermute x19 -> x18, starting transfers between devices: 28.3 us -> 26.7 us  [trade(): return lax.ppermute(x, 'seq', [(i, i ^ k) for i in range(n)])]
    ppermute x2, waiting for transfers between devices: 1.17 us -> 2.28 us  [swap(): return lax.ppermute(x, 'ten', [(0, 1), (1, 0)])]
    pallas_call x9 -> x10, Pallas kernels: 9.55 us -> 9.49 us  [call(): pl.pallas_call(body, out_shape=list(outputs), in_specs=in_specs or [VMEM]...]
  transfers between devices with their start and end apart: 21 -> 20, of which waited for: 10 -> 12; matrix products, arithmetic and copies ran while one was open for 0% -> 1% of each run, Pallas kernels for 10% -> 10%
where the time goes in v5:
time: 69.5 us; the launch traced here: 69.4 us
  waiting for transfers between devices  31.7 us (46%)
  starting transfers between devices  26.8 us (39%)
  Pallas kernels  9.49 us (14%)
  between operations  0.79 us (1%)
    ppermute x18, waiting for transfers between devices, trade(): return lax.ppermute(x, 'seq', [(i, i ^ k) for i in range(n)])  29.4 us
    ppermute x18, starting transfers between devices, trade(): return lax.ppermute(x, 'seq', [(i, i ^ k) for i in range(n)])  26.7 us
    pallas_call x10, Pallas kernels, call(): pl.pallas_call(body, out_shape=list(outputs), in_specs=in_specs or [VMEM]...  9.49 us
    ppermute x2, waiting for transfers between devices, swap(): return lax.ppermute(x, 'ten', [(0, 1), (1, 0)])  2.28 us
  transfers between devices with their start and end apart: 20, of which 12 were waited for; matrix products, arithmetic and copies ran while one was open for 1% of the time, Pallas kernels for 10%

profile of v5, /device:TPU:0, one launch (start us, length us, event | category | flops | bytes accessed | tf_op | source)
XLA Modules:
  0.0 69.4 jit_solution(14790982627424584219)
XLA Ops:
  0.6 1.7 %norm_select.1 = (bf16[64,512]{1,0:T(8,128)(2,1)S(1)}, bf16[64,512]{1,0:T(8,128)(2,1)S(1)}, bf16[64,512]{1,0:T(8,128)(2,1)S(1)}, bf16[64,512]{1,0:T(8,128)(2,1)S...) custom-call(bf16[64,8192]{1,0:T(8,128)(2,1)} %hidden_in.1, ...), custom_call_target="tpu_custom_call" | custom-call | flops 2097152 | bytes 1736960 | tf_op jit(solution)/shard_map/norm_select/pallas_call | solution.py:21
  2.4 4.1 %collective-permute-start = (bf16[64,512]{1,0:T(8,128)(2,1)S(1)}, bf16[64,512]{1,0:T(8,128)(2,1)S(1)}, u32[]{:S(2)}, u32[]{:S(2)}) collective-permute-start(bf16[64,512]{1,0:T(8,128)(2,1)S(1)} %get-tuple-element.30), channel_id=1, source_target_pairs={{0,8},{2,10},{4,12},{6,14},{8,0},{10,2},{12,4},{14,6},{1,9},{3,11}... | collective-permute-start | bytes 196616 | tf_op jit(solution)/shard_map/ppermute | solution.py:215
  6.5 1.3 %collective-permute-start.1 = (bf16[64,512]{1,0:T(8,128)(2,1)S(1)}, bf16[64,512]{1,0:T(8,128)(2,1)S(1)}, u32[]{:S(2)}, u32[]{:S(2)}) collective-permute-start(bf16[64,512]{1,0:T(8,128)(2,1)S(1)} %get-tuple-element.31), channel_id=1, source_target_pairs={{0,10},{2,8},{4,14},{6,12},{8,2},{10,0},{12,6},{14,4},{1,11},{3,9}... | collective-permute-start | bytes 196616 | tf_op jit(solution)/shard_map/ppermute | solution.py:215
  7.8 0.2 collective-permute-start.2
  8.0 3.9 %collective-permute-start.3 = (bf16[64,512]{1,0:T(8,128)(2,1)S(1)}, bf16[64,512]{1,0:T(8,128)(2,1)S(1)}, u32[]{:S(2)}, u32[]{:S(2)}) collective-permute-start(bf16[64,512]{1,0:T(8,128)(2,1)S(1)} %get-tuple-element.33), channel_id=1, source_target_pairs={{0,12},{2,14},{4,8},{6,10},{8,4},{10,6},{12,0},{14,2},{1,13},{3,15... | collective-permute-start | bytes 196616 | tf_op jit(solution)/shard_map/ppermute | solution.py:215
  11.9 0.0 collective-permute-start.4
  11.9 0.0 collective-permute-done.refs_0_.refs_4_
  11.9 3.0 %collective-permute-start.8 = (bf16[64,512]{1,0:T(8,128)(2,1)S(1)}, bf16[64,512]{1,0:T(8,128)(2,1)S(1)}, u32[]{:S(2)}, u32[]{:S(2)}) collective-permute-start(bf16[64,512]{1,0:T(8,128)(2,1)S(1)} %get-tuple-element.39), channel_id=1, source_target_pairs={{0,6},{2,4},{4,2},{6,0},{8,14},{10,12},{12,10},{14,8},{1,7},{3,5},... | collective-permute-start | bytes 196616 | tf_op jit(solution)/shard_map/ppermute | solution.py:215
  14.9 0.9 %collective-permute-done.1.refs_1_.refs_5_ = bf16[64,512]{1,0:T(8,128)(2,1)S(1)} collective-permute-done((bf16[64,512]{1,0:T(8,128)(2,1)S(1)}, bf16[64,512]{1,0:T(8,128)(2,1)S(1)}, u32[]{:S(2)}, u32[]{:S(2)}) %collective-permute-start.1) | collective-permute-done | bytes 65568 | tf_op jit(solution)/shard_map/ppermute | solution.py:215
  15.8 3.1 %collective-permute-start.9 = (bf16[64,512]{1,0:T(8,128)(2,1)S(1)}, bf16[64,512]{1,0:T(8,128)(2,1)S(1)}, u32[]{:S(2)}, u32[]{:S(2)}) collective-permute-start(bf16[64,512]{1,0:T(8,128)(2,1)S(1)} %get-tuple-element.40), channel_id=1, source_target_pairs={{0,14},{2,12},{4,10},{6,8},{8,6},{10,4},{12,2},{14,0},{1,15},{3,13... | collective-permute-start | bytes 196616 | tf_op jit(solution)/shard_map/ppermute | solution.py:215
  18.9 0.7 %collective-permute-start.5 = (bf16[64,512]{1,0:T(8,128)(2,1)S(1)}, bf16[64,512]{1,0:T(8,128)(2,1)S(1)}, u32[]{:S(2)}, u32[]{:S(2)}) collective-permute-start(bf16[64,512]{1,0:T(8,128)(2,1)S(1)} %get-tuple-element.36), channel_id=1, source_target_pairs={{0,2},{2,0},{4,6},{6,4},{8,10},{10,8},{12,14},{14,12},{1,3},{3,1},... | collective-permute-start | bytes 196616 | tf_op jit(solution)/shard_map/ppermute | solution.py:215
  19.6 0.0 collective-permute-done.3.refs_3_.refs_6_
  19.6 0.0 collective-permute-done.4.refs_4_.refs_2_
  19.6 2.5 %stage.1 = (bf16[1024,2560]{1,0:T(8,128)(2,1)S(1)}, bf16[64,2048]{1,0:T(8,128)(2,1)S(1)}, s32[1,512]{1,0:T(1,128)S(1)}) custom-call(s32[8]{0:T(128)} %counts_in.1, bf16[1024,2560]{1,0:T(8,128)(2,1)} %matrix_in.1, bf16[64,2048]{1,0:T(8,128)(2,1)} %queries_in.1, bf16[64,512]{1,0:T(8,128)(2,1)S(1)} %collective-permute-done.refs_0_.refs_4_, ...), custom_call_target="tpu_custom_call" | custom-call | bytes 11339808 | tf_op jit(solution)/shard_map/stage/pallas_call | solution.py:21
  22.1 0.0 collective-permute-done.8.refs_3_
  22.2 0.6 collective-permute-done.9.refs_7_
  22.8 0.3 compact.1.own
  23.1 0.1 collective-permute-start.10
  23.2 0.3 collective-permute-done.5
  23.5 0.1 collective-permute-start.6
  23.5 1.1 %collective-permute-done.10.other = bf16[256,512]{1,0:T(8,128)(2,1)S(1)} collective-permute-done((bf16[256,512]{1,0:T(8,128)(2,1)S(1)}, bf16[256,512]{1,0:T(8,128)(2,1)S(1)}, u32[]{:S(2)}, u32[]{:S(2)}) %collective-permute-start.10) | collective-permute-done | bytes 262176 | tf_op jit(solution)/shard_map/ppermute | solution.py:218
  24.7 1.0 %project.2 = (f32[128,1280]{1,0:T(8,128)S(1)}, bf16[128,1280]{1,0:T(8,128)(2,1)S(1)}) custom-call(bf16[256,512]{1,0:T(8,128)(2,1)S(1)} %compact.1.own, bf16[256,512]{1,0:T(8,128)(2,1)S(1)} %collective-permute-done.10.other, bf16[1024,2560]{1,0:T(8,128)(2,1)S(1)} %get-tuple-element.41.matrix), custom_call_target="tpu_custom_call" | custom-call | flops 671088640 | bytes 6750208 | tf_op jit(solution)/shard_map/project/pallas_call | solution.py:21
  25.7 0.0 copy-start
  25.7 1.0 %collective-permute-start.12 = (bf16[128,1280]{1,0:T(8,128)(2,1)S(1)}, bf16[128,1280]{1,0:T(8,128)(2,1)S(1)}, u32[]{:S(2)}, u32[]{:S(2)}) collective-permute-start(bf16[128,1280]{1,0:T(8,128)(2,1)S(1)} %get-tuple-element.42.after), channel_id=1, source_target_pairs={{0,4},{2,6},{4,0},{6,2},{8,12},{10,14},{12,8},{14,10},{1,5},{3,7},... | collective-permute-start | bytes 983048 | tf_op jit(solution)/shard_map/ppermute | solution.py:215
  26.6 1.0 %project.3 = (f32[128,1280]{1,0:T(8,128)S(1)}, bf16[128,1280]{1,0:T(8,128)(2,1)S(1)}) custom-call(bf16[256,512]{1,0:T(8,128)(2,1)S(1)} %compact.1.own, bf16[256,512]{1,0:T(8,128)(2,1)S(1)} %collective-permute-done.10.other, bf16[1024,2560]{1,0:T(8,128)(2,1)S(1)} %get-tuple-element.41.matrix), custom_call_target="tpu_custom_call" | custom-call | flops 671088640 | bytes 6750208 | tf_op jit(solution)/shard_map/project/pallas_call | solution.py:21
  27.6 1.2 %collective-permute-start.11 = (bf16[128,1280]{1,0:T(8,128)(2,1)S(1)}, bf16[128,1280]{1,0:T(8,128)(2,1)S(1)}, u32[]{:S(2)}, u32[]{:S(2)}) collective-permute-start(bf16[128,1280]{1,0:T(8,128)(2,1)S(1)} %get-tuple-element.45), channel_id=1, source_target_pairs={{0,2},{2,0},{4,6},{6,4},{8,10},{10,8},{12,14},{14,12},{1,3},{3,1},... | collective-permute-start | bytes 983048 | tf_op jit(solution)/shard_map/ppermute | solution.py:215
  28.8 0.9 %collective-permute-done.6 = bf16[128,512]{1,0:T(8,128)(2,1)S(1)} collective-permute-done((bf16[128,512]{1,0:T(8,128)(2,1)S(1)}, bf16[128,512]{1,0:T(8,128)(2,1)S(1)}, u32[]{:S(2)}, u32[]{:S(2)}) %collective-permute-start.6) | collective-permute-done | bytes 131104 | tf_op jit(solution)/shard_map/ppermute | solution.py:215
  29.8 1.3 %collective-permute-start.7 = (bf16[256,512]{1,0:T(8,128)(2,1)S(1)}, bf16[256,512]{1,0:T(8,128)(2,1)S(1)}, u32[]{:S(2)}, u32[]{:S(2)}) collective-permute-start(bf16[256,512]{1,0:T(8,128)(2,1)S(1)} %constant_dynamic-update-slice_fusion.held_a), channel_id=1, source_target_pairs={{0,8},{2,10},{4,12},{6,14},{8,0},{10,2},{12,4},{14,6},{1,9},{3,11}... | collective-permute-start | bytes 786440 | tf_op jit(solution)/shard_map/ppermute | solution.py:215
  31.1 12.3 %collective-permute-done.7.held_b = bf16[256,512]{1,0:T(8,128)(2,1)S(1)} collective-permute-done((bf16[256,512]{1,0:T(8,128)(2,1)S(1)}, bf16[256,512]{1,0:T(8,128)(2,1)S(1)}, u32[]{:S(2)}, u32[]{:S(2)}) %collective-permute-start.7) | collective-permute-done | bytes 262176 | tf_op jit(solution)/shard_map/ppermute | solution.py:215
  43.4 2.0 %attention.1 = (f32[64,2048]{1,0:T(8,128)}, f32[8,64]{1,0:T(8,128)S(1)}) custom-call(bf16[64,2048]{1,0:T(8,128)(2,1)S(1)} %get-tuple-element.35.queries, bf16[256,512]{1,0:T(8,128)(2,1)S(1)} %constant_dynamic-update-slice_fusion.held_a, bf16[256,512]{1,0:T(8,128)(2,1)S(1)} %collective-permute-done.7.held_b, bf16[128,1280]{1,0:T(8,128)(2,1)S(1)} %get-tuple-element.42.after), custom_call_target="tpu_custom_call" | custom-call | flops 268435456 | bytes 1640448 | tf_op jit(solution)/shard_map/attention/pallas_call | solution.py:21
  45.4 0.1 hop_sum.2
  45.5 0.1 hop_sum.3
  45.5 0.1 collective-permute-start.15
  45.6 1.2 %collective-permute-done.15 = f32[8,64]{1,0:T(8,128)S(1)} collective-permute-done((f32[8,64]{1,0:T(8,128)S(1)}, f32[8,64]{1,0:T(8,128)S(1)}, u32[]{:S(2)}, u32[]{:S(2)}) %collective-permute-start.15) | collective-permute-done | bytes 2080 | tf_op jit(solution)/shard_map/ppermute | solution.py:218
  46.8 1.4 %collective-permute-start.16 = (f32[4,64]{1,0:T(4,128)S(1)}, f32[4,64]{1,0:T(4,128)S(1)}, u32[]{:S(2)}, u32[]{:S(2)}) collective-permute-start(f32[4,64]{1,0:T(4,128)S(1)} %slice.19), channel_id=1, source_target_pairs={{0,2},{2,0},{4,6},{6,4},{8,10},{10,8},{12,14},{14,12},{1,3},{3,1},... | collective-permute-start | bytes 3080 | tf_op jit(solution)/shard_map/ppermute | solution.py:215
  48.2 0.6 collective-permute-start.14
  48.8 1.6 %collective-permute-done.16 = f32[4,64]{1,0:T(4,128)S(1)} collective-permute-done((f32[4,64]{1,0:T(4,128)S(1)}, f32[4,64]{1,0:T(4,128)S(1)}, u32[]{:S(2)}, u32[]{:S(2)}) %collective-permute-start.16) | collective-permute-done | bytes 1056 | tf_op jit(solution)/shard_map/ppermute | solution.py:215
  50.4 3.8 %collective-permute-done.13.refs_2_ = bf16[64,1280]{1,0:T(8,128)(2,1)S(1)} collective-permute-done((bf16[64,1280]{1,0:T(8,128)(2,1)S(1)}, bf16[64,1280]{1,0:T(8,128)(2,1)S(1)}, u32[]{:S(2)}, u32[]{:S(2)}) %collective-permute-start.13) | collective-permute-done | bytes 163872 | tf_op jit(solution)/shard_map/ppermute | solution.py:215
  54.2 0.0 collective-permute-done.14.refs_3_
  54.2 0.1 hop_sum_both.1
  54.3 1.8 %collective-permute-start.17 = (f32[2,64]{1,0:T(2,128)S(1)}, f32[2,64]{1,0:T(2,128)S(1)}, u32[]{:S(2)}, u32[]{:S(2)}) collective-permute-start(f32[2,64]{1,0:T(2,128)S(1)} %slice.21), channel_id=1, source_target_pairs={{0,4},{2,6},{4,0},{6,2},{8,12},{10,14},{12,8},{14,10},{1,5},{3,7},... | collective-permute-start | bytes 1544 | tf_op jit(solution)/shard_map/ppermute | solution.py:215
  56.1 1.8 %collective-permute-done.17 = f32[2,64]{1,0:T(2,128)S(1)} collective-permute-done((f32[2,64]{1,0:T(2,128)S(1)}, f32[2,64]{1,0:T(2,128)S(1)}, u32[]{:S(2)}, u32[]{:S(2)}) %collective-permute-start.17) | collective-permute-done | bytes 544 | tf_op jit(solution)/shard_map/ppermute | solution.py:215
  57.9 2.8 %collective-permute-start.18 = (f32[1,64]{1,0:T(1,128)S(1)}, f32[1,64]{1,0:T(1,128)S(1)}, u32[]{:S(2)}, u32[]{:S(2)}) collective-permute-start(f32[1,64]{1,0:T(1,128)S(1)} %slice.23), channel_id=1, source_target_pairs={{0,8},{2,10},{4,12},{6,14},{8,0},{10,2},{12,4},{14,6},{1,9},{3,11}... | collective-permute-start | bytes 776 | tf_op jit(solution)/shard_map/ppermute | solution.py:215
  60.8 0.2 collective-permute-start.19
  60.9 2.5 %collective-permute-done.18 = f32[1,64]{1,0:T(1,128)S(1)} collective-permute-done((f32[1,64]{1,0:T(1,128)S(1)}, f32[1,64]{1,0:T(1,128)S(1)}, u32[]{:S(2)}, u32[]{:S(2)}) %collective-permute-start.18) | collective-permute-done | bytes 288 | tf_op jit(solution)/shard_map/ppermute | solution.py:215
  63.5 0.5 multiply_bitcast_fusion
  64.0 4.6 %collective-permute-done.19.received = bf16[32,2560]{1,0:T(8,128)(2,1)S(1)} collective-permute-done((bf16[32,2560]{1,0:T(8,128)(2,1)S(1)}, bf16[32,2560]{1,0:T(8,128)(2,1)S(1)}, u32[]{:S(2)}, u32[]{:S(2)}) %collective-permute-start.19) | collective-permute-done | bytes 163872 | tf_op jit(solution)/shard_map/ppermute | solution.py:215
  68.6 0.8 %finish.1 = f32[32,2560]{1,0:T(8,128)} custom-call(f32[1,2560]{1,0:T(1,128)S(1)} %reshape.20.bias, f32[32,2560]{1,0:T(8,128)S(1)} %get-tuple-element.55.kept, bf16[32,2560]{1,0:T(8,128)(2,1)S(1)} %collective-permute-done.19.received), custom_call_target="tpu_custom_call" | custom-call | flops 655360 | bytes 829440 | tf_op jit(solution)/shard_map/finish/pallas_call | solution.py:21
  (16 shorter events, 0.1 us)
Async XLA Ops:
  2.4 9.5 %collective-permute-start = (bf16[64,512]{1,0:T(8,128)(2,1)S(1)}, bf16[64,512]{1,0:T(8,128)(2,1)S(1)}, u32[]{:S(2)}, u32[]{:S(2)}) collective-permute-start(bf16[64,512]{1,0:T(8,128)(2,1)S(1)} %get-tuple-element.30), channel_id=1, source_target_pairs={{0,8},{2,10},{4,12},{6,14},{8,0},{10,2},{12,4},{14,6},{1,9},{3,11}... | collective-permute-start | bytes 196616 | tf_op jit(solution)/shard_map/ppermute | solution.py:215
  6.5 9.3 %collective-permute-start.1 = (bf16[64,512]{1,0:T(8,128)(2,1)S(1)}, bf16[64,512]{1,0:T(8,128)(2,1)S(1)}, u32[]{:S(2)}, u32[]{:S(2)}) collective-permute-start(bf16[64,512]{1,0:T(8,128)(2,1)S(1)} %get-tuple-element.31), channel_id=1, source_target_pairs={{0,10},{2,8},{4,14},{6,12},{8,2},{10,0},{12,6},{14,4},{1,11},{3,9}... | collective-permute-start | bytes 196616 | tf_op jit(solution)/shard_map/ppermute | solution.py:215
  7.8 11.1 %collective-permute-start.2 = (bf16[64,512]{1,0:T(8,128)(2,1)S(1)}, bf16[64,512]{1,0:T(8,128)(2,1)S(1)}, u32[]{:S(2)}, u32[]{:S(2)}) collective-permute-start(bf16[64,512]{1,0:T(8,128)(2,1)S(1)} %get-tuple-element.32), channel_id=1, source_target_pairs={{0,2},{2,0},{4,6},{6,4},{8,10},{10,8},{12,14},{14,12},{1,3},{3,1},... | collective-permute-start | bytes 196616 | tf_op jit(solution)/shard_map/ppermute | solution.py:215
  8.0 11.6 %collective-permute-start.3 = (bf16[64,512]{1,0:T(8,128)(2,1)S(1)}, bf16[64,512]{1,0:T(8,128)(2,1)S(1)}, u32[]{:S(2)}, u32[]{:S(2)}) collective-permute-start(bf16[64,512]{1,0:T(8,128)(2,1)S(1)} %get-tuple-element.33), channel_id=1, source_target_pairs={{0,12},{2,14},{4,8},{6,10},{8,4},{10,6},{12,0},{14,2},{1,13},{3,15... | collective-permute-start | bytes 196616 | tf_op jit(solution)/shard_map/ppermute | solution.py:215
  11.9 7.7 %collective-permute-start.4 = (bf16[64,512]{1,0:T(8,128)(2,1)S(1)}, bf16[64,512]{1,0:T(8,128)(2,1)S(1)}, u32[]{:S(2)}, u32[]{:S(2)}) collective-permute-start(bf16[64,512]{1,0:T(8,128)(2,1)S(1)} %get-tuple-element.34), channel_id=1, source_target_pairs={{0,4},{2,6},{4,0},{6,2},{8,12},{10,14},{12,8},{14,10},{1,5},{3,7},... | collective-permute-start | bytes 196616 | tf_op jit(solution)/shard_map/ppermute | solution.py:215
  11.9 10.3 %collective-permute-start.8 = (bf16[64,512]{1,0:T(8,128)(2,1)S(1)}, bf16[64,512]{1,0:T(8,128)(2,1)S(1)}, u32[]{:S(2)}, u32[]{:S(2)}) collective-permute-start(bf16[64,512]{1,0:T(8,128)(2,1)S(1)} %get-tuple-element.39), channel_id=1, source_target_pairs={{0,6},{2,4},{4,2},{6,0},{8,14},{10,12},{12,10},{14,8},{1,7},{3,5},... | collective-permute-start | bytes 196616 | tf_op jit(solution)/shard_map/ppermute | solution.py:215
  15.8 7.0 %collective-permute-start.9 = (bf16[64,512]{1,0:T(8,128)(2,1)S(1)}, bf16[64,512]{1,0:T(8,128)(2,1)S(1)}, u32[]{:S(2)}, u32[]{:S(2)}) collective-permute-start(bf16[64,512]{1,0:T(8,128)(2,1)S(1)} %get-tuple-element.40), channel_id=1, source_target_pairs={{0,14},{2,12},{4,10},{6,8},{8,6},{10,4},{12,2},{14,0},{1,15},{3,13... | collective-permute-start | bytes 196616 | tf_op jit(solution)/shard_map/ppermute | solution.py:215
  18.9 4.5 %collective-permute-start.5 = (bf16[64,512]{1,0:T(8,128)(2,1)S(1)}, bf16[64,512]{1,0:T(8,128)(2,1)S(1)}, u32[]{:S(2)}, u32[]{:S(2)}) collective-permute-start(bf16[64,512]{1,0:T(8,128)(2,1)S(1)} %get-tuple-element.36), channel_id=1, source_target_pairs={{0,2},{2,0},{4,6},{6,4},{8,10},{10,8},{12,14},{14,12},{1,3},{3,1},... | collective-permute-start | bytes 196616 | tf_op jit(solution)/shard_map/ppermute | solution.py:215
  23.1 1.6 %collective-permute-start.10 = (bf16[256,512]{1,0:T(8,128)(2,1)S(1)}, bf16[256,512]{1,0:T(8,128)(2,1)S(1)}, u32[]{:S(2)}, u32[]{:S(2)}) collective-permute-start(bf16[256,512]{1,0:T(8,128)(2,1)S(1)} %compact.1.own), channel_id=1, source_target_pairs={{0,1},{1,0},{2,3},{3,2},{4,5},{5,4},{6,7},{7,6},{8,9},{9,8},{10,11... | collective-permute-start | bytes 786440 | tf_op jit(solution)/shard_map/ppermute | solution.py:218
  23.5 6.3 %collective-permute-start.6 = (bf16[128,512]{1,0:T(8,128)(2,1)S(1)}, bf16[128,512]{1,0:T(8,128)(2,1)S(1)}, u32[]{:S(2)}, u32[]{:S(2)}) collective-permute-start(bf16[128,512]{1,0:T(8,128)(2,1)S(1)} %pad_maximum_fusion), channel_id=1, source_target_pairs={{0,4},{2,6},{4,0},{6,2},{8,12},{10,14},{12,8},{14,10},{1,5},{3,7},... | collective-permute-start | bytes 393224 | tf_op jit(solution)/shard_map/ppermute | solution.py:215
  25.7 35.1 %copy-start = (f32[2560]{0:T(1024)S(1)}, f32[2560]{0:T(1024)}, u32[]{:S(2)}) copy-start(f32[2560]{0:T(1024)} %param.17) | copy-start | bytes 30724
  25.7 19.7 %collective-permute-start.12 = (bf16[128,1280]{1,0:T(8,128)(2,1)S(1)}, bf16[128,1280]{1,0:T(8,128)(2,1)S(1)}, u32[]{:S(2)}, u32[]{:S(2)}) collective-permute-start(bf16[128,1280]{1,0:T(8,128)(2,1)S(1)} %get-tuple-element.42.after), channel_id=1, source_target_pairs={{0,4},{2,6},{4,0},{6,2},{8,12},{10,14},{12,8},{14,10},{1,5},{3,7},... | collective-permute-start | bytes 983048 | tf_op jit(solution)/shard_map/ppermute | solution.py:215
  27.6 17.8 %collective-permute-start.11 = (bf16[128,1280]{1,0:T(8,128)(2,1)S(1)}, bf16[128,1280]{1,0:T(8,128)(2,1)S(1)}, u32[]{:S(2)}, u32[]{:S(2)}) collective-permute-start(bf16[128,1280]{1,0:T(8,128)(2,1)S(1)} %get-tuple-element.45), channel_id=1, source_target_pairs={{0,2},{2,0},{4,6},{6,4},{8,10},{10,8},{12,14},{14,12},{1,3},{3,1},... | collective-permute-start | bytes 983048 | tf_op jit(solution)/shard_map/ppermute | solution.py:215
  29.8 13.6 %collective-permute-start.7 = (bf16[256,512]{1,0:T(8,128)(2,1)S(1)}, bf16[256,512]{1,0:T(8,128)(2,1)S(1)}, u32[]{:S(2)}, u32[]{:S(2)}) collective-permute-start(bf16[256,512]{1,0:T(8,128)(2,1)S(1)} %constant_dynamic-update-slice_fusion.held_a), channel_id=1, source_target_pairs={{0,8},{2,10},{4,12},{6,14},{8,0},{10,2},{12,4},{14,6},{1,9},{3,11}... | collective-permute-start | bytes 786440 | tf_op jit(solution)/shard_map/ppermute | solution.py:215
  45.5 1.2 %collective-permute-start.15 = (f32[8,64]{1,0:T(8,128)S(1)}, f32[8,64]{1,0:T(8,128)S(1)}, u32[]{:S(2)}, u32[]{:S(2)}) collective-permute-start(f32[8,64]{1,0:T(8,128)S(1)} %get-tuple-element.53), channel_id=1, source_target_pairs={{0,1},{1,0},{2,3},{3,2},{4,5},{5,4},{6,7},{7,6},{8,9},{9,8},{10,11... | collective-permute-start | bytes 6152 | tf_op jit(solution)/shard_map/ppermute | solution.py:218
  46.8 3.6 %collective-permute-start.16 = (f32[4,64]{1,0:T(4,128)S(1)}, f32[4,64]{1,0:T(4,128)S(1)}, u32[]{:S(2)}, u32[]{:S(2)}) collective-permute-start(f32[4,64]{1,0:T(4,128)S(1)} %slice.19), channel_id=1, source_target_pairs={{0,2},{2,0},{4,6},{6,4},{8,10},{10,8},{12,14},{14,12},{1,3},{3,1},... | collective-permute-start | bytes 3080 | tf_op jit(solution)/shard_map/ppermute | solution.py:215
  48.2 6.0 %collective-permute-start.13 = (bf16[64,1280]{1,0:T(8,128)(2,1)S(1)}, bf16[64,1280]{1,0:T(8,128)(2,1)S(1)}, u32[]{:S(2)}, u32[]{:S(2)}) collective-permute-start(bf16[64,1280]{1,0:T(8,128)(2,1)S(1)} %get-tuple-element.51), channel_id=1, source_target_pairs={{0,4},{2,6},{4,0},{6,2},{8,12},{10,14},{12,8},{14,10},{1,5},{3,7},... | collective-permute-start | bytes 491528 | tf_op jit(solution)/shard_map/ppermute | solution.py:215
  48.2 6.0 %collective-permute-start.14 = (bf16[64,1280]{1,0:T(8,128)(2,1)S(1)}, bf16[64,1280]{1,0:T(8,128)(2,1)S(1)}, u32[]{:S(2)}, u32[]{:S(2)}) collective-permute-start(bf16[64,1280]{1,0:T(8,128)(2,1)S(1)} %get-tuple-element.52), channel_id=1, source_target_pairs={{0,2},{2,0},{4,6},{6,4},{8,10},{10,8},{12,14},{14,12},{1,3},{3,1},... | collective-permute-start | bytes 491528 | tf_op jit(solution)/shard_map/ppermute | solution.py:215
  54.3 3.6 %collective-permute-start.17 = (f32[2,64]{1,0:T(2,128)S(1)}, f32[2,64]{1,0:T(2,128)S(1)}, u32[]{:S(2)}, u32[]{:S(2)}) collective-permute-start(f32[2,64]{1,0:T(2,128)S(1)} %slice.21), channel_id=1, source_target_pairs={{0,4},{2,6},{4,0},{6,2},{8,12},{10,14},{12,8},{14,10},{1,5},{3,7},... | collective-permute-start | bytes 1544 | tf_op jit(solution)/shard_map/ppermute | solution.py:215
  57.9 5.5 %collective-permute-start.18 = (f32[1,64]{1,0:T(1,128)S(1)}, f32[1,64]{1,0:T(1,128)S(1)}, u32[]{:S(2)}, u32[]{:S(2)}) collective-permute-start(f32[1,64]{1,0:T(1,128)S(1)} %slice.23), channel_id=1, source_target_pairs={{0,8},{2,10},{4,12},{6,14},{8,0},{10,2},{12,4},{14,6},{1,9},{3,11}... | collective-permute-start | bytes 776 | tf_op jit(solution)/shard_map/ppermute | solution.py:215
  60.8 7.9 %collective-permute-start.19 = (bf16[32,2560]{1,0:T(8,128)(2,1)S(1)}, bf16[32,2560]{1,0:T(8,128)(2,1)S(1)}, u32[]{:S(2)}, u32[]{:S(2)}) collective-permute-start(bf16[32,2560]{1,0:T(8,128)(2,1)S(1)} %get-tuple-element.56), channel_id=1, source_target_pairs={{0,8},{2,10},{4,12},{6,14},{8,0},{10,2},{12,4},{14,6},{1,9},{3,11}... | collective-permute-start | bytes 491528 | tf_op jit(solution)/shard_map/ppermute | solution.py:215

commit v6 on v5

--- a/solution.py
+++ b/solution.py
@@ -100,7 +100,7 @@
         load.wait()
 
 
-def compact_kernel(n, target, *refs):
+def compact_kernel(n, target, after, *refs):
     blocks, out = refs[:n], refs[n]
     lines = out.shape[0] // n
     s = lax.axis_index("seq")
@@ -116,7 +116,7 @@
     return sorted(range(n), key=lambda k: [k & mask for mask in masks])
 
 
-def project_kernel(first, order, own, other, matrix, near, far):
+def project_kernel(first, order, own, other, matrix, after, near, far):
     survivors, half = own.shape
     lines = survivors // len(order)
     width = near.shape[1]
@@ -214,8 +214,15 @@
     def trade(x, k):
         return lax.ppermute(x, "seq", [(i, i ^ k) for i in range(n)])
 
+    def trade_across(x, k):
+        return lax.ppermute(x, ("seq", "ten"), [(2 * i + t, 2 * (i ^ k) + 1 - t) for i in range(n) for t in range(2)])
+
     def swap(x):
         return lax.ppermute(x, "ten", [(0, 1), (1, 0)])
+
+    def column_hop(columns, mask):
+        left = columns.shape[0] // 2
+        return columns[:left] + trade(columns[left:], mask)
 
     pair, *chosen = call(
         functools.partial(norm_select_kernel, n),
@@ -228,7 +235,6 @@
         remote=5,
         scratch=[pltpu.VMEM((rows, model), bf16), pltpu.VMEM((1, model), f32), pltpu.VMEM((1, rows), i32), dma((8,))],
     )
-    pair_other = trade(pair, 1)
     received = [chosen[0]] + [trade(chosen[k], k) for k in range(1, n)]
     turns = [k for i in range(n // 2) for k in (n // 2 + i, i) if k]
     matrix, queries, target = call(
@@ -236,55 +242,56 @@
         "stage",
         (counts, affine_matrix, queries, *[received[k] for k in turns[:5]]),
         [shape(affine_matrix.shape, bf16), shape(queries.shape, bf16), shape((1, n * rows), i32)],
-        0,
+        1500 * affine_matrix.size,
         in_specs=[ANY] * 8,
         remote=3,
         scratch=[pltpu.SMEM(counts.shape, i32), dma((3,))],
     )
-    held, order, mask = jnp.concatenate([pair, pair_other], axis=0), [0, 1], 2
-    while mask < n // 2:
+    held, order, mask = pair, [0], n // 2
+    while mask > 1:
         held = jnp.concatenate([held, trade(held, mask)], axis=0)
         order = order + [k ^ mask for k in order]
-        mask *= 2
-    held_other = trade(held, mask)
-    order = order + [k ^ mask for k in order]
+        mask //= 2
+    held_other = trade(held, 1)
+    order = order + [k ^ 1 for k in order]
 
     (own,) = call(
         functools.partial(compact_kernel, n),
         "compact",
-        (target, *received),
+        (target, held_other, *received),
         [shape((survivors, half), bf16)],
         2 * survivors * n * rows * half,
+        in_specs=[VMEM, ANY] + [VMEM] * n,
     )
     other = swap(own)
-
     rest = [1 << i for i in range(2, n.bit_length() - 1)]
     masks = [[1, 2] + rest, [2, 1] + rest]
+    context, columns = call(
+        functools.partial(attention_kernel, n, kv_heads, order, masks[0]),
+        "attention",
+        (queries, held, held_other, own),
+        [shape(queries.shape, f32), shape((n, rows), f32)],
+        4 * rows * n * rows * queries.shape[1],
+        limit=32,
+        in_specs=[VMEM] * 3 + [ANY],
+    )
+
     products = [
         call(
             functools.partial(project_kernel, c * chunk, halving_order(n, masks[c])),
             "project",
-            (own, other, matrix),
+            (own, other, matrix, columns),
             [shape((near, chunk), f32), shape((near, chunk), bf16)],
             4 * survivors * half * chunk,
+            in_specs=[VMEM] * 3 + [ANY],
         )
         for c in range(2)
     ]
-    context, columns = call(
-        functools.partial(attention_kernel, n, kv_heads, order, masks[0]),
-        "attention",
-        (queries, held, held_other, products[1][1]),
-        [shape(queries.shape, f32), shape((n, rows), f32)],
-        4 * rows * n * rows * queries.shape[1],
-        limit=32,
-        in_specs=[VMEM] * 3 + [ANY],
-    )
     kept = [product[0] for product in products]
     arrived = [trade(product[1], masks[c][0]) for c, product in enumerate(products)]
-    def column_hop(columns, mask):
-        left = columns.shape[0] // 2
-        return columns[:left] + trade(columns[left:], mask)
-
+    far = columns[n // 2 :]
+    columns = columns[: n // 2]
+    columns = columns + swap(columns) + trade(far, 1) + trade_across(far, 1)
     lines_left = near // 2
     for c in (1, 0):
         keep, sent, columns = call(
@@ -295,7 +302,7 @@
             near * chunk,
         )
         kept[c], arrived[c] = keep, trade(sent, masks[c][1])
-    columns = column_hop(columns + swap(columns), masks[0][0])
+    columns = column_hop(columns, masks[0][1])
     for mask in rest:
         lines_left //= 2
         keep, sent, columns = call(
@@ -306,7 +313,6 @@
             lines_left * width,
         )
         kept, arrived = [keep], [trade(sent, mask)]
-    for mask in masks[0][1:]:
         columns = column_hop(columns, mask)
 
     (triples,) = call(

time: 69.5 us -> 69.3 us (level)
  waiting for transfers between devices: 31.7 us -> 30.6 us
  starting transfers between devices: 26.8 us -> 27.6 us
    ppermute x2, waiting for transfers between devices: 2.28 us -> 0.01 us  [swap(): return lax.ppermute(x, 'ten', [(0, 1), (1, 0)])]
    ppermute x18, waiting for transfers between devices: 29.4 us -> 30.6 us  [trade(): return lax.ppermute(x, 'seq', [(i, i ^ k) for i in range(n)])]
  transfers between devices with their start and end apart: 20 -> 21, of which waited for: 12 -> 8; matrix products, arithmetic and copies ran while one was open for 1% -> 1% of each run, Pallas kernels for 10% -> 8%
where the time goes in v6:
time: 69.3 us; the launch traced here: 69.1 us
  waiting for transfers between devices  30.6 us (44%)
  starting transfers between devices  27.6 us (40%)
  Pallas kernels  9.53 us (14%)
  between operations  0.8 us (1%)
    ppermute x18, waiting for transfers between devices, trade(): return lax.ppermute(x, 'seq', [(i, i ^ k) for i in range(n)])  30.6 us
    ppermute x18, starting transfers between devices, trade(): return lax.ppermute(x, 'seq', [(i, i ^ k) for i in range(n)])  26.9 us
    pallas_call x10, Pallas kernels, call(): pl.pallas_call(body, out_shape=list(outputs), in_specs=in_specs or [VMEM]...  9.53 us
  transfers between devices with their start and end apart: 21, of which 8 were waited for; matrix products, arithmetic and copies ran while one was open for 1% of the time, Pallas kernels for 8%

profile of v6, /device:TPU:0, one launch (start us, length us, event | category | flops | bytes accessed | tf_op | source)
XLA Modules:
  0.0 69.1 jit_solution(17673201125612932518)
XLA Ops:
  0.6 1.7 %norm_select.1 = (bf16[64,512]{1,0:T(8,128)(2,1)S(1)}, bf16[64,512]{1,0:T(8,128)(2,1)S(1)}, bf16[64,512]{1,0:T(8,128)(2,1)S(1)}, bf16[64,512]{1,0:T(8,128)(2,1)S...) custom-call(bf16[64,8192]{1,0:T(8,128)(2,1)} %hidden_in.1, ...), custom_call_target="tpu_custom_call" | custom-call | flops 2097152 | bytes 1736960 | tf_op jit(solution)/shard_map/norm_select/pallas_call | solution.py:21
  2.4 4.1 %collective-permute-start.5 = (bf16[64,512]{1,0:T(8,128)(2,1)S(1)}, bf16[64,512]{1,0:T(8,128)(2,1)S(1)}, u32[]{:S(2)}, u32[]{:S(2)}) collective-permute-start(bf16[64,512]{1,0:T(8,128)(2,1)S(1)} %get-tuple-element.36), channel_id=1, source_target_pairs={{0,8},{2,10},{4,12},{6,14},{8,0},{10,2},{12,4},{14,6},{1,9},{3,11}... | collective-permute-start | bytes 196616 | tf_op jit(solution)/shard_map/ppermute | solution.py:215
  6.5 0.1 collective-permute-start
  6.6 3.8 %collective-permute-start.1 = (bf16[64,512]{1,0:T(8,128)(2,1)S(1)}, bf16[64,512]{1,0:T(8,128)(2,1)S(1)}, u32[]{:S(2)}, u32[]{:S(2)}) collective-permute-start(bf16[64,512]{1,0:T(8,128)(2,1)S(1)} %get-tuple-element.31), channel_id=1, source_target_pairs={{0,10},{2,8},{4,14},{6,12},{8,2},{10,0},{12,6},{14,4},{1,11},{3,9}... | collective-permute-start | bytes 196616 | tf_op jit(solution)/shard_map/ppermute | solution.py:215
  10.4 0.5 collective-permute-start.2
  10.9 1.3 %collective-permute-start.3 = (bf16[64,512]{1,0:T(8,128)(2,1)S(1)}, bf16[64,512]{1,0:T(8,128)(2,1)S(1)}, u32[]{:S(2)}, u32[]{:S(2)}) collective-permute-start(bf16[64,512]{1,0:T(8,128)(2,1)S(1)} %get-tuple-element.33), channel_id=1, source_target_pairs={{0,12},{2,14},{4,8},{6,10},{8,4},{10,6},{12,0},{14,2},{1,13},{3,15... | collective-permute-start | bytes 196616 | tf_op jit(solution)/shard_map/ppermute | solution.py:215
  12.2 0.0 collective-permute-done.5
  12.2 0.7 %collective-permute-start.6 = (bf16[128,512]{1,0:T(8,128)(2,1)S(1)}, bf16[128,512]{1,0:T(8,128)(2,1)S(1)}, u32[]{:S(2)}, u32[]{:S(2)}) collective-permute-start(bf16[128,512]{1,0:T(8,128)(2,1)S(1)} %pad_maximum_fusion), channel_id=1, source_target_pairs={{0,4},{2,6},{4,0},{6,2},{8,12},{10,14},{12,8},{14,10},{1,5},{3,7},... | collective-permute-start | bytes 393224 | tf_op jit(solution)/shard_map/ppermute | solution.py:215
  13.0 6.7 %collective-permute-done.6 = bf16[128,512]{1,0:T(8,128)(2,1)S(1)} collective-permute-done((bf16[128,512]{1,0:T(8,128)(2,1)S(1)}, bf16[128,512]{1,0:T(8,128)(2,1)S(1)}, u32[]{:S(2)}, u32[]{:S(2)}) %collective-permute-start.6) | collective-permute-done | bytes 131104 | tf_op jit(solution)/shard_map/ppermute | solution.py:215
  19.6 0.0 collective-permute-start.4
  19.6 0.0 collective-permute-done.refs_0_.refs_4_
  19.7 3.6 %collective-permute-start.8 = (bf16[64,512]{1,0:T(8,128)(2,1)S(1)}, bf16[64,512]{1,0:T(8,128)(2,1)S(1)}, u32[]{:S(2)}, u32[]{:S(2)}) collective-permute-start(bf16[64,512]{1,0:T(8,128)(2,1)S(1)} %get-tuple-element.39), channel_id=1, source_target_pairs={{0,6},{2,4},{4,2},{6,0},{8,14},{10,12},{12,10},{14,8},{1,7},{3,5},... | collective-permute-start | bytes 196616 | tf_op jit(solution)/shard_map/ppermute | solution.py:215
  23.3 0.0 collective-permute-done.1.refs_1_.refs_5_
  23.3 3.1 %collective-permute-start.9 = (bf16[64,512]{1,0:T(8,128)(2,1)S(1)}, bf16[64,512]{1,0:T(8,128)(2,1)S(1)}, u32[]{:S(2)}, u32[]{:S(2)}) collective-permute-start(bf16[64,512]{1,0:T(8,128)(2,1)S(1)} %get-tuple-element.40), channel_id=1, source_target_pairs={{0,14},{2,12},{4,10},{6,8},{8,6},{10,4},{12,2},{14,0},{1,15},{3,13... | collective-permute-start | bytes 196616 | tf_op jit(solution)/shard_map/ppermute | solution.py:215
  26.4 0.0 collective-permute-done.2.refs_2_.refs_1_
  26.4 1.5 %collective-permute-start.7 = (bf16[256,512]{1,0:T(8,128)(2,1)S(1)}, bf16[256,512]{1,0:T(8,128)(2,1)S(1)}, u32[]{:S(2)}, u32[]{:S(2)}) collective-permute-start(bf16[256,512]{1,0:T(8,128)(2,1)S(1)} %constant_dynamic-update-slice_fusion.held_a), channel_id=1, source_target_pairs={{0,2},{2,0},{4,6},{6,4},{8,10},{10,8},{12,14},{14,12},{1,3},{3,1},... | collective-permute-start | bytes 786440 | tf_op jit(solution)/shard_map/ppermute | solution.py:215
  27.9 0.0 collective-permute-done.4.refs_4_.refs_2_
  27.9 2.5 %stage.1 = (bf16[1024,2560]{1,0:T(8,128)(2,1)S(1)}, bf16[64,2048]{1,0:T(8,128)(2,1)S(1)}, s32[1,512]{1,0:T(1,128)S(1)}) custom-call(s32[8]{0:T(128)} %counts_in.1, bf16[1024,2560]{1,0:T(8,128)(2,1)} %matrix_in.1, bf16[64,2048]{1,0:T(8,128)(2,1)} %queries_in.1, bf16[64,512]{1,0:T(8,128)(2,1)S(1)} %collective-permute-done.refs_0_.refs_4_, ...), custom_call_target="tpu_custom_call" | custom-call | flops 3932160000 | bytes 11339808 | tf_op jit(solution)/shard_map/stage/pallas_call | solution.py:21
  30.4 0.0 collective-permute-done.8.refs_3_
  30.5 4.6 %collective-permute-done.7.after.held_b = bf16[256,512]{1,0:T(8,128)(2,1)S(1)} collective-permute-done((bf16[256,512]{1,0:T(8,128)(2,1)S(1)}, bf16[256,512]{1,0:T(8,128)(2,1)S(1)}, u32[]{:S(2)}, u32[]{:S(2)}) %collective-permute-start.7) | collective-permute-done | bytes 262176 | tf_op jit(solution)/shard_map/ppermute | solution.py:215
  35.0 0.3 compact.1.after.own
  35.4 0.1 collective-permute-start.10
  35.4 2.0 %attention.1 = (f32[64,2048]{1,0:T(8,128)}, f32[8,64]{1,0:T(8,128)S(1)}) custom-call(bf16[64,2048]{1,0:T(8,128)(2,1)S(1)} %get-tuple-element.35.queries, bf16[256,512]{1,0:T(8,128)(2,1)S(1)} %constant_dynamic-update-slice_fusion.held_a, bf16[256,512]{1,0:T(8,128)(2,1)S(1)} %collective-permute-done.7.after.held_b, bf16[256,512]{1,0:T(8,128)(2,1)S(1)} %compact.1.after.own), custom_call_target="tpu_custom_call" | custom-call | flops 268435456 | bytes 1574912 | tf_op jit(solution)/shard_map/attention/pallas_call | solution.py:21
  37.4 0.0 collective-permute-done.10.other
  37.4 1.0 %project.3 = (f32[128,1280]{1,0:T(8,128)S(1)}, bf16[128,1280]{1,0:T(8,128)(2,1)S(1)}) custom-call(bf16[256,512]{1,0:T(8,128)(2,1)S(1)} %compact.1.after.own, bf16[256,512]{1,0:T(8,128)(2,1)S(1)} %collective-permute-done.10.other, bf16[1024,2560]{1,0:T(8,128)(2,1)S(1)} %get-tuple-element.42.matrix, f32[8,64]{1,0:T(8,128)S(1)} %get-tuple-element.43.after), custom_call_target="tpu_custom_call" | custom-call | flops 671088640 | bytes 6752256 | tf_op jit(solution)/shard_map/project/pallas_call | solution.py:21
  38.4 0.0 copy-start
  38.4 0.1 collective-permute-start.12
  38.5 1.0 %project.2 = (f32[128,1280]{1,0:T(8,128)S(1)}, bf16[128,1280]{1,0:T(8,128)(2,1)S(1)}) custom-call(bf16[256,512]{1,0:T(8,128)(2,1)S(1)} %compact.1.after.own, bf16[256,512]{1,0:T(8,128)(2,1)S(1)} %collective-permute-done.10.other, bf16[1024,2560]{1,0:T(8,128)(2,1)S(1)} %get-tuple-element.42.matrix, f32[8,64]{1,0:T(8,128)S(1)} %get-tuple-element.43.after), custom_call_target="tpu_custom_call" | custom-call | flops 671088640 | bytes 6752256 | tf_op jit(solution)/shard_map/project/pallas_call | solution.py:21
  39.5 0.9 %collective-permute-start.11 = (bf16[128,1280]{1,0:T(8,128)(2,1)S(1)}, bf16[128,1280]{1,0:T(8,128)(2,1)S(1)}, u32[]{:S(2)}, u32[]{:S(2)}) collective-permute-start(bf16[128,1280]{1,0:T(8,128)(2,1)S(1)} %get-tuple-element.45), channel_id=1, source_target_pairs={{0,2},{2,0},{4,6},{6,4},{8,10},{10,8},{12,14},{14,12},{1,3},{3,1},... | collective-permute-start | bytes 983048 | tf_op jit(solution)/shard_map/ppermute | solution.py:215
  40.4 0.2 collective-permute-start.13
  40.6 1.2 %collective-permute-start.14 = (f32[4,64]{1,0:T(4,128)S(1)}, f32[4,64]{1,0:T(4,128)S(1)}, u32[]{:S(2)}, u32[]{:S(2)}) collective-permute-start(f32[4,64]{1,0:T(4,128)S(1)} %get-tuple-element.58), channel_id=1, source_target_pairs={{0,2},{2,0},{4,6},{6,4},{8,10},{10,8},{12,14},{14,12},{1,3},{3,1},... | collective-permute-start | bytes 3080 | tf_op jit(solution)/shard_map/ppermute | solution.py:215
  41.8 0.4 collective-permute-start.15
  42.3 7.5 %collective-permute-done.14 = f32[4,64]{1,0:T(4,128)S(1)} collective-permute-done((f32[4,64]{1,0:T(4,128)S(1)}, f32[4,64]{1,0:T(4,128)S(1)}, u32[]{:S(2)}, u32[]{:S(2)}) %collective-permute-start.14) | collective-permute-done | bytes 1056 | tf_op jit(solution)/shard_map/ppermute | solution.py:215
  49.8 0.1 hop_sum.2
  49.9 0.1 hop_sum.3
  50.0 1.8 %collective-permute-start.18 = (f32[2,64]{1,0:T(2,128)S(1)}, f32[2,64]{1,0:T(2,128)S(1)}, u32[]{:S(2)}, u32[]{:S(2)}) collective-permute-start(f32[2,64]{1,0:T(2,128)S(1)} %slice.21), channel_id=1, source_target_pairs={{0,4},{2,6},{4,0},{6,2},{8,12},{10,14},{12,8},{14,10},{1,5},{3,7},... | collective-permute-start | bytes 1544 | tf_op jit(solution)/shard_map/ppermute | solution.py:215
  51.7 0.3 collective-permute-start.16
  52.1 0.8 %collective-permute-start.17 = (bf16[64,1280]{1,0:T(8,128)(2,1)S(1)}, bf16[64,1280]{1,0:T(8,128)(2,1)S(1)}, u32[]{:S(2)}, u32[]{:S(2)}) collective-permute-start(bf16[64,1280]{1,0:T(8,128)(2,1)S(1)} %get-tuple-element.52), channel_id=1, source_target_pairs={{0,2},{2,0},{4,6},{6,4},{8,10},{10,8},{12,14},{14,12},{1,3},{3,1},... | collective-permute-start | bytes 491528 | tf_op jit(solution)/shard_map/ppermute | solution.py:215
  52.9 0.7 %collective-permute-done.18 = f32[2,64]{1,0:T(2,128)S(1)} collective-permute-done((f32[2,64]{1,0:T(2,128)S(1)}, f32[2,64]{1,0:T(2,128)S(1)}, u32[]{:S(2)}, u32[]{:S(2)}) %collective-permute-start.18) | collective-permute-done | bytes 544 | tf_op jit(solution)/shard_map/ppermute | solution.py:215
  53.6 4.1 %collective-permute-done.16.refs_2_ = bf16[64,1280]{1,0:T(8,128)(2,1)S(1)} collective-permute-done((bf16[64,1280]{1,0:T(8,128)(2,1)S(1)}, bf16[64,1280]{1,0:T(8,128)(2,1)S(1)}, u32[]{:S(2)}, u32[]{:S(2)}) %collective-permute-start.16) | collective-permute-done | bytes 163872 | tf_op jit(solution)/shard_map/ppermute | solution.py:215
  57.7 0.1 collective-permute-done.17.refs_3_
  57.8 0.1 hop_sum_both.1
  57.8 1.6 %collective-permute-start.19 = (f32[1,64]{1,0:T(1,128)S(1)}, f32[1,64]{1,0:T(1,128)S(1)}, u32[]{:S(2)}, u32[]{:S(2)}) collective-permute-start(f32[1,64]{1,0:T(1,128)S(1)} %slice.23), channel_id=1, source_target_pairs={{0,8},{2,10},{4,12},{6,14},{8,0},{10,2},{12,4},{14,6},{1,9},{3,11}... | collective-permute-start | bytes 776 | tf_op jit(solution)/shard_map/ppermute | solution.py:215
  59.4 1.5 %collective-permute-start.20 = (bf16[32,2560]{1,0:T(8,128)(2,1)S(1)}, bf16[32,2560]{1,0:T(8,128)(2,1)S(1)}, u32[]{:S(2)}, u32[]{:S(2)}) collective-permute-start(bf16[32,2560]{1,0:T(8,128)(2,1)S(1)} %get-tuple-element.56), channel_id=1, source_target_pairs={{0,8},{2,10},{4,12},{6,14},{8,0},{10,2},{12,4},{14,6},{1,9},{3,11}... | collective-permute-start | bytes 491528 | tf_op jit(solution)/shard_map/ppermute | solution.py:215
  60.9 2.4 %collective-permute-done.19 = f32[1,64]{1,0:T(1,128)S(1)} collective-permute-done((f32[1,64]{1,0:T(1,128)S(1)}, f32[1,64]{1,0:T(1,128)S(1)}, u32[]{:S(2)}, u32[]{:S(2)}) %collective-permute-start.19) | collective-permute-done | bytes 288 | tf_op jit(solution)/shard_map/ppermute | solution.py:215
  63.3 0.5 multiply_bitcast_fusion
  63.8 4.6 %collective-permute-done.20.received = bf16[32,2560]{1,0:T(8,128)(2,1)S(1)} collective-permute-done((bf16[32,2560]{1,0:T(8,128)(2,1)S(1)}, bf16[32,2560]{1,0:T(8,128)(2,1)S(1)}, u32[]{:S(2)}, u32[]{:S(2)}) %collective-permute-start.20) | collective-permute-done | bytes 163872 | tf_op jit(solution)/shard_map/ppermute | solution.py:215
  68.3 0.8 %finish.1 = f32[32,2560]{1,0:T(8,128)} custom-call(f32[1,2560]{1,0:T(1,128)S(1)} %reshape.20.bias, f32[32,2560]{1,0:T(8,128)S(1)} %get-tuple-element.55.kept, bf16[32,2560]{1,0:T(8,128)(2,1)S(1)} %collective-permute-done.20.received), custom_call_target="tpu_custom_call" | custom-call | flops 655360 | bytes 829440 | tf_op jit(solution)/shard_map/finish/pallas_call | solution.py:21
  (17 shorter events, 0.1 us)
Async XLA Ops:
  2.4 9.8 %collective-permute-start.5 = (bf16[64,512]{1,0:T(8,128)(2,1)S(1)}, bf16[64,512]{1,0:T(8,128)(2,1)S(1)}, u32[]{:S(2)}, u32[]{:S(2)}) collective-permute-start(bf16[64,512]{1,0:T(8,128)(2,1)S(1)} %get-tuple-element.36), channel_id=1, source_target_pairs={{0,8},{2,10},{4,12},{6,14},{8,0},{10,2},{12,4},{14,6},{1,9},{3,11}... | collective-permute-start | bytes 196616 | tf_op jit(solution)/shard_map/ppermute | solution.py:215
  6.5 13.2 %collective-permute-start = (bf16[64,512]{1,0:T(8,128)(2,1)S(1)}, bf16[64,512]{1,0:T(8,128)(2,1)S(1)}, u32[]{:S(2)}, u32[]{:S(2)}) collective-permute-start(bf16[64,512]{1,0:T(8,128)(2,1)S(1)} %get-tuple-element.30), channel_id=1, source_target_pairs={{0,8},{2,10},{4,12},{6,14},{8,0},{10,2},{12,4},{14,6},{1,9},{3,11}... | collective-permute-start | bytes 196616 | tf_op jit(solution)/shard_map/ppermute | solution.py:215
  6.6 16.7 %collective-permute-start.1 = (bf16[64,512]{1,0:T(8,128)(2,1)S(1)}, bf16[64,512]{1,0:T(8,128)(2,1)S(1)}, u32[]{:S(2)}, u32[]{:S(2)}) collective-permute-start(bf16[64,512]{1,0:T(8,128)(2,1)S(1)} %get-tuple-element.31), channel_id=1, source_target_pairs={{0,10},{2,8},{4,14},{6,12},{8,2},{10,0},{12,6},{14,4},{1,11},{3,9}... | collective-permute-start | bytes 196616 | tf_op jit(solution)/shard_map/ppermute | solution.py:215
  10.4 16.0 %collective-permute-start.2 = (bf16[64,512]{1,0:T(8,128)(2,1)S(1)}, bf16[64,512]{1,0:T(8,128)(2,1)S(1)}, u32[]{:S(2)}, u32[]{:S(2)}) collective-permute-start(bf16[64,512]{1,0:T(8,128)(2,1)S(1)} %get-tuple-element.32), channel_id=1, source_target_pairs={{0,2},{2,0},{4,6},{6,4},{8,10},{10,8},{12,14},{14,12},{1,3},{3,1},... | collective-permute-start | bytes 196616 | tf_op jit(solution)/shard_map/ppermute | solution.py:215
  10.9 17.0 %collective-permute-start.3 = (bf16[64,512]{1,0:T(8,128)(2,1)S(1)}, bf16[64,512]{1,0:T(8,128)(2,1)S(1)}, u32[]{:S(2)}, u32[]{:S(2)}) collective-permute-start(bf16[64,512]{1,0:T(8,128)(2,1)S(1)} %get-tuple-element.33), channel_id=1, source_target_pairs={{0,12},{2,14},{4,8},{6,10},{8,4},{10,6},{12,0},{14,2},{1,13},{3,15... | collective-permute-start | bytes 196616 | tf_op jit(solution)/shard_map/ppermute | solution.py:215
  12.2 7.4 %collective-permute-start.6 = (bf16[128,512]{1,0:T(8,128)(2,1)S(1)}, bf16[128,512]{1,0:T(8,128)(2,1)S(1)}, u32[]{:S(2)}, u32[]{:S(2)}) collective-permute-start(bf16[128,512]{1,0:T(8,128)(2,1)S(1)} %pad_maximum_fusion), channel_id=1, source_target_pairs={{0,4},{2,6},{4,0},{6,2},{8,12},{10,14},{12,8},{14,10},{1,5},{3,7},... | collective-permute-start | bytes 393224 | tf_op jit(solution)/shard_map/ppermute | solution.py:215
  19.6 8.3 %collective-permute-start.4 = (bf16[64,512]{1,0:T(8,128)(2,1)S(1)}, bf16[64,512]{1,0:T(8,128)(2,1)S(1)}, u32[]{:S(2)}, u32[]{:S(2)}) collective-permute-start(bf16[64,512]{1,0:T(8,128)(2,1)S(1)} %get-tuple-element.34), channel_id=1, source_target_pairs={{0,4},{2,6},{4,0},{6,2},{8,12},{10,14},{12,8},{14,10},{1,5},{3,7},... | collective-permute-start | bytes 196616 | tf_op jit(solution)/shard_map/ppermute | solution.py:215
  19.7 10.8 %collective-permute-start.8 = (bf16[64,512]{1,0:T(8,128)(2,1)S(1)}, bf16[64,512]{1,0:T(8,128)(2,1)S(1)}, u32[]{:S(2)}, u32[]{:S(2)}) collective-permute-start(bf16[64,512]{1,0:T(8,128)(2,1)S(1)} %get-tuple-element.39), channel_id=1, source_target_pairs={{0,6},{2,4},{4,2},{6,0},{8,14},{10,12},{12,10},{14,8},{1,7},{3,5},... | collective-permute-start | bytes 196616 | tf_op jit(solution)/shard_map/ppermute | solution.py:215
  23.3 7.2 %collective-permute-start.9 = (bf16[64,512]{1,0:T(8,128)(2,1)S(1)}, bf16[64,512]{1,0:T(8,128)(2,1)S(1)}, u32[]{:S(2)}, u32[]{:S(2)}) collective-permute-start(bf16[64,512]{1,0:T(8,128)(2,1)S(1)} %get-tuple-element.40), channel_id=1, source_target_pairs={{0,14},{2,12},{4,10},{6,8},{8,6},{10,4},{12,2},{14,0},{1,15},{3,13... | collective-permute-start | bytes 196616 | tf_op jit(solution)/shard_map/ppermute | solution.py:215
  26.4 8.7 %collective-permute-start.7 = (bf16[256,512]{1,0:T(8,128)(2,1)S(1)}, bf16[256,512]{1,0:T(8,128)(2,1)S(1)}, u32[]{:S(2)}, u32[]{:S(2)}) collective-permute-start(bf16[256,512]{1,0:T(8,128)(2,1)S(1)} %constant_dynamic-update-slice_fusion.held_a), channel_id=1, source_target_pairs={{0,2},{2,0},{4,6},{6,4},{8,10},{10,8},{12,14},{14,12},{1,3},{3,1},... | collective-permute-start | bytes 786440 | tf_op jit(solution)/shard_map/ppermute | solution.py:215
  35.4 2.1 %collective-permute-start.10 = (bf16[256,512]{1,0:T(8,128)(2,1)S(1)}, bf16[256,512]{1,0:T(8,128)(2,1)S(1)}, u32[]{:S(2)}, u32[]{:S(2)}) collective-permute-start(bf16[256,512]{1,0:T(8,128)(2,1)S(1)} %compact.1.after.own), channel_id=1, source_target_pairs={{0,1},{1,0},{2,3},{3,2},{4,5},{5,4},{6,7},{7,6},{8,9},{9,8},{10,11... | collective-permute-start | bytes 786440 | tf_op jit(solution)/shard_map/ppermute | solution.py:221
  38.4 21.0 %copy-start = (f32[2560]{0:T(1024)S(1)}, f32[2560]{0:T(1024)}, u32[]{:S(2)}) copy-start(f32[2560]{0:T(1024)} %param.17) | copy-start | bytes 30724
  38.4 11.3 %collective-permute-start.12 = (bf16[128,1280]{1,0:T(8,128)(2,1)S(1)}, bf16[128,1280]{1,0:T(8,128)(2,1)S(1)}, u32[]{:S(2)}, u32[]{:S(2)}) collective-permute-start(bf16[128,1280]{1,0:T(8,128)(2,1)S(1)} %get-tuple-element.47), channel_id=1, source_target_pairs={{0,4},{2,6},{4,0},{6,2},{8,12},{10,14},{12,8},{14,10},{1,5},{3,7},... | collective-permute-start | bytes 983048 | tf_op jit(solution)/shard_map/ppermute | solution.py:215
  39.5 10.3 %collective-permute-start.11 = (bf16[128,1280]{1,0:T(8,128)(2,1)S(1)}, bf16[128,1280]{1,0:T(8,128)(2,1)S(1)}, u32[]{:S(2)}, u32[]{:S(2)}) collective-permute-start(bf16[128,1280]{1,0:T(8,128)(2,1)S(1)} %get-tuple-element.45), channel_id=1, source_target_pairs={{0,2},{2,0},{4,6},{6,4},{8,10},{10,8},{12,14},{14,12},{1,3},{3,1},... | collective-permute-start | bytes 983048 | tf_op jit(solution)/shard_map/ppermute | solution.py:215
  40.4 1.9 %collective-permute-start.13 = (f32[4,64]{1,0:T(4,128)S(1)}, f32[4,64]{1,0:T(4,128)S(1)}, u32[]{:S(2)}, u32[]{:S(2)}) collective-permute-start(f32[4,64]{1,0:T(4,128)S(1)} %get-tuple-element.57), channel_id=1, source_target_pairs={{0,1},{1,0},{2,3},{3,2},{4,5},{5,4},{6,7},{7,6},{8,9},{9,8},{10,11... | collective-permute-start | bytes 3080 | tf_op jit(solution)/shard_map/ppermute | solution.py:221
  40.6 9.1 %collective-permute-start.14 = (f32[4,64]{1,0:T(4,128)S(1)}, f32[4,64]{1,0:T(4,128)S(1)}, u32[]{:S(2)}, u32[]{:S(2)}) collective-permute-start(f32[4,64]{1,0:T(4,128)S(1)} %get-tuple-element.58), channel_id=1, source_target_pairs={{0,2},{2,0},{4,6},{6,4},{8,10},{10,8},{12,14},{14,12},{1,3},{3,1},... | collective-permute-start | bytes 3080 | tf_op jit(solution)/shard_map/ppermute | solution.py:215
  41.8 7.9 %collective-permute-start.15 = (f32[4,64]{1,0:T(4,128)S(1)}, f32[4,64]{1,0:T(4,128)S(1)}, u32[]{:S(2)}, u32[]{:S(2)}) collective-permute-start(f32[4,64]{1,0:T(4,128)S(1)} %get-tuple-element.58), channel_id=1, source_target_pairs={{0,3},{1,2},{2,1},{3,0},{4,7},{5,6},{6,5},{7,4},{8,11},{9,10},{10,... | collective-permute-start | bytes 3080 | tf_op jit(solution)/shard_map/ppermute | solution.py:218
  50.0 3.6 %collective-permute-start.18 = (f32[2,64]{1,0:T(2,128)S(1)}, f32[2,64]{1,0:T(2,128)S(1)}, u32[]{:S(2)}, u32[]{:S(2)}) collective-permute-start(f32[2,64]{1,0:T(2,128)S(1)} %slice.21), channel_id=1, source_target_pairs={{0,4},{2,6},{4,0},{6,2},{8,12},{10,14},{12,8},{14,10},{1,5},{3,7},... | collective-permute-start | bytes 1544 | tf_op jit(solution)/shard_map/ppermute | solution.py:215
  51.7 5.9 %collective-permute-start.16 = (bf16[64,1280]{1,0:T(8,128)(2,1)S(1)}, bf16[64,1280]{1,0:T(8,128)(2,1)S(1)}, u32[]{:S(2)}, u32[]{:S(2)}) collective-permute-start(bf16[64,1280]{1,0:T(8,128)(2,1)S(1)} %get-tuple-element.51), channel_id=1, source_target_pairs={{0,4},{2,6},{4,0},{6,2},{8,12},{10,14},{12,8},{14,10},{1,5},{3,7},... | collective-permute-start | bytes 491528 | tf_op jit(solution)/shard_map/ppermute | solution.py:215
  52.1 5.7 %collective-permute-start.17 = (bf16[64,1280]{1,0:T(8,128)(2,1)S(1)}, bf16[64,1280]{1,0:T(8,128)(2,1)S(1)}, u32[]{:S(2)}, u32[]{:S(2)}) collective-permute-start(bf16[64,1280]{1,0:T(8,128)(2,1)S(1)} %get-tuple-element.52), channel_id=1, source_target_pairs={{0,2},{2,0},{4,6},{6,4},{8,10},{10,8},{12,14},{14,12},{1,3},{3,1},... | collective-permute-start | bytes 491528 | tf_op jit(solution)/shard_map/ppermute | solution.py:215
  57.8 5.4 %collective-permute-start.19 = (f32[1,64]{1,0:T(1,128)S(1)}, f32[1,64]{1,0:T(1,128)S(1)}, u32[]{:S(2)}, u32[]{:S(2)}) collective-permute-start(f32[1,64]{1,0:T(1,128)S(1)} %slice.23), channel_id=1, source_target_pairs={{0,8},{2,10},{4,12},{6,14},{8,0},{10,2},{12,4},{14,6},{1,9},{3,11}... | collective-permute-start | bytes 776 | tf_op jit(solution)/shard_map/ppermute | solution.py:215
  59.4 8.9 %collective-permute-start.20 = (bf16[32,2560]{1,0:T(8,128)(2,1)S(1)}, bf16[32,2560]{1,0:T(8,128)(2,1)S(1)}, u32[]{:S(2)}, u32[]{:S(2)}) collective-permute-start(bf16[32,2560]{1,0:T(8,128)(2,1)S(1)} %get-tuple-element.56), channel_id=1, source_target_pairs={{0,8},{2,10},{4,12},{6,14},{8,0},{10,2},{12,4},{14,6},{1,9},{3,11}... | collective-permute-start | bytes 491528 | tf_op jit(solution)/shard_map/ppermute | solution.py:215

commit v7 on v6

--- a/solution.py
+++ b/solution.py
@@ -30,8 +30,8 @@
     )(*inputs)
 
 
-def norm_select_kernel(n, hidden_in, gain_in, kept_in, keys_in, values_in, pair, *refs):
-    outs, (hidden, gain, kept, sems) = refs[:n], refs[n:]
+def norm_select_kernel(n, hidden_in, gain_in, kept_in, keys_in, values_in, *refs):
+    outs, (hidden, gain, kept, pair, sems) = refs[:n], refs[n:]
     rows, width = hidden.shape
     block = width // n
     half = block // 2
@@ -68,7 +68,8 @@
         start = pl.multiple_of(lax.bitwise_xor(s, k) * block + t * half, half)
         columns = pl.ds(start, half)
         normed = (hidden[:, columns].astype(jnp.float32) * scale * gain[:, columns]).astype(jnp.bfloat16)
-        outs[k][...] = lax.dot_general(
+        outs[k][:, half:] = pair[...]
+        outs[k][:, :half] = lax.dot_general(
             selector, normed, (((0,), (0,)), ((), ())), preferred_element_type=jnp.float32
         ).astype(jnp.bfloat16)
 
@@ -100,11 +101,11 @@
         load.wait()
 
 
-def compact_kernel(n, target, after, *refs):
+def compact_kernel(n, target, *refs):
     blocks, out = refs[:n], refs[n]
     lines = out.shape[0] // n
     s = lax.axis_index("seq")
-    received = jnp.concatenate([b[...] for b in blocks], axis=0)
+    received = jnp.concatenate([b[:, : out.shape[1]] for b in blocks], axis=0)
     line = lax.broadcasted_iota(jnp.int32, (lines, received.shape[0]), 0)
     pick = jnp.concatenate(
         [(line + lax.bitwise_xor(s, k) * lines == target[...]).astype(jnp.float32) for k in range(n)], axis=0
@@ -158,24 +159,25 @@
         sent[:, lanes] = total[rows:].astype(jnp.bfloat16)
 
 
-def attention_kernel(n, kv_heads, order, masks, queries, held_a, held_b, after, context, columns):
+def attention_kernel(n, kv_heads, masks, queries, after, *refs):
+    blocks, (context, columns) = refs[:n], refs[n:]
+    first = blocks[0].shape[1] - 2 * kv_heads * HEAD_SIZE
     rows = queries.shape[0]
     group = queries.shape[1] // (HEAD_SIZE * kv_heads)
     s = lax.axis_index("seq")
     keys_total = n * rows
     column = lax.broadcasted_iota(jnp.int32, (1, keys_total), 1)
     position = column
-    for at, k in enumerate(order):
-        inside = (column >= at * rows) & (column < (at + 1) * rows)
-        position = jnp.where(inside, column + (lax.bitwise_xor(s, k) - s - at) * rows, position)
+    for k in range(n):
+        inside = (column >= k * rows) & (column < (k + 1) * rows)
+        position = jnp.where(inside, column + (lax.bitwise_xor(s, k) - s - k) * rows, position)
     row = lax.rem(lax.broadcasted_iota(jnp.int32, (group * rows, keys_total), 0), rows)
     allowed = position <= row
     sums = jnp.zeros((1, keys_total), jnp.float32)
     for g in range(kv_heads):
-        key_lanes = slice(g * HEAD_SIZE, (g + 1) * HEAD_SIZE)
-        value_lanes = slice((kv_heads + g) * HEAD_SIZE, (kv_heads + g + 1) * HEAD_SIZE)
-        key = jnp.concatenate([held_a[:, key_lanes], held_b[:, key_lanes]], axis=0)
-        value = jnp.concatenate([held_a[:, value_lanes], held_b[:, value_lanes]], axis=0)
+        key_at, value_at = first + g * HEAD_SIZE, first + (kv_heads + g) * HEAD_SIZE
+        key = jnp.concatenate([b[:, key_at : key_at + HEAD_SIZE] for b in blocks], axis=0)
+        value = jnp.concatenate([b[:, value_at : value_at + HEAD_SIZE] for b in blocks], axis=0)
         heads = range(g * group, (g + 1) * group)
         stacked = jnp.concatenate([queries[:, h * HEAD_SIZE : (h + 1) * HEAD_SIZE] for h in heads], axis=0)
         scores = lax.dot_general(
@@ -188,9 +190,8 @@
         for i, h in enumerate(heads):
             context[:, h * HEAD_SIZE : (h + 1) * HEAD_SIZE] = mixed[i * rows : (i + 1) * rows]
         sums += jnp.sum(weights * inverse, axis=0, keepdims=True)
-    for at, k in enumerate(order):
-        i = halving_order(n, masks).index(k)
-        columns[i : i + 1, :] = sums[:, at * rows : (at + 1) * rows]
+    for i, k in enumerate(halving_order(n, masks)):
+        columns[i : i + 1, :] = sums[:, k * rows : (k + 1) * rows]
 
 
 def finish_kernel(bias, kept, received, out):
@@ -224,16 +225,16 @@
         left = columns.shape[0] // 2
         return columns[:left] + trade(columns[left:], mask)
 
-    pair, *chosen = call(
+    chosen = call(
         functools.partial(norm_select_kernel, n),
         "norm_select",
         (hidden, norm_gain.reshape(1, model), retained_lists.reshape(1, rows), keys, values),
-        [shape((rows, 2 * keys.shape[1]), bf16)] + [shape((rows, half), bf16)] * n,
+        [shape((rows, half + 2 * keys.shape[1]), bf16)] * n,
         4 * rows * model,
         limit=16,
         in_specs=[ANY] * 5,
         remote=5,
-        scratch=[pltpu.VMEM((rows, model), bf16), pltpu.VMEM((1, model), f32), pltpu.VMEM((1, rows), i32), dma((8,))],
+        scratch=[pltpu.VMEM((rows, model), bf16), pltpu.VMEM((1, model), f32), pltpu.VMEM((1, rows), i32), pltpu.VMEM((rows, 2 * keys.shape[1]), bf16), dma((8,))],
     )
     received = [chosen[0]] + [trade(chosen[k], k) for k in range(1, n)]
     turns = [k for i in range(n // 2) for k in (n // 2 + i, i) if k]
@@ -247,33 +248,24 @@
         remote=3,
         scratch=[pltpu.SMEM(counts.shape, i32), dma((3,))],
     )
-    held, order, mask = pair, [0], n // 2
-    while mask > 1:
-        held = jnp.concatenate([held, trade(held, mask)], axis=0)
-        order = order + [k ^ mask for k in order]
-        mask //= 2
-    held_other = trade(held, 1)
-    order = order + [k ^ 1 for k in order]
-
     (own,) = call(
         functools.partial(compact_kernel, n),
         "compact",
-        (target, held_other, *received),
+        (target, *received),
         [shape((survivors, half), bf16)],
         2 * survivors * n * rows * half,
-        in_specs=[VMEM, ANY] + [VMEM] * n,
     )
     other = swap(own)
     rest = [1 << i for i in range(2, n.bit_length() - 1)]
     masks = [[1, 2] + rest, [2, 1] + rest]
     context, columns = call(
-        functools.partial(attention_kernel, n, kv_heads, order, masks[0]),
+        functools.partial(attention_kernel, n, kv_heads, masks[0]),
         "attention",
-        (queries, held, held_other, own),
+        (queries, own, *received),
         [shape(queries.shape, f32), shape((n, rows), f32)],
         4 * rows * n * rows * queries.shape[1],
         limit=32,
-        in_specs=[VMEM] * 3 + [ANY],
+        in_specs=[VMEM, ANY] + [VMEM] * n,
     )
 
     products = [

time: 69.3 us -> 66.9 us (0.965)
  starting transfers between devices: 27.6 us -> 23 us
  waiting for transfers between devices: 30.6 us -> 32.9 us
    ppermute x18 -> x15, starting transfers between devices: 26.9 us -> 21.8 us  [trade(): return lax.ppermute(x, 'seq', [(i, i ^ k) for i in range(n)])]
    ppermute x18 -> x15, waiting for transfers between devices: 30.6 us -> 32.9 us  [trade(): return lax.ppermute(x, 'seq', [(i, i ^ k) for i in range(n)])]
    ppermute x1, starting transfers between devices: 0.43 us -> 1.17 us  [trade_across(): lax.ppermute(x, ('seq', 'ten'), [(2 * i + t, 2 * (i ^ k) + 1 - t) for i i...]
  transfers between devices with their start and end apart: 21 -> 18, of which waited for: 8 -> 10; matrix products, arithmetic and copies ran while one was open for 1% -> 1% of each run, Pallas kernels for 8% -> 8%
where the time goes in v7:
time: 66.9 us; the launch traced here: 66.8 us
  waiting for transfers between devices  32.9 us (49%)
  starting transfers between devices  23 us (34%)
  Pallas kernels  9.56 us (14%)
  between operations  0.76 us (1%)
    ppermute x15, waiting for transfers between devices, trade(): return lax.ppermute(x, 'seq', [(i, i ^ k) for i in range(n)])  32.9 us
    ppermute x15, starting transfers between devices, trade(): return lax.ppermute(x, 'seq', [(i, i ^ k) for i in range(n)])  21.8 us
    pallas_call x10, Pallas kernels, call(): pl.pallas_call(body, out_shape=list(outputs), in_specs=in_specs or [VMEM]...  9.56 us
  transfers between devices with their start and end apart: 18, of which 10 were waited for; matrix products, arithmetic and copies ran while one was open for 1% of the time, Pallas kernels for 8%

profile of v7, /device:TPU:0, one launch (start us, length us, event | category | flops | bytes accessed | tf_op | source)
XLA Modules:
  0.0 66.8 jit_solution(11738924831389518686)
XLA Ops:
  0.6 1.8 %norm_select.1 = (bf16[64,1024]{1,0:T(8,128)(2,1)S(1)}, bf16[64,1024]{1,0:T(8,128)(2,1)S(1)}, bf16[64,1024]{1,0:T(8,128)(2,1)S(1)}, bf16[64,1024]{1,0:T(8,128)(2...) custom-call(bf16[64,8192]{1,0:T(8,128)(2,1)} %hidden_in.1, ...), custom_call_target="tpu_custom_call" | custom-call | flops 2097152 | bytes 2195712 | tf_op jit(solution)/shard_map/norm_select/pallas_call | solution.py:21
  2.4 4.1 %collective-permute-start = (bf16[64,1024]{1,0:T(8,128)(2,1)S(1)}, bf16[64,1024]{1,0:T(8,128)(2,1)S(1)}, u32[]{:S(2)}, u32[]{:S(2)}) collective-permute-start(bf16[64,1024]{1,0:T(8,128)(2,1)S(1)} %get-tuple-element.29), channel_id=1, source_target_pairs={{0,8},{2,10},{4,12},{6,14},{8,0},{10,2},{12,4},{14,6},{1,9},{3,11}... | collective-permute-start | bytes 393224 | tf_op jit(solution)/shard_map/ppermute | solution.py:216
  6.5 1.3 %collective-permute-start.1 = (bf16[64,1024]{1,0:T(8,128)(2,1)S(1)}, bf16[64,1024]{1,0:T(8,128)(2,1)S(1)}, u32[]{:S(2)}, u32[]{:S(2)}) collective-permute-start(bf16[64,1024]{1,0:T(8,128)(2,1)S(1)} %get-tuple-element.30), channel_id=1, source_target_pairs={{0,10},{2,8},{4,14},{6,12},{8,2},{10,0},{12,6},{14,4},{1,11},{3,9}... | collective-permute-start | bytes 393224 | tf_op jit(solution)/shard_map/ppermute | solution.py:216
  7.8 0.2 collective-permute-start.2
  8.1 3.9 %collective-permute-start.3 = (bf16[64,1024]{1,0:T(8,128)(2,1)S(1)}, bf16[64,1024]{1,0:T(8,128)(2,1)S(1)}, u32[]{:S(2)}, u32[]{:S(2)}) collective-permute-start(bf16[64,1024]{1,0:T(8,128)(2,1)S(1)} %get-tuple-element.32), channel_id=1, source_target_pairs={{0,12},{2,14},{4,8},{6,10},{8,4},{10,6},{12,0},{14,2},{1,13},{3,15... | collective-permute-start | bytes 393224 | tf_op jit(solution)/shard_map/ppermute | solution.py:216
  11.9 0.0 collective-permute-start.4
  11.9 7.5 %collective-permute-done.refs_0_.refs_4_ = bf16[64,1024]{1,0:T(8,128)(2,1)S(1)} collective-permute-done((bf16[64,1024]{1,0:T(8,128)(2,1)S(1)}, bf16[64,1024]{1,0:T(8,128)(2,1)S(1)}, u32[]{:S(2)}, u32[]{:S(2)}) %collective-permute-start) | collective-permute-done | bytes 131104 | tf_op jit(solution)/shard_map/ppermute | solution.py:216
  19.4 0.9 %collective-permute-start.5 = (bf16[64,1024]{1,0:T(8,128)(2,1)S(1)}, bf16[64,1024]{1,0:T(8,128)(2,1)S(1)}, u32[]{:S(2)}, u32[]{:S(2)}) collective-permute-start(bf16[64,1024]{1,0:T(8,128)(2,1)S(1)} %get-tuple-element.37), channel_id=1, source_target_pairs={{0,6},{2,4},{4,2},{6,0},{8,14},{10,12},{12,10},{14,8},{1,7},{3,5},... | collective-permute-start | bytes 393224 | tf_op jit(solution)/shard_map/ppermute | solution.py:216
  20.2 3.2 %collective-permute-done.1.refs_1_.refs_5_ = bf16[64,1024]{1,0:T(8,128)(2,1)S(1)} collective-permute-done((bf16[64,1024]{1,0:T(8,128)(2,1)S(1)}, bf16[64,1024]{1,0:T(8,128)(2,1)S(1)}, u32[]{:S(2)}, u32[]{:S(2)}) %collective-permute-start.1) | collective-permute-done | bytes 131104 | tf_op jit(solution)/shard_map/ppermute | solution.py:216
  23.4 2.4 %collective-permute-start.6 = (bf16[64,1024]{1,0:T(8,128)(2,1)S(1)}, bf16[64,1024]{1,0:T(8,128)(2,1)S(1)}, u32[]{:S(2)}, u32[]{:S(2)}) collective-permute-start(bf16[64,1024]{1,0:T(8,128)(2,1)S(1)} %get-tuple-element.38), channel_id=1, source_target_pairs={{0,14},{2,12},{4,10},{6,8},{8,6},{10,4},{12,2},{14,0},{1,15},{3,13... | collective-permute-start | bytes 393224 | tf_op jit(solution)/shard_map/ppermute | solution.py:216
  25.8 0.0 collective-permute-done.2.refs_2_.refs_1_
  25.8 0.0 collective-permute-done.3.refs_3_.refs_6_
  25.8 0.0 collective-permute-done.4.refs_4_.refs_2_
  25.8 2.5 %stage.1 = (bf16[1024,2560]{1,0:T(8,128)(2,1)S(1)}, bf16[64,2048]{1,0:T(8,128)(2,1)S(1)}, s32[1,512]{1,0:T(1,128)S(1)}) custom-call(s32[8]{0:T(128)} %counts_in.1, bf16[1024,2560]{1,0:T(8,128)(2,1)} %matrix_in.1, bf16[64,2048]{1,0:T(8,128)(2,1)} %queries_in.1, bf16[64,1024]{1,0:T(8,128)(2,1)S(1)} %collective-permute-done.refs_0_.refs_4_, ...), custom_call_target="tpu_custom_call" | custom-call | flops 3932160000 | bytes 11667488 | tf_op jit(solution)/shard_map/stage/pallas_call | solution.py:21
  28.4 0.1 collective-permute-done.5.refs_3_
  28.4 2.6 %collective-permute-done.6.refs_7_ = bf16[64,1024]{1,0:T(8,128)(2,1)S(1)} collective-permute-done((bf16[64,1024]{1,0:T(8,128)(2,1)S(1)}, bf16[64,1024]{1,0:T(8,128)(2,1)S(1)}, u32[]{:S(2)}, u32[]{:S(2)}) %collective-permute-start.6) | collective-permute-done | bytes 131104 | tf_op jit(solution)/shard_map/ppermute | solution.py:216
  31.1 0.3 compact.1.after.own
  31.4 0.1 collective-permute-start.7
  31.5 2.0 %attention.1 = (f32[64,2048]{1,0:T(8,128)}, f32[8,64]{1,0:T(8,128)S(1)}) custom-call(bf16[64,2048]{1,0:T(8,128)(2,1)S(1)} %get-tuple-element.34.queries, bf16[256,512]{1,0:T(8,128)(2,1)S(1)} %compact.1.after.own, bf16[64,1024]{1,0:T(8,128)(2,1)S(1)} %get-tuple-element.36.refs_0_, bf16[64,1024]{1,0:T(8,128)(2,1)S(1)} %collective-permute-done.2.refs_2_.refs_1_, ...), custom_call_target="tpu_custom_call" | custom-call | flops 268435456 | bytes 2099200 | tf_op jit(solution)/shard_map/attention/pallas_call | solution.py:21
  33.5 0.0 collective-permute-done.7.other
  33.5 1.0 %project.3 = (f32[128,1280]{1,0:T(8,128)S(1)}, bf16[128,1280]{1,0:T(8,128)(2,1)S(1)}) custom-call(bf16[256,512]{1,0:T(8,128)(2,1)S(1)} %compact.1.after.own, bf16[256,512]{1,0:T(8,128)(2,1)S(1)} %collective-permute-done.7.other, bf16[1024,2560]{1,0:T(8,128)(2,1)S(1)} %get-tuple-element.40.matrix, f32[8,64]{1,0:T(8,128)S(1)} %get-tuple-element.41.after), custom_call_target="tpu_custom_call" | custom-call | flops 671088640 | bytes 6752256 | tf_op jit(solution)/shard_map/project/pallas_call | solution.py:21
  34.5 0.0 copy-start
  34.5 0.1 collective-permute-start.9
  34.6 1.0 %project.2 = (f32[128,1280]{1,0:T(8,128)S(1)}, bf16[128,1280]{1,0:T(8,128)(2,1)S(1)}) custom-call(bf16[256,512]{1,0:T(8,128)(2,1)S(1)} %compact.1.after.own, bf16[256,512]{1,0:T(8,128)(2,1)S(1)} %collective-permute-done.7.other, bf16[1024,2560]{1,0:T(8,128)(2,1)S(1)} %get-tuple-element.40.matrix, f32[8,64]{1,0:T(8,128)S(1)} %get-tuple-element.41.after), custom_call_target="tpu_custom_call" | custom-call | flops 671088640 | bytes 6752256 | tf_op jit(solution)/shard_map/project/pallas_call | solution.py:21
  35.6 1.6 %collective-permute-start.8 = (bf16[128,1280]{1,0:T(8,128)(2,1)S(1)}, bf16[128,1280]{1,0:T(8,128)(2,1)S(1)}, u32[]{:S(2)}, u32[]{:S(2)}) collective-permute-start(bf16[128,1280]{1,0:T(8,128)(2,1)S(1)} %get-tuple-element.43), channel_id=1, source_target_pairs={{0,2},{2,0},{4,6},{6,4},{8,10},{10,8},{12,14},{14,12},{1,3},{3,1},... | collective-permute-start | bytes 983048 | tf_op jit(solution)/shard_map/ppermute | solution.py:216
  37.2 0.0 collective-permute-start.10
  37.2 0.7 %collective-permute-start.11 = (f32[4,64]{1,0:T(4,128)S(1)}, f32[4,64]{1,0:T(4,128)S(1)}, u32[]{:S(2)}, u32[]{:S(2)}) collective-permute-start(f32[4,64]{1,0:T(4,128)S(1)} %get-tuple-element.56), channel_id=1, source_target_pairs={{0,2},{2,0},{4,6},{6,4},{8,10},{10,8},{12,14},{14,12},{1,3},{3,1},... | collective-permute-start | bytes 3080 | tf_op jit(solution)/shard_map/ppermute | solution.py:216
  37.9 1.2 %collective-permute-start.12 = (f32[4,64]{1,0:T(4,128)S(1)}, f32[4,64]{1,0:T(4,128)S(1)}, u32[]{:S(2)}, u32[]{:S(2)}) collective-permute-start(f32[4,64]{1,0:T(4,128)S(1)} %get-tuple-element.56), channel_id=1, source_target_pairs={{0,3},{1,2},{2,1},{3,0},{4,7},{5,6},{6,5},{7,4},{8,11},{9,10},{10,... | collective-permute-start | bytes 3080 | tf_op jit(solution)/shard_map/ppermute | solution.py:219
  39.0 0.0 collective-permute-done.10
  39.0 6.8 %collective-permute-done.11 = f32[4,64]{1,0:T(4,128)S(1)} collective-permute-done((f32[4,64]{1,0:T(4,128)S(1)}, f32[4,64]{1,0:T(4,128)S(1)}, u32[]{:S(2)}, u32[]{:S(2)}) %collective-permute-start.11) | collective-permute-done | bytes 1056 | tf_op jit(solution)/shard_map/ppermute | solution.py:216
  45.8 0.0 collective-permute-done.12
  45.8 0.0 collective-permute-done.9.received
  45.8 0.1 hop_sum.2
  45.9 0.0 collective-permute-done.8.received
  45.9 0.1 hop_sum.3
  46.0 1.8 %collective-permute-start.15 = (f32[2,64]{1,0:T(2,128)S(1)}, f32[2,64]{1,0:T(2,128)S(1)}, u32[]{:S(2)}, u32[]{:S(2)}) collective-permute-start(f32[2,64]{1,0:T(2,128)S(1)} %slice.21), channel_id=1, source_target_pairs={{0,4},{2,6},{4,0},{6,2},{8,12},{10,14},{12,8},{14,10},{1,5},{3,7},... | collective-permute-start | bytes 1544 | tf_op jit(solution)/shard_map/ppermute | solution.py:216
  47.8 0.3 collective-permute-start.13
  48.1 1.3 %collective-permute-start.14 = (bf16[64,1280]{1,0:T(8,128)(2,1)S(1)}, bf16[64,1280]{1,0:T(8,128)(2,1)S(1)}, u32[]{:S(2)}, u32[]{:S(2)}) collective-permute-start(bf16[64,1280]{1,0:T(8,128)(2,1)S(1)} %get-tuple-element.50), channel_id=1, source_target_pairs={{0,2},{2,0},{4,6},{6,4},{8,10},{10,8},{12,14},{14,12},{1,3},{3,1},... | collective-permute-start | bytes 491528 | tf_op jit(solution)/shard_map/ppermute | solution.py:216
  49.4 0.3 collective-permute-done.15
  49.6 4.1 %collective-permute-done.13.refs_2_ = bf16[64,1280]{1,0:T(8,128)(2,1)S(1)} collective-permute-done((bf16[64,1280]{1,0:T(8,128)(2,1)S(1)}, bf16[64,1280]{1,0:T(8,128)(2,1)S(1)}, u32[]{:S(2)}, u32[]{:S(2)}) %collective-permute-start.13) | collective-permute-done | bytes 163872 | tf_op jit(solution)/shard_map/ppermute | solution.py:216
  53.7 0.1 collective-permute-done.14.refs_3_
  53.8 0.1 hop_sum_both.1
  53.9 3.2 %collective-permute-start.16 = (f32[1,64]{1,0:T(1,128)S(1)}, f32[1,64]{1,0:T(1,128)S(1)}, u32[]{:S(2)}, u32[]{:S(2)}) collective-permute-start(f32[1,64]{1,0:T(1,128)S(1)} %slice.23), channel_id=1, source_target_pairs={{0,8},{2,10},{4,12},{6,14},{8,0},{10,2},{12,4},{14,6},{1,9},{3,11}... | collective-permute-start | bytes 776 | tf_op jit(solution)/shard_map/ppermute | solution.py:216
  57.1 0.1 collective-permute-start.17
  57.2 1.4 %collective-permute-done.16 = f32[1,64]{1,0:T(1,128)S(1)} collective-permute-done((f32[1,64]{1,0:T(1,128)S(1)}, f32[1,64]{1,0:T(1,128)S(1)}, u32[]{:S(2)}, u32[]{:S(2)}) %collective-permute-start.16) | collective-permute-done | bytes 288 | tf_op jit(solution)/shard_map/ppermute | solution.py:216
  58.6 0.5 multiply_bitcast_fusion
  59.1 6.9 %collective-permute-done.17.received = bf16[32,2560]{1,0:T(8,128)(2,1)S(1)} collective-permute-done((bf16[32,2560]{1,0:T(8,128)(2,1)S(1)}, bf16[32,2560]{1,0:T(8,128)(2,1)S(1)}, u32[]{:S(2)}, u32[]{:S(2)}) %collective-permute-start.17) | collective-permute-done | bytes 163872 | tf_op jit(solution)/shard_map/ppermute | solution.py:216
  66.0 0.8 %finish.1 = f32[32,2560]{1,0:T(8,128)} custom-call(f32[1,2560]{1,0:T(1,128)S(1)} %reshape.20.bias, f32[32,2560]{1,0:T(8,128)S(1)} %get-tuple-element.53.kept, bf16[32,2560]{1,0:T(8,128)(2,1)S(1)} %collective-permute-done.17.received), custom_call_target="tpu_custom_call" | custom-call | flops 655360 | bytes 829440 | tf_op jit(solution)/shard_map/finish/pallas_call | solution.py:21
  (7 shorter events, 0.0 us)
Async XLA Ops:
  2.4 17.0 %collective-permute-start = (bf16[64,1024]{1,0:T(8,128)(2,1)S(1)}, bf16[64,1024]{1,0:T(8,128)(2,1)S(1)}, u32[]{:S(2)}, u32[]{:S(2)}) collective-permute-start(bf16[64,1024]{1,0:T(8,128)(2,1)S(1)} %get-tuple-element.29), channel_id=1, source_target_pairs={{0,8},{2,10},{4,12},{6,14},{8,0},{10,2},{12,4},{14,6},{1,9},{3,11}... | collective-permute-start | bytes 393224 | tf_op jit(solution)/shard_map/ppermute | solution.py:216
  6.5 16.9 %collective-permute-start.1 = (bf16[64,1024]{1,0:T(8,128)(2,1)S(1)}, bf16[64,1024]{1,0:T(8,128)(2,1)S(1)}, u32[]{:S(2)}, u32[]{:S(2)}) collective-permute-start(bf16[64,1024]{1,0:T(8,128)(2,1)S(1)} %get-tuple-element.30), channel_id=1, source_target_pairs={{0,10},{2,8},{4,14},{6,12},{8,2},{10,0},{12,6},{14,4},{1,11},{3,9}... | collective-permute-start | bytes 393224 | tf_op jit(solution)/shard_map/ppermute | solution.py:216
  7.8 18.0 %collective-permute-start.2 = (bf16[64,1024]{1,0:T(8,128)(2,1)S(1)}, bf16[64,1024]{1,0:T(8,128)(2,1)S(1)}, u32[]{:S(2)}, u32[]{:S(2)}) collective-permute-start(bf16[64,1024]{1,0:T(8,128)(2,1)S(1)} %get-tuple-element.31), channel_id=1, source_target_pairs={{0,2},{2,0},{4,6},{6,4},{8,10},{10,8},{12,14},{14,12},{1,3},{3,1},... | collective-permute-start | bytes 393224 | tf_op jit(solution)/shard_map/ppermute | solution.py:216
  8.1 17.8 %collective-permute-start.3 = (bf16[64,1024]{1,0:T(8,128)(2,1)S(1)}, bf16[64,1024]{1,0:T(8,128)(2,1)S(1)}, u32[]{:S(2)}, u32[]{:S(2)}) collective-permute-start(bf16[64,1024]{1,0:T(8,128)(2,1)S(1)} %get-tuple-element.32), channel_id=1, source_target_pairs={{0,12},{2,14},{4,8},{6,10},{8,4},{10,6},{12,0},{14,2},{1,13},{3,15... | collective-permute-start | bytes 393224 | tf_op jit(solution)/shard_map/ppermute | solution.py:216
  11.9 13.9 %collective-permute-start.4 = (bf16[64,1024]{1,0:T(8,128)(2,1)S(1)}, bf16[64,1024]{1,0:T(8,128)(2,1)S(1)}, u32[]{:S(2)}, u32[]{:S(2)}) collective-permute-start(bf16[64,1024]{1,0:T(8,128)(2,1)S(1)} %get-tuple-element.33), channel_id=1, source_target_pairs={{0,4},{2,6},{4,0},{6,2},{8,12},{10,14},{12,8},{14,10},{1,5},{3,7},... | collective-permute-start | bytes 393224 | tf_op jit(solution)/shard_map/ppermute | solution.py:216
  19.4 9.1 %collective-permute-start.5 = (bf16[64,1024]{1,0:T(8,128)(2,1)S(1)}, bf16[64,1024]{1,0:T(8,128)(2,1)S(1)}, u32[]{:S(2)}, u32[]{:S(2)}) collective-permute-start(bf16[64,1024]{1,0:T(8,128)(2,1)S(1)} %get-tuple-element.37), channel_id=1, source_target_pairs={{0,6},{2,4},{4,2},{6,0},{8,14},{10,12},{12,10},{14,8},{1,7},{3,5},... | collective-permute-start | bytes 393224 | tf_op jit(solution)/shard_map/ppermute | solution.py:216
  23.4 7.7 %collective-permute-start.6 = (bf16[64,1024]{1,0:T(8,128)(2,1)S(1)}, bf16[64,1024]{1,0:T(8,128)(2,1)S(1)}, u32[]{:S(2)}, u32[]{:S(2)}) collective-permute-start(bf16[64,1024]{1,0:T(8,128)(2,1)S(1)} %get-tuple-element.38), channel_id=1, source_target_pairs={{0,14},{2,12},{4,10},{6,8},{8,6},{10,4},{12,2},{14,0},{1,15},{3,13... | collective-permute-start | bytes 393224 | tf_op jit(solution)/shard_map/ppermute | solution.py:216
  31.4 2.1 %collective-permute-start.7 = (bf16[256,512]{1,0:T(8,128)(2,1)S(1)}, bf16[256,512]{1,0:T(8,128)(2,1)S(1)}, u32[]{:S(2)}, u32[]{:S(2)}) collective-permute-start(bf16[256,512]{1,0:T(8,128)(2,1)S(1)} %compact.1.after.own), channel_id=1, source_target_pairs={{0,1},{1,0},{2,3},{3,2},{4,5},{5,4},{6,7},{7,6},{8,9},{9,8},{10,11... | collective-permute-start | bytes 786440 | tf_op jit(solution)/shard_map/ppermute | solution.py:222
  34.5 22.6 %copy-start = (f32[2560]{0:T(1024)S(1)}, f32[2560]{0:T(1024)}, u32[]{:S(2)}) copy-start(f32[2560]{0:T(1024)} %param.17) | copy-start | bytes 30724
  34.5 11.3 %collective-permute-start.9 = (bf16[128,1280]{1,0:T(8,128)(2,1)S(1)}, bf16[128,1280]{1,0:T(8,128)(2,1)S(1)}, u32[]{:S(2)}, u32[]{:S(2)}) collective-permute-start(bf16[128,1280]{1,0:T(8,128)(2,1)S(1)} %get-tuple-element.45), channel_id=1, source_target_pairs={{0,4},{2,6},{4,0},{6,2},{8,12},{10,14},{12,8},{14,10},{1,5},{3,7},... | collective-permute-start | bytes 983048 | tf_op jit(solution)/shard_map/ppermute | solution.py:216
  35.6 10.3 %collective-permute-start.8 = (bf16[128,1280]{1,0:T(8,128)(2,1)S(1)}, bf16[128,1280]{1,0:T(8,128)(2,1)S(1)}, u32[]{:S(2)}, u32[]{:S(2)}) collective-permute-start(bf16[128,1280]{1,0:T(8,128)(2,1)S(1)} %get-tuple-element.43), channel_id=1, source_target_pairs={{0,2},{2,0},{4,6},{6,4},{8,10},{10,8},{12,14},{14,12},{1,3},{3,1},... | collective-permute-start | bytes 983048 | tf_op jit(solution)/shard_map/ppermute | solution.py:216
  37.2 1.9 %collective-permute-start.10 = (f32[4,64]{1,0:T(4,128)S(1)}, f32[4,64]{1,0:T(4,128)S(1)}, u32[]{:S(2)}, u32[]{:S(2)}) collective-permute-start(f32[4,64]{1,0:T(4,128)S(1)} %get-tuple-element.55), channel_id=1, source_target_pairs={{0,1},{1,0},{2,3},{3,2},{4,5},{5,4},{6,7},{7,6},{8,9},{9,8},{10,11... | collective-permute-start | bytes 3080 | tf_op jit(solution)/shard_map/ppermute | solution.py:222
  37.2 8.6 %collective-permute-start.11 = (f32[4,64]{1,0:T(4,128)S(1)}, f32[4,64]{1,0:T(4,128)S(1)}, u32[]{:S(2)}, u32[]{:S(2)}) collective-permute-start(f32[4,64]{1,0:T(4,128)S(1)} %get-tuple-element.56), channel_id=1, source_target_pairs={{0,2},{2,0},{4,6},{6,4},{8,10},{10,8},{12,14},{14,12},{1,3},{3,1},... | collective-permute-start | bytes 3080 | tf_op jit(solution)/shard_map/ppermute | solution.py:216
  37.9 7.9 %collective-permute-start.12 = (f32[4,64]{1,0:T(4,128)S(1)}, f32[4,64]{1,0:T(4,128)S(1)}, u32[]{:S(2)}, u32[]{:S(2)}) collective-permute-start(f32[4,64]{1,0:T(4,128)S(1)} %get-tuple-element.56), channel_id=1, source_target_pairs={{0,3},{1,2},{2,1},{3,0},{4,7},{5,6},{6,5},{7,4},{8,11},{9,10},{10,... | collective-permute-start | bytes 3080 | tf_op jit(solution)/shard_map/ppermute | solution.py:219
  46.0 3.6 %collective-permute-start.15 = (f32[2,64]{1,0:T(2,128)S(1)}, f32[2,64]{1,0:T(2,128)S(1)}, u32[]{:S(2)}, u32[]{:S(2)}) collective-permute-start(f32[2,64]{1,0:T(2,128)S(1)} %slice.21), channel_id=1, source_target_pairs={{0,4},{2,6},{4,0},{6,2},{8,12},{10,14},{12,8},{14,10},{1,5},{3,7},... | collective-permute-start | bytes 1544 | tf_op jit(solution)/shard_map/ppermute | solution.py:216
  47.8 5.9 %collective-permute-start.13 = (bf16[64,1280]{1,0:T(8,128)(2,1)S(1)}, bf16[64,1280]{1,0:T(8,128)(2,1)S(1)}, u32[]{:S(2)}, u32[]{:S(2)}) collective-permute-start(bf16[64,1280]{1,0:T(8,128)(2,1)S(1)} %get-tuple-element.49), channel_id=1, source_target_pairs={{0,4},{2,6},{4,0},{6,2},{8,12},{10,14},{12,8},{14,10},{1,5},{3,7},... | collective-permute-start | bytes 491528 | tf_op jit(solution)/shard_map/ppermute | solution.py:216
  48.1 5.7 %collective-permute-start.14 = (bf16[64,1280]{1,0:T(8,128)(2,1)S(1)}, bf16[64,1280]{1,0:T(8,128)(2,1)S(1)}, u32[]{:S(2)}, u32[]{:S(2)}) collective-permute-start(bf16[64,1280]{1,0:T(8,128)(2,1)S(1)} %get-tuple-element.50), channel_id=1, source_target_pairs={{0,2},{2,0},{4,6},{6,4},{8,10},{10,8},{12,14},{14,12},{1,3},{3,1},... | collective-permute-start | bytes 491528 | tf_op jit(solution)/shard_map/ppermute | solution.py:216
  53.9 4.7 %collective-permute-start.16 = (f32[1,64]{1,0:T(1,128)S(1)}, f32[1,64]{1,0:T(1,128)S(1)}, u32[]{:S(2)}, u32[]{:S(2)}) collective-permute-start(f32[1,64]{1,0:T(1,128)S(1)} %slice.23), channel_id=1, source_target_pairs={{0,8},{2,10},{4,12},{6,14},{8,0},{10,2},{12,4},{14,6},{1,9},{3,11}... | collective-permute-start | bytes 776 | tf_op jit(solution)/shard_map/ppermute | solution.py:216
  57.1 8.9 %collective-permute-start.17 = (bf16[32,2560]{1,0:T(8,128)(2,1)S(1)}, bf16[32,2560]{1,0:T(8,128)(2,1)S(1)}, u32[]{:S(2)}, u32[]{:S(2)}) collective-permute-start(bf16[32,2560]{1,0:T(8,128)(2,1)S(1)} %get-tuple-element.54), channel_id=1, source_target_pairs={{0,8},{2,10},{4,12},{6,14},{8,0},{10,2},{12,4},{14,6},{1,9},{3,11}... | collective-permute-start | bytes 491528 | tf_op jit(solution)/shard_map/ppermute | solution.py:216

commit v8 on v7

--- a/solution.py
+++ b/solution.py
@@ -68,7 +68,8 @@
         start = pl.multiple_of(lax.bitwise_xor(s, k) * block + t * half, half)
         columns = pl.ds(start, half)
         normed = (hidden[:, columns].astype(jnp.float32) * scale * gain[:, columns]).astype(jnp.bfloat16)
-        outs[k][:, half:] = pair[...]
+        if k < n // 2:
+            outs[k][:, half:] = pair[...]
         outs[k][:, :half] = lax.dot_general(
             selector, normed, (((0,), (0,)), ((), ())), preferred_element_type=jnp.float32
         ).astype(jnp.bfloat16)
@@ -102,10 +103,13 @@
 
 
 def compact_kernel(n, target, *refs):
-    blocks, out = refs[:n], refs[n]
+    blocks, (out, held) = refs[:n], refs[n:]
+    rows, half = blocks[0].shape[0], out.shape[1]
+    for k in range(n // 2):
+        held[k * rows : (k + 1) * rows] = blocks[k][:, half:]
     lines = out.shape[0] // n
     s = lax.axis_index("seq")
-    received = jnp.concatenate([b[:, : out.shape[1]] for b in blocks], axis=0)
+    received = jnp.concatenate([b[:, :half] for b in blocks], axis=0)
     line = lax.broadcasted_iota(jnp.int32, (lines, received.shape[0]), 0)
     pick = jnp.concatenate(
         [(line + lax.bitwise_xor(s, k) * lines == target[...]).astype(jnp.float32) for k in range(n)], axis=0
@@ -117,7 +121,7 @@
     return sorted(range(n), key=lambda k: [k & mask for mask in masks])
 
 
-def project_kernel(first, order, own, other, matrix, after, near, far):
+def project_kernel(first, order, own, other, matrix, near, far):
     survivors, half = own.shape
     lines = survivors // len(order)
     width = near.shape[1]
@@ -138,17 +142,15 @@
                 far[i * lines : (i + 1) * lines, j : j + tile] = block.astype(jnp.bfloat16)
 
 
-def hop_sum_kernel(kept, received, columns_in, keep, sent, columns):
+def hop_sum_kernel(kept, received, after, keep, sent):
     rows = keep.shape[0]
-    columns[...] = columns_in[...]
     total = kept[...] + received[...].astype(jnp.float32)
     keep[...] = total[:rows]
     sent[...] = total[rows:].astype(jnp.bfloat16)
 
 
 def hop_sum_both_kernel(*refs):
-    *parts, columns_in, keep, sent, columns = refs
-    columns[...] = columns_in[...]
+    *parts, keep, sent = refs
     count = len(parts) // 2
     rows = keep.shape[0]
     width = keep.shape[1] // count
@@ -159,9 +161,15 @@
         sent[:, lanes] = total[rows:].astype(jnp.bfloat16)
 
 
-def attention_kernel(n, kv_heads, masks, queries, after, *refs):
-    blocks, (context, columns) = refs[:n], refs[n:]
-    first = blocks[0].shape[1] - 2 * kv_heads * HEAD_SIZE
+def column_sum_kernel(scale, after, *refs):
+    *parts, out = refs
+    total = parts[0][...]
+    for part in parts[1:]:
+        total += part[...]
+    out[...] = total * scale
+
+
+def attention_kernel(n, kv_heads, masks, queries, near, far, after, context, columns):
     rows = queries.shape[0]
     group = queries.shape[1] // (HEAD_SIZE * kv_heads)
     s = lax.axis_index("seq")
@@ -175,9 +183,10 @@
     allowed = position <= row
     sums = jnp.zeros((1, keys_total), jnp.float32)
     for g in range(kv_heads):
-        key_at, value_at = first + g * HEAD_SIZE, first + (kv_heads + g) * HEAD_SIZE
-        key = jnp.concatenate([b[:, key_at : key_at + HEAD_SIZE] for b in blocks], axis=0)
-        value = jnp.concatenate([b[:, value_at : value_at + HEAD_SIZE] for b in blocks], axis=0)
+        key_lanes = slice(g * HEAD_SIZE, (g + 1) * HEAD_SIZE)
+        value_lanes = slice((kv_heads + g) * HEAD_SIZE, (kv_heads + g + 1) * HEAD_SIZE)
+        key = jnp.concatenate([near[:, key_lanes], far[:, key_lanes]], axis=0)
+        value = jnp.concatenate([near[:, value_lanes], far[:, value_lanes]], axis=0)
         heads = range(g * group, (g + 1) * group)
         stacked = jnp.concatenate([queries[:, h * HEAD_SIZE : (h + 1) * HEAD_SIZE] for h in heads], axis=0)
         scores = lax.dot_general(
@@ -221,15 +230,11 @@
     def swap(x):
         return lax.ppermute(x, "ten", [(0, 1), (1, 0)])
 
-    def column_hop(columns, mask):
-        left = columns.shape[0] // 2
-        return columns[:left] + trade(columns[left:], mask)
-
     chosen = call(
         functools.partial(norm_select_kernel, n),
         "norm_select",
         (hidden, norm_gain.reshape(1, model), retained_lists.reshape(1, rows), keys, values),
-        [shape((rows, half + 2 * keys.shape[1]), bf16)] * n,
+        [shape((rows, half + 2 * keys.shape[1]), bf16)] * (n // 2) + [shape((rows, half), bf16)] * (n // 2),
         4 * rows * model,
         limit=16,
         in_specs=[ANY] * 5,
@@ -248,64 +253,79 @@
         remote=3,
         scratch=[pltpu.SMEM(counts.shape, i32), dma((3,))],
     )
-    (own,) = call(
+    own, held = call(
         functools.partial(compact_kernel, n),
         "compact",
         (target, *received),
-        [shape((survivors, half), bf16)],
+        [shape((survivors, half), bf16), shape((n // 2 * rows, 2 * keys.shape[1]), bf16)],
         2 * survivors * n * rows * half,
     )
     other = swap(own)
     rest = [1 << i for i in range(2, n.bit_length() - 1)]
     masks = [[1, 2] + rest, [2, 1] + rest]
-    context, columns = call(
-        functools.partial(attention_kernel, n, kv_heads, masks[0]),
-        "attention",
-        (queries, own, *received),
-        [shape(queries.shape, f32), shape((n, rows), f32)],
-        4 * rows * n * rows * queries.shape[1],
-        limit=32,
-        in_specs=[VMEM, ANY] + [VMEM] * n,
-    )
-
     products = [
         call(
             functools.partial(project_kernel, c * chunk, halving_order(n, masks[c])),
             "project",
-            (own, other, matrix, columns),
+            (own, other, matrix),
             [shape((near, chunk), f32), shape((near, chunk), bf16)],
             4 * survivors * half * chunk,
-            in_specs=[VMEM] * 3 + [ANY],
         )
         for c in range(2)
     ]
+    context, columns = call(
+        functools.partial(attention_kernel, n, kv_heads, masks[0]),
+        "attention",
+        (queries, held, trade(held, n // 2), products[1][1]),
+        [shape(queries.shape, f32), shape((n, rows), f32)],
+        4 * rows * n * rows * queries.shape[1],
+        limit=32,
+        in_specs=[VMEM] * 3 + [ANY],
+    )
     kept = [product[0] for product in products]
     arrived = [trade(product[1], masks[c][0]) for c, product in enumerate(products)]
-    far = columns[n // 2 :]
-    columns = columns[: n // 2]
-    columns = columns + swap(columns) + trade(far, 1) + trade_across(far, 1)
     lines_left = near // 2
     for c in (1, 0):
-        keep, sent, columns = call(
+        keep, sent = call(
             hop_sum_kernel,
             "hop_sum",
-            (kept[c], arrived[c], columns),
-            [shape((lines_left, chunk), f32), shape((lines_left, chunk), bf16), shape(columns.shape, f32)],
+            (kept[c], arrived[c], products[c][1] if c else columns),
+            [shape((lines_left, chunk), f32), shape((lines_left, chunk), bf16)],
             near * chunk,
+            in_specs=[VMEM] * 2 + [ANY],
         )
         kept[c], arrived[c] = keep, trade(sent, masks[c][1])
-    columns = column_hop(columns, masks[0][1])
+
+    def column_sum(pieces, after, scale=1.0, remote=0):
+        (total,) = call(
+            functools.partial(column_sum_kernel, scale),
+            "column_sum",
+            (after, *pieces),
+            [shape(pieces[0].shape, f32)],
+            0,
+            in_specs=[ANY] + [VMEM] * len(pieces),
+            remote=remote,
+        )
+        return total
+
+    pieces = [columns[i * (n // 4) : (i + 1) * (n // 4)] for i in range(4)]
+    pieces = pieces[:1] + [trade(x, mask) for x, mask in zip(pieces[1:], (2, 1, 3))]
     for mask in rest:
         lines_left //= 2
-        keep, sent, columns = call(
+        keep, sent = call(
             hop_sum_both_kernel,
             "hop_sum_both",
-            (*kept, *arrived, columns),
-            [shape((lines_left, width), f32), shape((lines_left, width), bf16), shape(columns.shape, f32)],
+            (*kept, *arrived),
+            [shape((lines_left, width), f32), shape((lines_left, width), bf16)],
             lines_left * width,
         )
         kept, arrived = [keep], [trade(sent, mask)]
-        columns = column_hop(columns, mask)
+        columns = column_sum(pieces, keep)
+        left = columns.shape[0] // 2
+        own, far = columns[:left], columns[left:]
+        pieces = [own, trade(far, mask)]
+        if mask == rest[-1]:
+            pieces += [swap(own), trade_across(far, mask)]
 
     (triples,) = call(
         finish_kernel,
@@ -314,7 +334,8 @@
         [shape((lines, width), f32)],
         n * lines * width,
     )
-    return (context, columns.reshape(rows) / QUERY_HEADS, triples)
+    scores = column_sum(pieces, triples, 1.0 / QUERY_HEADS, remote=1)
+    return (context, scores.reshape(rows), triples)
 
 
 def solution(mesh):

time: 66.9 us -> 62.7 us (0.937)
  waiting for transfers between devices: 32.9 us -> 24.3 us
  starting transfers between devices: 23 us -> 27.4 us
    ppermute x15 -> x17, waiting for transfers between devices: 32.9 us -> 22.7 us  [trade(): return lax.ppermute(x, 'seq', [(i, i ^ k) for i in range(n)])]
    ppermute x15 -> x17, starting transfers between devices: 21.8 us -> 24.8 us  [trade(): return lax.ppermute(x, 'seq', [(i, i ^ k) for i in range(n)])]
    ppermute x2, waiting for transfers between devices: 0.01 us -> 1.52 us  [swap(): return lax.ppermute(x, 'ten', [(0, 1), (1, 0)])]
    ppermute x1, starting transfers between devices: 1.17 us -> 2.58 us  [trade_across(): lax.ppermute(x, ('seq', 'ten'), [(2 * i + t, 2 * (i ^ k) + 1 - t) for i i...]
    pallas_call x10 -> x12, Pallas kernels: 9.56 us -> 10.1 us  [call(): pl.pallas_call(body, out_shape=list(outputs), in_specs=in_specs or [VMEM]...]
  transfers between devices with their start and end apart: 18 -> 20, of which waited for: 10 -> 10; matrix products, arithmetic and copies ran while one was open for 1% -> 0% of each run, Pallas kernels for 8% -> 10%
where the time goes in v8:
time: 62.7 us; the launch traced here: 62.6 us
  starting transfers between devices  27.4 us (44%)
  waiting for transfers between devices  24.3 us (39%)
  Pallas kernels  10.1 us (16%)
  between operations  0.75 us (1%)
    ppermute x17, starting transfers between devices, trade(): return lax.ppermute(x, 'seq', [(i, i ^ k) for i in range(n)])  24.8 us
    ppermute x17, waiting for transfers between devices, trade(): return lax.ppermute(x, 'seq', [(i, i ^ k) for i in range(n)])  22.7 us
    pallas_call x12, Pallas kernels, call(): pl.pallas_call(body, out_shape=list(outputs), in_specs=in_specs or [VMEM]...  10.1 us
    ppermute x1, starting transfers between devices, trade_across(): lax.ppermute(x, ('seq', 'ten'), [(2 * i + t, 2 * (i ^ k) + 1 - t) for i i...  2.58 us
    ppermute x2, waiting for transfers between devices, swap(): return lax.ppermute(x, 'ten', [(0, 1), (1, 0)])  1.52 us
  transfers between devices with their start and end apart: 20, of which 10 were waited for; matrix products, arithmetic and copies ran while one was open for 0% of the time, Pallas kernels for 10%

profile of v8, /device:TPU:0, one launch (start us, length us, event | category | flops | bytes accessed | tf_op | source)
XLA Modules:
  0.0 62.6 jit_solution(9039931909476978912)
XLA Ops:
  0.6 1.7 %norm_select.1 = (bf16[64,1024]{1,0:T(8,128)(2,1)S(1)}, bf16[64,1024]{1,0:T(8,128)(2,1)S(1)}, bf16[64,1024]{1,0:T(8,128)(2,1)S(1)}, bf16[64,1024]{1,0:T(8,128)(2...) custom-call(bf16[64,8192]{1,0:T(8,128)(2,1)} %hidden_in.1, ...), custom_call_target="tpu_custom_call" | custom-call | flops 2097152 | bytes 1933568 | tf_op jit(solution)/shard_map/norm_select/pallas_call | solution.py:21
  2.4 3.0 %collective-permute-start.2 = (bf16[64,1024]{1,0:T(8,128)(2,1)S(1)}, bf16[64,1024]{1,0:T(8,128)(2,1)S(1)}, u32[]{:S(2)}, u32[]{:S(2)}) collective-permute-start(bf16[64,1024]{1,0:T(8,128)(2,1)S(1)} %get-tuple-element.30), channel_id=1, source_target_pairs={{0,2},{2,0},{4,6},{6,4},{8,10},{10,8},{12,14},{14,12},{1,3},{3,1},... | collective-permute-start | bytes 393224 | tf_op jit(solution)/shard_map/ppermute | solution.py:225
  5.4 1.6 %collective-permute-start.4 = (bf16[64,1024]{1,0:T(8,128)(2,1)S(1)}, bf16[64,1024]{1,0:T(8,128)(2,1)S(1)}, u32[]{:S(2)}, u32[]{:S(2)}) collective-permute-start(bf16[64,1024]{1,0:T(8,128)(2,1)S(1)} %get-tuple-element.32), channel_id=1, source_target_pairs={{0,4},{2,6},{4,0},{6,2},{8,12},{10,14},{12,8},{14,10},{1,5},{3,7},... | collective-permute-start | bytes 393224 | tf_op jit(solution)/shard_map/ppermute | solution.py:225
  7.0 2.6 %collective-permute-start = (bf16[64,512]{1,0:T(8,128)(2,1)S(1)}, bf16[64,512]{1,0:T(8,128)(2,1)S(1)}, u32[]{:S(2)}, u32[]{:S(2)}) collective-permute-start(bf16[64,512]{1,0:T(8,128)(2,1)S(1)} %get-tuple-element.28), channel_id=1, source_target_pairs={{0,8},{2,10},{4,12},{6,14},{8,0},{10,2},{12,4},{14,6},{1,9},{3,11}... | collective-permute-start | bytes 196616 | tf_op jit(solution)/shard_map/ppermute | solution.py:225
  9.6 0.3 collective-permute-start.1
  9.9 2.5 %collective-permute-start.3 = (bf16[64,512]{1,0:T(8,128)(2,1)S(1)}, bf16[64,512]{1,0:T(8,128)(2,1)S(1)}, u32[]{:S(2)}, u32[]{:S(2)}) collective-permute-start(bf16[64,512]{1,0:T(8,128)(2,1)S(1)} %get-tuple-element.31), channel_id=1, source_target_pairs={{0,12},{2,14},{4,8},{6,10},{8,4},{10,6},{12,0},{14,2},{1,13},{3,15... | collective-permute-start | bytes 196616 | tf_op jit(solution)/shard_map/ppermute | solution.py:225
  12.3 1.4 %collective-permute-done.refs_0_.refs_4_ = bf16[64,512]{1,0:T(8,128)(2,1)S(1)} collective-permute-done((bf16[64,512]{1,0:T(8,128)(2,1)S(1)}, bf16[64,512]{1,0:T(8,128)(2,1)S(1)}, u32[]{:S(2)}, u32[]{:S(2)}) %collective-permute-start) | collective-permute-done | bytes 65568 | tf_op jit(solution)/shard_map/ppermute | solution.py:225
  13.7 1.9 %collective-permute-start.5 = (bf16[64,1024]{1,0:T(8,128)(2,1)S(1)}, bf16[64,1024]{1,0:T(8,128)(2,1)S(1)}, u32[]{:S(2)}, u32[]{:S(2)}) collective-permute-start(bf16[64,1024]{1,0:T(8,128)(2,1)S(1)} %get-tuple-element.36), channel_id=1, source_target_pairs={{0,6},{2,4},{4,2},{6,0},{8,14},{10,12},{12,10},{14,8},{1,7},{3,5},... | collective-permute-start | bytes 393224 | tf_op jit(solution)/shard_map/ppermute | solution.py:225
  15.6 2.4 %collective-permute-done.1.refs_1_.refs_5_ = bf16[64,512]{1,0:T(8,128)(2,1)S(1)} collective-permute-done((bf16[64,512]{1,0:T(8,128)(2,1)S(1)}, bf16[64,512]{1,0:T(8,128)(2,1)S(1)}, u32[]{:S(2)}, u32[]{:S(2)}) %collective-permute-start.1) | collective-permute-done | bytes 65568 | tf_op jit(solution)/shard_map/ppermute | solution.py:225
  18.1 2.8 %collective-permute-start.6 = (bf16[64,512]{1,0:T(8,128)(2,1)S(1)}, bf16[64,512]{1,0:T(8,128)(2,1)S(1)}, u32[]{:S(2)}, u32[]{:S(2)}) collective-permute-start(bf16[64,512]{1,0:T(8,128)(2,1)S(1)} %get-tuple-element.37), channel_id=1, source_target_pairs={{0,14},{2,12},{4,10},{6,8},{8,6},{10,4},{12,2},{14,0},{1,15},{3,13... | collective-permute-start | bytes 196616 | tf_op jit(solution)/shard_map/ppermute | solution.py:225
  20.9 0.0 collective-permute-done.3.refs_3_.refs_6_
  20.9 0.0 collective-permute-done.2.refs_2_.refs_1_
  20.9 0.0 collective-permute-done.4.refs_4_.refs_2_
  20.9 2.5 %stage.1 = (bf16[1024,2560]{1,0:T(8,128)(2,1)S(1)}, bf16[64,2048]{1,0:T(8,128)(2,1)S(1)}, s32[1,512]{1,0:T(1,128)S(1)}) custom-call(s32[8]{0:T(128)} %counts_in.1, bf16[1024,2560]{1,0:T(8,128)(2,1)} %matrix_in.1, bf16[64,2048]{1,0:T(8,128)(2,1)} %queries_in.1, bf16[64,512]{1,0:T(8,128)(2,1)S(1)} %collective-permute-done.refs_0_.refs_4_, ...), custom_call_target="tpu_custom_call" | custom-call | flops 3932160000 | bytes 11470880 | tf_op jit(solution)/shard_map/stage/pallas_call | solution.py:21
  23.5 1.6 %collective-permute-done.6.refs_7_ = bf16[64,512]{1,0:T(8,128)(2,1)S(1)} collective-permute-done((bf16[64,512]{1,0:T(8,128)(2,1)S(1)}, bf16[64,512]{1,0:T(8,128)(2,1)S(1)}, u32[]{:S(2)}, u32[]{:S(2)}) %collective-permute-start.6) | collective-permute-done | bytes 65568 | tf_op jit(solution)/shard_map/ppermute | solution.py:225
  25.0 0.3 compact.1
  25.4 0.1 collective-permute-start.8
  25.4 1.5 %collective-permute-done.8.other = bf16[256,512]{1,0:T(8,128)(2,1)S(1)} collective-permute-done((bf16[256,512]{1,0:T(8,128)(2,1)S(1)}, bf16[256,512]{1,0:T(8,128)(2,1)S(1)}, u32[]{:S(2)}, u32[]{:S(2)}) %collective-permute-start.8) | collective-permute-done | bytes 262176 | tf_op jit(solution)/shard_map/ppermute | solution.py:231
  27.0 1.0 %project.2 = (f32[128,1280]{1,0:T(8,128)S(1)}, bf16[128,1280]{1,0:T(8,128)(2,1)S(1)}) custom-call(bf16[256,512]{1,0:T(8,128)(2,1)S(1)} %get-tuple-element.39.own, bf16[256,512]{1,0:T(8,128)(2,1)S(1)} %collective-permute-done.8.other, bf16[1024,2560]{1,0:T(8,128)(2,1)S(1)} %get-tuple-element.40.matrix), custom_call_target="tpu_custom_call" | custom-call | flops 671088640 | bytes 6750208 | tf_op jit(solution)/shard_map/project/pallas_call | solution.py:21
  28.0 0.0 copy-start
  28.0 0.1 collective-permute-start.10
  28.0 1.0 %project.3 = (f32[128,1280]{1,0:T(8,128)S(1)}, bf16[128,1280]{1,0:T(8,128)(2,1)S(1)}) custom-call(bf16[256,512]{1,0:T(8,128)(2,1)S(1)} %get-tuple-element.39.own, bf16[256,512]{1,0:T(8,128)(2,1)S(1)} %collective-permute-done.8.other, bf16[1024,2560]{1,0:T(8,128)(2,1)S(1)} %get-tuple-element.40.matrix), custom_call_target="tpu_custom_call" | custom-call | flops 671088640 | bytes 6750208 | tf_op jit(solution)/shard_map/project/pallas_call | solution.py:21
  29.0 1.6 %collective-permute-start.9 = (bf16[128,1280]{1,0:T(8,128)(2,1)S(1)}, bf16[128,1280]{1,0:T(8,128)(2,1)S(1)}, u32[]{:S(2)}, u32[]{:S(2)}) collective-permute-start(bf16[128,1280]{1,0:T(8,128)(2,1)S(1)} %get-tuple-element.44), channel_id=1, source_target_pairs={{0,2},{2,0},{4,6},{6,4},{8,10},{10,8},{12,14},{14,12},{1,3},{3,1},... | collective-permute-start | bytes 983048 | tf_op jit(solution)/shard_map/ppermute | solution.py:225
  30.7 2.4 %collective-permute-start.7 = (bf16[256,512]{1,0:T(8,128)(2,1)S(1)}, bf16[256,512]{1,0:T(8,128)(2,1)S(1)}, u32[]{:S(2)}, u32[]{:S(2)}) collective-permute-start(bf16[256,512]{1,0:T(8,128)(2,1)S(1)} %get-tuple-element.38.near), channel_id=1, source_target_pairs={{0,8},{2,10},{4,12},{6,14},{8,0},{10,2},{12,4},{14,6},{1,9},{3,11}... | collective-permute-start | bytes 786440 | tf_op jit(solution)/shard_map/ppermute | solution.py:225
  33.1 12.3 %collective-permute-done.7.far = bf16[256,512]{1,0:T(8,128)(2,1)S(1)} collective-permute-done((bf16[256,512]{1,0:T(8,128)(2,1)S(1)}, bf16[256,512]{1,0:T(8,128)(2,1)S(1)}, u32[]{:S(2)}, u32[]{:S(2)}) %collective-permute-start.7) | collective-permute-done | bytes 262176 | tf_op jit(solution)/shard_map/ppermute | solution.py:225
  45.3 2.0 %attention.1 = (f32[64,2048]{1,0:T(8,128)}, f32[8,64]{1,0:T(8,128)S(1)}) custom-call(bf16[64,2048]{1,0:T(8,128)(2,1)S(1)} %get-tuple-element.33.queries, bf16[256,512]{1,0:T(8,128)(2,1)S(1)} %get-tuple-element.38.near, bf16[256,512]{1,0:T(8,128)(2,1)S(1)} %collective-permute-done.7.far, bf16[128,1280]{1,0:T(8,128)(2,1)S(1)} %get-tuple-element.41.after), custom_call_target="tpu_custom_call" | custom-call | flops 268435456 | bytes 1640448 | tf_op jit(solution)/shard_map/attention/pallas_call | solution.py:21
  47.3 0.0 collective-permute-done.10.received
  47.3 0.1 hop_sum.3
  47.4 0.6 collective-permute-start.12
  48.0 0.0 collective-permute-done.9.received
  48.0 0.1 hop_sum.2
  48.1 0.1 collective-permute-start.11
  48.2 2.0 %collective-permute-start.14 = (f32[2,64]{1,0:T(2,128)S(1)}, f32[2,64]{1,0:T(2,128)S(1)}, u32[]{:S(2)}, u32[]{:S(2)}) collective-permute-start(f32[2,64]{1,0:T(2,128)S(1)} %get-tuple-element.55), channel_id=1, source_target_pairs={{0,4},{2,6},{4,0},{6,2},{8,12},{10,14},{12,8},{14,10},{1,5},{3,7},... | collective-permute-start | bytes 1544 | tf_op jit(solution)/shard_map/ppermute | solution.py:225
  50.2 1.5 %collective-permute-start.15 = (f32[2,64]{1,0:T(2,128)S(1)}, f32[2,64]{1,0:T(2,128)S(1)}, u32[]{:S(2)}, u32[]{:S(2)}) collective-permute-start(f32[2,64]{1,0:T(2,128)S(1)} %get-tuple-element.54), channel_id=1, source_target_pairs={{0,2},{2,0},{4,6},{6,4},{8,10},{10,8},{12,14},{14,12},{1,3},{3,1},... | collective-permute-start | bytes 1544 | tf_op jit(solution)/shard_map/ppermute | solution.py:225
  51.7 0.1 collective-permute-start.16
  51.7 1.1 %collective-permute-done.12.refs_3_ = bf16[64,1280]{1,0:T(8,128)(2,1)S(1)} collective-permute-done((bf16[64,1280]{1,0:T(8,128)(2,1)S(1)}, bf16[64,1280]{1,0:T(8,128)(2,1)S(1)}, u32[]{:S(2)}, u32[]{:S(2)}) %collective-permute-start.12) | collective-permute-done | bytes 163872 | tf_op jit(solution)/shard_map/ppermute | solution.py:225
  52.8 0.7 %collective-permute-done.11.refs_2_ = bf16[64,1280]{1,0:T(8,128)(2,1)S(1)} collective-permute-done((bf16[64,1280]{1,0:T(8,128)(2,1)S(1)}, bf16[64,1280]{1,0:T(8,128)(2,1)S(1)}, u32[]{:S(2)}, u32[]{:S(2)}) %collective-permute-start.11) | collective-permute-done | bytes 163872 | tf_op jit(solution)/shard_map/ppermute | solution.py:225
  53.5 0.1 hop_sum_both.1
  53.6 1.2 %collective-permute-start.13 = (bf16[32,2560]{1,0:T(8,128)(2,1)S(1)}, bf16[32,2560]{1,0:T(8,128)(2,1)S(1)}, u32[]{:S(2)}, u32[]{:S(2)}) collective-permute-start(bf16[32,2560]{1,0:T(8,128)(2,1)S(1)} %get-tuple-element.52), channel_id=1, source_target_pairs={{0,8},{2,10},{4,12},{6,14},{8,0},{10,2},{12,4},{14,6},{1,9},{3,11}... | collective-permute-start | bytes 491528 | tf_op jit(solution)/shard_map/ppermute | solution.py:225
  54.8 0.1 collective-permute-done.14.refs_1_
  54.9 1.2 %collective-permute-done.16.refs_3_ = f32[2,64]{1,0:T(2,128)S(1)} collective-permute-done((f32[2,64]{1,0:T(2,128)S(1)}, f32[2,64]{1,0:T(2,128)S(1)}, u32[]{:S(2)}, u32[]{:S(2)}) %collective-permute-start.16) | collective-permute-done | bytes 544 | tf_op jit(solution)/shard_map/ppermute | solution.py:225
  56.1 0.5 collective-permute-start.17
  56.7 0.0 collective-permute-start.18
  56.7 2.6 %collective-permute-start.19 = (f32[1,64]{1,0:T(1,128)S(1)}, f32[1,64]{1,0:T(1,128)S(1)}, u32[]{:S(2)}, u32[]{:S(2)}) collective-permute-start(f32[1,64]{1,0:T(1,128)S(1)} %get-tuple-element.57), channel_id=1, source_target_pairs={{0,9},{1,8},{2,11},{3,10},{4,13},{5,12},{6,15},{7,14},{8,1},{9,0},... | collective-permute-start | bytes 776 | tf_op jit(solution)/shard_map/ppermute | solution.py:228
  59.2 2.0 %collective-permute-done.13.received = bf16[32,2560]{1,0:T(8,128)(2,1)S(1)} collective-permute-done((bf16[32,2560]{1,0:T(8,128)(2,1)S(1)}, bf16[32,2560]{1,0:T(8,128)(2,1)S(1)}, u32[]{:S(2)}, u32[]{:S(2)}) %collective-permute-start.13) | collective-permute-done | bytes 163872 | tf_op jit(solution)/shard_map/ppermute | solution.py:225
  61.3 0.8 %finish.1.after = f32[32,2560]{1,0:T(8,128)} custom-call(f32[1,2560]{1,0:T(1,128)S(1)} %reshape.20.bias, f32[32,2560]{1,0:T(8,128)S(1)} %get-tuple-element.51.kept.after, bf16[32,2560]{1,0:T(8,128)(2,1)S(1)} %collective-permute-done.13.received), custom_call_target="tpu_custom_call" | custom-call | flops 655360 | bytes 829440 | tf_op jit(solution)/shard_map/finish/pallas_call | solution.py:21
  62.0 0.0 collective-permute-done.18.refs_2_
  62.0 0.5 column_sum.3
  (9 shorter events, 0.0 us)
Async XLA Ops:
  2.4 18.5 %collective-permute-start.2 = (bf16[64,1024]{1,0:T(8,128)(2,1)S(1)}, bf16[64,1024]{1,0:T(8,128)(2,1)S(1)}, u32[]{:S(2)}, u32[]{:S(2)}) collective-permute-start(bf16[64,1024]{1,0:T(8,128)(2,1)S(1)} %get-tuple-element.30), channel_id=1, source_target_pairs={{0,2},{2,0},{4,6},{6,4},{8,10},{10,8},{12,14},{14,12},{1,3},{3,1},... | collective-permute-start | bytes 393224 | tf_op jit(solution)/shard_map/ppermute | solution.py:225
  5.4 15.5 %collective-permute-start.4 = (bf16[64,1024]{1,0:T(8,128)(2,1)S(1)}, bf16[64,1024]{1,0:T(8,128)(2,1)S(1)}, u32[]{:S(2)}, u32[]{:S(2)}) collective-permute-start(bf16[64,1024]{1,0:T(8,128)(2,1)S(1)} %get-tuple-element.32), channel_id=1, source_target_pairs={{0,4},{2,6},{4,0},{6,2},{8,12},{10,14},{12,8},{14,10},{1,5},{3,7},... | collective-permute-start | bytes 393224 | tf_op jit(solution)/shard_map/ppermute | solution.py:225
  7.0 6.7 %collective-permute-start = (bf16[64,512]{1,0:T(8,128)(2,1)S(1)}, bf16[64,512]{1,0:T(8,128)(2,1)S(1)}, u32[]{:S(2)}, u32[]{:S(2)}) collective-permute-start(bf16[64,512]{1,0:T(8,128)(2,1)S(1)} %get-tuple-element.28), channel_id=1, source_target_pairs={{0,8},{2,10},{4,12},{6,14},{8,0},{10,2},{12,4},{14,6},{1,9},{3,11}... | collective-permute-start | bytes 196616 | tf_op jit(solution)/shard_map/ppermute | solution.py:225
  9.6 8.5 %collective-permute-start.1 = (bf16[64,512]{1,0:T(8,128)(2,1)S(1)}, bf16[64,512]{1,0:T(8,128)(2,1)S(1)}, u32[]{:S(2)}, u32[]{:S(2)}) collective-permute-start(bf16[64,512]{1,0:T(8,128)(2,1)S(1)} %get-tuple-element.29), channel_id=1, source_target_pairs={{0,10},{2,8},{4,14},{6,12},{8,2},{10,0},{12,6},{14,4},{1,11},{3,9}... | collective-permute-start | bytes 196616 | tf_op jit(solution)/shard_map/ppermute | solution.py:225
  9.9 11.1 %collective-permute-start.3 = (bf16[64,512]{1,0:T(8,128)(2,1)S(1)}, bf16[64,512]{1,0:T(8,128)(2,1)S(1)}, u32[]{:S(2)}, u32[]{:S(2)}) collective-permute-start(bf16[64,512]{1,0:T(8,128)(2,1)S(1)} %get-tuple-element.31), channel_id=1, source_target_pairs={{0,12},{2,14},{4,8},{6,10},{8,4},{10,6},{12,0},{14,2},{1,13},{3,15... | collective-permute-start | bytes 196616 | tf_op jit(solution)/shard_map/ppermute | solution.py:225
  13.7 11.3 %collective-permute-start.5 = (bf16[64,1024]{1,0:T(8,128)(2,1)S(1)}, bf16[64,1024]{1,0:T(8,128)(2,1)S(1)}, u32[]{:S(2)}, u32[]{:S(2)}) collective-permute-start(bf16[64,1024]{1,0:T(8,128)(2,1)S(1)} %get-tuple-element.36), channel_id=1, source_target_pairs={{0,6},{2,4},{4,2},{6,0},{8,14},{10,12},{12,10},{14,8},{1,7},{3,5},... | collective-permute-start | bytes 393224 | tf_op jit(solution)/shard_map/ppermute | solution.py:225
  18.1 7.0 %collective-permute-start.6 = (bf16[64,512]{1,0:T(8,128)(2,1)S(1)}, bf16[64,512]{1,0:T(8,128)(2,1)S(1)}, u32[]{:S(2)}, u32[]{:S(2)}) collective-permute-start(bf16[64,512]{1,0:T(8,128)(2,1)S(1)} %get-tuple-element.37), channel_id=1, source_target_pairs={{0,14},{2,12},{4,10},{6,8},{8,6},{10,4},{12,2},{14,0},{1,15},{3,13... | collective-permute-start | bytes 196616 | tf_op jit(solution)/shard_map/ppermute | solution.py:225
  25.4 1.6 %collective-permute-start.8 = (bf16[256,512]{1,0:T(8,128)(2,1)S(1)}, bf16[256,512]{1,0:T(8,128)(2,1)S(1)}, u32[]{:S(2)}, u32[]{:S(2)}) collective-permute-start(bf16[256,512]{1,0:T(8,128)(2,1)S(1)} %get-tuple-element.39.own), channel_id=1, source_target_pairs={{0,1},{1,0},{2,3},{3,2},{4,5},{5,4},{6,7},{7,6},{8,9},{9,8},{10,11... | collective-permute-start | bytes 786440 | tf_op jit(solution)/shard_map/ppermute | solution.py:231
  28.0 23.8 %copy-start = (f32[2560]{0:T(1024)S(1)}, f32[2560]{0:T(1024)}, u32[]{:S(2)}) copy-start(f32[2560]{0:T(1024)} %param.17) | copy-start | bytes 30724
  28.0 19.4 %collective-permute-start.10 = (bf16[128,1280]{1,0:T(8,128)(2,1)S(1)}, bf16[128,1280]{1,0:T(8,128)(2,1)S(1)}, u32[]{:S(2)}, u32[]{:S(2)}) collective-permute-start(bf16[128,1280]{1,0:T(8,128)(2,1)S(1)} %get-tuple-element.41.after), channel_id=1, source_target_pairs={{0,4},{2,6},{4,0},{6,2},{8,12},{10,14},{12,8},{14,10},{1,5},{3,7},... | collective-permute-start | bytes 983048 | tf_op jit(solution)/shard_map/ppermute | solution.py:225
  29.0 19.0 %collective-permute-start.9 = (bf16[128,1280]{1,0:T(8,128)(2,1)S(1)}, bf16[128,1280]{1,0:T(8,128)(2,1)S(1)}, u32[]{:S(2)}, u32[]{:S(2)}) collective-permute-start(bf16[128,1280]{1,0:T(8,128)(2,1)S(1)} %get-tuple-element.44), channel_id=1, source_target_pairs={{0,2},{2,0},{4,6},{6,4},{8,10},{10,8},{12,14},{14,12},{1,3},{3,1},... | collective-permute-start | bytes 983048 | tf_op jit(solution)/shard_map/ppermute | solution.py:225
  30.7 14.6 %collective-permute-start.7 = (bf16[256,512]{1,0:T(8,128)(2,1)S(1)}, bf16[256,512]{1,0:T(8,128)(2,1)S(1)}, u32[]{:S(2)}, u32[]{:S(2)}) collective-permute-start(bf16[256,512]{1,0:T(8,128)(2,1)S(1)} %get-tuple-element.38.near), channel_id=1, source_target_pairs={{0,8},{2,10},{4,12},{6,14},{8,0},{10,2},{12,4},{14,6},{1,9},{3,11}... | collective-permute-start | bytes 786440 | tf_op jit(solution)/shard_map/ppermute | solution.py:225
  47.4 5.4 %collective-permute-start.12 = (bf16[64,1280]{1,0:T(8,128)(2,1)S(1)}, bf16[64,1280]{1,0:T(8,128)(2,1)S(1)}, u32[]{:S(2)}, u32[]{:S(2)}) collective-permute-start(bf16[64,1280]{1,0:T(8,128)(2,1)S(1)} %get-tuple-element.50), channel_id=1, source_target_pairs={{0,2},{2,0},{4,6},{6,4},{8,10},{10,8},{12,14},{14,12},{1,3},{3,1},... | collective-permute-start | bytes 491528 | tf_op jit(solution)/shard_map/ppermute | solution.py:225
  48.1 5.4 %collective-permute-start.11 = (bf16[64,1280]{1,0:T(8,128)(2,1)S(1)}, bf16[64,1280]{1,0:T(8,128)(2,1)S(1)}, u32[]{:S(2)}, u32[]{:S(2)}) collective-permute-start(bf16[64,1280]{1,0:T(8,128)(2,1)S(1)} %get-tuple-element.49), channel_id=1, source_target_pairs={{0,4},{2,6},{4,0},{6,2},{8,12},{10,14},{12,8},{14,10},{1,5},{3,7},... | collective-permute-start | bytes 491528 | tf_op jit(solution)/shard_map/ppermute | solution.py:225
  48.2 6.7 %collective-permute-start.14 = (f32[2,64]{1,0:T(2,128)S(1)}, f32[2,64]{1,0:T(2,128)S(1)}, u32[]{:S(2)}, u32[]{:S(2)}) collective-permute-start(f32[2,64]{1,0:T(2,128)S(1)} %get-tuple-element.55), channel_id=1, source_target_pairs={{0,4},{2,6},{4,0},{6,2},{8,12},{10,14},{12,8},{14,10},{1,5},{3,7},... | collective-permute-start | bytes 1544 | tf_op jit(solution)/shard_map/ppermute | solution.py:225
  50.2 4.7 %collective-permute-start.15 = (f32[2,64]{1,0:T(2,128)S(1)}, f32[2,64]{1,0:T(2,128)S(1)}, u32[]{:S(2)}, u32[]{:S(2)}) collective-permute-start(f32[2,64]{1,0:T(2,128)S(1)} %get-tuple-element.54), channel_id=1, source_target_pairs={{0,2},{2,0},{4,6},{6,4},{8,10},{10,8},{12,14},{14,12},{1,3},{3,1},... | collective-permute-start | bytes 1544 | tf_op jit(solution)/shard_map/ppermute | solution.py:225
  51.7 4.5 %collective-permute-start.16 = (f32[2,64]{1,0:T(2,128)S(1)}, f32[2,64]{1,0:T(2,128)S(1)}, u32[]{:S(2)}, u32[]{:S(2)}) collective-permute-start(f32[2,64]{1,0:T(2,128)S(1)} %get-tuple-element.53), channel_id=1, source_target_pairs={{0,6},{2,4},{4,2},{6,0},{8,14},{10,12},{12,10},{14,8},{1,7},{3,5},... | collective-permute-start | bytes 1544 | tf_op jit(solution)/shard_map/ppermute | solution.py:225
  53.6 7.7 %collective-permute-start.13 = (bf16[32,2560]{1,0:T(8,128)(2,1)S(1)}, bf16[32,2560]{1,0:T(8,128)(2,1)S(1)}, u32[]{:S(2)}, u32[]{:S(2)}) collective-permute-start(bf16[32,2560]{1,0:T(8,128)(2,1)S(1)} %get-tuple-element.52), channel_id=1, source_target_pairs={{0,8},{2,10},{4,12},{6,14},{8,0},{10,2},{12,4},{14,6},{1,9},{3,11}... | collective-permute-start | bytes 491528 | tf_op jit(solution)/shard_map/ppermute | solution.py:225
  56.1 5.9 %collective-permute-start.17 = (f32[1,64]{1,0:T(1,128)S(1)}, f32[1,64]{1,0:T(1,128)S(1)}, u32[]{:S(2)}, u32[]{:S(2)}) collective-permute-start(f32[1,64]{1,0:T(1,128)S(1)} %get-tuple-element.57), channel_id=1, source_target_pairs={{0,8},{2,10},{4,12},{6,14},{8,0},{10,2},{12,4},{14,6},{1,9},{3,11}... | collective-permute-start | bytes 776 | tf_op jit(solution)/shard_map/ppermute | solution.py:225
  56.7 5.4 %collective-permute-start.18 = (f32[1,64]{1,0:T(1,128)S(1)}, f32[1,64]{1,0:T(1,128)S(1)}, u32[]{:S(2)}, u32[]{:S(2)}) collective-permute-start(f32[1,64]{1,0:T(1,128)S(1)} %get-tuple-element.58.refs_0_), channel_id=1, source_target_pairs={{0,1},{1,0},{2,3},{3,2},{4,5},{5,4},{6,7},{7,6},{8,9},{9,8},{10,11... | collective-permute-start | bytes 776 | tf_op jit(solution)/shard_map/ppermute | solution.py:231
  56.7 5.4 %collective-permute-start.19 = (f32[1,64]{1,0:T(1,128)S(1)}, f32[1,64]{1,0:T(1,128)S(1)}, u32[]{:S(2)}, u32[]{:S(2)}) collective-permute-start(f32[1,64]{1,0:T(1,128)S(1)} %get-tuple-element.57), channel_id=1, source_target_pairs={{0,9},{1,8},{2,11},{3,10},{4,13},{5,12},{6,15},{7,14},{8,1},{9,0},... | collective-permute-start | bytes 776 | tf_op jit(solution)/shard_map/ppermute | solution.py:228

commit v9 on v8

--- a/solution.py
+++ b/solution.py
@@ -278,7 +278,7 @@
         "attention",
         (queries, held, trade(held, n // 2), products[1][1]),
         [shape(queries.shape, f32), shape((n, rows), f32)],
-        4 * rows * n * rows * queries.shape[1],
+        120 * rows * n * rows * queries.shape[1],
         limit=32,
         in_specs=[VMEM] * 3 + [ANY],
     )

time: 62.7 us -> 60.5 us (0.965)
  waiting for transfers between devices: 24.3 us -> 23 us
  starting transfers between devices: 27.4 us -> 26.6 us
    ppermute x17, waiting for transfers between devices: 22.7 us -> 21.5 us  [trade(): return lax.ppermute(x, 'seq', [(i, i ^ k) for i in range(n)])]
    ppermute x1, starting transfers between devices: 2.58 us -> 1.56 us  [trade_across(): lax.ppermute(x, ('seq', 'ten'), [(2 * i + t, 2 * (i ^ k) + 1 - t) for i i...]
  transfers between devices with their start and end apart: 20 -> 20, of which waited for: 10 -> 10; matrix products, arithmetic and copies ran while one was open for 0% -> 0% of each run, Pallas kernels for 10% -> 12%
where the time goes in v9:
time: 60.5 us; the launch traced here: 60.4 us
  starting transfers between devices  26.6 us (44%)
  waiting for transfers between devices  23 us (38%)
  Pallas kernels  10.1 us (17%)
  between operations  0.74 us (1%)
    ppermute x17, starting transfers between devices, trade(): return lax.ppermute(x, 'seq', [(i, i ^ k) for i in range(n)])  24.9 us
    ppermute x17, waiting for transfers between devices, trade(): return lax.ppermute(x, 'seq', [(i, i ^ k) for i in range(n)])  21.5 us
    pallas_call x12, Pallas kernels, call(): pl.pallas_call(body, out_shape=list(outputs), in_specs=in_specs or [VMEM]...  10.1 us
    ppermute x1, starting transfers between devices, trade_across(): lax.ppermute(x, ('seq', 'ten'), [(2 * i + t, 2 * (i ^ k) + 1 - t) for i i...  1.56 us
    ppermute x2, waiting for transfers between devices, swap(): return lax.ppermute(x, 'ten', [(0, 1), (1, 0)])  1.45 us
  transfers between devices with their start and end apart: 20, of which 10 were waited for; matrix products, arithmetic and copies ran while one was open for 0% of the time, Pallas kernels for 12%

profile of v9, /device:TPU:0, one launch (start us, length us, event | category | flops | bytes accessed | tf_op | source)
XLA Modules:
  0.0 60.4 jit_solution(8482597713336243289)
XLA Ops:
  0.6 1.7 %norm_select.1 = (bf16[64,1024]{1,0:T(8,128)(2,1)S(1)}, bf16[64,1024]{1,0:T(8,128)(2,1)S(1)}, bf16[64,1024]{1,0:T(8,128)(2,1)S(1)}, bf16[64,1024]{1,0:T(8,128)(2...) custom-call(bf16[64,8192]{1,0:T(8,128)(2,1)} %hidden_in.1, ...), custom_call_target="tpu_custom_call" | custom-call | flops 2097152 | bytes 1933568 | tf_op jit(solution)/shard_map/norm_select/pallas_call | solution.py:21
  2.4 3.0 %collective-permute-start.2 = (bf16[64,1024]{1,0:T(8,128)(2,1)S(1)}, bf16[64,1024]{1,0:T(8,128)(2,1)S(1)}, u32[]{:S(2)}, u32[]{:S(2)}) collective-permute-start(bf16[64,1024]{1,0:T(8,128)(2,1)S(1)} %get-tuple-element.30), channel_id=1, source_target_pairs={{0,2},{2,0},{4,6},{6,4},{8,10},{10,8},{12,14},{14,12},{1,3},{3,1},... | collective-permute-start | bytes 393224 | tf_op jit(solution)/shard_map/ppermute | solution.py:225
  5.4 1.6 %collective-permute-start.4 = (bf16[64,1024]{1,0:T(8,128)(2,1)S(1)}, bf16[64,1024]{1,0:T(8,128)(2,1)S(1)}, u32[]{:S(2)}, u32[]{:S(2)}) collective-permute-start(bf16[64,1024]{1,0:T(8,128)(2,1)S(1)} %get-tuple-element.32), channel_id=1, source_target_pairs={{0,4},{2,6},{4,0},{6,2},{8,12},{10,14},{12,8},{14,10},{1,5},{3,7},... | collective-permute-start | bytes 393224 | tf_op jit(solution)/shard_map/ppermute | solution.py:225
  7.0 2.6 %collective-permute-start = (bf16[64,512]{1,0:T(8,128)(2,1)S(1)}, bf16[64,512]{1,0:T(8,128)(2,1)S(1)}, u32[]{:S(2)}, u32[]{:S(2)}) collective-permute-start(bf16[64,512]{1,0:T(8,128)(2,1)S(1)} %get-tuple-element.28), channel_id=1, source_target_pairs={{0,8},{2,10},{4,12},{6,14},{8,0},{10,2},{12,4},{14,6},{1,9},{3,11}... | collective-permute-start | bytes 196616 | tf_op jit(solution)/shard_map/ppermute | solution.py:225
  9.6 0.3 collective-permute-start.1
  9.9 2.5 %collective-permute-start.3 = (bf16[64,512]{1,0:T(8,128)(2,1)S(1)}, bf16[64,512]{1,0:T(8,128)(2,1)S(1)}, u32[]{:S(2)}, u32[]{:S(2)}) collective-permute-start(bf16[64,512]{1,0:T(8,128)(2,1)S(1)} %get-tuple-element.31), channel_id=1, source_target_pairs={{0,12},{2,14},{4,8},{6,10},{8,4},{10,6},{12,0},{14,2},{1,13},{3,15... | collective-permute-start | bytes 196616 | tf_op jit(solution)/shard_map/ppermute | solution.py:225
  12.3 1.4 %collective-permute-done.refs_0_.refs_4_ = bf16[64,512]{1,0:T(8,128)(2,1)S(1)} collective-permute-done((bf16[64,512]{1,0:T(8,128)(2,1)S(1)}, bf16[64,512]{1,0:T(8,128)(2,1)S(1)}, u32[]{:S(2)}, u32[]{:S(2)}) %collective-permute-start) | collective-permute-done | bytes 65568 | tf_op jit(solution)/shard_map/ppermute | solution.py:225
  13.7 1.9 %collective-permute-start.5 = (bf16[64,1024]{1,0:T(8,128)(2,1)S(1)}, bf16[64,1024]{1,0:T(8,128)(2,1)S(1)}, u32[]{:S(2)}, u32[]{:S(2)}) collective-permute-start(bf16[64,1024]{1,0:T(8,128)(2,1)S(1)} %get-tuple-element.36), channel_id=1, source_target_pairs={{0,6},{2,4},{4,2},{6,0},{8,14},{10,12},{12,10},{14,8},{1,7},{3,5},... | collective-permute-start | bytes 393224 | tf_op jit(solution)/shard_map/ppermute | solution.py:225
  15.6 2.4 %collective-permute-done.1.refs_1_.refs_5_ = bf16[64,512]{1,0:T(8,128)(2,1)S(1)} collective-permute-done((bf16[64,512]{1,0:T(8,128)(2,1)S(1)}, bf16[64,512]{1,0:T(8,128)(2,1)S(1)}, u32[]{:S(2)}, u32[]{:S(2)}) %collective-permute-start.1) | collective-permute-done | bytes 65568 | tf_op jit(solution)/shard_map/ppermute | solution.py:225
  18.1 2.8 %collective-permute-start.6 = (bf16[64,512]{1,0:T(8,128)(2,1)S(1)}, bf16[64,512]{1,0:T(8,128)(2,1)S(1)}, u32[]{:S(2)}, u32[]{:S(2)}) collective-permute-start(bf16[64,512]{1,0:T(8,128)(2,1)S(1)} %get-tuple-element.37), channel_id=1, source_target_pairs={{0,14},{2,12},{4,10},{6,8},{8,6},{10,4},{12,2},{14,0},{1,15},{3,13... | collective-permute-start | bytes 196616 | tf_op jit(solution)/shard_map/ppermute | solution.py:225
  20.9 0.0 collective-permute-done.3.refs_3_.refs_6_
  20.9 0.0 collective-permute-done.2.refs_2_.refs_1_
  20.9 0.0 collective-permute-done.4.refs_4_.refs_2_
  20.9 2.5 %stage.1 = (bf16[1024,2560]{1,0:T(8,128)(2,1)S(1)}, bf16[64,2048]{1,0:T(8,128)(2,1)S(1)}, s32[1,512]{1,0:T(1,128)S(1)}) custom-call(s32[8]{0:T(128)} %counts_in.1, bf16[1024,2560]{1,0:T(8,128)(2,1)} %matrix_in.1, bf16[64,2048]{1,0:T(8,128)(2,1)} %queries_in.1, bf16[64,512]{1,0:T(8,128)(2,1)S(1)} %collective-permute-done.refs_0_.refs_4_, ...), custom_call_target="tpu_custom_call" | custom-call | flops 3932160000 | bytes 11470880 | tf_op jit(solution)/shard_map/stage/pallas_call | solution.py:21
  23.5 1.6 %collective-permute-done.6.refs_7_ = bf16[64,512]{1,0:T(8,128)(2,1)S(1)} collective-permute-done((bf16[64,512]{1,0:T(8,128)(2,1)S(1)}, bf16[64,512]{1,0:T(8,128)(2,1)S(1)}, u32[]{:S(2)}, u32[]{:S(2)}) %collective-permute-start.6) | collective-permute-done | bytes 65568 | tf_op jit(solution)/shard_map/ppermute | solution.py:225
  25.0 0.0 collective-permute-done.5.refs_3_
  25.0 0.3 compact.1
  25.4 0.1 collective-permute-start.8
  25.4 0.1 collective-permute-start.7
  25.5 1.4 %collective-permute-done.8.other = bf16[256,512]{1,0:T(8,128)(2,1)S(1)} collective-permute-done((bf16[256,512]{1,0:T(8,128)(2,1)S(1)}, bf16[256,512]{1,0:T(8,128)(2,1)S(1)}, u32[]{:S(2)}, u32[]{:S(2)}) %collective-permute-start.8) | collective-permute-done | bytes 262176 | tf_op jit(solution)/shard_map/ppermute | solution.py:231
  27.0 1.0 %project.2 = (f32[128,1280]{1,0:T(8,128)S(1)}, bf16[128,1280]{1,0:T(8,128)(2,1)S(1)}) custom-call(bf16[256,512]{1,0:T(8,128)(2,1)S(1)} %get-tuple-element.39.own, bf16[256,512]{1,0:T(8,128)(2,1)S(1)} %collective-permute-done.8.other, bf16[1024,2560]{1,0:T(8,128)(2,1)S(1)} %get-tuple-element.40.matrix), custom_call_target="tpu_custom_call" | custom-call | flops 671088640 | bytes 6750208 | tf_op jit(solution)/shard_map/project/pallas_call | solution.py:21
  28.0 1.7 %collective-permute-start.10 = (bf16[128,1280]{1,0:T(8,128)(2,1)S(1)}, bf16[128,1280]{1,0:T(8,128)(2,1)S(1)}, u32[]{:S(2)}, u32[]{:S(2)}) collective-permute-start(bf16[128,1280]{1,0:T(8,128)(2,1)S(1)} %get-tuple-element.41.after), channel_id=1, source_target_pairs={{0,4},{2,6},{4,0},{6,2},{8,12},{10,14},{12,8},{14,10},{1,5},{3,7},... | collective-permute-start | bytes 983048 | tf_op jit(solution)/shard_map/ppermute | solution.py:225
  29.6 1.0 %project.3 = (f32[128,1280]{1,0:T(8,128)S(1)}, bf16[128,1280]{1,0:T(8,128)(2,1)S(1)}) custom-call(bf16[256,512]{1,0:T(8,128)(2,1)S(1)} %get-tuple-element.39.own, bf16[256,512]{1,0:T(8,128)(2,1)S(1)} %collective-permute-done.8.other, bf16[1024,2560]{1,0:T(8,128)(2,1)S(1)} %get-tuple-element.40.matrix), custom_call_target="tpu_custom_call" | custom-call | flops 671088640 | bytes 6750208 | tf_op jit(solution)/shard_map/project/pallas_call | solution.py:21
  30.6 1.0 %collective-permute-start.9 = (bf16[128,1280]{1,0:T(8,128)(2,1)S(1)}, bf16[128,1280]{1,0:T(8,128)(2,1)S(1)}, u32[]{:S(2)}, u32[]{:S(2)}) collective-permute-start(bf16[128,1280]{1,0:T(8,128)(2,1)S(1)} %get-tuple-element.44), channel_id=1, source_target_pairs={{0,2},{2,0},{4,6},{6,4},{8,10},{10,8},{12,14},{14,12},{1,3},{3,1},... | collective-permute-start | bytes 983048 | tf_op jit(solution)/shard_map/ppermute | solution.py:225
  31.6 9.0 %collective-permute-done.7.far = bf16[256,512]{1,0:T(8,128)(2,1)S(1)} collective-permute-done((bf16[256,512]{1,0:T(8,128)(2,1)S(1)}, bf16[256,512]{1,0:T(8,128)(2,1)S(1)}, u32[]{:S(2)}, u32[]{:S(2)}) %collective-permute-start.7) | collective-permute-done | bytes 262176 | tf_op jit(solution)/shard_map/ppermute | solution.py:225
  40.6 2.0 %attention.1 = (f32[64,2048]{1,0:T(8,128)}, f32[8,64]{1,0:T(8,128)S(1)}) custom-call(bf16[64,2048]{1,0:T(8,128)(2,1)S(1)} %get-tuple-element.33.queries, bf16[256,512]{1,0:T(8,128)(2,1)S(1)} %get-tuple-element.38.near, bf16[256,512]{1,0:T(8,128)(2,1)S(1)} %collective-permute-done.7.far, bf16[128,1280]{1,0:T(8,128)(2,1)S(1)} %get-tuple-element.41.after), custom_call_target="tpu_custom_call" | custom-call | flops 8053063680 | bytes 1640448 | tf_op jit(solution)/shard_map/attention/pallas_call | solution.py:21
  42.6 0.7 %collective-permute-done.10.received = bf16[128,1280]{1,0:T(8,128)(2,1)S(1)} collective-permute-done((bf16[128,1280]{1,0:T(8,128)(2,1)S(1)}, bf16[128,1280]{1,0:T(8,128)(2,1)S(1)}, u32[]{:S(2)}, u32[]{:S(2)}) %collective-permute-start.10) | collective-permute-done | bytes 327712 | tf_op jit(solution)/shard_map/ppermute | solution.py:225
  43.3 0.1 hop_sum.3
  43.4 1.6 %collective-permute-start.12 = (bf16[64,1280]{1,0:T(8,128)(2,1)S(1)}, bf16[64,1280]{1,0:T(8,128)(2,1)S(1)}, u32[]{:S(2)}, u32[]{:S(2)}) collective-permute-start(bf16[64,1280]{1,0:T(8,128)(2,1)S(1)} %get-tuple-element.50), channel_id=1, source_target_pairs={{0,2},{2,0},{4,6},{6,4},{8,10},{10,8},{12,14},{14,12},{1,3},{3,1},... | collective-permute-start | bytes 491528 | tf_op jit(solution)/shard_map/ppermute | solution.py:225
  45.0 0.0 collective-permute-done.9.received
  45.0 0.1 hop_sum.2
  45.1 0.1 collective-permute-start.11
  45.2 2.0 %collective-permute-start.14 = (f32[2,64]{1,0:T(2,128)S(1)}, f32[2,64]{1,0:T(2,128)S(1)}, u32[]{:S(2)}, u32[]{:S(2)}) collective-permute-start(f32[2,64]{1,0:T(2,128)S(1)} %get-tuple-element.55), channel_id=1, source_target_pairs={{0,4},{2,6},{4,0},{6,2},{8,12},{10,14},{12,8},{14,10},{1,5},{3,7},... | collective-permute-start | bytes 1544 | tf_op jit(solution)/shard_map/ppermute | solution.py:225
  47.2 0.4 collective-permute-start.15
  47.6 1.1 %collective-permute-start.16 = (f32[2,64]{1,0:T(2,128)S(1)}, f32[2,64]{1,0:T(2,128)S(1)}, u32[]{:S(2)}, u32[]{:S(2)}) collective-permute-start(f32[2,64]{1,0:T(2,128)S(1)} %get-tuple-element.53), channel_id=1, source_target_pairs={{0,6},{2,4},{4,2},{6,0},{8,14},{10,12},{12,10},{14,8},{1,7},{3,5},... | collective-permute-start | bytes 1544 | tf_op jit(solution)/shard_map/ppermute | solution.py:225
  48.7 0.1 collective-permute-done.12.refs_3_
  48.9 1.6 %collective-permute-done.11.refs_2_ = bf16[64,1280]{1,0:T(8,128)(2,1)S(1)} collective-permute-done((bf16[64,1280]{1,0:T(8,128)(2,1)S(1)}, bf16[64,1280]{1,0:T(8,128)(2,1)S(1)}, u32[]{:S(2)}, u32[]{:S(2)}) %collective-permute-start.11) | collective-permute-done | bytes 163872 | tf_op jit(solution)/shard_map/ppermute | solution.py:225
  50.5 0.1 hop_sum_both.1
  50.6 0.7 %collective-permute-start.13 = (bf16[32,2560]{1,0:T(8,128)(2,1)S(1)}, bf16[32,2560]{1,0:T(8,128)(2,1)S(1)}, u32[]{:S(2)}, u32[]{:S(2)}) collective-permute-start(bf16[32,2560]{1,0:T(8,128)(2,1)S(1)} %get-tuple-element.52), channel_id=1, source_target_pairs={{0,8},{2,10},{4,12},{6,14},{8,0},{10,2},{12,4},{14,6},{1,9},{3,11}... | collective-permute-start | bytes 491528 | tf_op jit(solution)/shard_map/ppermute | solution.py:225
  51.2 0.0 collective-permute-done.14.refs_1_
  51.2 0.0 collective-permute-done.15.refs_2_
  51.2 0.9 %collective-permute-done.16.refs_3_ = f32[2,64]{1,0:T(2,128)S(1)} collective-permute-done((f32[2,64]{1,0:T(2,128)S(1)}, f32[2,64]{1,0:T(2,128)S(1)}, u32[]{:S(2)}, u32[]{:S(2)}) %collective-permute-start.16) | collective-permute-done | bytes 544 | tf_op jit(solution)/shard_map/ppermute | solution.py:225
  52.1 1.5 %collective-permute-start.17 = (f32[1,64]{1,0:T(1,128)S(1)}, f32[1,64]{1,0:T(1,128)S(1)}, u32[]{:S(2)}, u32[]{:S(2)}) collective-permute-start(f32[1,64]{1,0:T(1,128)S(1)} %get-tuple-element.57), channel_id=1, source_target_pairs={{0,8},{2,10},{4,12},{6,14},{8,0},{10,2},{12,4},{14,6},{1,9},{3,11}... | collective-permute-start | bytes 776 | tf_op jit(solution)/shard_map/ppermute | solution.py:225
  53.6 0.0 collective-permute-start.18
  53.7 1.6 %collective-permute-start.19 = (f32[1,64]{1,0:T(1,128)S(1)}, f32[1,64]{1,0:T(1,128)S(1)}, u32[]{:S(2)}, u32[]{:S(2)}) collective-permute-start(f32[1,64]{1,0:T(1,128)S(1)} %get-tuple-element.57), channel_id=1, source_target_pairs={{0,9},{1,8},{2,11},{3,10},{4,13},{5,12},{6,15},{7,14},{8,1},{9,0},... | collective-permute-start | bytes 776 | tf_op jit(solution)/shard_map/ppermute | solution.py:228
  55.2 3.9 %collective-permute-done.13.received = bf16[32,2560]{1,0:T(8,128)(2,1)S(1)} collective-permute-done((bf16[32,2560]{1,0:T(8,128)(2,1)S(1)}, bf16[32,2560]{1,0:T(8,128)(2,1)S(1)}, u32[]{:S(2)}, u32[]{:S(2)}) %collective-permute-start.13) | collective-permute-done | bytes 163872 | tf_op jit(solution)/shard_map/ppermute | solution.py:225
  59.1 0.8 %finish.1.after = f32[32,2560]{1,0:T(8,128)} custom-call(f32[1,2560]{1,0:T(1,128)S(1)} %reshape.20.bias, f32[32,2560]{1,0:T(8,128)S(1)} %get-tuple-element.51.kept.after, bf16[32,2560]{1,0:T(8,128)(2,1)S(1)} %collective-permute-done.13.received), custom_call_target="tpu_custom_call" | custom-call | flops 655360 | bytes 829440 | tf_op jit(solution)/shard_map/finish/pallas_call | solution.py:21
  59.9 0.5 column_sum.3
  (9 shorter events, 0.0 us)
Async XLA Ops:
  2.4 18.5 %collective-permute-start.2 = (bf16[64,1024]{1,0:T(8,128)(2,1)S(1)}, bf16[64,1024]{1,0:T(8,128)(2,1)S(1)}, u32[]{:S(2)}, u32[]{:S(2)}) collective-permute-start(bf16[64,1024]{1,0:T(8,128)(2,1)S(1)} %get-tuple-element.30), channel_id=1, source_target_pairs={{0,2},{2,0},{4,6},{6,4},{8,10},{10,8},{12,14},{14,12},{1,3},{3,1},... | collective-permute-start | bytes 393224 | tf_op jit(solution)/shard_map/ppermute | solution.py:225
  5.4 15.5 %collective-permute-start.4 = (bf16[64,1024]{1,0:T(8,128)(2,1)S(1)}, bf16[64,1024]{1,0:T(8,128)(2,1)S(1)}, u32[]{:S(2)}, u32[]{:S(2)}) collective-permute-start(bf16[64,1024]{1,0:T(8,128)(2,1)S(1)} %get-tuple-element.32), channel_id=1, source_target_pairs={{0,4},{2,6},{4,0},{6,2},{8,12},{10,14},{12,8},{14,10},{1,5},{3,7},... | collective-permute-start | bytes 393224 | tf_op jit(solution)/shard_map/ppermute | solution.py:225
  7.0 6.7 %collective-permute-start = (bf16[64,512]{1,0:T(8,128)(2,1)S(1)}, bf16[64,512]{1,0:T(8,128)(2,1)S(1)}, u32[]{:S(2)}, u32[]{:S(2)}) collective-permute-start(bf16[64,512]{1,0:T(8,128)(2,1)S(1)} %get-tuple-element.28), channel_id=1, source_target_pairs={{0,8},{2,10},{4,12},{6,14},{8,0},{10,2},{12,4},{14,6},{1,9},{3,11}... | collective-permute-start | bytes 196616 | tf_op jit(solution)/shard_map/ppermute | solution.py:225
  9.6 8.5 %collective-permute-start.1 = (bf16[64,512]{1,0:T(8,128)(2,1)S(1)}, bf16[64,512]{1,0:T(8,128)(2,1)S(1)}, u32[]{:S(2)}, u32[]{:S(2)}) collective-permute-start(bf16[64,512]{1,0:T(8,128)(2,1)S(1)} %get-tuple-element.29), channel_id=1, source_target_pairs={{0,10},{2,8},{4,14},{6,12},{8,2},{10,0},{12,6},{14,4},{1,11},{3,9}... | collective-permute-start | bytes 196616 | tf_op jit(solution)/shard_map/ppermute | solution.py:225
  9.9 11.1 %collective-permute-start.3 = (bf16[64,512]{1,0:T(8,128)(2,1)S(1)}, bf16[64,512]{1,0:T(8,128)(2,1)S(1)}, u32[]{:S(2)}, u32[]{:S(2)}) collective-permute-start(bf16[64,512]{1,0:T(8,128)(2,1)S(1)} %get-tuple-element.31), channel_id=1, source_target_pairs={{0,12},{2,14},{4,8},{6,10},{8,4},{10,6},{12,0},{14,2},{1,13},{3,15... | collective-permute-start | bytes 196616 | tf_op jit(solution)/shard_map/ppermute | solution.py:225
  13.7 11.3 %collective-permute-start.5 = (bf16[64,1024]{1,0:T(8,128)(2,1)S(1)}, bf16[64,1024]{1,0:T(8,128)(2,1)S(1)}, u32[]{:S(2)}, u32[]{:S(2)}) collective-permute-start(bf16[64,1024]{1,0:T(8,128)(2,1)S(1)} %get-tuple-element.36), channel_id=1, source_target_pairs={{0,6},{2,4},{4,2},{6,0},{8,14},{10,12},{12,10},{14,8},{1,7},{3,5},... | collective-permute-start | bytes 393224 | tf_op jit(solution)/shard_map/ppermute | solution.py:225
  18.1 7.0 %collective-permute-start.6 = (bf16[64,512]{1,0:T(8,128)(2,1)S(1)}, bf16[64,512]{1,0:T(8,128)(2,1)S(1)}, u32[]{:S(2)}, u32[]{:S(2)}) collective-permute-start(bf16[64,512]{1,0:T(8,128)(2,1)S(1)} %get-tuple-element.37), channel_id=1, source_target_pairs={{0,14},{2,12},{4,10},{6,8},{8,6},{10,4},{12,2},{14,0},{1,15},{3,13... | collective-permute-start | bytes 196616 | tf_op jit(solution)/shard_map/ppermute | solution.py:225
  25.4 1.6 %collective-permute-start.8 = (bf16[256,512]{1,0:T(8,128)(2,1)S(1)}, bf16[256,512]{1,0:T(8,128)(2,1)S(1)}, u32[]{:S(2)}, u32[]{:S(2)}) collective-permute-start(bf16[256,512]{1,0:T(8,128)(2,1)S(1)} %get-tuple-element.39.own), channel_id=1, source_target_pairs={{0,1},{1,0},{2,3},{3,2},{4,5},{5,4},{6,7},{7,6},{8,9},{9,8},{10,11... | collective-permute-start | bytes 786440 | tf_op jit(solution)/shard_map/ppermute | solution.py:231
  25.4 15.2 %collective-permute-start.7 = (bf16[256,512]{1,0:T(8,128)(2,1)S(1)}, bf16[256,512]{1,0:T(8,128)(2,1)S(1)}, u32[]{:S(2)}, u32[]{:S(2)}) collective-permute-start(bf16[256,512]{1,0:T(8,128)(2,1)S(1)} %get-tuple-element.38.near), channel_id=1, source_target_pairs={{0,8},{2,10},{4,12},{6,14},{8,0},{10,2},{12,4},{14,6},{1,9},{3,11}... | collective-permute-start | bytes 786440 | tf_op jit(solution)/shard_map/ppermute | solution.py:225
  28.0 15.3 %collective-permute-start.10 = (bf16[128,1280]{1,0:T(8,128)(2,1)S(1)}, bf16[128,1280]{1,0:T(8,128)(2,1)S(1)}, u32[]{:S(2)}, u32[]{:S(2)}) collective-permute-start(bf16[128,1280]{1,0:T(8,128)(2,1)S(1)} %get-tuple-element.41.after), channel_id=1, source_target_pairs={{0,4},{2,6},{4,0},{6,2},{8,12},{10,14},{12,8},{14,10},{1,5},{3,7},... | collective-permute-start | bytes 983048 | tf_op jit(solution)/shard_map/ppermute | solution.py:225
  30.6 14.4 %collective-permute-start.9 = (bf16[128,1280]{1,0:T(8,128)(2,1)S(1)}, bf16[128,1280]{1,0:T(8,128)(2,1)S(1)}, u32[]{:S(2)}, u32[]{:S(2)}) collective-permute-start(bf16[128,1280]{1,0:T(8,128)(2,1)S(1)} %get-tuple-element.44), channel_id=1, source_target_pairs={{0,2},{2,0},{4,6},{6,4},{8,10},{10,8},{12,14},{14,12},{1,3},{3,1},... | collective-permute-start | bytes 983048 | tf_op jit(solution)/shard_map/ppermute | solution.py:225
  40.6 8.1 %copy-start = (f32[2560]{0:T(1024)S(1)}, f32[2560]{0:T(1024)}, u32[]{:S(2)}) copy-start(f32[2560]{0:T(1024)} %param.17) | copy-start | bytes 30724
  43.4 5.5 %collective-permute-start.12 = (bf16[64,1280]{1,0:T(8,128)(2,1)S(1)}, bf16[64,1280]{1,0:T(8,128)(2,1)S(1)}, u32[]{:S(2)}, u32[]{:S(2)}) collective-permute-start(bf16[64,1280]{1,0:T(8,128)(2,1)S(1)} %get-tuple-element.50), channel_id=1, source_target_pairs={{0,2},{2,0},{4,6},{6,4},{8,10},{10,8},{12,14},{14,12},{1,3},{3,1},... | collective-permute-start | bytes 491528 | tf_op jit(solution)/shard_map/ppermute | solution.py:225
  45.1 5.4 %collective-permute-start.11 = (bf16[64,1280]{1,0:T(8,128)(2,1)S(1)}, bf16[64,1280]{1,0:T(8,128)(2,1)S(1)}, u32[]{:S(2)}, u32[]{:S(2)}) collective-permute-start(bf16[64,1280]{1,0:T(8,128)(2,1)S(1)} %get-tuple-element.49), channel_id=1, source_target_pairs={{0,4},{2,6},{4,0},{6,2},{8,12},{10,14},{12,8},{14,10},{1,5},{3,7},... | collective-permute-start | bytes 491528 | tf_op jit(solution)/shard_map/ppermute | solution.py:225
  45.2 6.0 %collective-permute-start.14 = (f32[2,64]{1,0:T(2,128)S(1)}, f32[2,64]{1,0:T(2,128)S(1)}, u32[]{:S(2)}, u32[]{:S(2)}) collective-permute-start(f32[2,64]{1,0:T(2,128)S(1)} %get-tuple-element.55), channel_id=1, source_target_pairs={{0,4},{2,6},{4,0},{6,2},{8,12},{10,14},{12,8},{14,10},{1,5},{3,7},... | collective-permute-start | bytes 1544 | tf_op jit(solution)/shard_map/ppermute | solution.py:225
  47.2 4.0 %collective-permute-start.15 = (f32[2,64]{1,0:T(2,128)S(1)}, f32[2,64]{1,0:T(2,128)S(1)}, u32[]{:S(2)}, u32[]{:S(2)}) collective-permute-start(f32[2,64]{1,0:T(2,128)S(1)} %get-tuple-element.54), channel_id=1, source_target_pairs={{0,2},{2,0},{4,6},{6,4},{8,10},{10,8},{12,14},{14,12},{1,3},{3,1},... | collective-permute-start | bytes 1544 | tf_op jit(solution)/shard_map/ppermute | solution.py:225
  47.6 4.5 %collective-permute-start.16 = (f32[2,64]{1,0:T(2,128)S(1)}, f32[2,64]{1,0:T(2,128)S(1)}, u32[]{:S(2)}, u32[]{:S(2)}) collective-permute-start(f32[2,64]{1,0:T(2,128)S(1)} %get-tuple-element.53), channel_id=1, source_target_pairs={{0,6},{2,4},{4,2},{6,0},{8,14},{10,12},{12,10},{14,8},{1,7},{3,5},... | collective-permute-start | bytes 1544 | tf_op jit(solution)/shard_map/ppermute | solution.py:225
  50.6 8.5 %collective-permute-start.13 = (bf16[32,2560]{1,0:T(8,128)(2,1)S(1)}, bf16[32,2560]{1,0:T(8,128)(2,1)S(1)}, u32[]{:S(2)}, u32[]{:S(2)}) collective-permute-start(bf16[32,2560]{1,0:T(8,128)(2,1)S(1)} %get-tuple-element.52), channel_id=1, source_target_pairs={{0,8},{2,10},{4,12},{6,14},{8,0},{10,2},{12,4},{14,6},{1,9},{3,11}... | collective-permute-start | bytes 491528 | tf_op jit(solution)/shard_map/ppermute | solution.py:225
  52.1 7.7 %collective-permute-start.17 = (f32[1,64]{1,0:T(1,128)S(1)}, f32[1,64]{1,0:T(1,128)S(1)}, u32[]{:S(2)}, u32[]{:S(2)}) collective-permute-start(f32[1,64]{1,0:T(1,128)S(1)} %get-tuple-element.57), channel_id=1, source_target_pairs={{0,8},{2,10},{4,12},{6,14},{8,0},{10,2},{12,4},{14,6},{1,9},{3,11}... | collective-permute-start | bytes 776 | tf_op jit(solution)/shard_map/ppermute | solution.py:225
  53.6 6.2 %collective-permute-start.18 = (f32[1,64]{1,0:T(1,128)S(1)}, f32[1,64]{1,0:T(1,128)S(1)}, u32[]{:S(2)}, u32[]{:S(2)}) collective-permute-start(f32[1,64]{1,0:T(1,128)S(1)} %get-tuple-element.58.refs_0_), channel_id=1, source_target_pairs={{0,1},{1,0},{2,3},{3,2},{4,5},{5,4},{6,7},{7,6},{8,9},{9,8},{10,11... | collective-permute-start | bytes 776 | tf_op jit(solution)/shard_map/ppermute | solution.py:231
  53.7 6.2 %collective-permute-start.19 = (f32[1,64]{1,0:T(1,128)S(1)}, f32[1,64]{1,0:T(1,128)S(1)}, u32[]{:S(2)}, u32[]{:S(2)}) collective-permute-start(f32[1,64]{1,0:T(1,128)S(1)} %get-tuple-element.57), channel_id=1, source_target_pairs={{0,9},{1,8},{2,11},{3,10},{4,13},{5,12},{6,15},{7,14},{8,1},{9,0},... | collective-permute-start | bytes 776 | tf_op jit(solution)/shard_map/ppermute | solution.py:228

commit v10 on v9

--- a/solution.py
+++ b/solution.py
@@ -73,6 +73,12 @@
         outs[k][:, :half] = lax.dot_general(
             selector, normed, (((0,), (0,)), ((), ())), preferred_element_type=jnp.float32
         ).astype(jnp.bfloat16)
+
+
+def relay_kernel(count, *refs):
+    blocks, outs = refs[:count], refs[len(refs) - count :]
+    for block, out in zip(blocks, outs):
+        out[...] = block[...]
 
 
 def stage_kernel(n, counts_in, matrix_in, queries_in, *refs):
@@ -241,15 +247,24 @@
         remote=5,
         scratch=[pltpu.VMEM((rows, model), bf16), pltpu.VMEM((1, model), f32), pltpu.VMEM((1, rows), i32), pltpu.VMEM((rows, 2 * keys.shape[1]), bf16), dma((8,))],
     )
-    received = [chosen[0]] + [trade(chosen[k], k) for k in range(1, n)]
-    turns = [k for i in range(n // 2) for k in (n // 2 + i, i) if k]
+    last = range(n - n // 4, n)
+    received = [chosen[0]] + [trade(chosen[k], k) for k in range(1, last[0])]
+    relayed = call(
+        functools.partial(relay_kernel, len(last)),
+        "relay",
+        (*[chosen[k] for k in last], *received[1 : n // 2]),
+        [shape((rows, half), bf16)] * len(last),
+        0,
+        in_specs=[VMEM] * len(last) + [ANY] * (n // 2 - 1),
+    )
+    received += [trade(x, k) for k, x in zip(last, relayed)]
     matrix, queries, target = call(
         functools.partial(stage_kernel, n),
         "stage",
-        (counts, affine_matrix, queries, *[received[k] for k in turns[:5]]),
+        (counts, affine_matrix, queries, *received[n // 2 : last[0]]),
         [shape(affine_matrix.shape, bf16), shape(queries.shape, bf16), shape((1, n * rows), i32)],
         1500 * affine_matrix.size,
-        in_specs=[ANY] * 8,
+        in_specs=[ANY] * (3 + n // 4),
         remote=3,
         scratch=[pltpu.SMEM(counts.shape, i32), dma((3,))],
     )

time: 60.5 us -> 62 us (1.025)
  waiting for transfers between devices: 23 us -> 25.1 us
  starting transfers between devices: 26.6 us -> 25.9 us
    ppermute x17, waiting for transfers between devices: 21.5 us -> 23.6 us  [trade(): return lax.ppermute(x, 'seq', [(i, i ^ k) for i in range(n)])]
    pallas_call x12 -> x13, Pallas kernels: 10.1 us -> 10.1 us  [call(): pl.pallas_call(body, out_shape=list(outputs), in_specs=in_specs or [VMEM]...]
where the time goes in v10:
time: 62 us; the launch traced here: 61.9 us
  starting transfers between devices  25.9 us (42%)
  waiting for transfers between devices  25.1 us (40%)
  Pallas kernels  10.1 us (16%)
  between operations  0.77 us (1%)
    ppermute x17, starting transfers between devices, trade(): return lax.ppermute(x, 'seq', [(i, i ^ k) for i in range(n)])  24.7 us
    ppermute x17, waiting for transfers between devices, trade(): return lax.ppermute(x, 'seq', [(i, i ^ k) for i in range(n)])  23.6 us
    pallas_call x13, Pallas kernels, call(): pl.pallas_call(body, out_shape=list(outputs), in_specs=in_specs or [VMEM]...  10.1 us
    ppermute x2, waiting for transfers between devices, swap(): return lax.ppermute(x, 'ten', [(0, 1), (1, 0)])  1.45 us
  transfers between devices with their start and end apart: 20, of which 10 were waited for; matrix products, arithmetic and copies ran while one was open for 0% of the time, Pallas kernels for 12%

profile of v10, /device:TPU:0, one launch (start us, length us, event | category | flops | bytes accessed | tf_op | source)
XLA Modules:
  0.0 61.9 jit_solution(9304305726434548222)
XLA Ops:
  0.6 1.7 %norm_select.1 = (bf16[64,1024]{1,0:T(8,128)(2,1)S(1)}, bf16[64,1024]{1,0:T(8,128)(2,1)S(1)}, bf16[64,1024]{1,0:T(8,128)(2,1)S(1)}, bf16[64,1024]{1,0:T(8,128)(2...) custom-call(bf16[64,8192]{1,0:T(8,128)(2,1)} %hidden_in.1, ...), custom_call_target="tpu_custom_call" | custom-call | flops 2097152 | bytes 1933568 | tf_op jit(solution)/shard_map/norm_select/pallas_call | solution.py:21
  2.4 3.0 %collective-permute-start.2 = (bf16[64,1024]{1,0:T(8,128)(2,1)S(1)}, bf16[64,1024]{1,0:T(8,128)(2,1)S(1)}, u32[]{:S(2)}, u32[]{:S(2)}) collective-permute-start(bf16[64,1024]{1,0:T(8,128)(2,1)S(1)} %get-tuple-element.35), channel_id=1, source_target_pairs={{0,2},{2,0},{4,6},{6,4},{8,10},{10,8},{12,14},{14,12},{1,3},{3,1},... | collective-permute-start | bytes 393224 | tf_op jit(solution)/shard_map/ppermute | solution.py:231
  5.4 1.6 %collective-permute-start.3 = (bf16[64,1024]{1,0:T(8,128)(2,1)S(1)}, bf16[64,1024]{1,0:T(8,128)(2,1)S(1)}, u32[]{:S(2)}, u32[]{:S(2)}) collective-permute-start(bf16[64,1024]{1,0:T(8,128)(2,1)S(1)} %get-tuple-element.36), channel_id=1, source_target_pairs={{0,4},{2,6},{4,0},{6,2},{8,12},{10,14},{12,8},{14,10},{1,5},{3,7},... | collective-permute-start | bytes 393224 | tf_op jit(solution)/shard_map/ppermute | solution.py:231
  7.0 0.0 collective-permute-start.4
  7.0 3.0 %collective-permute-start = (bf16[64,512]{1,0:T(8,128)(2,1)S(1)}, bf16[64,512]{1,0:T(8,128)(2,1)S(1)}, u32[]{:S(2)}, u32[]{:S(2)}) collective-permute-start(bf16[64,512]{1,0:T(8,128)(2,1)S(1)} %get-tuple-element.30), channel_id=1, source_target_pairs={{0,8},{2,10},{4,12},{6,14},{8,0},{10,2},{12,4},{14,6},{1,9},{3,11}... | collective-permute-start | bytes 196616 | tf_op jit(solution)/shard_map/ppermute | solution.py:231
  10.0 1.3 %collective-permute-start.1 = (bf16[64,512]{1,0:T(8,128)(2,1)S(1)}, bf16[64,512]{1,0:T(8,128)(2,1)S(1)}, u32[]{:S(2)}, u32[]{:S(2)}) collective-permute-start(bf16[64,512]{1,0:T(8,128)(2,1)S(1)} %get-tuple-element.31), channel_id=1, source_target_pairs={{0,10},{2,8},{4,14},{6,12},{8,2},{10,0},{12,6},{14,4},{1,11},{3,9}... | collective-permute-start | bytes 196616 | tf_op jit(solution)/shard_map/ppermute | solution.py:231
  11.3 0.0 collective-permute-done.2.refs_2_.refs_1_
  11.3 1.9 %collective-permute-done.3.refs_3_.refs_2_ = bf16[64,1024]{1,0:T(8,128)(2,1)S(1)} collective-permute-done((bf16[64,1024]{1,0:T(8,128)(2,1)S(1)}, bf16[64,1024]{1,0:T(8,128)(2,1)S(1)}, u32[]{:S(2)}, u32[]{:S(2)}) %collective-permute-start.3) | collective-permute-done | bytes 131104 | tf_op jit(solution)/shard_map/ppermute | solution.py:231
  13.2 1.9 %collective-permute-done.4.refs_4_.refs_3_ = bf16[64,1024]{1,0:T(8,128)(2,1)S(1)} collective-permute-done((bf16[64,1024]{1,0:T(8,128)(2,1)S(1)}, bf16[64,1024]{1,0:T(8,128)(2,1)S(1)}, u32[]{:S(2)}, u32[]{:S(2)}) %collective-permute-start.4) | collective-permute-done | bytes 131104 | tf_op jit(solution)/shard_map/ppermute | solution.py:231
  15.1 3.9 %collective-permute-start.5 = (bf16[64,512]{1,0:T(8,128)(2,1)S(1)}, bf16[64,512]{1,0:T(8,128)(2,1)S(1)}, u32[]{:S(2)}, u32[]{:S(2)}) collective-permute-start(bf16[64,512]{1,0:T(8,128)(2,1)S(1)} %get-tuple-element.40), channel_id=1, source_target_pairs={{0,12},{2,14},{4,8},{6,10},{8,4},{10,6},{12,0},{14,2},{1,13},{3,15... | collective-permute-start | bytes 196616 | tf_op jit(solution)/shard_map/ppermute | solution.py:231
  19.0 1.7 %collective-permute-start.6 = (bf16[64,512]{1,0:T(8,128)(2,1)S(1)}, bf16[64,512]{1,0:T(8,128)(2,1)S(1)}, u32[]{:S(2)}, u32[]{:S(2)}) collective-permute-start(bf16[64,512]{1,0:T(8,128)(2,1)S(1)} %get-tuple-element.41), channel_id=1, source_target_pairs={{0,14},{2,12},{4,10},{6,8},{8,6},{10,4},{12,2},{14,0},{1,15},{3,13... | collective-permute-start | bytes 196616 | tf_op jit(solution)/shard_map/ppermute | solution.py:231
  20.7 0.0 collective-permute-done.refs_0_.refs_4_
  20.7 0.0 collective-permute-done.1.refs_1_.refs_5_
  20.7 2.5 %stage.1 = (bf16[1024,2560]{1,0:T(8,128)(2,1)S(1)}, bf16[64,2048]{1,0:T(8,128)(2,1)S(1)}, s32[1,512]{1,0:T(1,128)S(1)}) custom-call(s32[8]{0:T(128)} %counts_in.1, bf16[1024,2560]{1,0:T(8,128)(2,1)} %matrix_in.1, bf16[64,2048]{1,0:T(8,128)(2,1)} %queries_in.1, bf16[64,512]{1,0:T(8,128)(2,1)S(1)} %collective-permute-done.refs_0_.refs_4_, ...), custom_call_target="tpu_custom_call" | custom-call | flops 3932160000 | bytes 11143200 | tf_op jit(solution)/shard_map/stage/pallas_call | solution.py:21
  23.2 0.0 collective-permute-done.5.refs_6_
  23.2 2.7 %collective-permute-done.6.refs_7_ = bf16[64,512]{1,0:T(8,128)(2,1)S(1)} collective-permute-done((bf16[64,512]{1,0:T(8,128)(2,1)S(1)}, bf16[64,512]{1,0:T(8,128)(2,1)S(1)}, u32[]{:S(2)}, u32[]{:S(2)}) %collective-permute-start.6) | collective-permute-done | bytes 65568 | tf_op jit(solution)/shard_map/ppermute | solution.py:231
  26.0 0.3 compact.1
  26.3 0.1 collective-permute-start.8
  26.3 0.1 collective-permute-start.7
  26.4 1.4 %collective-permute-done.8.other = bf16[256,512]{1,0:T(8,128)(2,1)S(1)} collective-permute-done((bf16[256,512]{1,0:T(8,128)(2,1)S(1)}, bf16[256,512]{1,0:T(8,128)(2,1)S(1)}, u32[]{:S(2)}, u32[]{:S(2)}) %collective-permute-start.8) | collective-permute-done | bytes 262176 | tf_op jit(solution)/shard_map/ppermute | solution.py:237
  27.9 1.0 %project.2 = (f32[128,1280]{1,0:T(8,128)S(1)}, bf16[128,1280]{1,0:T(8,128)(2,1)S(1)}) custom-call(bf16[256,512]{1,0:T(8,128)(2,1)S(1)} %get-tuple-element.43.own, bf16[256,512]{1,0:T(8,128)(2,1)S(1)} %collective-permute-done.8.other, bf16[1024,2560]{1,0:T(8,128)(2,1)S(1)} %get-tuple-element.44.matrix), custom_call_target="tpu_custom_call" | custom-call | flops 671088640 | bytes 6750208 | tf_op jit(solution)/shard_map/project/pallas_call | solution.py:21
  28.9 0.6 collective-permute-start.10
  29.4 1.0 %project.3 = (f32[128,1280]{1,0:T(8,128)S(1)}, bf16[128,1280]{1,0:T(8,128)(2,1)S(1)}) custom-call(bf16[256,512]{1,0:T(8,128)(2,1)S(1)} %get-tuple-element.43.own, bf16[256,512]{1,0:T(8,128)(2,1)S(1)} %collective-permute-done.8.other, bf16[1024,2560]{1,0:T(8,128)(2,1)S(1)} %get-tuple-element.44.matrix), custom_call_target="tpu_custom_call" | custom-call | flops 671088640 | bytes 6750208 | tf_op jit(solution)/shard_map/project/pallas_call | solution.py:21
  30.4 1.7 %collective-permute-start.9 = (bf16[128,1280]{1,0:T(8,128)(2,1)S(1)}, bf16[128,1280]{1,0:T(8,128)(2,1)S(1)}, u32[]{:S(2)}, u32[]{:S(2)}) collective-permute-start(bf16[128,1280]{1,0:T(8,128)(2,1)S(1)} %get-tuple-element.48), channel_id=1, source_target_pairs={{0,2},{2,0},{4,6},{6,4},{8,10},{10,8},{12,14},{14,12},{1,3},{3,1},... | collective-permute-start | bytes 983048 | tf_op jit(solution)/shard_map/ppermute | solution.py:231
  32.2 8.3 %collective-permute-done.7.far = bf16[256,512]{1,0:T(8,128)(2,1)S(1)} collective-permute-done((bf16[256,512]{1,0:T(8,128)(2,1)S(1)}, bf16[256,512]{1,0:T(8,128)(2,1)S(1)}, u32[]{:S(2)}, u32[]{:S(2)}) %collective-permute-start.7) | collective-permute-done | bytes 262176 | tf_op jit(solution)/shard_map/ppermute | solution.py:231
  40.4 2.0 %attention.1 = (f32[64,2048]{1,0:T(8,128)}, f32[8,64]{1,0:T(8,128)S(1)}) custom-call(bf16[64,2048]{1,0:T(8,128)(2,1)S(1)} %get-tuple-element.32.queries, bf16[256,512]{1,0:T(8,128)(2,1)S(1)} %get-tuple-element.42.near, bf16[256,512]{1,0:T(8,128)(2,1)S(1)} %collective-permute-done.7.far, bf16[128,1280]{1,0:T(8,128)(2,1)S(1)} %get-tuple-element.45.after), custom_call_target="tpu_custom_call" | custom-call | flops 8053063680 | bytes 1640448 | tf_op jit(solution)/shard_map/attention/pallas_call | solution.py:21
  42.4 1.8 %collective-permute-done.10.received = bf16[128,1280]{1,0:T(8,128)(2,1)S(1)} collective-permute-done((bf16[128,1280]{1,0:T(8,128)(2,1)S(1)}, bf16[128,1280]{1,0:T(8,128)(2,1)S(1)}, u32[]{:S(2)}, u32[]{:S(2)}) %collective-permute-start.10) | collective-permute-done | bytes 327712 | tf_op jit(solution)/shard_map/ppermute | solution.py:231
  44.2 0.1 hop_sum.3
  44.3 2.2 %collective-permute-start.12 = (bf16[64,1280]{1,0:T(8,128)(2,1)S(1)}, bf16[64,1280]{1,0:T(8,128)(2,1)S(1)}, u32[]{:S(2)}, u32[]{:S(2)}) collective-permute-start(bf16[64,1280]{1,0:T(8,128)(2,1)S(1)} %get-tuple-element.54), channel_id=1, source_target_pairs={{0,2},{2,0},{4,6},{6,4},{8,10},{10,8},{12,14},{14,12},{1,3},{3,1},... | collective-permute-start | bytes 491528 | tf_op jit(solution)/shard_map/ppermute | solution.py:231
  46.5 0.1 hop_sum.2
  46.6 0.1 collective-permute-start.11
  46.7 2.0 %collective-permute-start.14 = (f32[2,64]{1,0:T(2,128)S(1)}, f32[2,64]{1,0:T(2,128)S(1)}, u32[]{:S(2)}, u32[]{:S(2)}) collective-permute-start(f32[2,64]{1,0:T(2,128)S(1)} %get-tuple-element.59), channel_id=1, source_target_pairs={{0,4},{2,6},{4,0},{6,2},{8,12},{10,14},{12,8},{14,10},{1,5},{3,7},... | collective-permute-start | bytes 1544 | tf_op jit(solution)/shard_map/ppermute | solution.py:231
  48.7 0.0 collective-permute-start.15
  48.7 1.5 %collective-permute-start.16 = (f32[2,64]{1,0:T(2,128)S(1)}, f32[2,64]{1,0:T(2,128)S(1)}, u32[]{:S(2)}, u32[]{:S(2)}) collective-permute-start(f32[2,64]{1,0:T(2,128)S(1)} %get-tuple-element.57), channel_id=1, source_target_pairs={{0,6},{2,4},{4,2},{6,0},{8,14},{10,12},{12,10},{14,8},{1,7},{3,5},... | collective-permute-start | bytes 1544 | tf_op jit(solution)/shard_map/ppermute | solution.py:231
  50.2 0.0 collective-permute-done.12.refs_3_
  50.2 1.7 %collective-permute-done.11.refs_2_ = bf16[64,1280]{1,0:T(8,128)(2,1)S(1)} collective-permute-done((bf16[64,1280]{1,0:T(8,128)(2,1)S(1)}, bf16[64,1280]{1,0:T(8,128)(2,1)S(1)}, u32[]{:S(2)}, u32[]{:S(2)}) %collective-permute-start.11) | collective-permute-done | bytes 163872 | tf_op jit(solution)/shard_map/ppermute | solution.py:231
  52.0 0.1 hop_sum_both.1
  52.0 0.1 collective-permute-start.13
  52.1 0.0 collective-permute-done.14.refs_1_
  52.1 0.1 collective-permute-done.15.refs_2_
  52.2 0.9 %collective-permute-done.16.refs_3_ = f32[2,64]{1,0:T(2,128)S(1)} collective-permute-done((f32[2,64]{1,0:T(2,128)S(1)}, f32[2,64]{1,0:T(2,128)S(1)}, u32[]{:S(2)}, u32[]{:S(2)}) %collective-permute-start.16) | collective-permute-done | bytes 544 | tf_op jit(solution)/shard_map/ppermute | solution.py:231
  53.2 2.0 %collective-permute-start.17 = (f32[1,64]{1,0:T(1,128)S(1)}, f32[1,64]{1,0:T(1,128)S(1)}, u32[]{:S(2)}, u32[]{:S(2)}) collective-permute-start(f32[1,64]{1,0:T(1,128)S(1)} %get-tuple-element.61), channel_id=1, source_target_pairs={{0,8},{2,10},{4,12},{6,14},{8,0},{10,2},{12,4},{14,6},{1,9},{3,11}... | collective-permute-start | bytes 776 | tf_op jit(solution)/shard_map/ppermute | solution.py:231
  55.1 1.1 %collective-permute-start.19 = (f32[1,64]{1,0:T(1,128)S(1)}, f32[1,64]{1,0:T(1,128)S(1)}, u32[]{:S(2)}, u32[]{:S(2)}) collective-permute-start(f32[1,64]{1,0:T(1,128)S(1)} %get-tuple-element.61), channel_id=1, source_target_pairs={{0,9},{1,8},{2,11},{3,10},{4,13},{5,12},{6,15},{7,14},{8,1},{9,0},... | collective-permute-start | bytes 776 | tf_op jit(solution)/shard_map/ppermute | solution.py:234
  56.3 4.3 %collective-permute-done.13.received = bf16[32,2560]{1,0:T(8,128)(2,1)S(1)} collective-permute-done((bf16[32,2560]{1,0:T(8,128)(2,1)S(1)}, bf16[32,2560]{1,0:T(8,128)(2,1)S(1)}, u32[]{:S(2)}, u32[]{:S(2)}) %collective-permute-start.13) | collective-permute-done | bytes 163872 | tf_op jit(solution)/shard_map/ppermute | solution.py:231
  60.6 0.8 %finish.1.after = f32[32,2560]{1,0:T(8,128)} custom-call(f32[1,2560]{1,0:T(1,128)S(1)} %reshape.20.bias, f32[32,2560]{1,0:T(8,128)S(1)} %get-tuple-element.55.kept.after, bf16[32,2560]{1,0:T(8,128)(2,1)S(1)} %collective-permute-done.13.received), custom_call_target="tpu_custom_call" | custom-call | flops 655360 | bytes 829440 | tf_op jit(solution)/shard_map/finish/pallas_call | solution.py:21
  61.3 0.0 collective-permute-done.17.refs_1_
  61.3 0.0 collective-permute-done.18.refs_2_
  61.3 0.5 column_sum.3
  (10 shorter events, 0.0 us)
Async XLA Ops:
  2.4 8.9 %collective-permute-start.2 = (bf16[64,1024]{1,0:T(8,128)(2,1)S(1)}, bf16[64,1024]{1,0:T(8,128)(2,1)S(1)}, u32[]{:S(2)}, u32[]{:S(2)}) collective-permute-start(bf16[64,1024]{1,0:T(8,128)(2,1)S(1)} %get-tuple-element.35), channel_id=1, source_target_pairs={{0,2},{2,0},{4,6},{6,4},{8,10},{10,8},{12,14},{14,12},{1,3},{3,1},... | collective-permute-start | bytes 393224 | tf_op jit(solution)/shard_map/ppermute | solution.py:231
  5.4 7.8 %collective-permute-start.3 = (bf16[64,1024]{1,0:T(8,128)(2,1)S(1)}, bf16[64,1024]{1,0:T(8,128)(2,1)S(1)}, u32[]{:S(2)}, u32[]{:S(2)}) collective-permute-start(bf16[64,1024]{1,0:T(8,128)(2,1)S(1)} %get-tuple-element.36), channel_id=1, source_target_pairs={{0,4},{2,6},{4,0},{6,2},{8,12},{10,14},{12,8},{14,10},{1,5},{3,7},... | collective-permute-start | bytes 393224 | tf_op jit(solution)/shard_map/ppermute | solution.py:231
  7.0 8.1 %collective-permute-start.4 = (bf16[64,1024]{1,0:T(8,128)(2,1)S(1)}, bf16[64,1024]{1,0:T(8,128)(2,1)S(1)}, u32[]{:S(2)}, u32[]{:S(2)}) collective-permute-start(bf16[64,1024]{1,0:T(8,128)(2,1)S(1)} %get-tuple-element.37), channel_id=1, source_target_pairs={{0,6},{2,4},{4,2},{6,0},{8,14},{10,12},{12,10},{14,8},{1,7},{3,5},... | collective-permute-start | bytes 393224 | tf_op jit(solution)/shard_map/ppermute | solution.py:231
  7.0 13.7 %collective-permute-start = (bf16[64,512]{1,0:T(8,128)(2,1)S(1)}, bf16[64,512]{1,0:T(8,128)(2,1)S(1)}, u32[]{:S(2)}, u32[]{:S(2)}) collective-permute-start(bf16[64,512]{1,0:T(8,128)(2,1)S(1)} %get-tuple-element.30), channel_id=1, source_target_pairs={{0,8},{2,10},{4,12},{6,14},{8,0},{10,2},{12,4},{14,6},{1,9},{3,11}... | collective-permute-start | bytes 196616 | tf_op jit(solution)/shard_map/ppermute | solution.py:231
  10.0 10.7 %collective-permute-start.1 = (bf16[64,512]{1,0:T(8,128)(2,1)S(1)}, bf16[64,512]{1,0:T(8,128)(2,1)S(1)}, u32[]{:S(2)}, u32[]{:S(2)}) collective-permute-start(bf16[64,512]{1,0:T(8,128)(2,1)S(1)} %get-tuple-element.31), channel_id=1, source_target_pairs={{0,10},{2,8},{4,14},{6,12},{8,2},{10,0},{12,6},{14,4},{1,11},{3,9}... | collective-permute-start | bytes 196616 | tf_op jit(solution)/shard_map/ppermute | solution.py:231
  15.1 8.1 %collective-permute-start.5 = (bf16[64,512]{1,0:T(8,128)(2,1)S(1)}, bf16[64,512]{1,0:T(8,128)(2,1)S(1)}, u32[]{:S(2)}, u32[]{:S(2)}) collective-permute-start(bf16[64,512]{1,0:T(8,128)(2,1)S(1)} %get-tuple-element.40), channel_id=1, source_target_pairs={{0,12},{2,14},{4,8},{6,10},{8,4},{10,6},{12,0},{14,2},{1,13},{3,15... | collective-permute-start | bytes 196616 | tf_op jit(solution)/shard_map/ppermute | solution.py:231
  19.0 7.0 %collective-permute-start.6 = (bf16[64,512]{1,0:T(8,128)(2,1)S(1)}, bf16[64,512]{1,0:T(8,128)(2,1)S(1)}, u32[]{:S(2)}, u32[]{:S(2)}) collective-permute-start(bf16[64,512]{1,0:T(8,128)(2,1)S(1)} %get-tuple-element.41), channel_id=1, source_target_pairs={{0,14},{2,12},{4,10},{6,8},{8,6},{10,4},{12,2},{14,0},{1,15},{3,13... | collective-permute-start | bytes 196616 | tf_op jit(solution)/shard_map/ppermute | solution.py:231
  26.3 1.6 %collective-permute-start.8 = (bf16[256,512]{1,0:T(8,128)(2,1)S(1)}, bf16[256,512]{1,0:T(8,128)(2,1)S(1)}, u32[]{:S(2)}, u32[]{:S(2)}) collective-permute-start(bf16[256,512]{1,0:T(8,128)(2,1)S(1)} %get-tuple-element.43.own), channel_id=1, source_target_pairs={{0,1},{1,0},{2,3},{3,2},{4,5},{5,4},{6,7},{7,6},{8,9},{9,8},{10,11... | collective-permute-start | bytes 786440 | tf_op jit(solution)/shard_map/ppermute | solution.py:237
  26.3 14.1 %collective-permute-start.7 = (bf16[256,512]{1,0:T(8,128)(2,1)S(1)}, bf16[256,512]{1,0:T(8,128)(2,1)S(1)}, u32[]{:S(2)}, u32[]{:S(2)}) collective-permute-start(bf16[256,512]{1,0:T(8,128)(2,1)S(1)} %get-tuple-element.42.near), channel_id=1, source_target_pairs={{0,8},{2,10},{4,12},{6,14},{8,0},{10,2},{12,4},{14,6},{1,9},{3,11}... | collective-permute-start | bytes 786440 | tf_op jit(solution)/shard_map/ppermute | solution.py:231
  28.9 15.3 %collective-permute-start.10 = (bf16[128,1280]{1,0:T(8,128)(2,1)S(1)}, bf16[128,1280]{1,0:T(8,128)(2,1)S(1)}, u32[]{:S(2)}, u32[]{:S(2)}) collective-permute-start(bf16[128,1280]{1,0:T(8,128)(2,1)S(1)} %get-tuple-element.45.after), channel_id=1, source_target_pairs={{0,4},{2,6},{4,0},{6,2},{8,12},{10,14},{12,8},{14,10},{1,5},{3,7},... | collective-permute-start | bytes 983048 | tf_op jit(solution)/shard_map/ppermute | solution.py:231
  30.4 16.1 %collective-permute-start.9 = (bf16[128,1280]{1,0:T(8,128)(2,1)S(1)}, bf16[128,1280]{1,0:T(8,128)(2,1)S(1)}, u32[]{:S(2)}, u32[]{:S(2)}) collective-permute-start(bf16[128,1280]{1,0:T(8,128)(2,1)S(1)} %get-tuple-element.48), channel_id=1, source_target_pairs={{0,2},{2,0},{4,6},{6,4},{8,10},{10,8},{12,14},{14,12},{1,3},{3,1},... | collective-permute-start | bytes 983048 | tf_op jit(solution)/shard_map/ppermute | solution.py:231
  40.4 9.8 %copy-start = (f32[2560]{0:T(1024)S(1)}, f32[2560]{0:T(1024)}, u32[]{:S(2)}) copy-start(f32[2560]{0:T(1024)} %param.17) | copy-start | bytes 30724
  44.3 6.0 %collective-permute-start.12 = (bf16[64,1280]{1,0:T(8,128)(2,1)S(1)}, bf16[64,1280]{1,0:T(8,128)(2,1)S(1)}, u32[]{:S(2)}, u32[]{:S(2)}) collective-permute-start(bf16[64,1280]{1,0:T(8,128)(2,1)S(1)} %get-tuple-element.54), channel_id=1, source_target_pairs={{0,2},{2,0},{4,6},{6,4},{8,10},{10,8},{12,14},{14,12},{1,3},{3,1},... | collective-permute-start | bytes 491528 | tf_op jit(solution)/shard_map/ppermute | solution.py:231
  46.6 5.4 %collective-permute-start.11 = (bf16[64,1280]{1,0:T(8,128)(2,1)S(1)}, bf16[64,1280]{1,0:T(8,128)(2,1)S(1)}, u32[]{:S(2)}, u32[]{:S(2)}) collective-permute-start(bf16[64,1280]{1,0:T(8,128)(2,1)S(1)} %get-tuple-element.53), channel_id=1, source_target_pairs={{0,4},{2,6},{4,0},{6,2},{8,12},{10,14},{12,8},{14,10},{1,5},{3,7},... | collective-permute-start | bytes 491528 | tf_op jit(solution)/shard_map/ppermute | solution.py:231
  46.7 5.5 %collective-permute-start.14 = (f32[2,64]{1,0:T(2,128)S(1)}, f32[2,64]{1,0:T(2,128)S(1)}, u32[]{:S(2)}, u32[]{:S(2)}) collective-permute-start(f32[2,64]{1,0:T(2,128)S(1)} %get-tuple-element.59), channel_id=1, source_target_pairs={{0,4},{2,6},{4,0},{6,2},{8,12},{10,14},{12,8},{14,10},{1,5},{3,7},... | collective-permute-start | bytes 1544 | tf_op jit(solution)/shard_map/ppermute | solution.py:231
  48.7 3.6 %collective-permute-start.15 = (f32[2,64]{1,0:T(2,128)S(1)}, f32[2,64]{1,0:T(2,128)S(1)}, u32[]{:S(2)}, u32[]{:S(2)}) collective-permute-start(f32[2,64]{1,0:T(2,128)S(1)} %get-tuple-element.58), channel_id=1, source_target_pairs={{0,2},{2,0},{4,6},{6,4},{8,10},{10,8},{12,14},{14,12},{1,3},{3,1},... | collective-permute-start | bytes 1544 | tf_op jit(solution)/shard_map/ppermute | solution.py:231
  48.7 4.5 %collective-permute-start.16 = (f32[2,64]{1,0:T(2,128)S(1)}, f32[2,64]{1,0:T(2,128)S(1)}, u32[]{:S(2)}, u32[]{:S(2)}) collective-permute-start(f32[2,64]{1,0:T(2,128)S(1)} %get-tuple-element.57), channel_id=1, source_target_pairs={{0,6},{2,4},{4,2},{6,0},{8,14},{10,12},{12,10},{14,8},{1,7},{3,5},... | collective-permute-start | bytes 1544 | tf_op jit(solution)/shard_map/ppermute | solution.py:231
  52.0 8.5 %collective-permute-start.13 = (bf16[32,2560]{1,0:T(8,128)(2,1)S(1)}, bf16[32,2560]{1,0:T(8,128)(2,1)S(1)}, u32[]{:S(2)}, u32[]{:S(2)}) collective-permute-start(bf16[32,2560]{1,0:T(8,128)(2,1)S(1)} %get-tuple-element.56), channel_id=1, source_target_pairs={{0,8},{2,10},{4,12},{6,14},{8,0},{10,2},{12,4},{14,6},{1,9},{3,11}... | collective-permute-start | bytes 491528 | tf_op jit(solution)/shard_map/ppermute | solution.py:231
  53.2 8.2 %collective-permute-start.17 = (f32[1,64]{1,0:T(1,128)S(1)}, f32[1,64]{1,0:T(1,128)S(1)}, u32[]{:S(2)}, u32[]{:S(2)}) collective-permute-start(f32[1,64]{1,0:T(1,128)S(1)} %get-tuple-element.61), channel_id=1, source_target_pairs={{0,8},{2,10},{4,12},{6,14},{8,0},{10,2},{12,4},{14,6},{1,9},{3,11}... | collective-permute-start | bytes 776 | tf_op jit(solution)/shard_map/ppermute | solution.py:231
  55.1 6.2 %collective-permute-start.18 = (f32[1,64]{1,0:T(1,128)S(1)}, f32[1,64]{1,0:T(1,128)S(1)}, u32[]{:S(2)}, u32[]{:S(2)}) collective-permute-start(f32[1,64]{1,0:T(1,128)S(1)} %get-tuple-element.62.refs_0_), channel_id=1, source_target_pairs={{0,1},{1,0},{2,3},{3,2},{4,5},{5,4},{6,7},{7,6},{8,9},{9,8},{10,11... | collective-permute-start | bytes 776 | tf_op jit(solution)/shard_map/ppermute | solution.py:237
  55.1 6.2 %collective-permute-start.19 = (f32[1,64]{1,0:T(1,128)S(1)}, f32[1,64]{1,0:T(1,128)S(1)}, u32[]{:S(2)}, u32[]{:S(2)}) collective-permute-start(f32[1,64]{1,0:T(1,128)S(1)} %get-tuple-element.61), channel_id=1, source_target_pairs={{0,9},{1,8},{2,11},{3,10},{4,13},{5,12},{6,15},{7,14},{8,1},{9,0},... | collective-permute-start | bytes 776 | tf_op jit(solution)/shard_map/ppermute | solution.py:234

commit v11 on v10

--- a/solution.py
+++ b/solution.py
@@ -68,11 +68,17 @@
         start = pl.multiple_of(lax.bitwise_xor(s, k) * block + t * half, half)
         columns = pl.ds(start, half)
         normed = (hidden[:, columns].astype(jnp.float32) * scale * gain[:, columns]).astype(jnp.bfloat16)
-        if k < n // 2:
+        if outs[k].shape[1] > half:
             outs[k][:, half:] = pair[...]
         outs[k][:, :half] = lax.dot_general(
             selector, normed, (((0,), (0,)), ((), ())), preferred_element_type=jnp.float32
         ).astype(jnp.bfloat16)
+
+
+def gather_kernel(near, far, after, out):
+    rows = near.shape[0] + far.shape[0] - out.shape[0]
+    out[: near.shape[0] - rows] = near[rows:]
+    out[near.shape[0] - rows :] = far[...]
 
 
 def relay_kernel(count, *refs):
@@ -109,10 +115,10 @@
 
 
 def compact_kernel(n, target, *refs):
-    blocks, (out, held) = refs[:n], refs[n:]
+    blocks, (out, even) = refs[:n], refs[n:]
     rows, half = blocks[0].shape[0], out.shape[1]
-    for k in range(n // 2):
-        held[k * rows : (k + 1) * rows] = blocks[k][:, half:]
+    for i in range(n // 4):
+        even[i * rows : (i + 1) * rows] = blocks[2 * i][:, half:]
     lines = out.shape[0] // n
     s = lax.axis_index("seq")
     received = jnp.concatenate([b[:, :half] for b in blocks], axis=0)
@@ -175,24 +181,28 @@
     out[...] = total * scale
 
 
-def attention_kernel(n, kv_heads, masks, queries, near, far, after, context, columns):
+def attention_kernel(n, kv_heads, masks, queries, pair, near, far, odd, context, columns):
     rows = queries.shape[0]
     group = queries.shape[1] // (HEAD_SIZE * kv_heads)
     s = lax.axis_index("seq")
     keys_total = n * rows
     column = lax.broadcasted_iota(jnp.int32, (1, keys_total), 1)
     position = column
-    for k in range(n):
-        inside = (column >= k * rows) & (column < (k + 1) * rows)
-        position = jnp.where(inside, column + (lax.bitwise_xor(s, k) - s - k) * rows, position)
+    order = list(range(0, n, 2)) + list(range(1, n, 2))
+    first = pair.shape[1] - 2 * kv_heads * HEAD_SIZE
+    for at, k in enumerate(order):
+        inside = (column >= at * rows) & (column < (at + 1) * rows)
+        position = jnp.where(inside, column + (lax.bitwise_xor(s, k) - s - at) * rows, position)
     row = lax.rem(lax.broadcasted_iota(jnp.int32, (group * rows, keys_total), 0), rows)
     allowed = position <= row
     sums = jnp.zeros((1, keys_total), jnp.float32)
     for g in range(kv_heads):
         key_lanes = slice(g * HEAD_SIZE, (g + 1) * HEAD_SIZE)
         value_lanes = slice((kv_heads + g) * HEAD_SIZE, (kv_heads + g + 1) * HEAD_SIZE)
-        key = jnp.concatenate([near[:, key_lanes], far[:, key_lanes]], axis=0)
-        value = jnp.concatenate([near[:, value_lanes], far[:, value_lanes]], axis=0)
+        key, value = [
+            jnp.concatenate([near[:, x], far[:, x], pair[:, first + x.start : first + x.stop], odd[:, x]], axis=0)
+            for x in (key_lanes, value_lanes)
+        ]
         heads = range(g * group, (g + 1) * group)
         stacked = jnp.concatenate([queries[:, h * HEAD_SIZE : (h + 1) * HEAD_SIZE] for h in heads], axis=0)
         scores = lax.dot_general(
@@ -206,7 +216,8 @@
             context[:, h * HEAD_SIZE : (h + 1) * HEAD_SIZE] = mixed[i * rows : (i + 1) * rows]
         sums += jnp.sum(weights * inverse, axis=0, keepdims=True)
     for i, k in enumerate(halving_order(n, masks)):
-        columns[i : i + 1, :] = sums[:, k * rows : (k + 1) * rows]
+        at = order.index(k)
+        columns[i : i + 1, :] = sums[:, at * rows : (at + 1) * rows]
 
 
 def finish_kernel(bias, kept, received, out):
@@ -240,7 +251,7 @@
         functools.partial(norm_select_kernel, n),
         "norm_select",
         (hidden, norm_gain.reshape(1, model), retained_lists.reshape(1, rows), keys, values),
-        [shape((rows, half + 2 * keys.shape[1]), bf16)] * (n // 2) + [shape((rows, half), bf16)] * (n // 2),
+        [shape((rows, half + (2 * keys.shape[1] if k == 1 or k in range(0, n // 2, 2) else 0)), bf16) for k in range(n)],
         4 * rows * model,
         limit=16,
         in_specs=[ANY] * 5,
@@ -252,10 +263,10 @@
     relayed = call(
         functools.partial(relay_kernel, len(last)),
         "relay",
-        (*[chosen[k] for k in last], *received[1 : n // 2]),
+        (*[chosen[k] for k in last], received[1], received[3]),
         [shape((rows, half), bf16)] * len(last),
         0,
-        in_specs=[VMEM] * len(last) + [ANY] * (n // 2 - 1),
+        in_specs=[VMEM] * len(last) + [ANY] * 2,
     )
     received += [trade(x, k) for k, x in zip(last, relayed)]
     matrix, queries, target = call(
@@ -268,11 +279,11 @@
         remote=3,
         scratch=[pltpu.SMEM(counts.shape, i32), dma((3,))],
     )
-    own, held = call(
+    own, even = call(
         functools.partial(compact_kernel, n),
         "compact",
         (target, *received),
-        [shape((survivors, half), bf16), shape((n // 2 * rows, 2 * keys.shape[1]), bf16)],
+        [shape((survivors, half), bf16), shape((n // 4 * rows, 2 * keys.shape[1]), bf16)],
         2 * survivors * n * rows * half,
     )
     other = swap(own)
@@ -288,14 +299,22 @@
         )
         for c in range(2)
     ]
+    far = trade(even, n // 2)
+    (gathered,) = call(
+        gather_kernel,
+        "gather",
+        (even, far, products[0][1]),
+        [shape((n // 2 * rows - rows, even.shape[1]), bf16)],
+        1500 * affine_matrix.size,
+        in_specs=[VMEM] * 2 + [ANY],
+    )
     context, columns = call(
         functools.partial(attention_kernel, n, kv_heads, masks[0]),
         "attention",
-        (queries, held, trade(held, n // 2), products[1][1]),
+        (queries, received[1], even, far, trade(gathered, 1)),
         [shape(queries.shape, f32), shape((n, rows), f32)],
-        120 * rows * n * rows * queries.shape[1],
+        4 * rows * n * rows * queries.shape[1],
         limit=32,
-        in_specs=[VMEM] * 3 + [ANY],
     )
     kept = [product[0] for product in products]
     arrived = [trade(product[1], masks[c][0]) for c, product in enumerate(products)]

time: 62 us -> 60.1 us (0.969)
  waiting for transfers between devices: 25.1 us -> 23.9 us
    ppermute x17 -> x18, starting transfers between devices: 24.7 us -> 23.6 us  [trade(): return lax.ppermute(x, 'seq', [(i, i ^ k) for i in range(n)])]
    ppermute x2, waiting for transfers between devices: 1.45 us -> 0.39 us  [swap(): return lax.ppermute(x, 'ten', [(0, 1), (1, 0)])]
    ppermute x17 -> x18, waiting for transfers between devices: 23.6 us -> 23.5 us  [trade(): return lax.ppermute(x, 'seq', [(i, i ^ k) for i in range(n)])]
    pallas_call x13 -> x14, Pallas kernels: 10.1 us -> 10 us  [call(): pl.pallas_call(body, out_shape=list(outputs), in_specs=in_specs or [VMEM]...]
  transfers between devices with their start and end apart: 20 -> 21, of which waited for: 10 -> 9; matrix products, arithmetic and copies ran while one was open for 0% -> 0% of each run, Pallas kernels for 12% -> 12%
where the time goes in v11:
time: 60.1 us; the launch traced here: 60 us
  starting transfers between devices  25.3 us (42%)
  waiting for transfers between devices  23.9 us (40%)
  Pallas kernels  10 us (17%)
  between operations  0.76 us (1%)
    ppermute x18, starting transfers between devices, trade(): return lax.ppermute(x, 'seq', [(i, i ^ k) for i in range(n)])  23.6 us
    ppermute x18, waiting for transfers between devices, trade(): return lax.ppermute(x, 'seq', [(i, i ^ k) for i in range(n)])  23.5 us
    pallas_call x14, Pallas kernels, call(): pl.pallas_call(body, out_shape=list(outputs), in_specs=in_specs or [VMEM]...  10 us
    ppermute x1, starting transfers between devices, trade_across(): lax.ppermute(x, ('seq', 'ten'), [(2 * i + t, 2 * (i ^ k) + 1 - t) for i i...  1.6 us
  transfers between devices with their start and end apart: 21, of which 9 were waited for; matrix products, arithmetic and copies ran while one was open for 0% of the time, Pallas kernels for 12%

profile of v11, /device:TPU:0, one launch (start us, length us, event | category | flops | bytes accessed | tf_op | source)
XLA Modules:
  0.0 60.0 jit_solution(6896648894499699144)
XLA Ops:
  0.6 1.7 %norm_select.1 = (bf16[64,1024]{1,0:T(8,128)(2,1)S(1)}, bf16[64,1024]{1,0:T(8,128)(2,1)S(1)}, bf16[64,1024]{1,0:T(8,128)(2,1)S(1)}, bf16[64,512]{1,0:T(8,128)(2,...) custom-call(bf16[64,8192]{1,0:T(8,128)(2,1)} %hidden_in.1, ...), custom_call_target="tpu_custom_call" | custom-call | flops 2097152 | bytes 1868032 | tf_op jit(solution)/shard_map/norm_select/pallas_call | solution.py:21
  2.4 3.0 %collective-permute-start.2 = (bf16[64,1024]{1,0:T(8,128)(2,1)S(1)}, bf16[64,1024]{1,0:T(8,128)(2,1)S(1)}, u32[]{:S(2)}, u32[]{:S(2)}) collective-permute-start(bf16[64,1024]{1,0:T(8,128)(2,1)S(1)} %get-tuple-element.33), channel_id=1, source_target_pairs={{0,2},{2,0},{4,6},{6,4},{8,10},{10,8},{12,14},{14,12},{1,3},{3,1},... | collective-permute-start | bytes 393224 | tf_op jit(solution)/shard_map/ppermute | solution.py:242
  5.4 1.5 %collective-permute-start.4 = (bf16[64,512]{1,0:T(8,128)(2,1)S(1)}, bf16[64,512]{1,0:T(8,128)(2,1)S(1)}, u32[]{:S(2)}, u32[]{:S(2)}) collective-permute-start(bf16[64,512]{1,0:T(8,128)(2,1)S(1)} %get-tuple-element.37), channel_id=1, source_target_pairs={{0,6},{2,4},{4,2},{6,0},{8,14},{10,12},{12,10},{14,8},{1,7},{3,5},... | collective-permute-start | bytes 196616 | tf_op jit(solution)/shard_map/ppermute | solution.py:242
  6.9 2.6 %collective-permute-start = (bf16[64,512]{1,0:T(8,128)(2,1)S(1)}, bf16[64,512]{1,0:T(8,128)(2,1)S(1)}, u32[]{:S(2)}, u32[]{:S(2)}) collective-permute-start(bf16[64,512]{1,0:T(8,128)(2,1)S(1)} %get-tuple-element.30), channel_id=1, source_target_pairs={{0,8},{2,10},{4,12},{6,14},{8,0},{10,2},{12,4},{14,6},{1,9},{3,11}... | collective-permute-start | bytes 196616 | tf_op jit(solution)/shard_map/ppermute | solution.py:242
  9.5 1.3 %collective-permute-start.1 = (bf16[64,512]{1,0:T(8,128)(2,1)S(1)}, bf16[64,512]{1,0:T(8,128)(2,1)S(1)}, u32[]{:S(2)}, u32[]{:S(2)}) collective-permute-start(bf16[64,512]{1,0:T(8,128)(2,1)S(1)} %get-tuple-element.31), channel_id=1, source_target_pairs={{0,10},{2,8},{4,14},{6,12},{8,2},{10,0},{12,6},{14,4},{1,11},{3,9}... | collective-permute-start | bytes 196616 | tf_op jit(solution)/shard_map/ppermute | solution.py:242
  10.8 0.4 collective-permute-start.3
  11.3 0.0 collective-permute-done.4.refs_3_
  11.3 0.0 collective-permute-done.2.refs_2_.refs_1_.pair
  11.3 4.2 %collective-permute-start.5 = (bf16[64,512]{1,0:T(8,128)(2,1)S(1)}, bf16[64,512]{1,0:T(8,128)(2,1)S(1)}, u32[]{:S(2)}, u32[]{:S(2)}) collective-permute-start(bf16[64,512]{1,0:T(8,128)(2,1)S(1)} %get-tuple-element.40), channel_id=1, source_target_pairs={{0,12},{2,14},{4,8},{6,10},{8,4},{10,6},{12,0},{14,2},{1,13},{3,15... | collective-permute-start | bytes 196616 | tf_op jit(solution)/shard_map/ppermute | solution.py:242
  15.5 0.0 collective-permute-start.6
  15.5 2.2 %collective-permute-done.1.refs_1_.refs_5_ = bf16[64,512]{1,0:T(8,128)(2,1)S(1)} collective-permute-done((bf16[64,512]{1,0:T(8,128)(2,1)S(1)}, bf16[64,512]{1,0:T(8,128)(2,1)S(1)}, u32[]{:S(2)}, u32[]{:S(2)}) %collective-permute-start.1) | collective-permute-done | bytes 65568 | tf_op jit(solution)/shard_map/ppermute | solution.py:242
  17.7 2.5 %stage.1 = (bf16[1024,2560]{1,0:T(8,128)(2,1)S(1)}, bf16[64,2048]{1,0:T(8,128)(2,1)S(1)}, s32[1,512]{1,0:T(1,128)S(1)}) custom-call(s32[8]{0:T(128)} %counts_in.1, bf16[1024,2560]{1,0:T(8,128)(2,1)} %matrix_in.1, bf16[64,2048]{1,0:T(8,128)(2,1)} %queries_in.1, bf16[64,512]{1,0:T(8,128)(2,1)S(1)} %collective-permute-done.refs_0_.refs_4_, ...), custom_call_target="tpu_custom_call" | custom-call | flops 3932160000 | bytes 11143200 | tf_op jit(solution)/shard_map/stage/pallas_call | solution.py:21
  20.2 0.0 collective-permute-done.5.refs_6_
  20.3 2.2 %collective-permute-done.6.refs_7_ = bf16[64,512]{1,0:T(8,128)(2,1)S(1)} collective-permute-done((bf16[64,512]{1,0:T(8,128)(2,1)S(1)}, bf16[64,512]{1,0:T(8,128)(2,1)S(1)}, u32[]{:S(2)}, u32[]{:S(2)}) %collective-permute-start.6) | collective-permute-done | bytes 65568 | tf_op jit(solution)/shard_map/ppermute | solution.py:242
  22.4 0.3 compact.1
  22.7 0.1 collective-permute-start.8
  22.8 1.1 %collective-permute-start.7 = (bf16[128,512]{1,0:T(8,128)(2,1)S(1)}, bf16[128,512]{1,0:T(8,128)(2,1)S(1)}, u32[]{:S(2)}, u32[]{:S(2)}) collective-permute-start(bf16[128,512]{1,0:T(8,128)(2,1)S(1)} %get-tuple-element.42.near), channel_id=1, source_target_pairs={{0,8},{2,10},{4,12},{6,14},{8,0},{10,2},{12,4},{14,6},{1,9},{3,11}... | collective-permute-start | bytes 393224 | tf_op jit(solution)/shard_map/ppermute | solution.py:242
  23.9 0.4 collective-permute-done.8.other
  24.3 1.0 %project.3 = (f32[128,1280]{1,0:T(8,128)S(1)}, bf16[128,1280]{1,0:T(8,128)(2,1)S(1)}) custom-call(bf16[256,512]{1,0:T(8,128)(2,1)S(1)} %get-tuple-element.43.own, bf16[256,512]{1,0:T(8,128)(2,1)S(1)} %collective-permute-done.8.other, bf16[1024,2560]{1,0:T(8,128)(2,1)S(1)} %get-tuple-element.44.matrix), custom_call_target="tpu_custom_call" | custom-call | flops 671088640 | bytes 6750208 | tf_op jit(solution)/shard_map/project/pallas_call | solution.py:21
  25.3 2.1 %collective-permute-start.11 = (bf16[128,1280]{1,0:T(8,128)(2,1)S(1)}, bf16[128,1280]{1,0:T(8,128)(2,1)S(1)}, u32[]{:S(2)}, u32[]{:S(2)}) collective-permute-start(bf16[128,1280]{1,0:T(8,128)(2,1)S(1)} %get-tuple-element.51.after), channel_id=1, source_target_pairs={{0,4},{2,6},{4,0},{6,2},{8,12},{10,14},{12,8},{14,10},{1,5},{3,7},... | collective-permute-start | bytes 983048 | tf_op jit(solution)/shard_map/ppermute | solution.py:242
  27.4 1.0 %project.2 = (f32[128,1280]{1,0:T(8,128)S(1)}, bf16[128,1280]{1,0:T(8,128)(2,1)S(1)}) custom-call(bf16[256,512]{1,0:T(8,128)(2,1)S(1)} %get-tuple-element.43.own, bf16[256,512]{1,0:T(8,128)(2,1)S(1)} %collective-permute-done.8.other, bf16[1024,2560]{1,0:T(8,128)(2,1)S(1)} %get-tuple-element.44.matrix), custom_call_target="tpu_custom_call" | custom-call | flops 671088640 | bytes 6750208 | tf_op jit(solution)/shard_map/project/pallas_call | solution.py:21
  28.4 0.0 copy-start
  28.4 0.1 collective-permute-start.10
  28.5 4.1 %collective-permute-done.7.far = bf16[128,512]{1,0:T(8,128)(2,1)S(1)} collective-permute-done((bf16[128,512]{1,0:T(8,128)(2,1)S(1)}, bf16[128,512]{1,0:T(8,128)(2,1)S(1)}, u32[]{:S(2)}, u32[]{:S(2)}) %collective-permute-start.7) | collective-permute-done | bytes 131104 | tf_op jit(solution)/shard_map/ppermute | solution.py:242
  32.6 0.1 collective-permute-start.9
  32.6 9.6 %collective-permute-done.9.odd = bf16[192,512]{1,0:T(8,128)(2,1)S(1)} collective-permute-done((bf16[192,512]{1,0:T(8,128)(2,1)S(1)}, bf16[192,512]{1,0:T(8,128)(2,1)S(1)}, u32[]{:S(2)}, u32[]{:S(2)}) %collective-permute-start.9) | collective-permute-done | bytes 196640 | tf_op jit(solution)/shard_map/ppermute | solution.py:242
  42.2 2.0 %attention.1 = (f32[64,2048]{1,0:T(8,128)}, f32[8,64]{1,0:T(8,128)S(1)}) custom-call(bf16[64,2048]{1,0:T(8,128)(2,1)S(1)} %get-tuple-element.32.queries, bf16[64,1024]{1,0:T(8,128)(2,1)S(1)} %collective-permute-done.2.refs_2_.refs_1_.pair, bf16[128,512]{1,0:T(8,128)(2,1)S(1)} %get-tuple-element.42.near, bf16[128,512]{1,0:T(8,128)(2,1)S(1)} %collective-permute-done.7.far, ...), custom_call_target="tpu_custom_call" | custom-call | flops 268435456 | bytes 1378304 | tf_op jit(solution)/shard_map/attention/pallas_call | solution.py:21
  44.2 0.0 collective-permute-done.11.received
  44.2 0.1 hop_sum.3
  44.3 0.3 collective-permute-start.13
  44.6 0.0 collective-permute-done.10.received
  44.6 0.1 hop_sum.2
  44.7 0.4 collective-permute-start.12
  45.0 1.7 %collective-permute-start.15 = (f32[2,64]{1,0:T(2,128)S(1)}, f32[2,64]{1,0:T(2,128)S(1)}, u32[]{:S(2)}, u32[]{:S(2)}) collective-permute-start(f32[2,64]{1,0:T(2,128)S(1)} %get-tuple-element.59), channel_id=1, source_target_pairs={{0,4},{2,6},{4,0},{6,2},{8,12},{10,14},{12,8},{14,10},{1,5},{3,7},... | collective-permute-start | bytes 1544 | tf_op jit(solution)/shard_map/ppermute | solution.py:242
  46.8 1.7 %collective-permute-start.16 = (f32[2,64]{1,0:T(2,128)S(1)}, f32[2,64]{1,0:T(2,128)S(1)}, u32[]{:S(2)}, u32[]{:S(2)}) collective-permute-start(f32[2,64]{1,0:T(2,128)S(1)} %get-tuple-element.58), channel_id=1, source_target_pairs={{0,2},{2,0},{4,6},{6,4},{8,10},{10,8},{12,14},{14,12},{1,3},{3,1},... | collective-permute-start | bytes 1544 | tf_op jit(solution)/shard_map/ppermute | solution.py:242
  48.5 0.0 collective-permute-start.17
  48.6 1.1 %collective-permute-done.13.refs_3_ = bf16[64,1280]{1,0:T(8,128)(2,1)S(1)} collective-permute-done((bf16[64,1280]{1,0:T(8,128)(2,1)S(1)}, bf16[64,1280]{1,0:T(8,128)(2,1)S(1)}, u32[]{:S(2)}, u32[]{:S(2)}) %collective-permute-start.13) | collective-permute-done | bytes 163872 | tf_op jit(solution)/shard_map/ppermute | solution.py:242
  49.6 0.4 collective-permute-done.12.refs_2_
  50.1 0.1 hop_sum_both.1
  50.1 1.5 %collective-permute-start.14 = (bf16[32,2560]{1,0:T(8,128)(2,1)S(1)}, bf16[32,2560]{1,0:T(8,128)(2,1)S(1)}, u32[]{:S(2)}, u32[]{:S(2)}) collective-permute-start(bf16[32,2560]{1,0:T(8,128)(2,1)S(1)} %get-tuple-element.56), channel_id=1, source_target_pairs={{0,8},{2,10},{4,12},{6,14},{8,0},{10,2},{12,4},{14,6},{1,9},{3,11}... | collective-permute-start | bytes 491528 | tf_op jit(solution)/shard_map/ppermute | solution.py:242
  51.6 1.3 %collective-permute-done.17.refs_3_ = f32[2,64]{1,0:T(2,128)S(1)} collective-permute-done((f32[2,64]{1,0:T(2,128)S(1)}, f32[2,64]{1,0:T(2,128)S(1)}, u32[]{:S(2)}, u32[]{:S(2)}) %collective-permute-start.17) | collective-permute-done | bytes 544 | tf_op jit(solution)/shard_map/ppermute | solution.py:242
  53.0 1.5 %collective-permute-start.18 = (f32[1,64]{1,0:T(1,128)S(1)}, f32[1,64]{1,0:T(1,128)S(1)}, u32[]{:S(2)}, u32[]{:S(2)}) collective-permute-start(f32[1,64]{1,0:T(1,128)S(1)} %get-tuple-element.61), channel_id=1, source_target_pairs={{0,8},{2,10},{4,12},{6,14},{8,0},{10,2},{12,4},{14,6},{1,9},{3,11}... | collective-permute-start | bytes 776 | tf_op jit(solution)/shard_map/ppermute | solution.py:242
  54.5 1.6 %collective-permute-start.20 = (f32[1,64]{1,0:T(1,128)S(1)}, f32[1,64]{1,0:T(1,128)S(1)}, u32[]{:S(2)}, u32[]{:S(2)}) collective-permute-start(f32[1,64]{1,0:T(1,128)S(1)} %get-tuple-element.61), channel_id=1, source_target_pairs={{0,9},{1,8},{2,11},{3,10},{4,13},{5,12},{6,15},{7,14},{8,1},{9,0},... | collective-permute-start | bytes 776 | tf_op jit(solution)/shard_map/ppermute | solution.py:245
  56.1 2.6 %collective-permute-done.14.received = bf16[32,2560]{1,0:T(8,128)(2,1)S(1)} collective-permute-done((bf16[32,2560]{1,0:T(8,128)(2,1)S(1)}, bf16[32,2560]{1,0:T(8,128)(2,1)S(1)}, u32[]{:S(2)}, u32[]{:S(2)}) %collective-permute-start.14) | collective-permute-done | bytes 163872 | tf_op jit(solution)/shard_map/ppermute | solution.py:242
  58.7 0.8 %finish.1.after = f32[32,2560]{1,0:T(8,128)} custom-call(f32[1,2560]{1,0:T(1,128)S(1)} %reshape.20.bias, f32[32,2560]{1,0:T(8,128)S(1)} %get-tuple-element.55.kept.after, bf16[32,2560]{1,0:T(8,128)(2,1)S(1)} %collective-permute-done.14.received), custom_call_target="tpu_custom_call" | custom-call | flops 655360 | bytes 829440 | tf_op jit(solution)/shard_map/finish/pallas_call | solution.py:21
  59.5 0.0 collective-permute-done.19.refs_2_
  59.5 0.0 collective-permute-done.20.refs_3_
  59.5 0.5 column_sum.3
  (13 shorter events, 0.1 us)
Async XLA Ops:
  2.4 8.9 %collective-permute-start.2 = (bf16[64,1024]{1,0:T(8,128)(2,1)S(1)}, bf16[64,1024]{1,0:T(8,128)(2,1)S(1)}, u32[]{:S(2)}, u32[]{:S(2)}) collective-permute-start(bf16[64,1024]{1,0:T(8,128)(2,1)S(1)} %get-tuple-element.33), channel_id=1, source_target_pairs={{0,2},{2,0},{4,6},{6,4},{8,10},{10,8},{12,14},{14,12},{1,3},{3,1},... | collective-permute-start | bytes 393224 | tf_op jit(solution)/shard_map/ppermute | solution.py:242
  5.4 5.9 %collective-permute-start.4 = (bf16[64,512]{1,0:T(8,128)(2,1)S(1)}, bf16[64,512]{1,0:T(8,128)(2,1)S(1)}, u32[]{:S(2)}, u32[]{:S(2)}) collective-permute-start(bf16[64,512]{1,0:T(8,128)(2,1)S(1)} %get-tuple-element.37), channel_id=1, source_target_pairs={{0,6},{2,4},{4,2},{6,0},{8,14},{10,12},{12,10},{14,8},{1,7},{3,5},... | collective-permute-start | bytes 196616 | tf_op jit(solution)/shard_map/ppermute | solution.py:242
  6.9 8.5 %collective-permute-start = (bf16[64,512]{1,0:T(8,128)(2,1)S(1)}, bf16[64,512]{1,0:T(8,128)(2,1)S(1)}, u32[]{:S(2)}, u32[]{:S(2)}) collective-permute-start(bf16[64,512]{1,0:T(8,128)(2,1)S(1)} %get-tuple-element.30), channel_id=1, source_target_pairs={{0,8},{2,10},{4,12},{6,14},{8,0},{10,2},{12,4},{14,6},{1,9},{3,11}... | collective-permute-start | bytes 196616 | tf_op jit(solution)/shard_map/ppermute | solution.py:242
  9.5 8.2 %collective-permute-start.1 = (bf16[64,512]{1,0:T(8,128)(2,1)S(1)}, bf16[64,512]{1,0:T(8,128)(2,1)S(1)}, u32[]{:S(2)}, u32[]{:S(2)}) collective-permute-start(bf16[64,512]{1,0:T(8,128)(2,1)S(1)} %get-tuple-element.31), channel_id=1, source_target_pairs={{0,10},{2,8},{4,14},{6,12},{8,2},{10,0},{12,6},{14,4},{1,11},{3,9}... | collective-permute-start | bytes 196616 | tf_op jit(solution)/shard_map/ppermute | solution.py:242
  10.8 9.4 %collective-permute-start.3 = (bf16[64,1024]{1,0:T(8,128)(2,1)S(1)}, bf16[64,1024]{1,0:T(8,128)(2,1)S(1)}, u32[]{:S(2)}, u32[]{:S(2)}) collective-permute-start(bf16[64,1024]{1,0:T(8,128)(2,1)S(1)} %get-tuple-element.36), channel_id=1, source_target_pairs={{0,4},{2,6},{4,0},{6,2},{8,12},{10,14},{12,8},{14,10},{1,5},{3,7},... | collective-permute-start | bytes 393224 | tf_op jit(solution)/shard_map/ppermute | solution.py:242
  11.3 9.0 %collective-permute-start.5 = (bf16[64,512]{1,0:T(8,128)(2,1)S(1)}, bf16[64,512]{1,0:T(8,128)(2,1)S(1)}, u32[]{:S(2)}, u32[]{:S(2)}) collective-permute-start(bf16[64,512]{1,0:T(8,128)(2,1)S(1)} %get-tuple-element.40), channel_id=1, source_target_pairs={{0,12},{2,14},{4,8},{6,10},{8,4},{10,6},{12,0},{14,2},{1,13},{3,15... | collective-permute-start | bytes 196616 | tf_op jit(solution)/shard_map/ppermute | solution.py:242
  15.5 7.0 %collective-permute-start.6 = (bf16[64,512]{1,0:T(8,128)(2,1)S(1)}, bf16[64,512]{1,0:T(8,128)(2,1)S(1)}, u32[]{:S(2)}, u32[]{:S(2)}) collective-permute-start(bf16[64,512]{1,0:T(8,128)(2,1)S(1)} %get-tuple-element.41), channel_id=1, source_target_pairs={{0,14},{2,12},{4,10},{6,8},{8,6},{10,4},{12,2},{14,0},{1,15},{3,13... | collective-permute-start | bytes 196616 | tf_op jit(solution)/shard_map/ppermute | solution.py:242
  22.7 1.6 %collective-permute-start.8 = (bf16[256,512]{1,0:T(8,128)(2,1)S(1)}, bf16[256,512]{1,0:T(8,128)(2,1)S(1)}, u32[]{:S(2)}, u32[]{:S(2)}) collective-permute-start(bf16[256,512]{1,0:T(8,128)(2,1)S(1)} %get-tuple-element.43.own), channel_id=1, source_target_pairs={{0,1},{1,0},{2,3},{3,2},{4,5},{5,4},{6,7},{7,6},{8,9},{9,8},{10,11... | collective-permute-start | bytes 786440 | tf_op jit(solution)/shard_map/ppermute | solution.py:248
  22.8 9.7 %collective-permute-start.7 = (bf16[128,512]{1,0:T(8,128)(2,1)S(1)}, bf16[128,512]{1,0:T(8,128)(2,1)S(1)}, u32[]{:S(2)}, u32[]{:S(2)}) collective-permute-start(bf16[128,512]{1,0:T(8,128)(2,1)S(1)} %get-tuple-element.42.near), channel_id=1, source_target_pairs={{0,8},{2,10},{4,12},{6,14},{8,0},{10,2},{12,4},{14,6},{1,9},{3,11}... | collective-permute-start | bytes 393224 | tf_op jit(solution)/shard_map/ppermute | solution.py:242
  25.3 18.9 %collective-permute-start.11 = (bf16[128,1280]{1,0:T(8,128)(2,1)S(1)}, bf16[128,1280]{1,0:T(8,128)(2,1)S(1)}, u32[]{:S(2)}, u32[]{:S(2)}) collective-permute-start(bf16[128,1280]{1,0:T(8,128)(2,1)S(1)} %get-tuple-element.51.after), channel_id=1, source_target_pairs={{0,4},{2,6},{4,0},{6,2},{8,12},{10,14},{12,8},{14,10},{1,5},{3,7},... | collective-permute-start | bytes 983048 | tf_op jit(solution)/shard_map/ppermute | solution.py:242
  28.4 20.1 %copy-start = (f32[2560]{0:T(1024)S(1)}, f32[2560]{0:T(1024)}, u32[]{:S(2)}) copy-start(f32[2560]{0:T(1024)} %param.17) | copy-start | bytes 30724
  28.4 16.2 %collective-permute-start.10 = (bf16[128,1280]{1,0:T(8,128)(2,1)S(1)}, bf16[128,1280]{1,0:T(8,128)(2,1)S(1)}, u32[]{:S(2)}, u32[]{:S(2)}) collective-permute-start(bf16[128,1280]{1,0:T(8,128)(2,1)S(1)} %get-tuple-element.45.after), channel_id=1, source_target_pairs={{0,2},{2,0},{4,6},{6,4},{8,10},{10,8},{12,14},{14,12},{1,3},{3,1},... | collective-permute-start | bytes 983048 | tf_op jit(solution)/shard_map/ppermute | solution.py:242
  32.6 9.6 %collective-permute-start.9 = (bf16[192,512]{1,0:T(8,128)(2,1)S(1)}, bf16[192,512]{1,0:T(8,128)(2,1)S(1)}, u32[]{:S(2)}, u32[]{:S(2)}) collective-permute-start(bf16[192,512]{1,0:T(8,128)(2,1)S(1)} %gather.1), channel_id=1, source_target_pairs={{0,2},{2,0},{4,6},{6,4},{8,10},{10,8},{12,14},{14,12},{1,3},{3,1},... | collective-permute-start | bytes 589832 | tf_op jit(solution)/shard_map/ppermute | solution.py:242
  44.3 5.4 %collective-permute-start.13 = (bf16[64,1280]{1,0:T(8,128)(2,1)S(1)}, bf16[64,1280]{1,0:T(8,128)(2,1)S(1)}, u32[]{:S(2)}, u32[]{:S(2)}) collective-permute-start(bf16[64,1280]{1,0:T(8,128)(2,1)S(1)} %get-tuple-element.54), channel_id=1, source_target_pairs={{0,2},{2,0},{4,6},{6,4},{8,10},{10,8},{12,14},{14,12},{1,3},{3,1},... | collective-permute-start | bytes 491528 | tf_op jit(solution)/shard_map/ppermute | solution.py:242
  44.7 5.4 %collective-permute-start.12 = (bf16[64,1280]{1,0:T(8,128)(2,1)S(1)}, bf16[64,1280]{1,0:T(8,128)(2,1)S(1)}, u32[]{:S(2)}, u32[]{:S(2)}) collective-permute-start(bf16[64,1280]{1,0:T(8,128)(2,1)S(1)} %get-tuple-element.53), channel_id=1, source_target_pairs={{0,4},{2,6},{4,0},{6,2},{8,12},{10,14},{12,8},{14,10},{1,5},{3,7},... | collective-permute-start | bytes 491528 | tf_op jit(solution)/shard_map/ppermute | solution.py:242
  45.0 6.6 %collective-permute-start.15 = (f32[2,64]{1,0:T(2,128)S(1)}, f32[2,64]{1,0:T(2,128)S(1)}, u32[]{:S(2)}, u32[]{:S(2)}) collective-permute-start(f32[2,64]{1,0:T(2,128)S(1)} %get-tuple-element.59), channel_id=1, source_target_pairs={{0,4},{2,6},{4,0},{6,2},{8,12},{10,14},{12,8},{14,10},{1,5},{3,7},... | collective-permute-start | bytes 1544 | tf_op jit(solution)/shard_map/ppermute | solution.py:242
  46.8 4.9 %collective-permute-start.16 = (f32[2,64]{1,0:T(2,128)S(1)}, f32[2,64]{1,0:T(2,128)S(1)}, u32[]{:S(2)}, u32[]{:S(2)}) collective-permute-start(f32[2,64]{1,0:T(2,128)S(1)} %get-tuple-element.58), channel_id=1, source_target_pairs={{0,2},{2,0},{4,6},{6,4},{8,10},{10,8},{12,14},{14,12},{1,3},{3,1},... | collective-permute-start | bytes 1544 | tf_op jit(solution)/shard_map/ppermute | solution.py:242
  48.5 4.5 %collective-permute-start.17 = (f32[2,64]{1,0:T(2,128)S(1)}, f32[2,64]{1,0:T(2,128)S(1)}, u32[]{:S(2)}, u32[]{:S(2)}) collective-permute-start(f32[2,64]{1,0:T(2,128)S(1)} %get-tuple-element.57), channel_id=1, source_target_pairs={{0,6},{2,4},{4,2},{6,0},{8,14},{10,12},{12,10},{14,8},{1,7},{3,5},... | collective-permute-start | bytes 1544 | tf_op jit(solution)/shard_map/ppermute | solution.py:242
  50.1 8.6 %collective-permute-start.14 = (bf16[32,2560]{1,0:T(8,128)(2,1)S(1)}, bf16[32,2560]{1,0:T(8,128)(2,1)S(1)}, u32[]{:S(2)}, u32[]{:S(2)}) collective-permute-start(bf16[32,2560]{1,0:T(8,128)(2,1)S(1)} %get-tuple-element.56), channel_id=1, source_target_pairs={{0,8},{2,10},{4,12},{6,14},{8,0},{10,2},{12,4},{14,6},{1,9},{3,11}... | collective-permute-start | bytes 491528 | tf_op jit(solution)/shard_map/ppermute | solution.py:242
  53.0 6.5 %collective-permute-start.18 = (f32[1,64]{1,0:T(1,128)S(1)}, f32[1,64]{1,0:T(1,128)S(1)}, u32[]{:S(2)}, u32[]{:S(2)}) collective-permute-start(f32[1,64]{1,0:T(1,128)S(1)} %get-tuple-element.61), channel_id=1, source_target_pairs={{0,8},{2,10},{4,12},{6,14},{8,0},{10,2},{12,4},{14,6},{1,9},{3,11}... | collective-permute-start | bytes 776 | tf_op jit(solution)/shard_map/ppermute | solution.py:242
  54.5 5.0 %collective-permute-start.19 = (f32[1,64]{1,0:T(1,128)S(1)}, f32[1,64]{1,0:T(1,128)S(1)}, u32[]{:S(2)}, u32[]{:S(2)}) collective-permute-start(f32[1,64]{1,0:T(1,128)S(1)} %get-tuple-element.62.refs_0_), channel_id=1, source_target_pairs={{0,1},{1,0},{2,3},{3,2},{4,5},{5,4},{6,7},{7,6},{8,9},{9,8},{10,11... | collective-permute-start | bytes 776 | tf_op jit(solution)/shard_map/ppermute | solution.py:248
  54.5 5.0 %collective-permute-start.20 = (f32[1,64]{1,0:T(1,128)S(1)}, f32[1,64]{1,0:T(1,128)S(1)}, u32[]{:S(2)}, u32[]{:S(2)}) collective-permute-start(f32[1,64]{1,0:T(1,128)S(1)} %get-tuple-element.61), channel_id=1, source_target_pairs={{0,9},{1,8},{2,11},{3,10},{4,13},{5,12},{6,15},{7,14},{8,1},{9,0},... | collective-permute-start | bytes 776 | tf_op jit(solution)/shard_map/ppermute | solution.py:245

commit v12 on v11

--- a/solution.py
+++ b/solution.py
@@ -75,10 +75,8 @@
         ).astype(jnp.bfloat16)
 
 
-def gather_kernel(near, far, after, out):
-    rows = near.shape[0] + far.shape[0] - out.shape[0]
-    out[: near.shape[0] - rows] = near[rows:]
-    out[near.shape[0] - rows :] = far[...]
+def pass_kernel(block, after, out):
+    out[...] = block[...]
 
 
 def relay_kernel(count, *refs):
@@ -115,10 +113,11 @@
 
 
 def compact_kernel(n, target, *refs):
-    blocks, (out, even) = refs[:n], refs[n:]
+    blocks, (out, even, odd) = refs[:n], refs[n:]
     rows, half = blocks[0].shape[0], out.shape[1]
     for i in range(n // 4):
         even[i * rows : (i + 1) * rows] = blocks[2 * i][:, half:]
+        odd[i * rows : (i + 1) * rows] = blocks[2 * i + 1][:, half:]
     lines = out.shape[0] // n
     s = lax.axis_index("seq")
     received = jnp.concatenate([b[:, :half] for b in blocks], axis=0)
@@ -133,17 +132,24 @@
     return sorted(range(n), key=lambda k: [k & mask for mask in masks])
 
 
-def project_kernel(first, order, own, other, matrix, near, far):
-    survivors, half = own.shape
+def project_own_kernel(own, matrix, out):
+    half = own.shape[1]
+    mine = pl.ds(pl.multiple_of(lax.axis_index("ten") * half, half), half)
+    tile = out.shape[1] // 4 if out.shape[1] % 512 == 0 else out.shape[1]
+    for j in range(0, out.shape[1], tile):
+        out[:, j : j + tile] = jnp.dot(own[...], matrix[mine, j : j + tile], preferred_element_type=jnp.float32)
+
+
+def project_kernel(first, order, product, other, matrix, near, far):
+    survivors, half = other.shape
     lines = survivors // len(order)
     width = near.shape[1]
     t = lax.axis_index("ten")
-    mine = pl.ds(pl.multiple_of(t * half, half), half)
     others = pl.ds(pl.multiple_of((1 - t) * half, half), half)
     tile = width // 2 if width % 256 == 0 else width
     for j in range(0, width, tile):
         lanes = slice(first + j, first + j + tile)
-        part = jnp.dot(own[...], matrix[mine, lanes], preferred_element_type=jnp.float32)
+        part = product[:, lanes]
         part += jnp.dot(other[...], matrix[others, lanes], preferred_element_type=jnp.float32)
         for i, k in enumerate(order):
             block = part[k * lines : (k + 1) * lines]
@@ -181,7 +187,7 @@
     out[...] = total * scale
 
 
-def attention_kernel(n, kv_heads, masks, queries, pair, near, far, odd, context, columns):
+def attention_kernel(n, kv_heads, masks, queries, even_near, even_far, odd_near, odd_far, context, columns):
     rows = queries.shape[0]
     group = queries.shape[1] // (HEAD_SIZE * kv_heads)
     s = lax.axis_index("seq")
@@ -189,7 +195,6 @@
     column = lax.broadcasted_iota(jnp.int32, (1, keys_total), 1)
     position = column
     order = list(range(0, n, 2)) + list(range(1, n, 2))
-    first = pair.shape[1] - 2 * kv_heads * HEAD_SIZE
     for at, k in enumerate(order):
         inside = (column >= at * rows) & (column < (at + 1) * rows)
         position = jnp.where(inside, column + (lax.bitwise_xor(s, k) - s - at) * rows, position)
@@ -200,7 +205,7 @@
         key_lanes = slice(g * HEAD_SIZE, (g + 1) * HEAD_SIZE)
         value_lanes = slice((kv_heads + g) * HEAD_SIZE, (kv_heads + g + 1) * HEAD_SIZE)
         key, value = [
-            jnp.concatenate([near[:, x], far[:, x], pair[:, first + x.start : first + x.stop], odd[:, x]], axis=0)
+            jnp.concatenate([block[:, x] for block in (even_near, even_far, odd_near, odd_far)], axis=0)
             for x in (key_lanes, value_lanes)
         ]
         heads = range(g * group, (g + 1) * group)
@@ -251,7 +256,7 @@
         functools.partial(norm_select_kernel, n),
         "norm_select",
         (hidden, norm_gain.reshape(1, model), retained_lists.reshape(1, rows), keys, values),
-        [shape((rows, half + (2 * keys.shape[1] if k == 1 or k in range(0, n // 2, 2) else 0)), bf16) for k in range(n)],
+        [shape((rows, half + (2 * keys.shape[1] if k < n // 2 else 0)), bf16) for k in range(n)],
         4 * rows * model,
         limit=16,
         in_specs=[ANY] * 5,
@@ -279,39 +284,46 @@
         remote=3,
         scratch=[pltpu.SMEM(counts.shape, i32), dma((3,))],
     )
-    own, even = call(
+    own, even, odd = call(
         functools.partial(compact_kernel, n),
         "compact",
         (target, *received),
-        [shape((survivors, half), bf16), shape((n // 4 * rows, 2 * keys.shape[1]), bf16)],
+        [shape((survivors, half), bf16)] + [shape((n // 4 * rows, 2 * keys.shape[1]), bf16)] * 2,
         2 * survivors * n * rows * half,
     )
     other = swap(own)
     rest = [1 << i for i in range(2, n.bit_length() - 1)]
     masks = [[1, 2] + rest, [2, 1] + rest]
+    (product,) = call(
+        project_own_kernel,
+        "project_own",
+        (own, matrix),
+        [shape((survivors, width), f32)],
+        2 * survivors * half * width,
+    )
     products = [
         call(
             functools.partial(project_kernel, c * chunk, halving_order(n, masks[c])),
             "project",
-            (own, other, matrix),
+            (product, other, matrix),
             [shape((near, chunk), f32), shape((near, chunk), bf16)],
-            4 * survivors * half * chunk,
+            2 * survivors * half * chunk,
         )
         for c in range(2)
     ]
     far = trade(even, n // 2)
-    (gathered,) = call(
-        gather_kernel,
-        "gather",
-        (even, far, products[0][1]),
-        [shape((n // 2 * rows - rows, even.shape[1]), bf16)],
+    (passed,) = call(
+        pass_kernel,
+        "pass",
+        (far, products[1][1]),
+        [shape(far.shape, bf16)],
         1500 * affine_matrix.size,
-        in_specs=[VMEM] * 2 + [ANY],
+        in_specs=[VMEM, ANY],
     )
     context, columns = call(
         functools.partial(attention_kernel, n, kv_heads, masks[0]),
         "attention",
-        (queries, received[1], even, far, trade(gathered, 1)),
+        (queries, even, far, odd, trade(passed, 1)),
         [shape(queries.shape, f32), shape((n, rows), f32)],
         4 * rows * n * rows * queries.shape[1],
         limit=32,
@@ -319,11 +331,11 @@
     kept = [product[0] for product in products]
     arrived = [trade(product[1], masks[c][0]) for c, product in enumerate(products)]
     lines_left = near // 2
-    for c in (1, 0):
+    for c in (0, 1):
         keep, sent = call(
             hop_sum_kernel,
             "hop_sum",
-            (kept[c], arrived[c], products[c][1] if c else columns),
+            (kept[c], arrived[c], kept[0] if c else columns),
             [shape((lines_left, chunk), f32), shape((lines_left, chunk), bf16)],
             near * chunk,
             in_specs=[VMEM] * 2 + [ANY],

time: 60.1 us -> 59 us (0.982)
  waiting for transfers between devices: 23.9 us -> 19 us
  starting transfers between devices: 25.3 us -> 28.8 us
    ppermute x18, waiting for transfers between devices: 23.5 us -> 18.5 us  [trade(): return lax.ppermute(x, 'seq', [(i, i ^ k) for i in range(n)])]
    ppermute x18, starting transfers between devices: 23.6 us -> 28.3 us  [trade(): return lax.ppermute(x, 'seq', [(i, i ^ k) for i in range(n)])]
    ppermute x1, starting transfers between devices: 1.6 us -> 0.46 us  [trade_across(): lax.ppermute(x, ('seq', 'ten'), [(2 * i + t, 2 * (i ^ k) + 1 - t) for i i...]
    pallas_call x14 -> x15, Pallas kernels: 10 us -> 10.2 us  [call(): pl.pallas_call(body, out_shape=list(outputs), in_specs=in_specs or [VMEM]...]
  transfers between devices with their start and end apart: 21 -> 21, of which waited for: 9 -> 9; matrix products, arithmetic and copies ran while one was open for 0% -> 0% of each run, Pallas kernels for 12% -> 13%
where the time goes in v12:
time: 59 us; the launch traced here: 58.9 us
  starting transfers between devices  28.8 us (49%)
  waiting for transfers between devices  19 us (32%)
  Pallas kernels  10.2 us (17%)
  between operations  0.78 us (1%)
    ppermute x18, starting transfers between devices, trade(): return lax.ppermute(x, 'seq', [(i, i ^ k) for i in range(n)])  28.3 us
    ppermute x18, waiting for transfers between devices, trade(): return lax.ppermute(x, 'seq', [(i, i ^ k) for i in range(n)])  18.5 us
    pallas_call x15, Pallas kernels, call(): pl.pallas_call(body, out_shape=list(outputs), in_specs=in_specs or [VMEM]...  10.2 us
  transfers between devices with their start and end apart: 21, of which 9 were waited for; matrix products, arithmetic and copies ran while one was open for 0% of the time, Pallas kernels for 13%

profile of v12, /device:TPU:0, one launch (start us, length us, event | category | flops | bytes accessed | tf_op | source)
XLA Modules:
  0.0 58.9 jit_solution(10285428891606949943)
XLA Ops:
  0.6 1.8 %norm_select.1 = (bf16[64,1024]{1,0:T(8,128)(2,1)S(1)}, bf16[64,1024]{1,0:T(8,128)(2,1)S(1)}, bf16[64,1024]{1,0:T(8,128)(2,1)S(1)}, bf16[64,1024]{1,0:T(8,128)(2...) custom-call(bf16[64,8192]{1,0:T(8,128)(2,1)} %hidden_in.1, ...), custom_call_target="tpu_custom_call" | custom-call | flops 2097152 | bytes 1933568 | tf_op jit(solution)/shard_map/norm_select/pallas_call | solution.py:21
  2.4 3.0 %collective-permute-start.2 = (bf16[64,1024]{1,0:T(8,128)(2,1)S(1)}, bf16[64,1024]{1,0:T(8,128)(2,1)S(1)}, u32[]{:S(2)}, u32[]{:S(2)}) collective-permute-start(bf16[64,1024]{1,0:T(8,128)(2,1)S(1)} %get-tuple-element.36), channel_id=1, source_target_pairs={{0,2},{2,0},{4,6},{6,4},{8,10},{10,8},{12,14},{14,12},{1,3},{3,1},... | collective-permute-start | bytes 393224 | tf_op jit(solution)/shard_map/ppermute | solution.py:247
  5.4 1.5 %collective-permute-start.4 = (bf16[64,1024]{1,0:T(8,128)(2,1)S(1)}, bf16[64,1024]{1,0:T(8,128)(2,1)S(1)}, u32[]{:S(2)}, u32[]{:S(2)}) collective-permute-start(bf16[64,1024]{1,0:T(8,128)(2,1)S(1)} %get-tuple-element.38), channel_id=1, source_target_pairs={{0,6},{2,4},{4,2},{6,0},{8,14},{10,12},{12,10},{14,8},{1,7},{3,5},... | collective-permute-start | bytes 393224 | tf_op jit(solution)/shard_map/ppermute | solution.py:247
  6.9 2.6 %collective-permute-start = (bf16[64,512]{1,0:T(8,128)(2,1)S(1)}, bf16[64,512]{1,0:T(8,128)(2,1)S(1)}, u32[]{:S(2)}, u32[]{:S(2)}) collective-permute-start(bf16[64,512]{1,0:T(8,128)(2,1)S(1)} %get-tuple-element.31), channel_id=1, source_target_pairs={{0,8},{2,10},{4,12},{6,14},{8,0},{10,2},{12,4},{14,6},{1,9},{3,11}... | collective-permute-start | bytes 196616 | tf_op jit(solution)/shard_map/ppermute | solution.py:247
  9.5 1.3 %collective-permute-start.1 = (bf16[64,512]{1,0:T(8,128)(2,1)S(1)}, bf16[64,512]{1,0:T(8,128)(2,1)S(1)}, u32[]{:S(2)}, u32[]{:S(2)}) collective-permute-start(bf16[64,512]{1,0:T(8,128)(2,1)S(1)} %get-tuple-element.32), channel_id=1, source_target_pairs={{0,10},{2,8},{4,14},{6,12},{8,2},{10,0},{12,6},{14,4},{1,11},{3,9}... | collective-permute-start | bytes 196616 | tf_op jit(solution)/shard_map/ppermute | solution.py:247
  10.8 0.4 collective-permute-start.3
  11.3 0.8 %collective-permute-done.4.refs_3_ = bf16[64,1024]{1,0:T(8,128)(2,1)S(1)} collective-permute-done((bf16[64,1024]{1,0:T(8,128)(2,1)S(1)}, bf16[64,1024]{1,0:T(8,128)(2,1)S(1)}, u32[]{:S(2)}, u32[]{:S(2)}) %collective-permute-start.4) | collective-permute-done | bytes 131104 | tf_op jit(solution)/shard_map/ppermute | solution.py:247
  12.0 6.4 %collective-permute-start.5 = (bf16[64,512]{1,0:T(8,128)(2,1)S(1)}, bf16[64,512]{1,0:T(8,128)(2,1)S(1)}, u32[]{:S(2)}, u32[]{:S(2)}) collective-permute-start(bf16[64,512]{1,0:T(8,128)(2,1)S(1)} %get-tuple-element.41), channel_id=1, source_target_pairs={{0,12},{2,14},{4,8},{6,10},{8,4},{10,6},{12,0},{14,2},{1,13},{3,15... | collective-permute-start | bytes 196616 | tf_op jit(solution)/shard_map/ppermute | solution.py:247
  18.5 0.0 collective-permute-start.6
  18.5 2.5 %stage.1 = (bf16[1024,2560]{1,0:T(8,128)(2,1)S(1)}, bf16[64,2048]{1,0:T(8,128)(2,1)S(1)}, s32[1,512]{1,0:T(1,128)S(1)}) custom-call(s32[8]{0:T(128)} %counts_in.1, bf16[1024,2560]{1,0:T(8,128)(2,1)} %matrix_in.1, bf16[64,2048]{1,0:T(8,128)(2,1)} %queries_in.1, bf16[64,512]{1,0:T(8,128)(2,1)S(1)} %collective-permute-done.refs_0_.refs_4_, ...), custom_call_target="tpu_custom_call" | custom-call | flops 3932160000 | bytes 11143200 | tf_op jit(solution)/shard_map/stage/pallas_call | solution.py:21
  21.0 0.0 collective-permute-done.5.refs_6_
  21.0 4.4 %collective-permute-done.6.refs_7_ = bf16[64,512]{1,0:T(8,128)(2,1)S(1)} collective-permute-done((bf16[64,512]{1,0:T(8,128)(2,1)S(1)}, bf16[64,512]{1,0:T(8,128)(2,1)S(1)}, u32[]{:S(2)}, u32[]{:S(2)}) %collective-permute-start.6) | collective-permute-done | bytes 65568 | tf_op jit(solution)/shard_map/ppermute | solution.py:247
  25.4 0.3 compact.1
  25.7 0.1 collective-permute-start.8
  25.8 0.1 collective-permute-start.7
  25.9 1.0 %project_own.1.product = f32[256,2560]{1,0:T(8,128)S(1)} custom-call(bf16[256,512]{1,0:T(8,128)(2,1)S(1)} %get-tuple-element.45.own, bf16[1024,2560]{1,0:T(8,128)(2,1)S(1)} %get-tuple-element.46.matrix), custom_call_target="tpu_custom_call" | custom-call | flops 671088640 | bytes 8126464 | tf_op jit(solution)/shard_map/project_own/pallas_call | solution.py:21
  26.9 0.4 collective-permute-done.8.other
  27.3 0.6 project.3
  27.9 0.1 collective-permute-start.10
  28.0 0.6 project.2
  28.6 0.0 copy-start
  28.6 1.4 %collective-permute-start.11 = (bf16[128,1280]{1,0:T(8,128)(2,1)S(1)}, bf16[128,1280]{1,0:T(8,128)(2,1)S(1)}, u32[]{:S(2)}, u32[]{:S(2)}) collective-permute-start(bf16[128,1280]{1,0:T(8,128)(2,1)S(1)} %get-tuple-element.47.after), channel_id=1, source_target_pairs={{0,4},{2,6},{4,0},{6,2},{8,12},{10,14},{12,8},{14,10},{1,5},{3,7},... | collective-permute-start | bytes 983048 | tf_op jit(solution)/shard_map/ppermute | solution.py:247
  30.0 2.9 %collective-permute-done.7.block.even_far = bf16[128,512]{1,0:T(8,128)(2,1)S(1)} collective-permute-done((bf16[128,512]{1,0:T(8,128)(2,1)S(1)}, bf16[128,512]{1,0:T(8,128)(2,1)S(1)}, u32[]{:S(2)}, u32[]{:S(2)}) %collective-permute-start.7) | collective-permute-done | bytes 131104 | tf_op jit(solution)/shard_map/ppermute | solution.py:247
  33.0 1.2 %collective-permute-start.9 = (bf16[128,512]{1,0:T(8,128)(2,1)S(1)}, bf16[128,512]{1,0:T(8,128)(2,1)S(1)}, u32[]{:S(2)}, u32[]{:S(2)}) collective-permute-start(bf16[128,512]{1,0:T(8,128)(2,1)S(1)} %pass.1), channel_id=1, source_target_pairs={{0,2},{2,0},{4,6},{6,4},{8,10},{10,8},{12,14},{14,12},{1,3},{3,1},... | collective-permute-start | bytes 393224 | tf_op jit(solution)/shard_map/ppermute | solution.py:247
  34.2 6.3 %collective-permute-done.9.odd_far = bf16[128,512]{1,0:T(8,128)(2,1)S(1)} collective-permute-done((bf16[128,512]{1,0:T(8,128)(2,1)S(1)}, bf16[128,512]{1,0:T(8,128)(2,1)S(1)}, u32[]{:S(2)}, u32[]{:S(2)}) %collective-permute-start.9) | collective-permute-done | bytes 131104 | tf_op jit(solution)/shard_map/ppermute | solution.py:247
  40.5 2.0 %attention.1 = (f32[64,2048]{1,0:T(8,128)}, f32[8,64]{1,0:T(8,128)S(1)}) custom-call(bf16[64,2048]{1,0:T(8,128)(2,1)S(1)} %get-tuple-element.33.queries, bf16[128,512]{1,0:T(8,128)(2,1)S(1)} %get-tuple-element.43.even_near, bf16[128,512]{1,0:T(8,128)(2,1)S(1)} %collective-permute-done.7.block.even_far, bf16[128,512]{1,0:T(8,128)(2,1)S(1)} %get-tuple-element.44.odd_near, ...), custom_call_target="tpu_custom_call" | custom-call | flops 268435456 | bytes 1312768 | tf_op jit(solution)/shard_map/attention/pallas_call | solution.py:21
  42.5 0.0 collective-permute-done.10.received
  42.5 0.1 hop_sum.2
  42.6 0.0 collective-permute-done.11.received
  42.6 0.1 hop_sum.3
  42.7 0.4 collective-permute-start.13
  43.0 1.1 %collective-permute-start.12 = (bf16[64,1280]{1,0:T(8,128)(2,1)S(1)}, bf16[64,1280]{1,0:T(8,128)(2,1)S(1)}, u32[]{:S(2)}, u32[]{:S(2)}) collective-permute-start(bf16[64,1280]{1,0:T(8,128)(2,1)S(1)} %get-tuple-element.55), channel_id=1, source_target_pairs={{0,4},{2,6},{4,0},{6,2},{8,12},{10,14},{12,8},{14,10},{1,5},{3,7},... | collective-permute-start | bytes 491528 | tf_op jit(solution)/shard_map/ppermute | solution.py:247
  44.2 0.9 %collective-permute-start.15 = (f32[2,64]{1,0:T(2,128)S(1)}, f32[2,64]{1,0:T(2,128)S(1)}, u32[]{:S(2)}, u32[]{:S(2)}) collective-permute-start(f32[2,64]{1,0:T(2,128)S(1)} %get-tuple-element.61), channel_id=1, source_target_pairs={{0,4},{2,6},{4,0},{6,2},{8,12},{10,14},{12,8},{14,10},{1,5},{3,7},... | collective-permute-start | bytes 1544 | tf_op jit(solution)/shard_map/ppermute | solution.py:247
  45.1 1.7 %collective-permute-start.16 = (f32[2,64]{1,0:T(2,128)S(1)}, f32[2,64]{1,0:T(2,128)S(1)}, u32[]{:S(2)}, u32[]{:S(2)}) collective-permute-start(f32[2,64]{1,0:T(2,128)S(1)} %get-tuple-element.60), channel_id=1, source_target_pairs={{0,2},{2,0},{4,6},{6,4},{8,10},{10,8},{12,14},{14,12},{1,3},{3,1},... | collective-permute-start | bytes 1544 | tf_op jit(solution)/shard_map/ppermute | solution.py:247
  46.8 0.8 %collective-permute-start.17 = (f32[2,64]{1,0:T(2,128)S(1)}, f32[2,64]{1,0:T(2,128)S(1)}, u32[]{:S(2)}, u32[]{:S(2)}) collective-permute-start(f32[2,64]{1,0:T(2,128)S(1)} %get-tuple-element.59), channel_id=1, source_target_pairs={{0,6},{2,4},{4,2},{6,0},{8,14},{10,12},{12,10},{14,8},{1,7},{3,5},... | collective-permute-start | bytes 1544 | tf_op jit(solution)/shard_map/ppermute | solution.py:247
  47.7 0.5 collective-permute-done.13.refs_3_
  48.2 0.3 collective-permute-done.12.refs_2_
  48.5 0.1 hop_sum_both.1
  48.6 2.6 %collective-permute-start.14 = (bf16[32,2560]{1,0:T(8,128)(2,1)S(1)}, bf16[32,2560]{1,0:T(8,128)(2,1)S(1)}, u32[]{:S(2)}, u32[]{:S(2)}) collective-permute-start(bf16[32,2560]{1,0:T(8,128)(2,1)S(1)} %get-tuple-element.58), channel_id=1, source_target_pairs={{0,8},{2,10},{4,12},{6,14},{8,0},{10,2},{12,4},{14,6},{1,9},{3,11}... | collective-permute-start | bytes 491528 | tf_op jit(solution)/shard_map/ppermute | solution.py:247
  51.2 0.0 collective-permute-done.15.refs_1_
  51.2 0.0 collective-permute-done.16.refs_2_
  51.2 0.1 collective-permute-done.17.refs_3_
  51.3 2.6 %collective-permute-start.18 = (f32[1,64]{1,0:T(1,128)S(1)}, f32[1,64]{1,0:T(1,128)S(1)}, u32[]{:S(2)}, u32[]{:S(2)}) collective-permute-start(f32[1,64]{1,0:T(1,128)S(1)} %get-tuple-element.63), channel_id=1, source_target_pairs={{0,8},{2,10},{4,12},{6,14},{8,0},{10,2},{12,4},{14,6},{1,9},{3,11}... | collective-permute-start | bytes 776 | tf_op jit(solution)/shard_map/ppermute | solution.py:247
  53.9 0.5 collective-permute-start.20
  54.4 3.2 %collective-permute-done.14.received = bf16[32,2560]{1,0:T(8,128)(2,1)S(1)} collective-permute-done((bf16[32,2560]{1,0:T(8,128)(2,1)S(1)}, bf16[32,2560]{1,0:T(8,128)(2,1)S(1)}, u32[]{:S(2)}, u32[]{:S(2)}) %collective-permute-start.14) | collective-permute-done | bytes 163872 | tf_op jit(solution)/shard_map/ppermute | solution.py:247
  57.6 0.8 %finish.1.after = f32[32,2560]{1,0:T(8,128)} custom-call(f32[1,2560]{1,0:T(1,128)S(1)} %reshape.20.bias, f32[32,2560]{1,0:T(8,128)S(1)} %get-tuple-element.57.kept.after, bf16[32,2560]{1,0:T(8,128)(2,1)S(1)} %collective-permute-done.14.received), custom_call_target="tpu_custom_call" | custom-call | flops 655360 | bytes 829440 | tf_op jit(solution)/shard_map/finish/pallas_call | solution.py:21
  58.3 0.0 collective-permute-done.18.refs_1_
  58.3 0.5 column_sum.3
  (14 shorter events, 0.1 us)
Async XLA Ops:
  2.4 8.9 %collective-permute-start.2 = (bf16[64,1024]{1,0:T(8,128)(2,1)S(1)}, bf16[64,1024]{1,0:T(8,128)(2,1)S(1)}, u32[]{:S(2)}, u32[]{:S(2)}) collective-permute-start(bf16[64,1024]{1,0:T(8,128)(2,1)S(1)} %get-tuple-element.36), channel_id=1, source_target_pairs={{0,2},{2,0},{4,6},{6,4},{8,10},{10,8},{12,14},{14,12},{1,3},{3,1},... | collective-permute-start | bytes 393224 | tf_op jit(solution)/shard_map/ppermute | solution.py:247
  5.4 6.6 %collective-permute-start.4 = (bf16[64,1024]{1,0:T(8,128)(2,1)S(1)}, bf16[64,1024]{1,0:T(8,128)(2,1)S(1)}, u32[]{:S(2)}, u32[]{:S(2)}) collective-permute-start(bf16[64,1024]{1,0:T(8,128)(2,1)S(1)} %get-tuple-element.38), channel_id=1, source_target_pairs={{0,6},{2,4},{4,2},{6,0},{8,14},{10,12},{12,10},{14,8},{1,7},{3,5},... | collective-permute-start | bytes 393224 | tf_op jit(solution)/shard_map/ppermute | solution.py:247
  6.9 11.5 %collective-permute-start = (bf16[64,512]{1,0:T(8,128)(2,1)S(1)}, bf16[64,512]{1,0:T(8,128)(2,1)S(1)}, u32[]{:S(2)}, u32[]{:S(2)}) collective-permute-start(bf16[64,512]{1,0:T(8,128)(2,1)S(1)} %get-tuple-element.31), channel_id=1, source_target_pairs={{0,8},{2,10},{4,12},{6,14},{8,0},{10,2},{12,4},{14,6},{1,9},{3,11}... | collective-permute-start | bytes 196616 | tf_op jit(solution)/shard_map/ppermute | solution.py:247
  9.5 8.9 %collective-permute-start.1 = (bf16[64,512]{1,0:T(8,128)(2,1)S(1)}, bf16[64,512]{1,0:T(8,128)(2,1)S(1)}, u32[]{:S(2)}, u32[]{:S(2)}) collective-permute-start(bf16[64,512]{1,0:T(8,128)(2,1)S(1)} %get-tuple-element.32), channel_id=1, source_target_pairs={{0,10},{2,8},{4,14},{6,12},{8,2},{10,0},{12,6},{14,4},{1,11},{3,9}... | collective-permute-start | bytes 196616 | tf_op jit(solution)/shard_map/ppermute | solution.py:247
  10.8 10.2 %collective-permute-start.3 = (bf16[64,1024]{1,0:T(8,128)(2,1)S(1)}, bf16[64,1024]{1,0:T(8,128)(2,1)S(1)}, u32[]{:S(2)}, u32[]{:S(2)}) collective-permute-start(bf16[64,1024]{1,0:T(8,128)(2,1)S(1)} %get-tuple-element.37), channel_id=1, source_target_pairs={{0,4},{2,6},{4,0},{6,2},{8,12},{10,14},{12,8},{14,10},{1,5},{3,7},... | collective-permute-start | bytes 393224 | tf_op jit(solution)/shard_map/ppermute | solution.py:247
  12.0 9.0 %collective-permute-start.5 = (bf16[64,512]{1,0:T(8,128)(2,1)S(1)}, bf16[64,512]{1,0:T(8,128)(2,1)S(1)}, u32[]{:S(2)}, u32[]{:S(2)}) collective-permute-start(bf16[64,512]{1,0:T(8,128)(2,1)S(1)} %get-tuple-element.41), channel_id=1, source_target_pairs={{0,12},{2,14},{4,8},{6,10},{8,4},{10,6},{12,0},{14,2},{1,13},{3,15... | collective-permute-start | bytes 196616 | tf_op jit(solution)/shard_map/ppermute | solution.py:247
  18.5 7.0 %collective-permute-start.6 = (bf16[64,512]{1,0:T(8,128)(2,1)S(1)}, bf16[64,512]{1,0:T(8,128)(2,1)S(1)}, u32[]{:S(2)}, u32[]{:S(2)}) collective-permute-start(bf16[64,512]{1,0:T(8,128)(2,1)S(1)} %get-tuple-element.42), channel_id=1, source_target_pairs={{0,14},{2,12},{4,10},{6,8},{8,6},{10,4},{12,2},{14,0},{1,15},{3,13... | collective-permute-start | bytes 196616 | tf_op jit(solution)/shard_map/ppermute | solution.py:247
  25.7 1.6 %collective-permute-start.8 = (bf16[256,512]{1,0:T(8,128)(2,1)S(1)}, bf16[256,512]{1,0:T(8,128)(2,1)S(1)}, u32[]{:S(2)}, u32[]{:S(2)}) collective-permute-start(bf16[256,512]{1,0:T(8,128)(2,1)S(1)} %get-tuple-element.45.own), channel_id=1, source_target_pairs={{0,1},{1,0},{2,3},{3,2},{4,5},{5,4},{6,7},{7,6},{8,9},{9,8},{10,11... | collective-permute-start | bytes 786440 | tf_op jit(solution)/shard_map/ppermute | solution.py:253
  25.8 7.1 %collective-permute-start.7 = (bf16[128,512]{1,0:T(8,128)(2,1)S(1)}, bf16[128,512]{1,0:T(8,128)(2,1)S(1)}, u32[]{:S(2)}, u32[]{:S(2)}) collective-permute-start(bf16[128,512]{1,0:T(8,128)(2,1)S(1)} %get-tuple-element.43.even_near), channel_id=1, source_target_pairs={{0,8},{2,10},{4,12},{6,14},{8,0},{10,2},{12,4},{14,6},{1,9},{3,11}... | collective-permute-start | bytes 393224 | tf_op jit(solution)/shard_map/ppermute | solution.py:247
  27.9 14.6 %collective-permute-start.10 = (bf16[128,1280]{1,0:T(8,128)(2,1)S(1)}, bf16[128,1280]{1,0:T(8,128)(2,1)S(1)}, u32[]{:S(2)}, u32[]{:S(2)}) collective-permute-start(bf16[128,1280]{1,0:T(8,128)(2,1)S(1)} %get-tuple-element.50), channel_id=1, source_target_pairs={{0,2},{2,0},{4,6},{6,4},{8,10},{10,8},{12,14},{14,12},{1,3},{3,1},... | collective-permute-start | bytes 983048 | tf_op jit(solution)/shard_map/ppermute | solution.py:247
  28.6 19.1 %copy-start = (f32[2560]{0:T(1024)S(1)}, f32[2560]{0:T(1024)}, u32[]{:S(2)}) copy-start(f32[2560]{0:T(1024)} %param.17) | copy-start | bytes 30724
  28.6 14.0 %collective-permute-start.11 = (bf16[128,1280]{1,0:T(8,128)(2,1)S(1)}, bf16[128,1280]{1,0:T(8,128)(2,1)S(1)}, u32[]{:S(2)}, u32[]{:S(2)}) collective-permute-start(bf16[128,1280]{1,0:T(8,128)(2,1)S(1)} %get-tuple-element.47.after), channel_id=1, source_target_pairs={{0,4},{2,6},{4,0},{6,2},{8,12},{10,14},{12,8},{14,10},{1,5},{3,7},... | collective-permute-start | bytes 983048 | tf_op jit(solution)/shard_map/ppermute | solution.py:247
  33.0 7.6 %collective-permute-start.9 = (bf16[128,512]{1,0:T(8,128)(2,1)S(1)}, bf16[128,512]{1,0:T(8,128)(2,1)S(1)}, u32[]{:S(2)}, u32[]{:S(2)}) collective-permute-start(bf16[128,512]{1,0:T(8,128)(2,1)S(1)} %pass.1), channel_id=1, source_target_pairs={{0,2},{2,0},{4,6},{6,4},{8,10},{10,8},{12,14},{14,12},{1,3},{3,1},... | collective-permute-start | bytes 393224 | tf_op jit(solution)/shard_map/ppermute | solution.py:247
  42.7 5.5 %collective-permute-start.13 = (bf16[64,1280]{1,0:T(8,128)(2,1)S(1)}, bf16[64,1280]{1,0:T(8,128)(2,1)S(1)}, u32[]{:S(2)}, u32[]{:S(2)}) collective-permute-start(bf16[64,1280]{1,0:T(8,128)(2,1)S(1)} %get-tuple-element.56), channel_id=1, source_target_pairs={{0,2},{2,0},{4,6},{6,4},{8,10},{10,8},{12,14},{14,12},{1,3},{3,1},... | collective-permute-start | bytes 491528 | tf_op jit(solution)/shard_map/ppermute | solution.py:247
  43.0 5.5 %collective-permute-start.12 = (bf16[64,1280]{1,0:T(8,128)(2,1)S(1)}, bf16[64,1280]{1,0:T(8,128)(2,1)S(1)}, u32[]{:S(2)}, u32[]{:S(2)}) collective-permute-start(bf16[64,1280]{1,0:T(8,128)(2,1)S(1)} %get-tuple-element.55), channel_id=1, source_target_pairs={{0,4},{2,6},{4,0},{6,2},{8,12},{10,14},{12,8},{14,10},{1,5},{3,7},... | collective-permute-start | bytes 491528 | tf_op jit(solution)/shard_map/ppermute | solution.py:247
  44.2 7.0 %collective-permute-start.15 = (f32[2,64]{1,0:T(2,128)S(1)}, f32[2,64]{1,0:T(2,128)S(1)}, u32[]{:S(2)}, u32[]{:S(2)}) collective-permute-start(f32[2,64]{1,0:T(2,128)S(1)} %get-tuple-element.61), channel_id=1, source_target_pairs={{0,4},{2,6},{4,0},{6,2},{8,12},{10,14},{12,8},{14,10},{1,5},{3,7},... | collective-permute-start | bytes 1544 | tf_op jit(solution)/shard_map/ppermute | solution.py:247
  45.1 6.1 %collective-permute-start.16 = (f32[2,64]{1,0:T(2,128)S(1)}, f32[2,64]{1,0:T(2,128)S(1)}, u32[]{:S(2)}, u32[]{:S(2)}) collective-permute-start(f32[2,64]{1,0:T(2,128)S(1)} %get-tuple-element.60), channel_id=1, source_target_pairs={{0,2},{2,0},{4,6},{6,4},{8,10},{10,8},{12,14},{14,12},{1,3},{3,1},... | collective-permute-start | bytes 1544 | tf_op jit(solution)/shard_map/ppermute | solution.py:247
  46.8 4.5 %collective-permute-start.17 = (f32[2,64]{1,0:T(2,128)S(1)}, f32[2,64]{1,0:T(2,128)S(1)}, u32[]{:S(2)}, u32[]{:S(2)}) collective-permute-start(f32[2,64]{1,0:T(2,128)S(1)} %get-tuple-element.59), channel_id=1, source_target_pairs={{0,6},{2,4},{4,2},{6,0},{8,14},{10,12},{12,10},{14,8},{1,7},{3,5},... | collective-permute-start | bytes 1544 | tf_op jit(solution)/shard_map/ppermute | solution.py:247
  48.6 9.0 %collective-permute-start.14 = (bf16[32,2560]{1,0:T(8,128)(2,1)S(1)}, bf16[32,2560]{1,0:T(8,128)(2,1)S(1)}, u32[]{:S(2)}, u32[]{:S(2)}) collective-permute-start(bf16[32,2560]{1,0:T(8,128)(2,1)S(1)} %get-tuple-element.58), channel_id=1, source_target_pairs={{0,8},{2,10},{4,12},{6,14},{8,0},{10,2},{12,4},{14,6},{1,9},{3,11}... | collective-permute-start | bytes 491528 | tf_op jit(solution)/shard_map/ppermute | solution.py:247
  51.3 7.0 %collective-permute-start.18 = (f32[1,64]{1,0:T(1,128)S(1)}, f32[1,64]{1,0:T(1,128)S(1)}, u32[]{:S(2)}, u32[]{:S(2)}) collective-permute-start(f32[1,64]{1,0:T(1,128)S(1)} %get-tuple-element.63), channel_id=1, source_target_pairs={{0,8},{2,10},{4,12},{6,14},{8,0},{10,2},{12,4},{14,6},{1,9},{3,11}... | collective-permute-start | bytes 776 | tf_op jit(solution)/shard_map/ppermute | solution.py:247
  53.9 4.4 %collective-permute-start.19 = (f32[1,64]{1,0:T(1,128)S(1)}, f32[1,64]{1,0:T(1,128)S(1)}, u32[]{:S(2)}, u32[]{:S(2)}) collective-permute-start(f32[1,64]{1,0:T(1,128)S(1)} %get-tuple-element.64.refs_0_), channel_id=1, source_target_pairs={{0,1},{1,0},{2,3},{3,2},{4,5},{5,4},{6,7},{7,6},{8,9},{9,8},{10,11... | collective-permute-start | bytes 776 | tf_op jit(solution)/shard_map/ppermute | solution.py:253
  53.9 4.4 %collective-permute-start.20 = (f32[1,64]{1,0:T(1,128)S(1)}, f32[1,64]{1,0:T(1,128)S(1)}, u32[]{:S(2)}, u32[]{:S(2)}) collective-permute-start(f32[1,64]{1,0:T(1,128)S(1)} %get-tuple-element.63), channel_id=1, source_target_pairs={{0,9},{1,8},{2,11},{3,10},{4,13},{5,12},{6,15},{7,14},{8,1},{9,0},... | collective-permute-start | bytes 776 | tf_op jit(solution)/shard_map/ppermute | solution.py:250

commit v13 on v12

--- a/solution.py
+++ b/solution.py
@@ -75,8 +75,10 @@
         ).astype(jnp.bfloat16)
 
 
-def pass_kernel(block, after, out):
-    out[...] = block[...]
+def gather_kernel(near, far, after, out):
+    rows = near.shape[0] + far.shape[0] - out.shape[0]
+    out[: near.shape[0] - rows] = near[rows:]
+    out[near.shape[0] - rows :] = far[...]
 
 
 def relay_kernel(count, *refs):
@@ -113,11 +115,11 @@
 
 
 def compact_kernel(n, target, *refs):
-    blocks, (out, even, odd) = refs[:n], refs[n:]
+    blocks, (out, even, pair) = refs[:n], refs[n:]
+    pair[...] = blocks[1][:, out.shape[1] :]
     rows, half = blocks[0].shape[0], out.shape[1]
     for i in range(n // 4):
         even[i * rows : (i + 1) * rows] = blocks[2 * i][:, half:]
-        odd[i * rows : (i + 1) * rows] = blocks[2 * i + 1][:, half:]
     lines = out.shape[0] // n
     s = lax.axis_index("seq")
     received = jnp.concatenate([b[:, :half] for b in blocks], axis=0)
@@ -187,7 +189,7 @@
     out[...] = total * scale
 
 
-def attention_kernel(n, kv_heads, masks, queries, even_near, even_far, odd_near, odd_far, context, columns):
+def attention_kernel(n, kv_heads, masks, queries, near, far, pair, odd, after, context, columns):
     rows = queries.shape[0]
     group = queries.shape[1] // (HEAD_SIZE * kv_heads)
     s = lax.axis_index("seq")
@@ -205,7 +207,7 @@
         key_lanes = slice(g * HEAD_SIZE, (g + 1) * HEAD_SIZE)
         value_lanes = slice((kv_heads + g) * HEAD_SIZE, (kv_heads + g + 1) * HEAD_SIZE)
         key, value = [
-            jnp.concatenate([block[:, x] for block in (even_near, even_far, odd_near, odd_far)], axis=0)
+            jnp.concatenate([block[:, x] for block in (near, far, pair, odd)], axis=0)
             for x in (key_lanes, value_lanes)
         ]
         heads = range(g * group, (g + 1) * group)
@@ -256,7 +258,7 @@
         functools.partial(norm_select_kernel, n),
         "norm_select",
         (hidden, norm_gain.reshape(1, model), retained_lists.reshape(1, rows), keys, values),
-        [shape((rows, half + (2 * keys.shape[1] if k < n // 2 else 0)), bf16) for k in range(n)],
+        [shape((rows, half + (2 * keys.shape[1] if k == 1 or k in range(0, n // 2, 2) else 0)), bf16) for k in range(n)],
         4 * rows * model,
         limit=16,
         in_specs=[ANY] * 5,
@@ -284,11 +286,11 @@
         remote=3,
         scratch=[pltpu.SMEM(counts.shape, i32), dma((3,))],
     )
-    own, even, odd = call(
+    own, even, pair = call(
         functools.partial(compact_kernel, n),
         "compact",
         (target, *received),
-        [shape((survivors, half), bf16)] + [shape((n // 4 * rows, 2 * keys.shape[1]), bf16)] * 2,
+        [shape((survivors, half), bf16)] + [shape((x * rows, 2 * keys.shape[1]), bf16) for x in (n // 4, 1)],
         2 * survivors * n * rows * half,
     )
     other = swap(own)
@@ -312,22 +314,15 @@
         for c in range(2)
     ]
     far = trade(even, n // 2)
-    (passed,) = call(
-        pass_kernel,
-        "pass",
-        (far, products[1][1]),
-        [shape(far.shape, bf16)],
+    (gathered,) = call(
+        gather_kernel,
+        "gather",
+        (even, far, products[1][1]),
+        [shape((n // 2 * rows - rows, even.shape[1]), bf16)],
         1500 * affine_matrix.size,
-        in_specs=[VMEM, ANY],
-    )
-    context, columns = call(
-        functools.partial(attention_kernel, n, kv_heads, masks[0]),
-        "attention",
-        (queries, even, far, odd, trade(passed, 1)),
-        [shape(queries.shape, f32), shape((n, rows), f32)],
-        4 * rows * n * rows * queries.shape[1],
-        limit=32,
-    )
+        in_specs=[VMEM] * 2 + [ANY],
+    )
+    odd = trade(gathered, 1)
     kept = [product[0] for product in products]
     arrived = [trade(product[1], masks[c][0]) for c, product in enumerate(products)]
     lines_left = near // 2
@@ -335,12 +330,22 @@
         keep, sent = call(
             hop_sum_kernel,
             "hop_sum",
-            (kept[c], arrived[c], kept[0] if c else columns),
+            (kept[c], arrived[c], kept[0] if c else products[1][1]),
             [shape((lines_left, chunk), f32), shape((lines_left, chunk), bf16)],
             near * chunk,
             in_specs=[VMEM] * 2 + [ANY],
         )
         kept[c], arrived[c] = keep, trade(sent, masks[c][1])
+
+    context, columns = call(
+        functools.partial(attention_kernel, n, kv_heads, masks[0]),
+        "attention",
+        (queries, even, far, pair, odd, kept[0]),
+        [shape(queries.shape, f32), shape((n, rows), f32)],
+        4 * rows * n * rows * queries.shape[1],
+        limit=32,
+        in_specs=[VMEM] * 5 + [ANY],
+    )
 
     def column_sum(pieces, after, scale=1.0, remote=0):
         (total,) = call(

time: 59 us -> 56.4 us (0.956)
  starting transfers between devices: 28.8 us -> 26.1 us
    ppermute x18, starting transfers between devices: 28.3 us -> 23.4 us  [trade(): return lax.ppermute(x, 'seq', [(i, i ^ k) for i in range(n)])]
    ppermute x1, starting transfers between devices: 0.46 us -> 2.66 us  [trade_across(): lax.ppermute(x, ('seq', 'ten'), [(2 * i + t, 2 * (i ^ k) + 1 - t) for i i...]
  transfers between devices with their start and end apart: 21 -> 21, of which waited for: 9 -> 8; matrix products, arithmetic and copies ran while one was open for 0% -> 0% of each run, Pallas kernels for 13% -> 14%
where the time goes in v13:
time: 56.4 us; the launch traced here: 56.2 us
  starting transfers between devices  26.1 us (46%)
  waiting for transfers between devices  19.1 us (34%)
  Pallas kernels  10.2 us (18%)
  between operations  0.79 us (1%)
    ppermute x18, starting transfers between devices, trade(): return lax.ppermute(x, 'seq', [(i, i ^ k) for i in range(n)])  23.4 us
    ppermute x18, waiting for transfers between devices, trade(): return lax.ppermute(x, 'seq', [(i, i ^ k) for i in range(n)])  19.1 us
    pallas_call x15, Pallas kernels, call(): pl.pallas_call(body, out_shape=list(outputs), in_specs=in_specs or [VMEM]...  10.2 us
    ppermute x1, starting transfers between devices, trade_across(): lax.ppermute(x, ('seq', 'ten'), [(2 * i + t, 2 * (i ^ k) + 1 - t) for i i...  2.66 us
  transfers between devices with their start and end apart: 21, of which 8 were waited for; matrix products, arithmetic and copies ran while one was open for 0% of the time, Pallas kernels for 14%

profile of v13, /device:TPU:0, one launch (start us, length us, event | category | flops | bytes accessed | tf_op | source)
XLA Modules:
  0.0 56.2 jit_solution(13326345400361171273)
XLA Ops:
  0.6 1.7 %norm_select.1 = (bf16[64,1024]{1,0:T(8,128)(2,1)S(1)}, bf16[64,1024]{1,0:T(8,128)(2,1)S(1)}, bf16[64,1024]{1,0:T(8,128)(2,1)S(1)}, bf16[64,512]{1,0:T(8,128)(2,...) custom-call(bf16[64,8192]{1,0:T(8,128)(2,1)} %hidden_in.1, ...), custom_call_target="tpu_custom_call" | custom-call | flops 2097152 | bytes 1868032 | tf_op jit(solution)/shard_map/norm_select/pallas_call | solution.py:21
  2.4 3.0 %collective-permute-start.2 = (bf16[64,1024]{1,0:T(8,128)(2,1)S(1)}, bf16[64,1024]{1,0:T(8,128)(2,1)S(1)}, u32[]{:S(2)}, u32[]{:S(2)}) collective-permute-start(bf16[64,1024]{1,0:T(8,128)(2,1)S(1)} %get-tuple-element.36), channel_id=1, source_target_pairs={{0,2},{2,0},{4,6},{6,4},{8,10},{10,8},{12,14},{14,12},{1,3},{3,1},... | collective-permute-start | bytes 393224 | tf_op jit(solution)/shard_map/ppermute | solution.py:249
  5.4 1.5 %collective-permute-start.4 = (bf16[64,512]{1,0:T(8,128)(2,1)S(1)}, bf16[64,512]{1,0:T(8,128)(2,1)S(1)}, u32[]{:S(2)}, u32[]{:S(2)}) collective-permute-start(bf16[64,512]{1,0:T(8,128)(2,1)S(1)} %get-tuple-element.38), channel_id=1, source_target_pairs={{0,6},{2,4},{4,2},{6,0},{8,14},{10,12},{12,10},{14,8},{1,7},{3,5},... | collective-permute-start | bytes 196616 | tf_op jit(solution)/shard_map/ppermute | solution.py:249
  6.9 2.6 %collective-permute-start = (bf16[64,512]{1,0:T(8,128)(2,1)S(1)}, bf16[64,512]{1,0:T(8,128)(2,1)S(1)}, u32[]{:S(2)}, u32[]{:S(2)}) collective-permute-start(bf16[64,512]{1,0:T(8,128)(2,1)S(1)} %get-tuple-element.31), channel_id=1, source_target_pairs={{0,8},{2,10},{4,12},{6,14},{8,0},{10,2},{12,4},{14,6},{1,9},{3,11}... | collective-permute-start | bytes 196616 | tf_op jit(solution)/shard_map/ppermute | solution.py:249
  9.5 1.3 %collective-permute-start.1 = (bf16[64,512]{1,0:T(8,128)(2,1)S(1)}, bf16[64,512]{1,0:T(8,128)(2,1)S(1)}, u32[]{:S(2)}, u32[]{:S(2)}) collective-permute-start(bf16[64,512]{1,0:T(8,128)(2,1)S(1)} %get-tuple-element.32), channel_id=1, source_target_pairs={{0,10},{2,8},{4,14},{6,12},{8,2},{10,0},{12,6},{14,4},{1,11},{3,9}... | collective-permute-start | bytes 196616 | tf_op jit(solution)/shard_map/ppermute | solution.py:249
  10.8 0.4 collective-permute-start.3
  11.3 0.0 collective-permute-done.4.refs_3_
  11.3 0.0 collective-permute-done.2.refs_2_.refs_1_
  11.3 4.2 %collective-permute-start.5 = (bf16[64,512]{1,0:T(8,128)(2,1)S(1)}, bf16[64,512]{1,0:T(8,128)(2,1)S(1)}, u32[]{:S(2)}, u32[]{:S(2)}) collective-permute-start(bf16[64,512]{1,0:T(8,128)(2,1)S(1)} %get-tuple-element.41), channel_id=1, source_target_pairs={{0,12},{2,14},{4,8},{6,10},{8,4},{10,6},{12,0},{14,2},{1,13},{3,15... | collective-permute-start | bytes 196616 | tf_op jit(solution)/shard_map/ppermute | solution.py:249
  15.4 0.0 collective-permute-start.6
  15.5 0.0 collective-permute-done.refs_0_.refs_4_
  15.5 2.3 %collective-permute-done.1.refs_1_.refs_5_ = bf16[64,512]{1,0:T(8,128)(2,1)S(1)} collective-permute-done((bf16[64,512]{1,0:T(8,128)(2,1)S(1)}, bf16[64,512]{1,0:T(8,128)(2,1)S(1)}, u32[]{:S(2)}, u32[]{:S(2)}) %collective-permute-start.1) | collective-permute-done | bytes 65568 | tf_op jit(solution)/shard_map/ppermute | solution.py:249
  17.8 2.5 %stage.1 = (bf16[1024,2560]{1,0:T(8,128)(2,1)S(1)}, bf16[64,2048]{1,0:T(8,128)(2,1)S(1)}, s32[1,512]{1,0:T(1,128)S(1)}) custom-call(s32[8]{0:T(128)} %counts_in.1, bf16[1024,2560]{1,0:T(8,128)(2,1)} %matrix_in.1, bf16[64,2048]{1,0:T(8,128)(2,1)} %queries_in.1, bf16[64,512]{1,0:T(8,128)(2,1)S(1)} %collective-permute-done.refs_0_.refs_4_, ...), custom_call_target="tpu_custom_call" | custom-call | flops 3932160000 | bytes 11143200 | tf_op jit(solution)/shard_map/stage/pallas_call | solution.py:21
  20.3 0.0 collective-permute-done.3.refs_2_
  20.3 0.0 collective-permute-done.5.refs_6_
  20.3 2.1 %collective-permute-done.6.refs_7_ = bf16[64,512]{1,0:T(8,128)(2,1)S(1)} collective-permute-done((bf16[64,512]{1,0:T(8,128)(2,1)S(1)}, bf16[64,512]{1,0:T(8,128)(2,1)S(1)}, u32[]{:S(2)}, u32[]{:S(2)}) %collective-permute-start.6) | collective-permute-done | bytes 65568 | tf_op jit(solution)/shard_map/ppermute | solution.py:249
  22.4 0.3 compact.1
  22.7 0.1 collective-permute-start.8
  22.8 1.1 %collective-permute-start.7 = (bf16[128,512]{1,0:T(8,128)(2,1)S(1)}, bf16[128,512]{1,0:T(8,128)(2,1)S(1)}, u32[]{:S(2)}, u32[]{:S(2)}) collective-permute-start(bf16[128,512]{1,0:T(8,128)(2,1)S(1)} %get-tuple-element.43.near), channel_id=1, source_target_pairs={{0,8},{2,10},{4,12},{6,14},{8,0},{10,2},{12,4},{14,6},{1,9},{3,11}... | collective-permute-start | bytes 393224 | tf_op jit(solution)/shard_map/ppermute | solution.py:249
  23.9 1.0 %project_own.1.product = f32[256,2560]{1,0:T(8,128)S(1)} custom-call(bf16[256,512]{1,0:T(8,128)(2,1)S(1)} %get-tuple-element.45.own, bf16[1024,2560]{1,0:T(8,128)(2,1)S(1)} %get-tuple-element.46.matrix), custom_call_target="tpu_custom_call" | custom-call | flops 671088640 | bytes 8126464 | tf_op jit(solution)/shard_map/project_own/pallas_call | solution.py:21
  24.9 0.6 %project.3 = (f32[128,1280]{1,0:T(8,128)S(1)}, bf16[128,1280]{1,0:T(8,128)(2,1)S(1)}) custom-call(f32[256,2560]{1,0:T(8,128)S(1)} %project_own.1.product, bf16[256,512]{1,0:T(8,128)(2,1)S(1)} %collective-permute-done.8.other, bf16[1024,2560]{1,0:T(8,128)(2,1)S(1)} %get-tuple-element.46.matrix), custom_call_target="tpu_custom_call" | custom-call | flops 335544320 | bytes 9109504 | tf_op jit(solution)/shard_map/project/pallas_call | solution.py:21
  25.5 0.9 %collective-permute-start.10 = (bf16[128,1280]{1,0:T(8,128)(2,1)S(1)}, bf16[128,1280]{1,0:T(8,128)(2,1)S(1)}, u32[]{:S(2)}, u32[]{:S(2)}) collective-permute-start(bf16[128,1280]{1,0:T(8,128)(2,1)S(1)} %get-tuple-element.49), channel_id=1, source_target_pairs={{0,2},{2,0},{4,6},{6,4},{8,10},{10,8},{12,14},{14,12},{1,3},{3,1},... | collective-permute-start | bytes 983048 | tf_op jit(solution)/shard_map/ppermute | solution.py:249
  26.4 0.6 %project.2 = (f32[128,1280]{1,0:T(8,128)S(1)}, bf16[128,1280]{1,0:T(8,128)(2,1)S(1)}) custom-call(f32[256,2560]{1,0:T(8,128)S(1)} %project_own.1.product, bf16[256,512]{1,0:T(8,128)(2,1)S(1)} %collective-permute-done.8.other, bf16[1024,2560]{1,0:T(8,128)(2,1)S(1)} %get-tuple-element.46.matrix), custom_call_target="tpu_custom_call" | custom-call | flops 335544320 | bytes 9109504 | tf_op jit(solution)/shard_map/project/pallas_call | solution.py:21
  27.0 0.0 copy-start
  27.0 1.7 %collective-permute-start.11 = (bf16[128,1280]{1,0:T(8,128)(2,1)S(1)}, bf16[128,1280]{1,0:T(8,128)(2,1)S(1)}, u32[]{:S(2)}, u32[]{:S(2)}) collective-permute-start(bf16[128,1280]{1,0:T(8,128)(2,1)S(1)} %get-tuple-element.47.after), channel_id=1, source_target_pairs={{0,4},{2,6},{4,0},{6,2},{8,12},{10,14},{12,8},{14,10},{1,5},{3,7},... | collective-permute-start | bytes 983048 | tf_op jit(solution)/shard_map/ppermute | solution.py:249
  28.7 3.8 %collective-permute-done.7.far = bf16[128,512]{1,0:T(8,128)(2,1)S(1)} collective-permute-done((bf16[128,512]{1,0:T(8,128)(2,1)S(1)}, bf16[128,512]{1,0:T(8,128)(2,1)S(1)}, u32[]{:S(2)}, u32[]{:S(2)}) %collective-permute-start.7) | collective-permute-done | bytes 131104 | tf_op jit(solution)/shard_map/ppermute | solution.py:249
  32.5 0.1 collective-permute-start.9
  32.6 3.1 %collective-permute-done.10.received = bf16[128,1280]{1,0:T(8,128)(2,1)S(1)} collective-permute-done((bf16[128,1280]{1,0:T(8,128)(2,1)S(1)}, bf16[128,1280]{1,0:T(8,128)(2,1)S(1)}, u32[]{:S(2)}, u32[]{:S(2)}) %collective-permute-start.10) | collective-permute-done | bytes 327712 | tf_op jit(solution)/shard_map/ppermute | solution.py:249
  35.7 0.1 hop_sum.2
  35.8 3.4 %collective-permute-done.11.received = bf16[128,1280]{1,0:T(8,128)(2,1)S(1)} collective-permute-done((bf16[128,1280]{1,0:T(8,128)(2,1)S(1)}, bf16[128,1280]{1,0:T(8,128)(2,1)S(1)}, u32[]{:S(2)}, u32[]{:S(2)}) %collective-permute-start.11) | collective-permute-done | bytes 327712 | tf_op jit(solution)/shard_map/ppermute | solution.py:249
  39.2 0.1 hop_sum.3
  39.2 0.1 collective-permute-start.13
  39.3 1.0 %collective-permute-start.12 = (bf16[64,1280]{1,0:T(8,128)(2,1)S(1)}, bf16[64,1280]{1,0:T(8,128)(2,1)S(1)}, u32[]{:S(2)}, u32[]{:S(2)}) collective-permute-start(bf16[64,1280]{1,0:T(8,128)(2,1)S(1)} %get-tuple-element.54), channel_id=1, source_target_pairs={{0,4},{2,6},{4,0},{6,2},{8,12},{10,14},{12,8},{14,10},{1,5},{3,7},... | collective-permute-start | bytes 491528 | tf_op jit(solution)/shard_map/ppermute | solution.py:249
  40.3 0.0 collective-permute-done.9.odd
  40.3 2.0 %attention.1 = (f32[64,2048]{1,0:T(8,128)}, f32[8,64]{1,0:T(8,128)S(1)}) custom-call(bf16[64,2048]{1,0:T(8,128)(2,1)S(1)} %get-tuple-element.33.queries, bf16[128,512]{1,0:T(8,128)(2,1)S(1)} %get-tuple-element.43.near, bf16[128,512]{1,0:T(8,128)(2,1)S(1)} %collective-permute-done.7.far, bf16[64,512]{1,0:T(8,128)(2,1)S(1)} %get-tuple-element.44.pair, ...), custom_call_target="tpu_custom_call" | custom-call | flops 268435456 | bytes 1640448 | tf_op jit(solution)/shard_map/attention/pallas_call | solution.py:21
  42.3 2.5 %collective-permute-start.15 = (f32[2,64]{1,0:T(2,128)S(1)}, f32[2,64]{1,0:T(2,128)S(1)}, u32[]{:S(2)}, u32[]{:S(2)}) collective-permute-start(f32[2,64]{1,0:T(2,128)S(1)} %get-tuple-element.61), channel_id=1, source_target_pairs={{0,4},{2,6},{4,0},{6,2},{8,12},{10,14},{12,8},{14,10},{1,5},{3,7},... | collective-permute-start | bytes 1544 | tf_op jit(solution)/shard_map/ppermute | solution.py:249
  44.8 0.6 %collective-permute-start.16 = (f32[2,64]{1,0:T(2,128)S(1)}, f32[2,64]{1,0:T(2,128)S(1)}, u32[]{:S(2)}, u32[]{:S(2)}) collective-permute-start(f32[2,64]{1,0:T(2,128)S(1)} %get-tuple-element.60), channel_id=1, source_target_pairs={{0,2},{2,0},{4,6},{6,4},{8,10},{10,8},{12,14},{14,12},{1,3},{3,1},... | collective-permute-start | bytes 1544 | tf_op jit(solution)/shard_map/ppermute | solution.py:249
  45.4 0.9 %collective-permute-start.17 = (f32[2,64]{1,0:T(2,128)S(1)}, f32[2,64]{1,0:T(2,128)S(1)}, u32[]{:S(2)}, u32[]{:S(2)}) collective-permute-start(f32[2,64]{1,0:T(2,128)S(1)} %get-tuple-element.59), channel_id=1, source_target_pairs={{0,6},{2,4},{4,2},{6,0},{8,14},{10,12},{12,10},{14,8},{1,7},{3,5},... | collective-permute-start | bytes 1544 | tf_op jit(solution)/shard_map/ppermute | solution.py:249
  46.3 0.0 collective-permute-done.13.refs_3_
  46.3 0.1 hop_sum_both.1
  46.3 1.1 %collective-permute-start.14 = (bf16[32,2560]{1,0:T(8,128)(2,1)S(1)}, bf16[32,2560]{1,0:T(8,128)(2,1)S(1)}, u32[]{:S(2)}, u32[]{:S(2)}) collective-permute-start(bf16[32,2560]{1,0:T(8,128)(2,1)S(1)} %get-tuple-element.57), channel_id=1, source_target_pairs={{0,8},{2,10},{4,12},{6,14},{8,0},{10,2},{12,4},{14,6},{1,9},{3,11}... | collective-permute-start | bytes 491528 | tf_op jit(solution)/shard_map/ppermute | solution.py:249
  47.5 0.9 %collective-permute-done.16.refs_2_ = f32[2,64]{1,0:T(2,128)S(1)} collective-permute-done((f32[2,64]{1,0:T(2,128)S(1)}, f32[2,64]{1,0:T(2,128)S(1)}, u32[]{:S(2)}, u32[]{:S(2)}) %collective-permute-start.16) | collective-permute-done | bytes 544 | tf_op jit(solution)/shard_map/ppermute | solution.py:249
  48.3 1.5 %collective-permute-done.17.refs_3_ = f32[2,64]{1,0:T(2,128)S(1)} collective-permute-done((f32[2,64]{1,0:T(2,128)S(1)}, f32[2,64]{1,0:T(2,128)S(1)}, u32[]{:S(2)}, u32[]{:S(2)}) %collective-permute-start.17) | collective-permute-done | bytes 544 | tf_op jit(solution)/shard_map/ppermute | solution.py:249
  49.9 0.4 collective-permute-start.18
  50.3 2.7 %collective-permute-start.20 = (f32[1,64]{1,0:T(1,128)S(1)}, f32[1,64]{1,0:T(1,128)S(1)}, u32[]{:S(2)}, u32[]{:S(2)}) collective-permute-start(f32[1,64]{1,0:T(1,128)S(1)} %get-tuple-element.63), channel_id=1, source_target_pairs={{0,9},{1,8},{2,11},{3,10},{4,13},{5,12},{6,15},{7,14},{8,1},{9,0},... | collective-permute-start | bytes 776 | tf_op jit(solution)/shard_map/ppermute | solution.py:252
  53.0 2.0 %collective-permute-done.14.received = bf16[32,2560]{1,0:T(8,128)(2,1)S(1)} collective-permute-done((bf16[32,2560]{1,0:T(8,128)(2,1)S(1)}, bf16[32,2560]{1,0:T(8,128)(2,1)S(1)}, u32[]{:S(2)}, u32[]{:S(2)}) %collective-permute-start.14) | collective-permute-done | bytes 163872 | tf_op jit(solution)/shard_map/ppermute | solution.py:249
  54.9 0.8 %finish.1.after = f32[32,2560]{1,0:T(8,128)} custom-call(f32[1,2560]{1,0:T(1,128)S(1)} %reshape.20.bias, f32[32,2560]{1,0:T(8,128)S(1)} %get-tuple-element.56.kept.after, bf16[32,2560]{1,0:T(8,128)(2,1)S(1)} %collective-permute-done.14.received), custom_call_target="tpu_custom_call" | custom-call | flops 655360 | bytes 829440 | tf_op jit(solution)/shard_map/finish/pallas_call | solution.py:21
  55.7 0.5 column_sum.3
  (14 shorter events, 0.1 us)
Async XLA Ops:
  2.4 8.9 %collective-permute-start.2 = (bf16[64,1024]{1,0:T(8,128)(2,1)S(1)}, bf16[64,1024]{1,0:T(8,128)(2,1)S(1)}, u32[]{:S(2)}, u32[]{:S(2)}) collective-permute-start(bf16[64,1024]{1,0:T(8,128)(2,1)S(1)} %get-tuple-element.36), channel_id=1, source_target_pairs={{0,2},{2,0},{4,6},{6,4},{8,10},{10,8},{12,14},{14,12},{1,3},{3,1},... | collective-permute-start | bytes 393224 | tf_op jit(solution)/shard_map/ppermute | solution.py:249
  5.4 5.9 %collective-permute-start.4 = (bf16[64,512]{1,0:T(8,128)(2,1)S(1)}, bf16[64,512]{1,0:T(8,128)(2,1)S(1)}, u32[]{:S(2)}, u32[]{:S(2)}) collective-permute-start(bf16[64,512]{1,0:T(8,128)(2,1)S(1)} %get-tuple-element.38), channel_id=1, source_target_pairs={{0,6},{2,4},{4,2},{6,0},{8,14},{10,12},{12,10},{14,8},{1,7},{3,5},... | collective-permute-start | bytes 196616 | tf_op jit(solution)/shard_map/ppermute | solution.py:249
  6.9 8.5 %collective-permute-start = (bf16[64,512]{1,0:T(8,128)(2,1)S(1)}, bf16[64,512]{1,0:T(8,128)(2,1)S(1)}, u32[]{:S(2)}, u32[]{:S(2)}) collective-permute-start(bf16[64,512]{1,0:T(8,128)(2,1)S(1)} %get-tuple-element.31), channel_id=1, source_target_pairs={{0,8},{2,10},{4,12},{6,14},{8,0},{10,2},{12,4},{14,6},{1,9},{3,11}... | collective-permute-start | bytes 196616 | tf_op jit(solution)/shard_map/ppermute | solution.py:249
  9.5 8.2 %collective-permute-start.1 = (bf16[64,512]{1,0:T(8,128)(2,1)S(1)}, bf16[64,512]{1,0:T(8,128)(2,1)S(1)}, u32[]{:S(2)}, u32[]{:S(2)}) collective-permute-start(bf16[64,512]{1,0:T(8,128)(2,1)S(1)} %get-tuple-element.32), channel_id=1, source_target_pairs={{0,10},{2,8},{4,14},{6,12},{8,2},{10,0},{12,6},{14,4},{1,11},{3,9}... | collective-permute-start | bytes 196616 | tf_op jit(solution)/shard_map/ppermute | solution.py:249
  10.8 9.5 %collective-permute-start.3 = (bf16[64,1024]{1,0:T(8,128)(2,1)S(1)}, bf16[64,1024]{1,0:T(8,128)(2,1)S(1)}, u32[]{:S(2)}, u32[]{:S(2)}) collective-permute-start(bf16[64,1024]{1,0:T(8,128)(2,1)S(1)} %get-tuple-element.37), channel_id=1, source_target_pairs={{0,4},{2,6},{4,0},{6,2},{8,12},{10,14},{12,8},{14,10},{1,5},{3,7},... | collective-permute-start | bytes 393224 | tf_op jit(solution)/shard_map/ppermute | solution.py:249
  11.3 9.0 %collective-permute-start.5 = (bf16[64,512]{1,0:T(8,128)(2,1)S(1)}, bf16[64,512]{1,0:T(8,128)(2,1)S(1)}, u32[]{:S(2)}, u32[]{:S(2)}) collective-permute-start(bf16[64,512]{1,0:T(8,128)(2,1)S(1)} %get-tuple-element.41), channel_id=1, source_target_pairs={{0,12},{2,14},{4,8},{6,10},{8,4},{10,6},{12,0},{14,2},{1,13},{3,15... | collective-permute-start | bytes 196616 | tf_op jit(solution)/shard_map/ppermute | solution.py:249
  15.4 7.0 %collective-permute-start.6 = (bf16[64,512]{1,0:T(8,128)(2,1)S(1)}, bf16[64,512]{1,0:T(8,128)(2,1)S(1)}, u32[]{:S(2)}, u32[]{:S(2)}) collective-permute-start(bf16[64,512]{1,0:T(8,128)(2,1)S(1)} %get-tuple-element.42), channel_id=1, source_target_pairs={{0,14},{2,12},{4,10},{6,8},{8,6},{10,4},{12,2},{14,0},{1,15},{3,13... | collective-permute-start | bytes 196616 | tf_op jit(solution)/shard_map/ppermute | solution.py:249
  22.7 2.2 %collective-permute-start.8 = (bf16[256,512]{1,0:T(8,128)(2,1)S(1)}, bf16[256,512]{1,0:T(8,128)(2,1)S(1)}, u32[]{:S(2)}, u32[]{:S(2)}) collective-permute-start(bf16[256,512]{1,0:T(8,128)(2,1)S(1)} %get-tuple-element.45.own), channel_id=1, source_target_pairs={{0,1},{1,0},{2,3},{3,2},{4,5},{5,4},{6,7},{7,6},{8,9},{9,8},{10,11... | collective-permute-start | bytes 786440 | tf_op jit(solution)/shard_map/ppermute | solution.py:255
  22.8 9.7 %collective-permute-start.7 = (bf16[128,512]{1,0:T(8,128)(2,1)S(1)}, bf16[128,512]{1,0:T(8,128)(2,1)S(1)}, u32[]{:S(2)}, u32[]{:S(2)}) collective-permute-start(bf16[128,512]{1,0:T(8,128)(2,1)S(1)} %get-tuple-element.43.near), channel_id=1, source_target_pairs={{0,8},{2,10},{4,12},{6,14},{8,0},{10,2},{12,4},{14,6},{1,9},{3,11}... | collective-permute-start | bytes 393224 | tf_op jit(solution)/shard_map/ppermute | solution.py:249
  25.5 10.2 %collective-permute-start.10 = (bf16[128,1280]{1,0:T(8,128)(2,1)S(1)}, bf16[128,1280]{1,0:T(8,128)(2,1)S(1)}, u32[]{:S(2)}, u32[]{:S(2)}) collective-permute-start(bf16[128,1280]{1,0:T(8,128)(2,1)S(1)} %get-tuple-element.49), channel_id=1, source_target_pairs={{0,2},{2,0},{4,6},{6,4},{8,10},{10,8},{12,14},{14,12},{1,3},{3,1},... | collective-permute-start | bytes 983048 | tf_op jit(solution)/shard_map/ppermute | solution.py:249
  27.0 19.2 %copy-start = (f32[2560]{0:T(1024)S(1)}, f32[2560]{0:T(1024)}, u32[]{:S(2)}) copy-start(f32[2560]{0:T(1024)} %param.17) | copy-start | bytes 30724
  27.0 12.2 %collective-permute-start.11 = (bf16[128,1280]{1,0:T(8,128)(2,1)S(1)}, bf16[128,1280]{1,0:T(8,128)(2,1)S(1)}, u32[]{:S(2)}, u32[]{:S(2)}) collective-permute-start(bf16[128,1280]{1,0:T(8,128)(2,1)S(1)} %get-tuple-element.47.after), channel_id=1, source_target_pairs={{0,4},{2,6},{4,0},{6,2},{8,12},{10,14},{12,8},{14,10},{1,5},{3,7},... | collective-permute-start | bytes 983048 | tf_op jit(solution)/shard_map/ppermute | solution.py:249
  32.5 7.8 %collective-permute-start.9 = (bf16[192,512]{1,0:T(8,128)(2,1)S(1)}, bf16[192,512]{1,0:T(8,128)(2,1)S(1)}, u32[]{:S(2)}, u32[]{:S(2)}) collective-permute-start(bf16[192,512]{1,0:T(8,128)(2,1)S(1)} %gather.1), channel_id=1, source_target_pairs={{0,2},{2,0},{4,6},{6,4},{8,10},{10,8},{12,14},{14,12},{1,3},{3,1},... | collective-permute-start | bytes 589832 | tf_op jit(solution)/shard_map/ppermute | solution.py:249
  39.2 7.0 %collective-permute-start.13 = (bf16[64,1280]{1,0:T(8,128)(2,1)S(1)}, bf16[64,1280]{1,0:T(8,128)(2,1)S(1)}, u32[]{:S(2)}, u32[]{:S(2)}) collective-permute-start(bf16[64,1280]{1,0:T(8,128)(2,1)S(1)} %get-tuple-element.55), channel_id=1, source_target_pairs={{0,2},{2,0},{4,6},{6,4},{8,10},{10,8},{12,14},{14,12},{1,3},{3,1},... | collective-permute-start | bytes 491528 | tf_op jit(solution)/shard_map/ppermute | solution.py:249
  39.3 7.0 %collective-permute-start.12 = (bf16[64,1280]{1,0:T(8,128)(2,1)S(1)}, bf16[64,1280]{1,0:T(8,128)(2,1)S(1)}, u32[]{:S(2)}, u32[]{:S(2)}) collective-permute-start(bf16[64,1280]{1,0:T(8,128)(2,1)S(1)} %get-tuple-element.54), channel_id=1, source_target_pairs={{0,4},{2,6},{4,0},{6,2},{8,12},{10,14},{12,8},{14,10},{1,5},{3,7},... | collective-permute-start | bytes 491528 | tf_op jit(solution)/shard_map/ppermute | solution.py:249
  42.3 5.1 %collective-permute-start.15 = (f32[2,64]{1,0:T(2,128)S(1)}, f32[2,64]{1,0:T(2,128)S(1)}, u32[]{:S(2)}, u32[]{:S(2)}) collective-permute-start(f32[2,64]{1,0:T(2,128)S(1)} %get-tuple-element.61), channel_id=1, source_target_pairs={{0,4},{2,6},{4,0},{6,2},{8,12},{10,14},{12,8},{14,10},{1,5},{3,7},... | collective-permute-start | bytes 1544 | tf_op jit(solution)/shard_map/ppermute | solution.py:249
  44.8 3.6 %collective-permute-start.16 = (f32[2,64]{1,0:T(2,128)S(1)}, f32[2,64]{1,0:T(2,128)S(1)}, u32[]{:S(2)}, u32[]{:S(2)}) collective-permute-start(f32[2,64]{1,0:T(2,128)S(1)} %get-tuple-element.60), channel_id=1, source_target_pairs={{0,2},{2,0},{4,6},{6,4},{8,10},{10,8},{12,14},{14,12},{1,3},{3,1},... | collective-permute-start | bytes 1544 | tf_op jit(solution)/shard_map/ppermute | solution.py:249
  45.4 4.5 %collective-permute-start.17 = (f32[2,64]{1,0:T(2,128)S(1)}, f32[2,64]{1,0:T(2,128)S(1)}, u32[]{:S(2)}, u32[]{:S(2)}) collective-permute-start(f32[2,64]{1,0:T(2,128)S(1)} %get-tuple-element.59), channel_id=1, source_target_pairs={{0,6},{2,4},{4,2},{6,0},{8,14},{10,12},{12,10},{14,8},{1,7},{3,5},... | collective-permute-start | bytes 1544 | tf_op jit(solution)/shard_map/ppermute | solution.py:249
  46.3 8.6 %collective-permute-start.14 = (bf16[32,2560]{1,0:T(8,128)(2,1)S(1)}, bf16[32,2560]{1,0:T(8,128)(2,1)S(1)}, u32[]{:S(2)}, u32[]{:S(2)}) collective-permute-start(bf16[32,2560]{1,0:T(8,128)(2,1)S(1)} %get-tuple-element.57), channel_id=1, source_target_pairs={{0,8},{2,10},{4,12},{6,14},{8,0},{10,2},{12,4},{14,6},{1,9},{3,11}... | collective-permute-start | bytes 491528 | tf_op jit(solution)/shard_map/ppermute | solution.py:249
  49.9 5.8 %collective-permute-start.18 = (f32[1,64]{1,0:T(1,128)S(1)}, f32[1,64]{1,0:T(1,128)S(1)}, u32[]{:S(2)}, u32[]{:S(2)}) collective-permute-start(f32[1,64]{1,0:T(1,128)S(1)} %get-tuple-element.63), channel_id=1, source_target_pairs={{0,8},{2,10},{4,12},{6,14},{8,0},{10,2},{12,4},{14,6},{1,9},{3,11}... | collective-permute-start | bytes 776 | tf_op jit(solution)/shard_map/ppermute | solution.py:249
  50.3 5.4 %collective-permute-start.19 = (f32[1,64]{1,0:T(1,128)S(1)}, f32[1,64]{1,0:T(1,128)S(1)}, u32[]{:S(2)}, u32[]{:S(2)}) collective-permute-start(f32[1,64]{1,0:T(1,128)S(1)} %get-tuple-element.64.refs_0_), channel_id=1, source_target_pairs={{0,1},{1,0},{2,3},{3,2},{4,5},{5,4},{6,7},{7,6},{8,9},{9,8},{10,11... | collective-permute-start | bytes 776 | tf_op jit(solution)/shard_map/ppermute | solution.py:255
  50.3 5.4 %collective-permute-start.20 = (f32[1,64]{1,0:T(1,128)S(1)}, f32[1,64]{1,0:T(1,128)S(1)}, u32[]{:S(2)}, u32[]{:S(2)}) collective-permute-start(f32[1,64]{1,0:T(1,128)S(1)} %get-tuple-element.63), channel_id=1, source_target_pairs={{0,9},{1,8},{2,11},{3,10},{4,13},{5,12},{6,15},{7,14},{8,1},{9,0},... | collective-permute-start | bytes 776 | tf_op jit(solution)/shard_map/ppermute | solution.py:252

commit v14 on v13

--- a/solution.py
+++ b/solution.py
@@ -173,9 +173,10 @@
     *parts, keep, sent = refs
     count = len(parts) // 2
     rows = keep.shape[0]
-    width = keep.shape[1] // count
+    first = 0
     for c in range(count):
-        lanes = slice(c * width, (c + 1) * width)
+        lanes = slice(first, first + parts[c].shape[1])
+        first = lanes.stop
         total = parts[c][...] + parts[count + c][...].astype(jnp.float32)
         keep[:, lanes] = total[:rows]
         sent[:, lanes] = total[rows:].astype(jnp.bfloat16)
@@ -227,8 +228,13 @@
         columns[i : i + 1, :] = sums[:, at * rows : (at + 1) * rows]
 
 
-def finish_kernel(bias, kept, received, out):
+def finish_kernel(bias, kept, received, *refs):
+    *parts, out, scores = refs
     out[...] = kept[...] + received[...].astype(jnp.float32) + bias[...]
+    total = parts[0][...]
+    for part in parts[1:]:
+        total += part[...]
+    scores[...] = total / QUERY_HEADS
 
 
 def shards(queries, keys, values, hidden, norm_gain, retained_lists, counts, affine_matrix, affine_offset_vector):
@@ -239,7 +245,8 @@
     width = affine_matrix.shape[1]
     survivors = n * rows // 2
     lines = survivors // n
-    chunk = width // 2
+    cut = width * 3 // 5 // HEAD_SIZE * HEAD_SIZE
+    chunks = [cut, width - cut]
     near = survivors // 2
     f32, bf16, i32 = jnp.float32, jnp.bfloat16, jnp.int32
     shape = jax.ShapeDtypeStruct
@@ -305,13 +312,13 @@
     )
     products = [
         call(
-            functools.partial(project_kernel, c * chunk, halving_order(n, masks[c])),
+            functools.partial(project_kernel, c * cut, halving_order(n, masks[c])),
             "project",
             (product, other, matrix),
             [shape((near, chunk), f32), shape((near, chunk), bf16)],
             2 * survivors * half * chunk,
         )
-        for c in range(2)
+        for c, chunk in enumerate(chunks)
     ]
     far = trade(even, n // 2)
     (gathered,) = call(
@@ -326,7 +333,7 @@
     kept = [product[0] for product in products]
     arrived = [trade(product[1], masks[c][0]) for c, product in enumerate(products)]
     lines_left = near // 2
-    for c in (0, 1):
+    for c, chunk in enumerate(chunks):
         keep, sent = call(
             hop_sum_kernel,
             "hop_sum",
@@ -378,14 +385,13 @@
         if mask == rest[-1]:
             pieces += [swap(own), trade_across(far, mask)]
 
-    (triples,) = call(
+    triples, scores = call(
         finish_kernel,
         "finish",
-        (affine_offset_vector.reshape(1, width), kept[0], arrived[0]),
-        [shape((lines, width), f32)],
+        (affine_offset_vector.reshape(1, width), kept[0], arrived[0], *pieces),
+        [shape((lines, width), f32), shape((1, rows), f32)],
         n * lines * width,
     )
-    scores = column_sum(pieces, triples, 1.0 / QUERY_HEADS, remote=1)
     return (context, scores.reshape(rows), triples)
 
 

time: 56.4 us -> 57.3 us (1.016)
  starting transfers between devices: 26.1 us -> 28 us
  Pallas kernels: 10.2 us -> 9.56 us
    ppermute x18, starting transfers between devices: 23.4 us -> 25.3 us  [trade(): return lax.ppermute(x, 'seq', [(i, i ^ k) for i in range(n)])]
    pallas_call x15 -> x14, Pallas kernels: 10.2 us -> 9.56 us  [call(): pl.pallas_call(body, out_shape=list(outputs), in_specs=in_specs or [VMEM]...]
  transfers between devices with their start and end apart: 21 -> 21, of which waited for: 8 -> 8; matrix products, arithmetic and copies ran while one was open for 0% -> 0% of each run, Pallas kernels for 14% -> 12%
where the time goes in v14:
time: 57.3 us; the launch traced here: 57.2 us
  starting transfers between devices  28 us (49%)
  waiting for transfers between devices  18.8 us (33%)
  Pallas kernels  9.56 us (17%)
  between operations  0.78 us (1%)
    ppermute x18, starting transfers between devices, trade(): return lax.ppermute(x, 'seq', [(i, i ^ k) for i in range(n)])  25.3 us
    ppermute x18, waiting for transfers between devices, trade(): return lax.ppermute(x, 'seq', [(i, i ^ k) for i in range(n)])  18.8 us
    pallas_call x14, Pallas kernels, call(): pl.pallas_call(body, out_shape=list(outputs), in_specs=in_specs or [VMEM]...  9.56 us
    ppermute x1, starting transfers between devices, trade_across(): lax.ppermute(x, ('seq', 'ten'), [(2 * i + t, 2 * (i ^ k) + 1 - t) for i i...  2.57 us
  transfers between devices with their start and end apart: 21, of which 8 were waited for; matrix products, arithmetic and copies ran while one was open for 0% of the time, Pallas kernels for 12%

profile of v14, /device:TPU:0, one launch (start us, length us, event | category | flops | bytes accessed | tf_op | source)
XLA Modules:
  0.0 57.2 jit_solution(9414701210231324156)
XLA Ops:
  0.6 1.7 %norm_select.1 = (bf16[64,1024]{1,0:T(8,128)(2,1)S(1)}, bf16[64,1024]{1,0:T(8,128)(2,1)S(1)}, bf16[64,1024]{1,0:T(8,128)(2,1)S(1)}, bf16[64,512]{1,0:T(8,128)(2,...) custom-call(bf16[64,8192]{1,0:T(8,128)(2,1)} %hidden_in.1, ...), custom_call_target="tpu_custom_call" | custom-call | flops 2097152 | bytes 1868032 | tf_op jit(solution)/shard_map/norm_select/pallas_call | solution.py:21
  2.4 3.0 %collective-permute-start.2 = (bf16[64,1024]{1,0:T(8,128)(2,1)S(1)}, bf16[64,1024]{1,0:T(8,128)(2,1)S(1)}, u32[]{:S(2)}, u32[]{:S(2)}) collective-permute-start(bf16[64,1024]{1,0:T(8,128)(2,1)S(1)} %get-tuple-element.38), channel_id=1, source_target_pairs={{0,2},{2,0},{4,6},{6,4},{8,10},{10,8},{12,14},{14,12},{1,3},{3,1},... | collective-permute-start | bytes 393224 | tf_op jit(solution)/shard_map/ppermute | solution.py:256
  5.4 1.5 %collective-permute-start.4 = (bf16[64,512]{1,0:T(8,128)(2,1)S(1)}, bf16[64,512]{1,0:T(8,128)(2,1)S(1)}, u32[]{:S(2)}, u32[]{:S(2)}) collective-permute-start(bf16[64,512]{1,0:T(8,128)(2,1)S(1)} %get-tuple-element.40), channel_id=1, source_target_pairs={{0,6},{2,4},{4,2},{6,0},{8,14},{10,12},{12,10},{14,8},{1,7},{3,5},... | collective-permute-start | bytes 196616 | tf_op jit(solution)/shard_map/ppermute | solution.py:256
  6.9 2.6 %collective-permute-start = (bf16[64,512]{1,0:T(8,128)(2,1)S(1)}, bf16[64,512]{1,0:T(8,128)(2,1)S(1)}, u32[]{:S(2)}, u32[]{:S(2)}) collective-permute-start(bf16[64,512]{1,0:T(8,128)(2,1)S(1)} %get-tuple-element.33), channel_id=1, source_target_pairs={{0,8},{2,10},{4,12},{6,14},{8,0},{10,2},{12,4},{14,6},{1,9},{3,11}... | collective-permute-start | bytes 196616 | tf_op jit(solution)/shard_map/ppermute | solution.py:256
  9.5 1.3 %collective-permute-start.1 = (bf16[64,512]{1,0:T(8,128)(2,1)S(1)}, bf16[64,512]{1,0:T(8,128)(2,1)S(1)}, u32[]{:S(2)}, u32[]{:S(2)}) collective-permute-start(bf16[64,512]{1,0:T(8,128)(2,1)S(1)} %get-tuple-element.34), channel_id=1, source_target_pairs={{0,10},{2,8},{4,14},{6,12},{8,2},{10,0},{12,6},{14,4},{1,11},{3,9}... | collective-permute-start | bytes 196616 | tf_op jit(solution)/shard_map/ppermute | solution.py:256
  10.8 0.4 collective-permute-start.3
  11.3 0.0 collective-permute-done.4.refs_3_
  11.3 0.0 collective-permute-done.2.refs_2_.refs_1_
  11.3 4.2 %collective-permute-start.5 = (bf16[64,512]{1,0:T(8,128)(2,1)S(1)}, bf16[64,512]{1,0:T(8,128)(2,1)S(1)}, u32[]{:S(2)}, u32[]{:S(2)}) collective-permute-start(bf16[64,512]{1,0:T(8,128)(2,1)S(1)} %get-tuple-element.43), channel_id=1, source_target_pairs={{0,12},{2,14},{4,8},{6,10},{8,4},{10,6},{12,0},{14,2},{1,13},{3,15... | collective-permute-start | bytes 196616 | tf_op jit(solution)/shard_map/ppermute | solution.py:256
  15.4 0.0 collective-permute-start.6
  15.5 0.0 collective-permute-done.refs_0_.refs_4_
  15.5 2.3 %collective-permute-done.1.refs_1_.refs_5_ = bf16[64,512]{1,0:T(8,128)(2,1)S(1)} collective-permute-done((bf16[64,512]{1,0:T(8,128)(2,1)S(1)}, bf16[64,512]{1,0:T(8,128)(2,1)S(1)}, u32[]{:S(2)}, u32[]{:S(2)}) %collective-permute-start.1) | collective-permute-done | bytes 65568 | tf_op jit(solution)/shard_map/ppermute | solution.py:256
  17.8 2.5 %stage.1 = (bf16[1024,2560]{1,0:T(8,128)(2,1)S(1)}, bf16[64,2048]{1,0:T(8,128)(2,1)S(1)}, s32[1,512]{1,0:T(1,128)S(1)}) custom-call(s32[8]{0:T(128)} %counts_in.1, bf16[1024,2560]{1,0:T(8,128)(2,1)} %matrix_in.1, bf16[64,2048]{1,0:T(8,128)(2,1)} %queries_in.1, bf16[64,512]{1,0:T(8,128)(2,1)S(1)} %collective-permute-done.refs_0_.refs_4_, ...), custom_call_target="tpu_custom_call" | custom-call | flops 3932160000 | bytes 11143200 | tf_op jit(solution)/shard_map/stage/pallas_call | solution.py:21
  20.3 0.0 collective-permute-done.3.refs_2_
  20.3 0.0 collective-permute-done.5.refs_6_
  20.3 2.1 %collective-permute-done.6.refs_7_ = bf16[64,512]{1,0:T(8,128)(2,1)S(1)} collective-permute-done((bf16[64,512]{1,0:T(8,128)(2,1)S(1)}, bf16[64,512]{1,0:T(8,128)(2,1)S(1)}, u32[]{:S(2)}, u32[]{:S(2)}) %collective-permute-start.6) | collective-permute-done | bytes 65568 | tf_op jit(solution)/shard_map/ppermute | solution.py:256
  22.4 0.3 compact.1
  22.7 0.1 collective-permute-start.8
  22.8 1.1 %collective-permute-start.7 = (bf16[128,512]{1,0:T(8,128)(2,1)S(1)}, bf16[128,512]{1,0:T(8,128)(2,1)S(1)}, u32[]{:S(2)}, u32[]{:S(2)}) collective-permute-start(bf16[128,512]{1,0:T(8,128)(2,1)S(1)} %get-tuple-element.45.near), channel_id=1, source_target_pairs={{0,8},{2,10},{4,12},{6,14},{8,0},{10,2},{12,4},{14,6},{1,9},{3,11}... | collective-permute-start | bytes 393224 | tf_op jit(solution)/shard_map/ppermute | solution.py:256
  23.9 1.0 %project_own.1.product = f32[256,2560]{1,0:T(8,128)S(1)} custom-call(bf16[256,512]{1,0:T(8,128)(2,1)S(1)} %get-tuple-element.47.own, bf16[1024,2560]{1,0:T(8,128)(2,1)S(1)} %get-tuple-element.48.matrix), custom_call_target="tpu_custom_call" | custom-call | flops 671088640 | bytes 8126464 | tf_op jit(solution)/shard_map/project_own/pallas_call | solution.py:21
  24.9 0.0 collective-permute-done.8.other
  24.9 0.6 %project.3 = (f32[128,1536]{1,0:T(8,128)S(1)}, bf16[128,1536]{1,0:T(8,128)(2,1)S(1)}) custom-call(f32[256,2560]{1,0:T(8,128)S(1)} %project_own.1.product, bf16[256,512]{1,0:T(8,128)(2,1)S(1)} %collective-permute-done.8.other, bf16[1024,2560]{1,0:T(8,128)(2,1)S(1)} %get-tuple-element.48.matrix), custom_call_target="tpu_custom_call" | custom-call | flops 402653184 | bytes 9306112 | tf_op jit(solution)/shard_map/project/pallas_call | solution.py:21
  25.5 0.9 %collective-permute-start.10 = (bf16[128,1536]{1,0:T(8,128)(2,1)S(1)}, bf16[128,1536]{1,0:T(8,128)(2,1)S(1)}, u32[]{:S(2)}, u32[]{:S(2)}) collective-permute-start(bf16[128,1536]{1,0:T(8,128)(2,1)S(1)} %get-tuple-element.51), channel_id=1, source_target_pairs={{0,2},{2,0},{4,6},{6,4},{8,10},{10,8},{12,14},{14,12},{1,3},{3,1},... | collective-permute-start | bytes 1179656 | tf_op jit(solution)/shard_map/ppermute | solution.py:256
  26.4 0.4 project.2
  26.9 0.0 copy-start
  26.9 1.7 %collective-permute-start.11 = (bf16[128,1024]{1,0:T(8,128)(2,1)S(1)}, bf16[128,1024]{1,0:T(8,128)(2,1)S(1)}, u32[]{:S(2)}, u32[]{:S(2)}) collective-permute-start(bf16[128,1024]{1,0:T(8,128)(2,1)S(1)} %get-tuple-element.49.after), channel_id=1, source_target_pairs={{0,4},{2,6},{4,0},{6,2},{8,12},{10,14},{12,8},{14,10},{1,5},{3,7},... | collective-permute-start | bytes 786440 | tf_op jit(solution)/shard_map/ppermute | solution.py:256
  28.5 4.0 %collective-permute-done.7.far = bf16[128,512]{1,0:T(8,128)(2,1)S(1)} collective-permute-done((bf16[128,512]{1,0:T(8,128)(2,1)S(1)}, bf16[128,512]{1,0:T(8,128)(2,1)S(1)}, u32[]{:S(2)}, u32[]{:S(2)}) %collective-permute-start.7) | collective-permute-done | bytes 131104 | tf_op jit(solution)/shard_map/ppermute | solution.py:256
  32.6 0.1 collective-permute-start.9
  32.6 4.9 %collective-permute-done.10.received = bf16[128,1536]{1,0:T(8,128)(2,1)S(1)} collective-permute-done((bf16[128,1536]{1,0:T(8,128)(2,1)S(1)}, bf16[128,1536]{1,0:T(8,128)(2,1)S(1)}, u32[]{:S(2)}, u32[]{:S(2)}) %collective-permute-start.10) | collective-permute-done | bytes 393248 | tf_op jit(solution)/shard_map/ppermute | solution.py:256
  37.6 0.1 hop_sum.2
  37.6 0.0 collective-permute-done.11.received
  37.7 0.9 %collective-permute-start.13 = (bf16[64,1024]{1,0:T(8,128)(2,1)S(1)}, bf16[64,1024]{1,0:T(8,128)(2,1)S(1)}, u32[]{:S(2)}, u32[]{:S(2)}) collective-permute-start(bf16[64,1024]{1,0:T(8,128)(2,1)S(1)} %get-tuple-element.57), channel_id=1, source_target_pairs={{0,2},{2,0},{4,6},{6,4},{8,10},{10,8},{12,14},{14,12},{1,3},{3,1},... | collective-permute-start | bytes 393224 | tf_op jit(solution)/shard_map/ppermute | solution.py:256
  38.6 1.7 %collective-permute-start.12 = (bf16[64,1536]{1,0:T(8,128)(2,1)S(1)}, bf16[64,1536]{1,0:T(8,128)(2,1)S(1)}, u32[]{:S(2)}, u32[]{:S(2)}) collective-permute-start(bf16[64,1536]{1,0:T(8,128)(2,1)S(1)} %get-tuple-element.56), channel_id=1, source_target_pairs={{0,4},{2,6},{4,0},{6,2},{8,12},{10,14},{12,8},{14,10},{1,5},{3,7},... | collective-permute-start | bytes 589832 | tf_op jit(solution)/shard_map/ppermute | solution.py:256
  40.2 1.5 %collective-permute-done.9.odd = bf16[192,512]{1,0:T(8,128)(2,1)S(1)} collective-permute-done((bf16[192,512]{1,0:T(8,128)(2,1)S(1)}, bf16[192,512]{1,0:T(8,128)(2,1)S(1)}, u32[]{:S(2)}, u32[]{:S(2)}) %collective-permute-start.9) | collective-permute-done | bytes 196640 | tf_op jit(solution)/shard_map/ppermute | solution.py:256
  41.8 2.0 %attention.1 = (f32[64,2048]{1,0:T(8,128)}, f32[8,64]{1,0:T(8,128)S(1)}) custom-call(bf16[64,2048]{1,0:T(8,128)(2,1)S(1)} %get-tuple-element.35.queries, bf16[128,512]{1,0:T(8,128)(2,1)S(1)} %get-tuple-element.45.near, bf16[128,512]{1,0:T(8,128)(2,1)S(1)} %collective-permute-done.7.far, bf16[64,512]{1,0:T(8,128)(2,1)S(1)} %get-tuple-element.46.pair, ...), custom_call_target="tpu_custom_call" | custom-call | flops 268435456 | bytes 1705984 | tf_op jit(solution)/shard_map/attention/pallas_call | solution.py:21
  43.8 2.4 %collective-permute-start.15 = (f32[2,64]{1,0:T(2,128)S(1)}, f32[2,64]{1,0:T(2,128)S(1)}, u32[]{:S(2)}, u32[]{:S(2)}) collective-permute-start(f32[2,64]{1,0:T(2,128)S(1)} %get-tuple-element.65), channel_id=1, source_target_pairs={{0,4},{2,6},{4,0},{6,2},{8,12},{10,14},{12,8},{14,10},{1,5},{3,7},... | collective-permute-start | bytes 1544 | tf_op jit(solution)/shard_map/ppermute | solution.py:256
  46.2 0.0 collective-permute-start.16
  46.2 1.5 %collective-permute-start.17 = (f32[2,64]{1,0:T(2,128)S(1)}, f32[2,64]{1,0:T(2,128)S(1)}, u32[]{:S(2)}, u32[]{:S(2)}) collective-permute-start(f32[2,64]{1,0:T(2,128)S(1)} %get-tuple-element.63), channel_id=1, source_target_pairs={{0,6},{2,4},{4,2},{6,0},{8,14},{10,12},{12,10},{14,8},{1,7},{3,5},... | collective-permute-start | bytes 1544 | tf_op jit(solution)/shard_map/ppermute | solution.py:256
  47.6 0.0 collective-permute-done.13.refs_3_
  47.7 0.1 hop_sum_both.1
  47.7 1.5 %collective-permute-start.14 = (bf16[32,2560]{1,0:T(8,128)(2,1)S(1)}, bf16[32,2560]{1,0:T(8,128)(2,1)S(1)}, u32[]{:S(2)}, u32[]{:S(2)}) collective-permute-start(bf16[32,2560]{1,0:T(8,128)(2,1)S(1)} %get-tuple-element.59), channel_id=1, source_target_pairs={{0,8},{2,10},{4,12},{6,14},{8,0},{10,2},{12,4},{14,6},{1,9},{3,11}... | collective-permute-start | bytes 491528 | tf_op jit(solution)/shard_map/ppermute | solution.py:256
  49.3 0.0 collective-permute-done.15.refs_1_
  49.3 0.5 collective-permute-done.16.refs_2_
  49.7 0.9 %collective-permute-done.17.refs_3_ = f32[2,64]{1,0:T(2,128)S(1)} collective-permute-done((f32[2,64]{1,0:T(2,128)S(1)}, f32[2,64]{1,0:T(2,128)S(1)}, u32[]{:S(2)}, u32[]{:S(2)}) %collective-permute-start.17) | collective-permute-done | bytes 544 | tf_op jit(solution)/shard_map/ppermute | solution.py:256
  50.7 0.5 collective-permute-start.18
  51.2 2.6 %collective-permute-start.20 = (f32[1,64]{1,0:T(1,128)S(1)}, f32[1,64]{1,0:T(1,128)S(1)}, u32[]{:S(2)}, u32[]{:S(2)}) collective-permute-start(f32[1,64]{1,0:T(1,128)S(1)} %get-tuple-element.67), channel_id=1, source_target_pairs={{0,9},{1,8},{2,11},{3,10},{4,13},{5,12},{6,15},{7,14},{8,1},{9,0},... | collective-permute-start | bytes 776 | tf_op jit(solution)/shard_map/ppermute | solution.py:259
  53.8 2.6 %collective-permute-done.18.refs_1_ = f32[1,64]{1,0:T(1,128)S(1)} collective-permute-done((f32[1,64]{1,0:T(1,128)S(1)}, f32[1,64]{1,0:T(1,128)S(1)}, u32[]{:S(2)}, u32[]{:S(2)}) %collective-permute-start.18) | collective-permute-done | bytes 288 | tf_op jit(solution)/shard_map/ppermute | solution.py:256
  56.4 0.8 %finish.1 = (f32[32,2560]{1,0:T(8,128)}, f32[1,64]{1,0:T(1,128)}) custom-call(f32[1,2560]{1,0:T(1,128)S(1)} %reshape.20.bias, f32[32,2560]{1,0:T(8,128)S(1)} %get-tuple-element.58.after.kept, bf16[32,2560]{1,0:T(8,128)(2,1)S(1)} %collective-permute-done.14.received, f32[1,64]{1,0:T(1,128)S(1)} %get-tuple-element.68.refs_0_, ...), custom_call_target="tpu_custom_call" | custom-call | flops 655360 | bytes 830720 | tf_op jit(solution)/shard_map/finish/pallas_call | solution.py:21
  (13 shorter events, 0.1 us)
Async XLA Ops:
  2.4 8.9 %collective-permute-start.2 = (bf16[64,1024]{1,0:T(8,128)(2,1)S(1)}, bf16[64,1024]{1,0:T(8,128)(2,1)S(1)}, u32[]{:S(2)}, u32[]{:S(2)}) collective-permute-start(bf16[64,1024]{1,0:T(8,128)(2,1)S(1)} %get-tuple-element.38), channel_id=1, source_target_pairs={{0,2},{2,0},{4,6},{6,4},{8,10},{10,8},{12,14},{14,12},{1,3},{3,1},... | collective-permute-start | bytes 393224 | tf_op jit(solution)/shard_map/ppermute | solution.py:256
  5.4 5.9 %collective-permute-start.4 = (bf16[64,512]{1,0:T(8,128)(2,1)S(1)}, bf16[64,512]{1,0:T(8,128)(2,1)S(1)}, u32[]{:S(2)}, u32[]{:S(2)}) collective-permute-start(bf16[64,512]{1,0:T(8,128)(2,1)S(1)} %get-tuple-element.40), channel_id=1, source_target_pairs={{0,6},{2,4},{4,2},{6,0},{8,14},{10,12},{12,10},{14,8},{1,7},{3,5},... | collective-permute-start | bytes 196616 | tf_op jit(solution)/shard_map/ppermute | solution.py:256
  6.9 8.5 %collective-permute-start = (bf16[64,512]{1,0:T(8,128)(2,1)S(1)}, bf16[64,512]{1,0:T(8,128)(2,1)S(1)}, u32[]{:S(2)}, u32[]{:S(2)}) collective-permute-start(bf16[64,512]{1,0:T(8,128)(2,1)S(1)} %get-tuple-element.33), channel_id=1, source_target_pairs={{0,8},{2,10},{4,12},{6,14},{8,0},{10,2},{12,4},{14,6},{1,9},{3,11}... | collective-permute-start | bytes 196616 | tf_op jit(solution)/shard_map/ppermute | solution.py:256
  9.5 8.2 %collective-permute-start.1 = (bf16[64,512]{1,0:T(8,128)(2,1)S(1)}, bf16[64,512]{1,0:T(8,128)(2,1)S(1)}, u32[]{:S(2)}, u32[]{:S(2)}) collective-permute-start(bf16[64,512]{1,0:T(8,128)(2,1)S(1)} %get-tuple-element.34), channel_id=1, source_target_pairs={{0,10},{2,8},{4,14},{6,12},{8,2},{10,0},{12,6},{14,4},{1,11},{3,9}... | collective-permute-start | bytes 196616 | tf_op jit(solution)/shard_map/ppermute | solution.py:256
  10.8 9.5 %collective-permute-start.3 = (bf16[64,1024]{1,0:T(8,128)(2,1)S(1)}, bf16[64,1024]{1,0:T(8,128)(2,1)S(1)}, u32[]{:S(2)}, u32[]{:S(2)}) collective-permute-start(bf16[64,1024]{1,0:T(8,128)(2,1)S(1)} %get-tuple-element.39), channel_id=1, source_target_pairs={{0,4},{2,6},{4,0},{6,2},{8,12},{10,14},{12,8},{14,10},{1,5},{3,7},... | collective-permute-start | bytes 393224 | tf_op jit(solution)/shard_map/ppermute | solution.py:256
  11.3 9.0 %collective-permute-start.5 = (bf16[64,512]{1,0:T(8,128)(2,1)S(1)}, bf16[64,512]{1,0:T(8,128)(2,1)S(1)}, u32[]{:S(2)}, u32[]{:S(2)}) collective-permute-start(bf16[64,512]{1,0:T(8,128)(2,1)S(1)} %get-tuple-element.43), channel_id=1, source_target_pairs={{0,12},{2,14},{4,8},{6,10},{8,4},{10,6},{12,0},{14,2},{1,13},{3,15... | collective-permute-start | bytes 196616 | tf_op jit(solution)/shard_map/ppermute | solution.py:256
  15.4 7.0 %collective-permute-start.6 = (bf16[64,512]{1,0:T(8,128)(2,1)S(1)}, bf16[64,512]{1,0:T(8,128)(2,1)S(1)}, u32[]{:S(2)}, u32[]{:S(2)}) collective-permute-start(bf16[64,512]{1,0:T(8,128)(2,1)S(1)} %get-tuple-element.44), channel_id=1, source_target_pairs={{0,14},{2,12},{4,10},{6,8},{8,6},{10,4},{12,2},{14,0},{1,15},{3,13... | collective-permute-start | bytes 196616 | tf_op jit(solution)/shard_map/ppermute | solution.py:256
  22.7 2.2 %collective-permute-start.8 = (bf16[256,512]{1,0:T(8,128)(2,1)S(1)}, bf16[256,512]{1,0:T(8,128)(2,1)S(1)}, u32[]{:S(2)}, u32[]{:S(2)}) collective-permute-start(bf16[256,512]{1,0:T(8,128)(2,1)S(1)} %get-tuple-element.47.own), channel_id=1, source_target_pairs={{0,1},{1,0},{2,3},{3,2},{4,5},{5,4},{6,7},{7,6},{8,9},{9,8},{10,11... | collective-permute-start | bytes 786440 | tf_op jit(solution)/shard_map/ppermute | solution.py:262
  22.8 9.7 %collective-permute-start.7 = (bf16[128,512]{1,0:T(8,128)(2,1)S(1)}, bf16[128,512]{1,0:T(8,128)(2,1)S(1)}, u32[]{:S(2)}, u32[]{:S(2)}) collective-permute-start(bf16[128,512]{1,0:T(8,128)(2,1)S(1)} %get-tuple-element.45.near), channel_id=1, source_target_pairs={{0,8},{2,10},{4,12},{6,14},{8,0},{10,2},{12,4},{14,6},{1,9},{3,11}... | collective-permute-start | bytes 393224 | tf_op jit(solution)/shard_map/ppermute | solution.py:256
  25.5 12.0 %collective-permute-start.10 = (bf16[128,1536]{1,0:T(8,128)(2,1)S(1)}, bf16[128,1536]{1,0:T(8,128)(2,1)S(1)}, u32[]{:S(2)}, u32[]{:S(2)}) collective-permute-start(bf16[128,1536]{1,0:T(8,128)(2,1)S(1)} %get-tuple-element.51), channel_id=1, source_target_pairs={{0,2},{2,0},{4,6},{6,4},{8,10},{10,8},{12,14},{14,12},{1,3},{3,1},... | collective-permute-start | bytes 1179656 | tf_op jit(solution)/shard_map/ppermute | solution.py:256
  26.9 26.9 %copy-start = (f32[2560]{0:T(1024)S(1)}, f32[2560]{0:T(1024)}, u32[]{:S(2)}) copy-start(f32[2560]{0:T(1024)} %param.17) | copy-start | bytes 30724
  26.9 10.8 %collective-permute-start.11 = (bf16[128,1024]{1,0:T(8,128)(2,1)S(1)}, bf16[128,1024]{1,0:T(8,128)(2,1)S(1)}, u32[]{:S(2)}, u32[]{:S(2)}) collective-permute-start(bf16[128,1024]{1,0:T(8,128)(2,1)S(1)} %get-tuple-element.49.after), channel_id=1, source_target_pairs={{0,4},{2,6},{4,0},{6,2},{8,12},{10,14},{12,8},{14,10},{1,5},{3,7},... | collective-permute-start | bytes 786440 | tf_op jit(solution)/shard_map/ppermute | solution.py:256
  32.6 9.2 %collective-permute-start.9 = (bf16[192,512]{1,0:T(8,128)(2,1)S(1)}, bf16[192,512]{1,0:T(8,128)(2,1)S(1)}, u32[]{:S(2)}, u32[]{:S(2)}) collective-permute-start(bf16[192,512]{1,0:T(8,128)(2,1)S(1)} %gather.1), channel_id=1, source_target_pairs={{0,2},{2,0},{4,6},{6,4},{8,10},{10,8},{12,14},{14,12},{1,3},{3,1},... | collective-permute-start | bytes 589832 | tf_op jit(solution)/shard_map/ppermute | solution.py:256
  37.7 10.0 %collective-permute-start.13 = (bf16[64,1024]{1,0:T(8,128)(2,1)S(1)}, bf16[64,1024]{1,0:T(8,128)(2,1)S(1)}, u32[]{:S(2)}, u32[]{:S(2)}) collective-permute-start(bf16[64,1024]{1,0:T(8,128)(2,1)S(1)} %get-tuple-element.57), channel_id=1, source_target_pairs={{0,2},{2,0},{4,6},{6,4},{8,10},{10,8},{12,14},{14,12},{1,3},{3,1},... | collective-permute-start | bytes 393224 | tf_op jit(solution)/shard_map/ppermute | solution.py:256
  38.6 9.1 %collective-permute-start.12 = (bf16[64,1536]{1,0:T(8,128)(2,1)S(1)}, bf16[64,1536]{1,0:T(8,128)(2,1)S(1)}, u32[]{:S(2)}, u32[]{:S(2)}) collective-permute-start(bf16[64,1536]{1,0:T(8,128)(2,1)S(1)} %get-tuple-element.56), channel_id=1, source_target_pairs={{0,4},{2,6},{4,0},{6,2},{8,12},{10,14},{12,8},{14,10},{1,5},{3,7},... | collective-permute-start | bytes 589832 | tf_op jit(solution)/shard_map/ppermute | solution.py:256
  43.8 5.5 %collective-permute-start.15 = (f32[2,64]{1,0:T(2,128)S(1)}, f32[2,64]{1,0:T(2,128)S(1)}, u32[]{:S(2)}, u32[]{:S(2)}) collective-permute-start(f32[2,64]{1,0:T(2,128)S(1)} %get-tuple-element.65), channel_id=1, source_target_pairs={{0,4},{2,6},{4,0},{6,2},{8,12},{10,14},{12,8},{14,10},{1,5},{3,7},... | collective-permute-start | bytes 1544 | tf_op jit(solution)/shard_map/ppermute | solution.py:256
  46.2 3.6 %collective-permute-start.16 = (f32[2,64]{1,0:T(2,128)S(1)}, f32[2,64]{1,0:T(2,128)S(1)}, u32[]{:S(2)}, u32[]{:S(2)}) collective-permute-start(f32[2,64]{1,0:T(2,128)S(1)} %get-tuple-element.64), channel_id=1, source_target_pairs={{0,2},{2,0},{4,6},{6,4},{8,10},{10,8},{12,14},{14,12},{1,3},{3,1},... | collective-permute-start | bytes 1544 | tf_op jit(solution)/shard_map/ppermute | solution.py:256
  46.2 4.5 %collective-permute-start.17 = (f32[2,64]{1,0:T(2,128)S(1)}, f32[2,64]{1,0:T(2,128)S(1)}, u32[]{:S(2)}, u32[]{:S(2)}) collective-permute-start(f32[2,64]{1,0:T(2,128)S(1)} %get-tuple-element.63), channel_id=1, source_target_pairs={{0,6},{2,4},{4,2},{6,0},{8,14},{10,12},{12,10},{14,8},{1,7},{3,5},... | collective-permute-start | bytes 1544 | tf_op jit(solution)/shard_map/ppermute | solution.py:256
  47.7 8.7 %collective-permute-start.14 = (bf16[32,2560]{1,0:T(8,128)(2,1)S(1)}, bf16[32,2560]{1,0:T(8,128)(2,1)S(1)}, u32[]{:S(2)}, u32[]{:S(2)}) collective-permute-start(bf16[32,2560]{1,0:T(8,128)(2,1)S(1)} %get-tuple-element.59), channel_id=1, source_target_pairs={{0,8},{2,10},{4,12},{6,14},{8,0},{10,2},{12,4},{14,6},{1,9},{3,11}... | collective-permute-start | bytes 491528 | tf_op jit(solution)/shard_map/ppermute | solution.py:256
  50.7 5.7 %collective-permute-start.18 = (f32[1,64]{1,0:T(1,128)S(1)}, f32[1,64]{1,0:T(1,128)S(1)}, u32[]{:S(2)}, u32[]{:S(2)}) collective-permute-start(f32[1,64]{1,0:T(1,128)S(1)} %get-tuple-element.67), channel_id=1, source_target_pairs={{0,8},{2,10},{4,12},{6,14},{8,0},{10,2},{12,4},{14,6},{1,9},{3,11}... | collective-permute-start | bytes 776 | tf_op jit(solution)/shard_map/ppermute | solution.py:256
  51.2 5.2 %collective-permute-start.19 = (f32[1,64]{1,0:T(1,128)S(1)}, f32[1,64]{1,0:T(1,128)S(1)}, u32[]{:S(2)}, u32[]{:S(2)}) collective-permute-start(f32[1,64]{1,0:T(1,128)S(1)} %get-tuple-element.68.refs_0_), channel_id=1, source_target_pairs={{0,1},{1,0},{2,3},{3,2},{4,5},{5,4},{6,7},{7,6},{8,9},{9,8},{10,11... | collective-permute-start | bytes 776 | tf_op jit(solution)/shard_map/ppermute | solution.py:262
  51.2 5.2 %collective-permute-start.20 = (f32[1,64]{1,0:T(1,128)S(1)}, f32[1,64]{1,0:T(1,128)S(1)}, u32[]{:S(2)}, u32[]{:S(2)}) collective-permute-start(f32[1,64]{1,0:T(1,128)S(1)} %get-tuple-element.67), channel_id=1, source_target_pairs={{0,9},{1,8},{2,11},{3,10},{4,13},{5,12},{6,15},{7,14},{8,1},{9,0},... | collective-permute-start | bytes 776 | tf_op jit(solution)/shard_map/ppermute | solution.py:259

commit v15 on v14

--- a/solution.py
+++ b/solution.py
@@ -245,7 +245,7 @@
     width = affine_matrix.shape[1]
     survivors = n * rows // 2
     lines = survivors // n
-    cut = width * 3 // 5 // HEAD_SIZE * HEAD_SIZE
+    cut = width // 2
     chunks = [cut, width - cut]
     near = survivors // 2
     f32, bf16, i32 = jnp.float32, jnp.bfloat16, jnp.int32
@@ -272,24 +272,25 @@
         remote=5,
         scratch=[pltpu.VMEM((rows, model), bf16), pltpu.VMEM((1, model), f32), pltpu.VMEM((1, rows), i32), pltpu.VMEM((rows, 2 * keys.shape[1]), bf16), dma((8,))],
     )
-    last = range(n - n // 4, n)
-    received = [chosen[0]] + [trade(chosen[k], k) for k in range(1, last[0])]
+    received = {0: chosen[0]}
+    received.update({k: trade(chosen[k], k) for k in [1, *range(n // 2, n)]})
     relayed = call(
-        functools.partial(relay_kernel, len(last)),
+        functools.partial(relay_kernel, n // 2 - 2),
         "relay",
-        (*[chosen[k] for k in last], received[1], received[3]),
-        [shape((rows, half), bf16)] * len(last),
+        (*chosen[2 : n // 2], received[1]),
+        [shape(x.shape, bf16) for x in chosen[2 : n // 2]],
         0,
-        in_specs=[VMEM] * len(last) + [ANY] * 2,
-    )
-    received += [trade(x, k) for k, x in zip(last, relayed)]
+        in_specs=[VMEM] * (n // 2 - 2) + [ANY],
+    )
+    received.update({k: trade(x, k) for k, x in zip(range(2, n // 2), relayed)})
+    received = [received[k] for k in range(n)]
     matrix, queries, target = call(
         functools.partial(stage_kernel, n),
         "stage",
-        (counts, affine_matrix, queries, *received[n // 2 : last[0]]),
+        (counts, affine_matrix, queries, *received[n // 2 : n // 2 + 2]),
         [shape(affine_matrix.shape, bf16), shape(queries.shape, bf16), shape((1, n * rows), i32)],
         1500 * affine_matrix.size,
-        in_specs=[ANY] * (3 + n // 4),
+        in_specs=[ANY] * 5,
         remote=3,
         scratch=[pltpu.SMEM(counts.shape, i32), dma((3,))],
     )

time: 57.3 us -> 56.2 us (0.981)
  waiting for transfers between devices: 18.8 us -> 15.1 us
  starting transfers between devices: 28 us -> 30.5 us
    ppermute x18, waiting for transfers between devices: 18.8 us -> 15.1 us  [trade(): return lax.ppermute(x, 'seq', [(i, i ^ k) for i in range(n)])]
    ppermute x18, starting transfers between devices: 25.3 us -> 27.6 us  [trade(): return lax.ppermute(x, 'seq', [(i, i ^ k) for i in range(n)])]
where the time goes in v15:
time: 56.2 us; the launch traced here: 56 us
  starting transfers between devices  30.5 us (54%)
  waiting for transfers between devices  15.1 us (27%)
  Pallas kernels  9.71 us (17%)
  between operations  0.76 us (1%)
    ppermute x18, starting transfers between devices, trade(): return lax.ppermute(x, 'seq', [(i, i ^ k) for i in range(n)])  27.6 us
    ppermute x18, waiting for transfers between devices, trade(): return lax.ppermute(x, 'seq', [(i, i ^ k) for i in range(n)])  15.1 us
    pallas_call x14, Pallas kernels, call(): pl.pallas_call(body, out_shape=list(outputs), in_specs=in_specs or [VMEM]...  9.71 us
    ppermute x1, starting transfers between devices, trade_across(): lax.ppermute(x, ('seq', 'ten'), [(2 * i + t, 2 * (i ^ k) + 1 - t) for i i...  2.76 us
  transfers between devices with their start and end apart: 21, of which 8 were waited for; matrix products, arithmetic and copies ran while one was open for 0% of the time, Pallas kernels for 12%

profile of v15, /device:TPU:0, one launch (start us, length us, event | category | flops | bytes accessed | tf_op | source)
XLA Modules:
  0.0 56.0 jit_solution(11035473248641346949)
XLA Ops:
  0.6 1.7 %norm_select.1 = (bf16[64,1024]{1,0:T(8,128)(2,1)S(1)}, bf16[64,1024]{1,0:T(8,128)(2,1)S(1)}, bf16[64,1024]{1,0:T(8,128)(2,1)S(1)}, bf16[64,512]{1,0:T(8,128)(2,...) custom-call(bf16[64,8192]{1,0:T(8,128)(2,1)} %hidden_in.1, ...), custom_call_target="tpu_custom_call" | custom-call | flops 2097152 | bytes 1868032 | tf_op jit(solution)/shard_map/norm_select/pallas_call | solution.py:21
  2.4 3.0 %collective-permute-start.2 = (bf16[64,1024]{1,0:T(8,128)(2,1)S(1)}, bf16[64,1024]{1,0:T(8,128)(2,1)S(1)}, u32[]{:S(2)}, u32[]{:S(2)}) collective-permute-start(bf16[64,1024]{1,0:T(8,128)(2,1)S(1)} %get-tuple-element.38), channel_id=1, source_target_pairs={{0,2},{2,0},{4,6},{6,4},{8,10},{10,8},{12,14},{14,12},{1,3},{3,1},... | collective-permute-start | bytes 393224 | tf_op jit(solution)/shard_map/ppermute | solution.py:256
  5.4 2.6 %collective-permute-start = (bf16[64,512]{1,0:T(8,128)(2,1)S(1)}, bf16[64,512]{1,0:T(8,128)(2,1)S(1)}, u32[]{:S(2)}, u32[]{:S(2)}) collective-permute-start(bf16[64,512]{1,0:T(8,128)(2,1)S(1)} %get-tuple-element.33), channel_id=1, source_target_pairs={{0,8},{2,10},{4,12},{6,14},{8,0},{10,2},{12,4},{14,6},{1,9},{3,11}... | collective-permute-start | bytes 196616 | tf_op jit(solution)/shard_map/ppermute | solution.py:256
  8.0 3.9 %collective-permute-start.5 = (bf16[64,512]{1,0:T(8,128)(2,1)S(1)}, bf16[64,512]{1,0:T(8,128)(2,1)S(1)}, u32[]{:S(2)}, u32[]{:S(2)}) collective-permute-start(bf16[64,512]{1,0:T(8,128)(2,1)S(1)} %get-tuple-element.43), channel_id=1, source_target_pairs={{0,12},{2,14},{4,8},{6,10},{8,4},{10,6},{12,0},{14,2},{1,13},{3,15... | collective-permute-start | bytes 196616 | tf_op jit(solution)/shard_map/ppermute | solution.py:256
  11.9 1.2 %collective-permute-start.6 = (bf16[64,512]{1,0:T(8,128)(2,1)S(1)}, bf16[64,512]{1,0:T(8,128)(2,1)S(1)}, u32[]{:S(2)}, u32[]{:S(2)}) collective-permute-start(bf16[64,512]{1,0:T(8,128)(2,1)S(1)} %get-tuple-element.44), channel_id=1, source_target_pairs={{0,14},{2,12},{4,10},{6,8},{8,6},{10,4},{12,2},{14,0},{1,15},{3,13... | collective-permute-start | bytes 196616 | tf_op jit(solution)/shard_map/ppermute | solution.py:256
  13.1 0.0 collective-permute-done.2.refs_2_.refs_1_
  13.1 0.1 collective-permute-start.3
  13.2 0.0 collective-permute-done.refs_0_.refs_4_
  13.2 1.8 %collective-permute-start.4 = (bf16[64,512]{1,0:T(8,128)(2,1)S(1)}, bf16[64,512]{1,0:T(8,128)(2,1)S(1)}, u32[]{:S(2)}, u32[]{:S(2)}) collective-permute-start(bf16[64,512]{1,0:T(8,128)(2,1)S(1)} %get-tuple-element.42), channel_id=1, source_target_pairs={{0,6},{2,4},{4,2},{6,0},{8,14},{10,12},{12,10},{14,8},{1,7},{3,5},... | collective-permute-start | bytes 196616 | tf_op jit(solution)/shard_map/ppermute | solution.py:256
  15.0 2.8 %collective-permute-done.1.refs_1_.refs_5_ = bf16[64,512]{1,0:T(8,128)(2,1)S(1)} collective-permute-done((bf16[64,512]{1,0:T(8,128)(2,1)S(1)}, bf16[64,512]{1,0:T(8,128)(2,1)S(1)}, u32[]{:S(2)}, u32[]{:S(2)}) %collective-permute-start.1) | collective-permute-done | bytes 65568 | tf_op jit(solution)/shard_map/ppermute | solution.py:256
  17.8 2.5 %stage.1 = (bf16[1024,2560]{1,0:T(8,128)(2,1)S(1)}, bf16[64,2048]{1,0:T(8,128)(2,1)S(1)}, s32[1,512]{1,0:T(1,128)S(1)}) custom-call(s32[8]{0:T(128)} %counts_in.1, bf16[1024,2560]{1,0:T(8,128)(2,1)} %matrix_in.1, bf16[64,2048]{1,0:T(8,128)(2,1)} %queries_in.1, bf16[64,512]{1,0:T(8,128)(2,1)S(1)} %collective-permute-done.refs_0_.refs_4_, ...), custom_call_target="tpu_custom_call" | custom-call | flops 3932160000 | bytes 11143200 | tf_op jit(solution)/shard_map/stage/pallas_call | solution.py:21
  20.3 0.0 collective-permute-done.5.refs_6_
  20.3 0.9 %collective-permute-done.4.refs_3_ = bf16[64,512]{1,0:T(8,128)(2,1)S(1)} collective-permute-done((bf16[64,512]{1,0:T(8,128)(2,1)S(1)}, bf16[64,512]{1,0:T(8,128)(2,1)S(1)}, u32[]{:S(2)}, u32[]{:S(2)}) %collective-permute-start.4) | collective-permute-done | bytes 65568 | tf_op jit(solution)/shard_map/ppermute | solution.py:256
  21.3 0.3 compact.1
  21.6 0.1 collective-permute-start.8
  21.7 1.7 %collective-permute-start.7 = (bf16[128,512]{1,0:T(8,128)(2,1)S(1)}, bf16[128,512]{1,0:T(8,128)(2,1)S(1)}, u32[]{:S(2)}, u32[]{:S(2)}) collective-permute-start(bf16[128,512]{1,0:T(8,128)(2,1)S(1)} %get-tuple-element.45.near), channel_id=1, source_target_pairs={{0,8},{2,10},{4,12},{6,14},{8,0},{10,2},{12,4},{14,6},{1,9},{3,11}... | collective-permute-start | bytes 393224 | tf_op jit(solution)/shard_map/ppermute | solution.py:256
  23.4 1.0 %project_own.1.product = f32[256,2560]{1,0:T(8,128)S(1)} custom-call(bf16[256,512]{1,0:T(8,128)(2,1)S(1)} %get-tuple-element.47.own, bf16[1024,2560]{1,0:T(8,128)(2,1)S(1)} %get-tuple-element.48.matrix), custom_call_target="tpu_custom_call" | custom-call | flops 671088640 | bytes 8126464 | tf_op jit(solution)/shard_map/project_own/pallas_call | solution.py:21
  24.4 0.0 collective-permute-done.8.other
  24.4 0.6 %project.3 = (f32[128,1280]{1,0:T(8,128)S(1)}, bf16[128,1280]{1,0:T(8,128)(2,1)S(1)}) custom-call(f32[256,2560]{1,0:T(8,128)S(1)} %project_own.1.product, bf16[256,512]{1,0:T(8,128)(2,1)S(1)} %collective-permute-done.8.other, bf16[1024,2560]{1,0:T(8,128)(2,1)S(1)} %get-tuple-element.48.matrix), custom_call_target="tpu_custom_call" | custom-call | flops 335544320 | bytes 9109504 | tf_op jit(solution)/shard_map/project/pallas_call | solution.py:21
  25.0 1.6 %collective-permute-start.10 = (bf16[128,1280]{1,0:T(8,128)(2,1)S(1)}, bf16[128,1280]{1,0:T(8,128)(2,1)S(1)}, u32[]{:S(2)}, u32[]{:S(2)}) collective-permute-start(bf16[128,1280]{1,0:T(8,128)(2,1)S(1)} %get-tuple-element.51), channel_id=1, source_target_pairs={{0,2},{2,0},{4,6},{6,4},{8,10},{10,8},{12,14},{14,12},{1,3},{3,1},... | collective-permute-start | bytes 983048 | tf_op jit(solution)/shard_map/ppermute | solution.py:256
  26.6 0.6 %project.2 = (f32[128,1280]{1,0:T(8,128)S(1)}, bf16[128,1280]{1,0:T(8,128)(2,1)S(1)}) custom-call(f32[256,2560]{1,0:T(8,128)S(1)} %project_own.1.product, bf16[256,512]{1,0:T(8,128)(2,1)S(1)} %collective-permute-done.8.other, bf16[1024,2560]{1,0:T(8,128)(2,1)S(1)} %get-tuple-element.48.matrix), custom_call_target="tpu_custom_call" | custom-call | flops 335544320 | bytes 9109504 | tf_op jit(solution)/shard_map/project/pallas_call | solution.py:21
  27.2 0.0 copy-start
  27.2 2.2 %collective-permute-start.11 = (bf16[128,1280]{1,0:T(8,128)(2,1)S(1)}, bf16[128,1280]{1,0:T(8,128)(2,1)S(1)}, u32[]{:S(2)}, u32[]{:S(2)}) collective-permute-start(bf16[128,1280]{1,0:T(8,128)(2,1)S(1)} %get-tuple-element.49.after), channel_id=1, source_target_pairs={{0,4},{2,6},{4,0},{6,2},{8,12},{10,14},{12,8},{14,10},{1,5},{3,7},... | collective-permute-start | bytes 983048 | tf_op jit(solution)/shard_map/ppermute | solution.py:256
  29.4 2.0 %collective-permute-done.7.far = bf16[128,512]{1,0:T(8,128)(2,1)S(1)} collective-permute-done((bf16[128,512]{1,0:T(8,128)(2,1)S(1)}, bf16[128,512]{1,0:T(8,128)(2,1)S(1)}, u32[]{:S(2)}, u32[]{:S(2)}) %collective-permute-start.7) | collective-permute-done | bytes 131104 | tf_op jit(solution)/shard_map/ppermute | solution.py:256
  31.4 1.7 %collective-permute-start.9 = (bf16[192,512]{1,0:T(8,128)(2,1)S(1)}, bf16[192,512]{1,0:T(8,128)(2,1)S(1)}, u32[]{:S(2)}, u32[]{:S(2)}) collective-permute-start(bf16[192,512]{1,0:T(8,128)(2,1)S(1)} %gather.1), channel_id=1, source_target_pairs={{0,2},{2,0},{4,6},{6,4},{8,10},{10,8},{12,14},{14,12},{1,3},{3,1},... | collective-permute-start | bytes 589832 | tf_op jit(solution)/shard_map/ppermute | solution.py:256
  33.1 2.5 %collective-permute-done.10.received = bf16[128,1280]{1,0:T(8,128)(2,1)S(1)} collective-permute-done((bf16[128,1280]{1,0:T(8,128)(2,1)S(1)}, bf16[128,1280]{1,0:T(8,128)(2,1)S(1)}, u32[]{:S(2)}, u32[]{:S(2)}) %collective-permute-start.10) | collective-permute-done | bytes 327712 | tf_op jit(solution)/shard_map/ppermute | solution.py:256
  35.6 0.1 hop_sum.2
  35.7 2.6 %collective-permute-done.11.received = bf16[128,1280]{1,0:T(8,128)(2,1)S(1)} collective-permute-done((bf16[128,1280]{1,0:T(8,128)(2,1)S(1)}, bf16[128,1280]{1,0:T(8,128)(2,1)S(1)}, u32[]{:S(2)}, u32[]{:S(2)}) %collective-permute-start.11) | collective-permute-done | bytes 327712 | tf_op jit(solution)/shard_map/ppermute | solution.py:256
  38.3 0.1 hop_sum.3
  38.4 1.6 %collective-permute-start.13 = (bf16[64,1280]{1,0:T(8,128)(2,1)S(1)}, bf16[64,1280]{1,0:T(8,128)(2,1)S(1)}, u32[]{:S(2)}, u32[]{:S(2)}) collective-permute-start(bf16[64,1280]{1,0:T(8,128)(2,1)S(1)} %get-tuple-element.57), channel_id=1, source_target_pairs={{0,2},{2,0},{4,6},{6,4},{8,10},{10,8},{12,14},{14,12},{1,3},{3,1},... | collective-permute-start | bytes 491528 | tf_op jit(solution)/shard_map/ppermute | solution.py:256
  40.0 0.0 collective-permute-start.12
  40.0 0.0 collective-permute-done.9.odd
  40.0 2.0 %attention.1 = (f32[64,2048]{1,0:T(8,128)}, f32[8,64]{1,0:T(8,128)S(1)}) custom-call(bf16[64,2048]{1,0:T(8,128)(2,1)S(1)} %get-tuple-element.35.queries, bf16[128,512]{1,0:T(8,128)(2,1)S(1)} %get-tuple-element.45.near, bf16[128,512]{1,0:T(8,128)(2,1)S(1)} %collective-permute-done.7.far, bf16[64,512]{1,0:T(8,128)(2,1)S(1)} %get-tuple-element.46.pair, ...), custom_call_target="tpu_custom_call" | custom-call | flops 268435456 | bytes 1640448 | tf_op jit(solution)/shard_map/attention/pallas_call | solution.py:21
  42.0 2.0 %collective-permute-start.15 = (f32[2,64]{1,0:T(2,128)S(1)}, f32[2,64]{1,0:T(2,128)S(1)}, u32[]{:S(2)}, u32[]{:S(2)}) collective-permute-start(f32[2,64]{1,0:T(2,128)S(1)} %get-tuple-element.65), channel_id=1, source_target_pairs={{0,4},{2,6},{4,0},{6,2},{8,12},{10,14},{12,8},{14,10},{1,5},{3,7},... | collective-permute-start | bytes 1544 | tf_op jit(solution)/shard_map/ppermute | solution.py:256
  44.0 1.3 %collective-permute-start.16 = (f32[2,64]{1,0:T(2,128)S(1)}, f32[2,64]{1,0:T(2,128)S(1)}, u32[]{:S(2)}, u32[]{:S(2)}) collective-permute-start(f32[2,64]{1,0:T(2,128)S(1)} %get-tuple-element.64), channel_id=1, source_target_pairs={{0,2},{2,0},{4,6},{6,4},{8,10},{10,8},{12,14},{14,12},{1,3},{3,1},... | collective-permute-start | bytes 1544 | tf_op jit(solution)/shard_map/ppermute | solution.py:256
  45.4 0.1 collective-permute-start.17
  45.5 0.3 collective-permute-done.12.refs_2_
  45.8 0.1 hop_sum_both.1
  45.8 2.5 %collective-permute-start.14 = (bf16[32,2560]{1,0:T(8,128)(2,1)S(1)}, bf16[32,2560]{1,0:T(8,128)(2,1)S(1)}, u32[]{:S(2)}, u32[]{:S(2)}) collective-permute-start(bf16[32,2560]{1,0:T(8,128)(2,1)S(1)} %get-tuple-element.59), channel_id=1, source_target_pairs={{0,8},{2,10},{4,12},{6,14},{8,0},{10,2},{12,4},{14,6},{1,9},{3,11}... | collective-permute-start | bytes 491528 | tf_op jit(solution)/shard_map/ppermute | solution.py:256
  48.3 0.0 collective-permute-done.15.refs_1_
  48.3 0.0 collective-permute-done.16.refs_2_
  48.3 1.5 %collective-permute-done.17.refs_3_ = f32[2,64]{1,0:T(2,128)S(1)} collective-permute-done((f32[2,64]{1,0:T(2,128)S(1)}, f32[2,64]{1,0:T(2,128)S(1)}, u32[]{:S(2)}, u32[]{:S(2)}) %collective-permute-start.17) | collective-permute-done | bytes 544 | tf_op jit(solution)/shard_map/ppermute | solution.py:256
  49.8 0.3 collective-permute-start.18
  50.2 0.0 collective-permute-start.19
  50.2 2.8 %collective-permute-start.20 = (f32[1,64]{1,0:T(1,128)S(1)}, f32[1,64]{1,0:T(1,128)S(1)}, u32[]{:S(2)}, u32[]{:S(2)}) collective-permute-start(f32[1,64]{1,0:T(1,128)S(1)} %get-tuple-element.67), channel_id=1, source_target_pairs={{0,9},{1,8},{2,11},{3,10},{4,13},{5,12},{6,15},{7,14},{8,1},{9,0},... | collective-permute-start | bytes 776 | tf_op jit(solution)/shard_map/ppermute | solution.py:259
  53.0 2.3 %collective-permute-done.18.refs_1_ = f32[1,64]{1,0:T(1,128)S(1)} collective-permute-done((f32[1,64]{1,0:T(1,128)S(1)}, f32[1,64]{1,0:T(1,128)S(1)}, u32[]{:S(2)}, u32[]{:S(2)}) %collective-permute-start.18) | collective-permute-done | bytes 288 | tf_op jit(solution)/shard_map/ppermute | solution.py:256
  55.3 0.0 collective-permute-done.14.received
  55.3 0.8 %finish.1 = (f32[32,2560]{1,0:T(8,128)}, f32[1,64]{1,0:T(1,128)}) custom-call(f32[1,2560]{1,0:T(1,128)S(1)} %reshape.20.bias, f32[32,2560]{1,0:T(8,128)S(1)} %get-tuple-element.58.after.kept, bf16[32,2560]{1,0:T(8,128)(2,1)S(1)} %collective-permute-done.14.received, f32[1,64]{1,0:T(1,128)S(1)} %get-tuple-element.68.refs_0_, ...), custom_call_target="tpu_custom_call" | custom-call | flops 655360 | bytes 830720 | tf_op jit(solution)/shard_map/finish/pallas_call | solution.py:21
  (13 shorter events, 0.1 us)
Async XLA Ops:
  2.4 10.7 %collective-permute-start.2 = (bf16[64,1024]{1,0:T(8,128)(2,1)S(1)}, bf16[64,1024]{1,0:T(8,128)(2,1)S(1)}, u32[]{:S(2)}, u32[]{:S(2)}) collective-permute-start(bf16[64,1024]{1,0:T(8,128)(2,1)S(1)} %get-tuple-element.38), channel_id=1, source_target_pairs={{0,2},{2,0},{4,6},{6,4},{8,10},{10,8},{12,14},{14,12},{1,3},{3,1},... | collective-permute-start | bytes 393224 | tf_op jit(solution)/shard_map/ppermute | solution.py:256
  5.4 7.8 %collective-permute-start = (bf16[64,512]{1,0:T(8,128)(2,1)S(1)}, bf16[64,512]{1,0:T(8,128)(2,1)S(1)}, u32[]{:S(2)}, u32[]{:S(2)}) collective-permute-start(bf16[64,512]{1,0:T(8,128)(2,1)S(1)} %get-tuple-element.33), channel_id=1, source_target_pairs={{0,8},{2,10},{4,12},{6,14},{8,0},{10,2},{12,4},{14,6},{1,9},{3,11}... | collective-permute-start | bytes 196616 | tf_op jit(solution)/shard_map/ppermute | solution.py:256
  8.0 9.8 %collective-permute-start.1 = (bf16[64,512]{1,0:T(8,128)(2,1)S(1)}, bf16[64,512]{1,0:T(8,128)(2,1)S(1)}, u32[]{:S(2)}, u32[]{:S(2)}) collective-permute-start(bf16[64,512]{1,0:T(8,128)(2,1)S(1)} %get-tuple-element.34), channel_id=1, source_target_pairs={{0,10},{2,8},{4,14},{6,12},{8,2},{10,0},{12,6},{14,4},{1,11},{3,9}... | collective-permute-start | bytes 196616 | tf_op jit(solution)/shard_map/ppermute | solution.py:256
  8.0 12.3 %collective-permute-start.5 = (bf16[64,512]{1,0:T(8,128)(2,1)S(1)}, bf16[64,512]{1,0:T(8,128)(2,1)S(1)}, u32[]{:S(2)}, u32[]{:S(2)}) collective-permute-start(bf16[64,512]{1,0:T(8,128)(2,1)S(1)} %get-tuple-element.43), channel_id=1, source_target_pairs={{0,12},{2,14},{4,8},{6,10},{8,4},{10,6},{12,0},{14,2},{1,13},{3,15... | collective-permute-start | bytes 196616 | tf_op jit(solution)/shard_map/ppermute | solution.py:256
  11.9 8.4 %collective-permute-start.6 = (bf16[64,512]{1,0:T(8,128)(2,1)S(1)}, bf16[64,512]{1,0:T(8,128)(2,1)S(1)}, u32[]{:S(2)}, u32[]{:S(2)}) collective-permute-start(bf16[64,512]{1,0:T(8,128)(2,1)S(1)} %get-tuple-element.44), channel_id=1, source_target_pairs={{0,14},{2,12},{4,10},{6,8},{8,6},{10,4},{12,2},{14,0},{1,15},{3,13... | collective-permute-start | bytes 196616 | tf_op jit(solution)/shard_map/ppermute | solution.py:256
  13.1 8.2 %collective-permute-start.3 = (bf16[64,1024]{1,0:T(8,128)(2,1)S(1)}, bf16[64,1024]{1,0:T(8,128)(2,1)S(1)}, u32[]{:S(2)}, u32[]{:S(2)}) collective-permute-start(bf16[64,1024]{1,0:T(8,128)(2,1)S(1)} %get-tuple-element.41), channel_id=1, source_target_pairs={{0,4},{2,6},{4,0},{6,2},{8,12},{10,14},{12,8},{14,10},{1,5},{3,7},... | collective-permute-start | bytes 393224 | tf_op jit(solution)/shard_map/ppermute | solution.py:256
  13.2 8.1 %collective-permute-start.4 = (bf16[64,512]{1,0:T(8,128)(2,1)S(1)}, bf16[64,512]{1,0:T(8,128)(2,1)S(1)}, u32[]{:S(2)}, u32[]{:S(2)}) collective-permute-start(bf16[64,512]{1,0:T(8,128)(2,1)S(1)} %get-tuple-element.42), channel_id=1, source_target_pairs={{0,6},{2,4},{4,2},{6,0},{8,14},{10,12},{12,10},{14,8},{1,7},{3,5},... | collective-permute-start | bytes 196616 | tf_op jit(solution)/shard_map/ppermute | solution.py:256
  21.6 2.8 %collective-permute-start.8 = (bf16[256,512]{1,0:T(8,128)(2,1)S(1)}, bf16[256,512]{1,0:T(8,128)(2,1)S(1)}, u32[]{:S(2)}, u32[]{:S(2)}) collective-permute-start(bf16[256,512]{1,0:T(8,128)(2,1)S(1)} %get-tuple-element.47.own), channel_id=1, source_target_pairs={{0,1},{1,0},{2,3},{3,2},{4,5},{5,4},{6,7},{7,6},{8,9},{9,8},{10,11... | collective-permute-start | bytes 786440 | tf_op jit(solution)/shard_map/ppermute | solution.py:262
  21.7 9.7 %collective-permute-start.7 = (bf16[128,512]{1,0:T(8,128)(2,1)S(1)}, bf16[128,512]{1,0:T(8,128)(2,1)S(1)}, u32[]{:S(2)}, u32[]{:S(2)}) collective-permute-start(bf16[128,512]{1,0:T(8,128)(2,1)S(1)} %get-tuple-element.45.near), channel_id=1, source_target_pairs={{0,8},{2,10},{4,12},{6,14},{8,0},{10,2},{12,4},{14,6},{1,9},{3,11}... | collective-permute-start | bytes 393224 | tf_op jit(solution)/shard_map/ppermute | solution.py:256
  25.0 10.6 %collective-permute-start.10 = (bf16[128,1280]{1,0:T(8,128)(2,1)S(1)}, bf16[128,1280]{1,0:T(8,128)(2,1)S(1)}, u32[]{:S(2)}, u32[]{:S(2)}) collective-permute-start(bf16[128,1280]{1,0:T(8,128)(2,1)S(1)} %get-tuple-element.51), channel_id=1, source_target_pairs={{0,2},{2,0},{4,6},{6,4},{8,10},{10,8},{12,14},{14,12},{1,3},{3,1},... | collective-permute-start | bytes 983048 | tf_op jit(solution)/shard_map/ppermute | solution.py:256
  27.2 25.7 %copy-start = (f32[2560]{0:T(1024)S(1)}, f32[2560]{0:T(1024)}, u32[]{:S(2)}) copy-start(f32[2560]{0:T(1024)} %param.17) | copy-start | bytes 30724
  27.2 11.1 %collective-permute-start.11 = (bf16[128,1280]{1,0:T(8,128)(2,1)S(1)}, bf16[128,1280]{1,0:T(8,128)(2,1)S(1)}, u32[]{:S(2)}, u32[]{:S(2)}) collective-permute-start(bf16[128,1280]{1,0:T(8,128)(2,1)S(1)} %get-tuple-element.49.after), channel_id=1, source_target_pairs={{0,4},{2,6},{4,0},{6,2},{8,12},{10,14},{12,8},{14,10},{1,5},{3,7},... | collective-permute-start | bytes 983048 | tf_op jit(solution)/shard_map/ppermute | solution.py:256
  31.4 8.6 %collective-permute-start.9 = (bf16[192,512]{1,0:T(8,128)(2,1)S(1)}, bf16[192,512]{1,0:T(8,128)(2,1)S(1)}, u32[]{:S(2)}, u32[]{:S(2)}) collective-permute-start(bf16[192,512]{1,0:T(8,128)(2,1)S(1)} %gather.1), channel_id=1, source_target_pairs={{0,2},{2,0},{4,6},{6,4},{8,10},{10,8},{12,14},{14,12},{1,3},{3,1},... | collective-permute-start | bytes 589832 | tf_op jit(solution)/shard_map/ppermute | solution.py:256
  38.4 7.1 %collective-permute-start.13 = (bf16[64,1280]{1,0:T(8,128)(2,1)S(1)}, bf16[64,1280]{1,0:T(8,128)(2,1)S(1)}, u32[]{:S(2)}, u32[]{:S(2)}) collective-permute-start(bf16[64,1280]{1,0:T(8,128)(2,1)S(1)} %get-tuple-element.57), channel_id=1, source_target_pairs={{0,2},{2,0},{4,6},{6,4},{8,10},{10,8},{12,14},{14,12},{1,3},{3,1},... | collective-permute-start | bytes 491528 | tf_op jit(solution)/shard_map/ppermute | solution.py:256
  40.0 5.8 %collective-permute-start.12 = (bf16[64,1280]{1,0:T(8,128)(2,1)S(1)}, bf16[64,1280]{1,0:T(8,128)(2,1)S(1)}, u32[]{:S(2)}, u32[]{:S(2)}) collective-permute-start(bf16[64,1280]{1,0:T(8,128)(2,1)S(1)} %get-tuple-element.56), channel_id=1, source_target_pairs={{0,4},{2,6},{4,0},{6,2},{8,12},{10,14},{12,8},{14,10},{1,5},{3,7},... | collective-permute-start | bytes 491528 | tf_op jit(solution)/shard_map/ppermute | solution.py:256
  42.0 6.3 %collective-permute-start.15 = (f32[2,64]{1,0:T(2,128)S(1)}, f32[2,64]{1,0:T(2,128)S(1)}, u32[]{:S(2)}, u32[]{:S(2)}) collective-permute-start(f32[2,64]{1,0:T(2,128)S(1)} %get-tuple-element.65), channel_id=1, source_target_pairs={{0,4},{2,6},{4,0},{6,2},{8,12},{10,14},{12,8},{14,10},{1,5},{3,7},... | collective-permute-start | bytes 1544 | tf_op jit(solution)/shard_map/ppermute | solution.py:256
  44.0 4.3 %collective-permute-start.16 = (f32[2,64]{1,0:T(2,128)S(1)}, f32[2,64]{1,0:T(2,128)S(1)}, u32[]{:S(2)}, u32[]{:S(2)}) collective-permute-start(f32[2,64]{1,0:T(2,128)S(1)} %get-tuple-element.64), channel_id=1, source_target_pairs={{0,2},{2,0},{4,6},{6,4},{8,10},{10,8},{12,14},{14,12},{1,3},{3,1},... | collective-permute-start | bytes 1544 | tf_op jit(solution)/shard_map/ppermute | solution.py:256
  45.4 4.5 %collective-permute-start.17 = (f32[2,64]{1,0:T(2,128)S(1)}, f32[2,64]{1,0:T(2,128)S(1)}, u32[]{:S(2)}, u32[]{:S(2)}) collective-permute-start(f32[2,64]{1,0:T(2,128)S(1)} %get-tuple-element.63), channel_id=1, source_target_pairs={{0,6},{2,4},{4,2},{6,0},{8,14},{10,12},{12,10},{14,8},{1,7},{3,5},... | collective-permute-start | bytes 1544 | tf_op jit(solution)/shard_map/ppermute | solution.py:256
  45.8 9.4 %collective-permute-start.14 = (bf16[32,2560]{1,0:T(8,128)(2,1)S(1)}, bf16[32,2560]{1,0:T(8,128)(2,1)S(1)}, u32[]{:S(2)}, u32[]{:S(2)}) collective-permute-start(bf16[32,2560]{1,0:T(8,128)(2,1)S(1)} %get-tuple-element.59), channel_id=1, source_target_pairs={{0,8},{2,10},{4,12},{6,14},{8,0},{10,2},{12,4},{14,6},{1,9},{3,11}... | collective-permute-start | bytes 491528 | tf_op jit(solution)/shard_map/ppermute | solution.py:256
  49.8 5.4 %collective-permute-start.18 = (f32[1,64]{1,0:T(1,128)S(1)}, f32[1,64]{1,0:T(1,128)S(1)}, u32[]{:S(2)}, u32[]{:S(2)}) collective-permute-start(f32[1,64]{1,0:T(1,128)S(1)} %get-tuple-element.67), channel_id=1, source_target_pairs={{0,8},{2,10},{4,12},{6,14},{8,0},{10,2},{12,4},{14,6},{1,9},{3,11}... | collective-permute-start | bytes 776 | tf_op jit(solution)/shard_map/ppermute | solution.py:256
  50.2 5.1 %collective-permute-start.19 = (f32[1,64]{1,0:T(1,128)S(1)}, f32[1,64]{1,0:T(1,128)S(1)}, u32[]{:S(2)}, u32[]{:S(2)}) collective-permute-start(f32[1,64]{1,0:T(1,128)S(1)} %get-tuple-element.68.refs_0_), channel_id=1, source_target_pairs={{0,1},{1,0},{2,3},{3,2},{4,5},{5,4},{6,7},{7,6},{8,9},{9,8},{10,11... | collective-permute-start | bytes 776 | tf_op jit(solution)/shard_map/ppermute | solution.py:262
  50.2 5.1 %collective-permute-start.20 = (f32[1,64]{1,0:T(1,128)S(1)}, f32[1,64]{1,0:T(1,128)S(1)}, u32[]{:S(2)}, u32[]{:S(2)}) collective-permute-start(f32[1,64]{1,0:T(1,128)S(1)} %get-tuple-element.67), channel_id=1, source_target_pairs={{0,9},{1,8},{2,11},{3,10},{4,13},{5,12},{6,15},{7,14},{8,1},{9,0},... | collective-permute-start | bytes 776 | tf_op jit(solution)/shard_map/ppermute | solution.py:259

commit v16 on v15

--- a/solution.py
+++ b/solution.py
@@ -245,7 +245,7 @@
     width = affine_matrix.shape[1]
     survivors = n * rows // 2
     lines = survivors // n
-    cut = width // 2
+    cut = width * 11 // 20 // HEAD_SIZE * HEAD_SIZE
     chunks = [cut, width - cut]
     near = survivors // 2
     f32, bf16, i32 = jnp.float32, jnp.bfloat16, jnp.int32
@@ -254,6 +254,9 @@
 
     def trade(x, k):
         return lax.ppermute(x, "seq", [(i, i ^ k) for i in range(n)])
+
+    def give_later(x, k):
+        return lax.ppermute(x, "seq", [(i, i ^ k) for i in range(n) if i < i ^ k])
 
     def trade_across(x, k):
         return lax.ppermute(x, ("seq", "ten"), [(2 * i + t, 2 * (i ^ k) + 1 - t) for i in range(n) for t in range(2)])
@@ -321,7 +324,7 @@
         )
         for c, chunk in enumerate(chunks)
     ]
-    far = trade(even, n // 2)
+    far = give_later(even, n // 2)
     (gathered,) = call(
         gather_kernel,
         "gather",

time: 56.2 us -> 58 us (1.032)
  starting transfers between devices: 30.5 us -> 31.6 us
  waiting for transfers between devices: 15.1 us -> 15.8 us
    ppermute x0 -> x1, starting transfers between devices: none -> 3.58 us  [give_later(): return lax.ppermute(x, 'seq', [(i, i ^ k) for i in range(n) if i < i ^ k])]
    ppermute x18 -> x17, starting transfers between devices: 27.6 us -> 24.9 us  [trade(): return lax.ppermute(x, 'seq', [(i, i ^ k) for i in range(n)])]
    ppermute x18 -> x17, waiting for transfers between devices: 15.1 us -> 15.8 us  [trade(): return lax.ppermute(x, 'seq', [(i, i ^ k) for i in range(n)])]
  transfers between devices with their start and end apart: 21 -> 21, of which waited for: 8 -> 7; matrix products, arithmetic and copies ran while one was open for 0% -> 0% of each run, Pallas kernels for 12% -> 12%
where the time goes in v16:
time: 58 us; the launch traced here: 57.9 us
  starting transfers between devices  31.6 us (54%)
  waiting for transfers between devices  15.8 us (27%)
  Pallas kernels  9.67 us (17%)
  between operations  0.79 us (1%)
    ppermute x17, starting transfers between devices, trade(): return lax.ppermute(x, 'seq', [(i, i ^ k) for i in range(n)])  24.9 us
    ppermute x17, waiting for transfers between devices, trade(): return lax.ppermute(x, 'seq', [(i, i ^ k) for i in range(n)])  15.8 us
    pallas_call x14, Pallas kernels, call(): pl.pallas_call(body, out_shape=list(outputs), in_specs=in_specs or [VMEM]...  9.67 us
    ppermute x1, starting transfers between devices, give_later(): return lax.ppermute(x, 'seq', [(i, i ^ k) for i in range(n) if i < i ^ k])  3.58 us
    ppermute x1, starting transfers between devices, trade_across(): lax.ppermute(x, ('seq', 'ten'), [(2 * i + t, 2 * (i ^ k) + 1 - t) for i i...  2.95 us
  transfers between devices with their start and end apart: 21, of which 7 were waited for; matrix products, arithmetic and copies ran while one was open for 0% of the time, Pallas kernels for 12%

profile of v16, /device:TPU:0, one launch (start us, length us, event | category | flops | bytes accessed | tf_op | source)
XLA Modules:
  0.0 57.9 jit_solution(9550077037544087568)
XLA Ops:
  0.6 1.7 %norm_select.1 = (bf16[64,1024]{1,0:T(8,128)(2,1)S(1)}, bf16[64,1024]{1,0:T(8,128)(2,1)S(1)}, bf16[64,1024]{1,0:T(8,128)(2,1)S(1)}, bf16[64,512]{1,0:T(8,128)(2,...) custom-call(bf16[64,8192]{1,0:T(8,128)(2,1)} %hidden_in.1, ...), custom_call_target="tpu_custom_call" | custom-call | flops 2097152 | bytes 1868032 | tf_op jit(solution)/shard_map/norm_select/pallas_call | solution.py:21
  2.4 3.0 %collective-permute-start.2 = (bf16[64,1024]{1,0:T(8,128)(2,1)S(1)}, bf16[64,1024]{1,0:T(8,128)(2,1)S(1)}, u32[]{:S(2)}, u32[]{:S(2)}) collective-permute-start(bf16[64,1024]{1,0:T(8,128)(2,1)S(1)} %get-tuple-element.38), channel_id=1, source_target_pairs={{0,2},{2,0},{4,6},{6,4},{8,10},{10,8},{12,14},{14,12},{1,3},{3,1},... | collective-permute-start | bytes 393224 | tf_op jit(solution)/shard_map/ppermute | solution.py:256
  5.4 2.6 %collective-permute-start = (bf16[64,512]{1,0:T(8,128)(2,1)S(1)}, bf16[64,512]{1,0:T(8,128)(2,1)S(1)}, u32[]{:S(2)}, u32[]{:S(2)}) collective-permute-start(bf16[64,512]{1,0:T(8,128)(2,1)S(1)} %get-tuple-element.33), channel_id=1, source_target_pairs={{0,8},{2,10},{4,12},{6,14},{8,0},{10,2},{12,4},{14,6},{1,9},{3,11}... | collective-permute-start | bytes 196616 | tf_op jit(solution)/shard_map/ppermute | solution.py:256
  8.0 0.0 collective-permute-start.1
  8.0 3.9 %collective-permute-start.5 = (bf16[64,512]{1,0:T(8,128)(2,1)S(1)}, bf16[64,512]{1,0:T(8,128)(2,1)S(1)}, u32[]{:S(2)}, u32[]{:S(2)}) collective-permute-start(bf16[64,512]{1,0:T(8,128)(2,1)S(1)} %get-tuple-element.43), channel_id=1, source_target_pairs={{0,12},{2,14},{4,8},{6,10},{8,4},{10,6},{12,0},{14,2},{1,13},{3,15... | collective-permute-start | bytes 196616 | tf_op jit(solution)/shard_map/ppermute | solution.py:256
  11.9 1.2 %collective-permute-start.6 = (bf16[64,512]{1,0:T(8,128)(2,1)S(1)}, bf16[64,512]{1,0:T(8,128)(2,1)S(1)}, u32[]{:S(2)}, u32[]{:S(2)}) collective-permute-start(bf16[64,512]{1,0:T(8,128)(2,1)S(1)} %get-tuple-element.44), channel_id=1, source_target_pairs={{0,14},{2,12},{4,10},{6,8},{8,6},{10,4},{12,2},{14,0},{1,15},{3,13... | collective-permute-start | bytes 196616 | tf_op jit(solution)/shard_map/ppermute | solution.py:256
  13.1 0.1 collective-permute-start.3
  13.2 0.0 collective-permute-done.refs_0_.refs_4_
  13.2 1.8 %collective-permute-start.4 = (bf16[64,512]{1,0:T(8,128)(2,1)S(1)}, bf16[64,512]{1,0:T(8,128)(2,1)S(1)}, u32[]{:S(2)}, u32[]{:S(2)}) collective-permute-start(bf16[64,512]{1,0:T(8,128)(2,1)S(1)} %get-tuple-element.42), channel_id=1, source_target_pairs={{0,6},{2,4},{4,2},{6,0},{8,14},{10,12},{12,10},{14,8},{1,7},{3,5},... | collective-permute-start | bytes 196616 | tf_op jit(solution)/shard_map/ppermute | solution.py:256
  15.0 2.8 %collective-permute-done.1.refs_1_.refs_5_ = bf16[64,512]{1,0:T(8,128)(2,1)S(1)} collective-permute-done((bf16[64,512]{1,0:T(8,128)(2,1)S(1)}, bf16[64,512]{1,0:T(8,128)(2,1)S(1)}, u32[]{:S(2)}, u32[]{:S(2)}) %collective-permute-start.1) | collective-permute-done | bytes 65568 | tf_op jit(solution)/shard_map/ppermute | solution.py:256
  17.8 2.5 %stage.1 = (bf16[1024,2560]{1,0:T(8,128)(2,1)S(1)}, bf16[64,2048]{1,0:T(8,128)(2,1)S(1)}, s32[1,512]{1,0:T(1,128)S(1)}) custom-call(s32[8]{0:T(128)} %counts_in.1, bf16[1024,2560]{1,0:T(8,128)(2,1)} %matrix_in.1, bf16[64,2048]{1,0:T(8,128)(2,1)} %queries_in.1, bf16[64,512]{1,0:T(8,128)(2,1)S(1)} %collective-permute-done.refs_0_.refs_4_, ...), custom_call_target="tpu_custom_call" | custom-call | flops 3932160000 | bytes 11143200 | tf_op jit(solution)/shard_map/stage/pallas_call | solution.py:21
  20.3 0.0 collective-permute-done.6.refs_7_
  20.3 0.9 %collective-permute-done.4.refs_3_ = bf16[64,512]{1,0:T(8,128)(2,1)S(1)} collective-permute-done((bf16[64,512]{1,0:T(8,128)(2,1)S(1)}, bf16[64,512]{1,0:T(8,128)(2,1)S(1)}, u32[]{:S(2)}, u32[]{:S(2)}) %collective-permute-start.4) | collective-permute-done | bytes 65568 | tf_op jit(solution)/shard_map/ppermute | solution.py:256
  21.3 0.0 collective-permute-done.3.refs_2_
  21.3 0.3 compact.1
  21.6 0.1 collective-permute-start.8
  21.7 3.6 %collective-permute-start.7 = (bf16[128,512]{1,0:T(8,128)(2,1)S(1)}, bf16[128,512]{1,0:T(8,128)(2,1)S(1)}, u32[]{:S(2)}, u32[]{:S(2)}) collective-permute-start(bf16[128,512]{1,0:T(8,128)(2,1)S(1)} %get-tuple-element.45.near), channel_id=1, source_target_pairs={{0,8},{2,10},{4,12},{6,14},{1,9},{3,11},{5,13},{7,15},{16,24},{18,... | collective-permute-start | bytes 393224 | tf_op jit(solution)/shard_map/ppermute | solution.py:259
  25.3 1.0 %project_own.1.product = f32[256,2560]{1,0:T(8,128)S(1)} custom-call(bf16[256,512]{1,0:T(8,128)(2,1)S(1)} %get-tuple-element.47.own, bf16[1024,2560]{1,0:T(8,128)(2,1)S(1)} %get-tuple-element.48.matrix), custom_call_target="tpu_custom_call" | custom-call | flops 671088640 | bytes 8126464 | tf_op jit(solution)/shard_map/project_own/pallas_call | solution.py:21
  26.3 0.0 collective-permute-done.8.other
  26.3 0.6 %project.3 = (f32[128,1408]{1,0:T(8,128)S(1)}, bf16[128,1408]{1,0:T(8,128)(2,1)S(1)}) custom-call(f32[256,2560]{1,0:T(8,128)S(1)} %project_own.1.product, bf16[256,512]{1,0:T(8,128)(2,1)S(1)} %collective-permute-done.8.other, bf16[1024,2560]{1,0:T(8,128)(2,1)S(1)} %get-tuple-element.48.matrix), custom_call_target="tpu_custom_call" | custom-call | flops 369098752 | bytes 9207808 | tf_op jit(solution)/shard_map/project/pallas_call | solution.py:21
  26.9 1.6 %collective-permute-start.10 = (bf16[128,1408]{1,0:T(8,128)(2,1)S(1)}, bf16[128,1408]{1,0:T(8,128)(2,1)S(1)}, u32[]{:S(2)}, u32[]{:S(2)}) collective-permute-start(bf16[128,1408]{1,0:T(8,128)(2,1)S(1)} %get-tuple-element.51), channel_id=1, source_target_pairs={{0,2},{2,0},{4,6},{6,4},{8,10},{10,8},{12,14},{14,12},{1,3},{3,1},... | collective-permute-start | bytes 1081352 | tf_op jit(solution)/shard_map/ppermute | solution.py:256
  28.5 0.5 project.2
  29.0 0.0 copy-start
  29.0 2.2 %collective-permute-start.11 = (bf16[128,1152]{1,0:T(8,128)(2,1)S(1)}, bf16[128,1152]{1,0:T(8,128)(2,1)S(1)}, u32[]{:S(2)}, u32[]{:S(2)}) collective-permute-start(bf16[128,1152]{1,0:T(8,128)(2,1)S(1)} %get-tuple-element.49.after), channel_id=1, source_target_pairs={{0,4},{2,6},{4,0},{6,2},{8,12},{10,14},{12,8},{14,10},{1,5},{3,7},... | collective-permute-start | bytes 884744 | tf_op jit(solution)/shard_map/ppermute | solution.py:256
  31.2 0.6 collective-permute-start.9
  31.8 6.4 %collective-permute-done.10.received = bf16[128,1408]{1,0:T(8,128)(2,1)S(1)} collective-permute-done((bf16[128,1408]{1,0:T(8,128)(2,1)S(1)}, bf16[128,1408]{1,0:T(8,128)(2,1)S(1)}, u32[]{:S(2)}, u32[]{:S(2)}) %collective-permute-start.10) | collective-permute-done | bytes 360480 | tf_op jit(solution)/shard_map/ppermute | solution.py:256
  38.2 0.1 hop_sum.2
  38.3 0.0 collective-permute-done.11.received
  38.3 0.1 hop_sum.3
  38.4 1.6 %collective-permute-start.13 = (bf16[64,1152]{1,0:T(8,128)(2,1)S(1)}, bf16[64,1152]{1,0:T(8,128)(2,1)S(1)}, u32[]{:S(2)}, u32[]{:S(2)}) collective-permute-start(bf16[64,1152]{1,0:T(8,128)(2,1)S(1)} %get-tuple-element.57), channel_id=1, source_target_pairs={{0,2},{2,0},{4,6},{6,4},{8,10},{10,8},{12,14},{14,12},{1,3},{3,1},... | collective-permute-start | bytes 442376 | tf_op jit(solution)/shard_map/ppermute | solution.py:256
  40.0 2.1 %collective-permute-start.12 = (bf16[64,1408]{1,0:T(8,128)(2,1)S(1)}, bf16[64,1408]{1,0:T(8,128)(2,1)S(1)}, u32[]{:S(2)}, u32[]{:S(2)}) collective-permute-start(bf16[64,1408]{1,0:T(8,128)(2,1)S(1)} %get-tuple-element.56), channel_id=1, source_target_pairs={{0,4},{2,6},{4,0},{6,2},{8,12},{10,14},{12,8},{14,10},{1,5},{3,7},... | collective-permute-start | bytes 540680 | tf_op jit(solution)/shard_map/ppermute | solution.py:256
  42.1 0.3 collective-permute-done.9.odd
  42.4 2.0 %attention.1 = (f32[64,2048]{1,0:T(8,128)}, f32[8,64]{1,0:T(8,128)S(1)}) custom-call(bf16[64,2048]{1,0:T(8,128)(2,1)S(1)} %get-tuple-element.35.queries, bf16[128,512]{1,0:T(8,128)(2,1)S(1)} %get-tuple-element.45.near, bf16[128,512]{1,0:T(8,128)(2,1)S(1)} %collective-permute-done.7.far, bf16[64,512]{1,0:T(8,128)(2,1)S(1)} %get-tuple-element.46.pair, ...), custom_call_target="tpu_custom_call" | custom-call | flops 268435456 | bytes 1673216 | tf_op jit(solution)/shard_map/attention/pallas_call | solution.py:21
  44.4 2.2 %collective-permute-start.15 = (f32[2,64]{1,0:T(2,128)S(1)}, f32[2,64]{1,0:T(2,128)S(1)}, u32[]{:S(2)}, u32[]{:S(2)}) collective-permute-start(f32[2,64]{1,0:T(2,128)S(1)} %get-tuple-element.65), channel_id=1, source_target_pairs={{0,4},{2,6},{4,0},{6,2},{8,12},{10,14},{12,8},{14,10},{1,5},{3,7},... | collective-permute-start | bytes 1544 | tf_op jit(solution)/shard_map/ppermute | solution.py:256
  46.6 1.5 %collective-permute-start.16 = (f32[2,64]{1,0:T(2,128)S(1)}, f32[2,64]{1,0:T(2,128)S(1)}, u32[]{:S(2)}, u32[]{:S(2)}) collective-permute-start(f32[2,64]{1,0:T(2,128)S(1)} %get-tuple-element.64), channel_id=1, source_target_pairs={{0,2},{2,0},{4,6},{6,4},{8,10},{10,8},{12,14},{14,12},{1,3},{3,1},... | collective-permute-start | bytes 1544 | tf_op jit(solution)/shard_map/ppermute | solution.py:256
  48.1 0.1 hop_sum_both.1
  48.2 0.5 collective-permute-start.14
  48.7 0.0 collective-permute-done.15.refs_1_
  48.7 1.4 %collective-permute-done.16.refs_2_ = f32[2,64]{1,0:T(2,128)S(1)} collective-permute-done((f32[2,64]{1,0:T(2,128)S(1)}, f32[2,64]{1,0:T(2,128)S(1)}, u32[]{:S(2)}, u32[]{:S(2)}) %collective-permute-start.16) | collective-permute-done | bytes 544 | tf_op jit(solution)/shard_map/ppermute | solution.py:256
  50.1 2.4 %collective-permute-done.17.refs_3_ = f32[2,64]{1,0:T(2,128)S(1)} collective-permute-done((f32[2,64]{1,0:T(2,128)S(1)}, f32[2,64]{1,0:T(2,128)S(1)}, u32[]{:S(2)}, u32[]{:S(2)}) %collective-permute-start.17) | collective-permute-done | bytes 544 | tf_op jit(solution)/shard_map/ppermute | solution.py:256
  52.6 0.1 collective-permute-start.18
  52.6 0.1 collective-permute-start.19
  52.7 2.9 %collective-permute-start.20 = (f32[1,64]{1,0:T(1,128)S(1)}, f32[1,64]{1,0:T(1,128)S(1)}, u32[]{:S(2)}, u32[]{:S(2)}) collective-permute-start(f32[1,64]{1,0:T(1,128)S(1)} %get-tuple-element.67), channel_id=1, source_target_pairs={{0,9},{1,8},{2,11},{3,10},{4,13},{5,12},{6,15},{7,14},{8,1},{9,0},... | collective-permute-start | bytes 776 | tf_op jit(solution)/shard_map/ppermute | solution.py:262
  55.7 1.4 %collective-permute-done.18.refs_1_ = f32[1,64]{1,0:T(1,128)S(1)} collective-permute-done((f32[1,64]{1,0:T(1,128)S(1)}, f32[1,64]{1,0:T(1,128)S(1)}, u32[]{:S(2)}, u32[]{:S(2)}) %collective-permute-start.18) | collective-permute-done | bytes 288 | tf_op jit(solution)/shard_map/ppermute | solution.py:256
  57.1 0.0 collective-permute-done.19.refs_2_
  57.1 0.0 collective-permute-done.20.refs_3_
  57.1 0.0 collective-permute-done.14.received
  57.1 0.8 %finish.1 = (f32[32,2560]{1,0:T(8,128)}, f32[1,64]{1,0:T(1,128)}) custom-call(f32[1,2560]{1,0:T(1,128)S(1)} %reshape.20.bias, f32[32,2560]{1,0:T(8,128)S(1)} %get-tuple-element.58.after.kept, bf16[32,2560]{1,0:T(8,128)(2,1)S(1)} %collective-permute-done.14.received, f32[1,64]{1,0:T(1,128)S(1)} %get-tuple-element.68.refs_0_, ...), custom_call_target="tpu_custom_call" | custom-call | flops 655360 | bytes 830720 | tf_op jit(solution)/shard_map/finish/pallas_call | solution.py:21
  (13 shorter events, 0.1 us)
Async XLA Ops:
  2.4 10.7 %collective-permute-start.2 = (bf16[64,1024]{1,0:T(8,128)(2,1)S(1)}, bf16[64,1024]{1,0:T(8,128)(2,1)S(1)}, u32[]{:S(2)}, u32[]{:S(2)}) collective-permute-start(bf16[64,1024]{1,0:T(8,128)(2,1)S(1)} %get-tuple-element.38), channel_id=1, source_target_pairs={{0,2},{2,0},{4,6},{6,4},{8,10},{10,8},{12,14},{14,12},{1,3},{3,1},... | collective-permute-start | bytes 393224 | tf_op jit(solution)/shard_map/ppermute | solution.py:256
  5.4 7.8 %collective-permute-start = (bf16[64,512]{1,0:T(8,128)(2,1)S(1)}, bf16[64,512]{1,0:T(8,128)(2,1)S(1)}, u32[]{:S(2)}, u32[]{:S(2)}) collective-permute-start(bf16[64,512]{1,0:T(8,128)(2,1)S(1)} %get-tuple-element.33), channel_id=1, source_target_pairs={{0,8},{2,10},{4,12},{6,14},{8,0},{10,2},{12,4},{14,6},{1,9},{3,11}... | collective-permute-start | bytes 196616 | tf_op jit(solution)/shard_map/ppermute | solution.py:256
  8.0 9.8 %collective-permute-start.1 = (bf16[64,512]{1,0:T(8,128)(2,1)S(1)}, bf16[64,512]{1,0:T(8,128)(2,1)S(1)}, u32[]{:S(2)}, u32[]{:S(2)}) collective-permute-start(bf16[64,512]{1,0:T(8,128)(2,1)S(1)} %get-tuple-element.34), channel_id=1, source_target_pairs={{0,10},{2,8},{4,14},{6,12},{8,2},{10,0},{12,6},{14,4},{1,11},{3,9}... | collective-permute-start | bytes 196616 | tf_op jit(solution)/shard_map/ppermute | solution.py:256
  8.0 12.3 %collective-permute-start.5 = (bf16[64,512]{1,0:T(8,128)(2,1)S(1)}, bf16[64,512]{1,0:T(8,128)(2,1)S(1)}, u32[]{:S(2)}, u32[]{:S(2)}) collective-permute-start(bf16[64,512]{1,0:T(8,128)(2,1)S(1)} %get-tuple-element.43), channel_id=1, source_target_pairs={{0,12},{2,14},{4,8},{6,10},{8,4},{10,6},{12,0},{14,2},{1,13},{3,15... | collective-permute-start | bytes 196616 | tf_op jit(solution)/shard_map/ppermute | solution.py:256
  11.9 8.4 %collective-permute-start.6 = (bf16[64,512]{1,0:T(8,128)(2,1)S(1)}, bf16[64,512]{1,0:T(8,128)(2,1)S(1)}, u32[]{:S(2)}, u32[]{:S(2)}) collective-permute-start(bf16[64,512]{1,0:T(8,128)(2,1)S(1)} %get-tuple-element.44), channel_id=1, source_target_pairs={{0,14},{2,12},{4,10},{6,8},{8,6},{10,4},{12,2},{14,0},{1,15},{3,13... | collective-permute-start | bytes 196616 | tf_op jit(solution)/shard_map/ppermute | solution.py:256
  13.1 8.2 %collective-permute-start.3 = (bf16[64,1024]{1,0:T(8,128)(2,1)S(1)}, bf16[64,1024]{1,0:T(8,128)(2,1)S(1)}, u32[]{:S(2)}, u32[]{:S(2)}) collective-permute-start(bf16[64,1024]{1,0:T(8,128)(2,1)S(1)} %get-tuple-element.41), channel_id=1, source_target_pairs={{0,4},{2,6},{4,0},{6,2},{8,12},{10,14},{12,8},{14,10},{1,5},{3,7},... | collective-permute-start | bytes 393224 | tf_op jit(solution)/shard_map/ppermute | solution.py:256
  13.2 8.1 %collective-permute-start.4 = (bf16[64,512]{1,0:T(8,128)(2,1)S(1)}, bf16[64,512]{1,0:T(8,128)(2,1)S(1)}, u32[]{:S(2)}, u32[]{:S(2)}) collective-permute-start(bf16[64,512]{1,0:T(8,128)(2,1)S(1)} %get-tuple-element.42), channel_id=1, source_target_pairs={{0,6},{2,4},{4,2},{6,0},{8,14},{10,12},{12,10},{14,8},{1,7},{3,5},... | collective-permute-start | bytes 196616 | tf_op jit(solution)/shard_map/ppermute | solution.py:256
  21.6 4.7 %collective-permute-start.8 = (bf16[256,512]{1,0:T(8,128)(2,1)S(1)}, bf16[256,512]{1,0:T(8,128)(2,1)S(1)}, u32[]{:S(2)}, u32[]{:S(2)}) collective-permute-start(bf16[256,512]{1,0:T(8,128)(2,1)S(1)} %get-tuple-element.47.own), channel_id=1, source_target_pairs={{0,1},{1,0},{2,3},{3,2},{4,5},{5,4},{6,7},{7,6},{8,9},{9,8},{10,11... | collective-permute-start | bytes 786440 | tf_op jit(solution)/shard_map/ppermute | solution.py:265
  21.7 9.5 %collective-permute-start.7 = (bf16[128,512]{1,0:T(8,128)(2,1)S(1)}, bf16[128,512]{1,0:T(8,128)(2,1)S(1)}, u32[]{:S(2)}, u32[]{:S(2)}) collective-permute-start(bf16[128,512]{1,0:T(8,128)(2,1)S(1)} %get-tuple-element.45.near), channel_id=1, source_target_pairs={{0,8},{2,10},{4,12},{6,14},{1,9},{3,11},{5,13},{7,15},{16,24},{18,... | collective-permute-start | bytes 393224 | tf_op jit(solution)/shard_map/ppermute | solution.py:259
  26.9 11.3 %collective-permute-start.10 = (bf16[128,1408]{1,0:T(8,128)(2,1)S(1)}, bf16[128,1408]{1,0:T(8,128)(2,1)S(1)}, u32[]{:S(2)}, u32[]{:S(2)}) collective-permute-start(bf16[128,1408]{1,0:T(8,128)(2,1)S(1)} %get-tuple-element.51), channel_id=1, source_target_pairs={{0,2},{2,0},{4,6},{6,4},{8,10},{10,8},{12,14},{14,12},{1,3},{3,1},... | collective-permute-start | bytes 1081352 | tf_op jit(solution)/shard_map/ppermute | solution.py:256
  29.0 26.7 %copy-start = (f32[2560]{0:T(1024)S(1)}, f32[2560]{0:T(1024)}, u32[]{:S(2)}) copy-start(f32[2560]{0:T(1024)} %param.17) | copy-start | bytes 30724
  29.0 9.3 %collective-permute-start.11 = (bf16[128,1152]{1,0:T(8,128)(2,1)S(1)}, bf16[128,1152]{1,0:T(8,128)(2,1)S(1)}, u32[]{:S(2)}, u32[]{:S(2)}) collective-permute-start(bf16[128,1152]{1,0:T(8,128)(2,1)S(1)} %get-tuple-element.49.after), channel_id=1, source_target_pairs={{0,4},{2,6},{4,0},{6,2},{8,12},{10,14},{12,8},{14,10},{1,5},{3,7},... | collective-permute-start | bytes 884744 | tf_op jit(solution)/shard_map/ppermute | solution.py:256
  31.2 11.2 %collective-permute-start.9 = (bf16[192,512]{1,0:T(8,128)(2,1)S(1)}, bf16[192,512]{1,0:T(8,128)(2,1)S(1)}, u32[]{:S(2)}, u32[]{:S(2)}) collective-permute-start(bf16[192,512]{1,0:T(8,128)(2,1)S(1)} %gather.1), channel_id=1, source_target_pairs={{0,2},{2,0},{4,6},{6,4},{8,10},{10,8},{12,14},{14,12},{1,3},{3,1},... | collective-permute-start | bytes 589832 | tf_op jit(solution)/shard_map/ppermute | solution.py:256
  38.4 9.7 %collective-permute-start.13 = (bf16[64,1152]{1,0:T(8,128)(2,1)S(1)}, bf16[64,1152]{1,0:T(8,128)(2,1)S(1)}, u32[]{:S(2)}, u32[]{:S(2)}) collective-permute-start(bf16[64,1152]{1,0:T(8,128)(2,1)S(1)} %get-tuple-element.57), channel_id=1, source_target_pairs={{0,2},{2,0},{4,6},{6,4},{8,10},{10,8},{12,14},{14,12},{1,3},{3,1},... | collective-permute-start | bytes 442376 | tf_op jit(solution)/shard_map/ppermute | solution.py:256
  40.0 8.1 %collective-permute-start.12 = (bf16[64,1408]{1,0:T(8,128)(2,1)S(1)}, bf16[64,1408]{1,0:T(8,128)(2,1)S(1)}, u32[]{:S(2)}, u32[]{:S(2)}) collective-permute-start(bf16[64,1408]{1,0:T(8,128)(2,1)S(1)} %get-tuple-element.56), channel_id=1, source_target_pairs={{0,4},{2,6},{4,0},{6,2},{8,12},{10,14},{12,8},{14,10},{1,5},{3,7},... | collective-permute-start | bytes 540680 | tf_op jit(solution)/shard_map/ppermute | solution.py:256
  44.4 4.3 %collective-permute-start.15 = (f32[2,64]{1,0:T(2,128)S(1)}, f32[2,64]{1,0:T(2,128)S(1)}, u32[]{:S(2)}, u32[]{:S(2)}) collective-permute-start(f32[2,64]{1,0:T(2,128)S(1)} %get-tuple-element.65), channel_id=1, source_target_pairs={{0,4},{2,6},{4,0},{6,2},{8,12},{10,14},{12,8},{14,10},{1,5},{3,7},... | collective-permute-start | bytes 1544 | tf_op jit(solution)/shard_map/ppermute | solution.py:256
  46.6 3.6 %collective-permute-start.16 = (f32[2,64]{1,0:T(2,128)S(1)}, f32[2,64]{1,0:T(2,128)S(1)}, u32[]{:S(2)}, u32[]{:S(2)}) collective-permute-start(f32[2,64]{1,0:T(2,128)S(1)} %get-tuple-element.64), channel_id=1, source_target_pairs={{0,2},{2,0},{4,6},{6,4},{8,10},{10,8},{12,14},{14,12},{1,3},{3,1},... | collective-permute-start | bytes 1544 | tf_op jit(solution)/shard_map/ppermute | solution.py:256
  48.1 4.5 %collective-permute-start.17 = (f32[2,64]{1,0:T(2,128)S(1)}, f32[2,64]{1,0:T(2,128)S(1)}, u32[]{:S(2)}, u32[]{:S(2)}) collective-permute-start(f32[2,64]{1,0:T(2,128)S(1)} %get-tuple-element.63), channel_id=1, source_target_pairs={{0,6},{2,4},{4,2},{6,0},{8,14},{10,12},{12,10},{14,8},{1,7},{3,5},... | collective-permute-start | bytes 1544 | tf_op jit(solution)/shard_map/ppermute | solution.py:256
  48.2 8.9 %collective-permute-start.14 = (bf16[32,2560]{1,0:T(8,128)(2,1)S(1)}, bf16[32,2560]{1,0:T(8,128)(2,1)S(1)}, u32[]{:S(2)}, u32[]{:S(2)}) collective-permute-start(bf16[32,2560]{1,0:T(8,128)(2,1)S(1)} %get-tuple-element.59), channel_id=1, source_target_pairs={{0,8},{2,10},{4,12},{6,14},{8,0},{10,2},{12,4},{14,6},{1,9},{3,11}... | collective-permute-start | bytes 491528 | tf_op jit(solution)/shard_map/ppermute | solution.py:256
  52.6 4.5 %collective-permute-start.18 = (f32[1,64]{1,0:T(1,128)S(1)}, f32[1,64]{1,0:T(1,128)S(1)}, u32[]{:S(2)}, u32[]{:S(2)}) collective-permute-start(f32[1,64]{1,0:T(1,128)S(1)} %get-tuple-element.67), channel_id=1, source_target_pairs={{0,8},{2,10},{4,12},{6,14},{8,0},{10,2},{12,4},{14,6},{1,9},{3,11}... | collective-permute-start | bytes 776 | tf_op jit(solution)/shard_map/ppermute | solution.py:256
  52.6 4.4 %collective-permute-start.19 = (f32[1,64]{1,0:T(1,128)S(1)}, f32[1,64]{1,0:T(1,128)S(1)}, u32[]{:S(2)}, u32[]{:S(2)}) collective-permute-start(f32[1,64]{1,0:T(1,128)S(1)} %get-tuple-element.68.refs_0_), channel_id=1, source_target_pairs={{0,1},{1,0},{2,3},{3,2},{4,5},{5,4},{6,7},{7,6},{8,9},{9,8},{10,11... | collective-permute-start | bytes 776 | tf_op jit(solution)/shard_map/ppermute | solution.py:265
  52.7 4.4 %collective-permute-start.20 = (f32[1,64]{1,0:T(1,128)S(1)}, f32[1,64]{1,0:T(1,128)S(1)}, u32[]{:S(2)}, u32[]{:S(2)}) collective-permute-start(f32[1,64]{1,0:T(1,128)S(1)} %get-tuple-element.67), channel_id=1, source_target_pairs={{0,9},{1,8},{2,11},{3,10},{4,13},{5,12},{6,15},{7,14},{8,1},{9,0},... | collective-permute-start | bytes 776 | tf_op jit(solution)/shard_map/ppermute | solution.py:262

commit v17 on v15

--- a/solution.py
+++ b/solution.py
@@ -134,7 +134,8 @@
     return sorted(range(n), key=lambda k: [k & mask for mask in masks])
 
 
-def project_own_kernel(own, matrix, out):
+def project_own_kernel(own, matrix, even_in, out, even):
+    even[...] = even_in[...]
     half = own.shape[1]
     mine = pl.ds(pl.multiple_of(lax.axis_index("ten") * half, half), half)
     tile = out.shape[1] // 4 if out.shape[1] % 512 == 0 else out.shape[1]
@@ -304,11 +305,11 @@
     other = swap(own)
     rest = [1 << i for i in range(2, n.bit_length() - 1)]
     masks = [[1, 2] + rest, [2, 1] + rest]
-    (product,) = call(
+    product, even = call(
         project_own_kernel,
         "project_own",
-        (own, matrix),
-        [shape((survivors, width), f32)],
+        (own, matrix, even),
+        [shape((survivors, width), f32), shape(even.shape, bf16)],
         2 * survivors * half * width,
     )
     products = [

time: 56.2 us -> 56.2 us (level)
  starting transfers between devices: 30.5 us -> 29.8 us
  waiting for transfers between devices: 15.1 us -> 15.7 us
    ppermute x18, waiting for transfers between devices: 15.1 us -> 15.7 us  [trade(): return lax.ppermute(x, 'seq', [(i, i ^ k) for i in range(n)])]
  transfers between devices with their start and end apart: 21 -> 21, of which waited for: 8 -> 7; matrix products, arithmetic and copies ran while one was open for 0% -> 0% of each run, Pallas kernels for 12% -> 12%
where the time goes in v17:
time: 56.2 us; the launch traced here: 56 us
  starting transfers between devices  29.8 us (53%)
  waiting for transfers between devices  15.7 us (28%)
  Pallas kernels  9.71 us (17%)
  between operations  0.76 us (1%)
    ppermute x18, starting transfers between devices, trade(): return lax.ppermute(x, 'seq', [(i, i ^ k) for i in range(n)])  27.4 us
    ppermute x18, waiting for transfers between devices, trade(): return lax.ppermute(x, 'seq', [(i, i ^ k) for i in range(n)])  15.7 us
    pallas_call x14, Pallas kernels, call(): pl.pallas_call(body, out_shape=list(outputs), in_specs=in_specs or [VMEM]...  9.71 us
    ppermute x1, starting transfers between devices, trade_across(): lax.ppermute(x, ('seq', 'ten'), [(2 * i + t, 2 * (i ^ k) + 1 - t) for i i...  2.36 us
  transfers between devices with their start and end apart: 21, of which 7 were waited for; matrix products, arithmetic and copies ran while one was open for 0% of the time, Pallas kernels for 12%

profile of v17, /device:TPU:0, one launch (start us, length us, event | category | flops | bytes accessed | tf_op | source)
XLA Modules:
  0.0 56.0 jit_solution(14146043088762011468)
XLA Ops:
  0.6 1.7 %norm_select.1 = (bf16[64,1024]{1,0:T(8,128)(2,1)S(1)}, bf16[64,1024]{1,0:T(8,128)(2,1)S(1)}, bf16[64,1024]{1,0:T(8,128)(2,1)S(1)}, bf16[64,512]{1,0:T(8,128)(2,...) custom-call(bf16[64,8192]{1,0:T(8,128)(2,1)} %hidden_in.1, ...), custom_call_target="tpu_custom_call" | custom-call | flops 2097152 | bytes 1868032 | tf_op jit(solution)/shard_map/norm_select/pallas_call | solution.py:21
  2.4 3.0 %collective-permute-start.2 = (bf16[64,1024]{1,0:T(8,128)(2,1)S(1)}, bf16[64,1024]{1,0:T(8,128)(2,1)S(1)}, u32[]{:S(2)}, u32[]{:S(2)}) collective-permute-start(bf16[64,1024]{1,0:T(8,128)(2,1)S(1)} %get-tuple-element.40), channel_id=1, source_target_pairs={{0,2},{2,0},{4,6},{6,4},{8,10},{10,8},{12,14},{14,12},{1,3},{3,1},... | collective-permute-start | bytes 393224 | tf_op jit(solution)/shard_map/ppermute | solution.py:257
  5.4 2.6 %collective-permute-start = (bf16[64,512]{1,0:T(8,128)(2,1)S(1)}, bf16[64,512]{1,0:T(8,128)(2,1)S(1)}, u32[]{:S(2)}, u32[]{:S(2)}) collective-permute-start(bf16[64,512]{1,0:T(8,128)(2,1)S(1)} %get-tuple-element.35), channel_id=1, source_target_pairs={{0,8},{2,10},{4,12},{6,14},{8,0},{10,2},{12,4},{14,6},{1,9},{3,11}... | collective-permute-start | bytes 196616 | tf_op jit(solution)/shard_map/ppermute | solution.py:257
  8.0 0.0 collective-permute-start.1
  8.0 3.9 %collective-permute-start.5 = (bf16[64,512]{1,0:T(8,128)(2,1)S(1)}, bf16[64,512]{1,0:T(8,128)(2,1)S(1)}, u32[]{:S(2)}, u32[]{:S(2)}) collective-permute-start(bf16[64,512]{1,0:T(8,128)(2,1)S(1)} %get-tuple-element.45), channel_id=1, source_target_pairs={{0,12},{2,14},{4,8},{6,10},{8,4},{10,6},{12,0},{14,2},{1,13},{3,15... | collective-permute-start | bytes 196616 | tf_op jit(solution)/shard_map/ppermute | solution.py:257
  11.9 1.2 %collective-permute-start.6 = (bf16[64,512]{1,0:T(8,128)(2,1)S(1)}, bf16[64,512]{1,0:T(8,128)(2,1)S(1)}, u32[]{:S(2)}, u32[]{:S(2)}) collective-permute-start(bf16[64,512]{1,0:T(8,128)(2,1)S(1)} %get-tuple-element.46), channel_id=1, source_target_pairs={{0,14},{2,12},{4,10},{6,8},{8,6},{10,4},{12,2},{14,0},{1,15},{3,13... | collective-permute-start | bytes 196616 | tf_op jit(solution)/shard_map/ppermute | solution.py:257
  13.1 0.0 collective-permute-done.2.refs_2_.refs_1_
  13.1 0.1 collective-permute-start.3
  13.2 0.0 collective-permute-done.refs_0_.refs_4_
  13.2 1.8 %collective-permute-start.4 = (bf16[64,512]{1,0:T(8,128)(2,1)S(1)}, bf16[64,512]{1,0:T(8,128)(2,1)S(1)}, u32[]{:S(2)}, u32[]{:S(2)}) collective-permute-start(bf16[64,512]{1,0:T(8,128)(2,1)S(1)} %get-tuple-element.44), channel_id=1, source_target_pairs={{0,6},{2,4},{4,2},{6,0},{8,14},{10,12},{12,10},{14,8},{1,7},{3,5},... | collective-permute-start | bytes 196616 | tf_op jit(solution)/shard_map/ppermute | solution.py:257
  15.0 2.8 %collective-permute-done.1.refs_1_.refs_5_ = bf16[64,512]{1,0:T(8,128)(2,1)S(1)} collective-permute-done((bf16[64,512]{1,0:T(8,128)(2,1)S(1)}, bf16[64,512]{1,0:T(8,128)(2,1)S(1)}, u32[]{:S(2)}, u32[]{:S(2)}) %collective-permute-start.1) | collective-permute-done | bytes 65568 | tf_op jit(solution)/shard_map/ppermute | solution.py:257
  17.8 2.5 %stage.1 = (bf16[1024,2560]{1,0:T(8,128)(2,1)S(1)}, bf16[64,2048]{1,0:T(8,128)(2,1)S(1)}, s32[1,512]{1,0:T(1,128)S(1)}) custom-call(s32[8]{0:T(128)} %counts_in.1, bf16[1024,2560]{1,0:T(8,128)(2,1)} %matrix_in.1, bf16[64,2048]{1,0:T(8,128)(2,1)} %queries_in.1, bf16[64,512]{1,0:T(8,128)(2,1)S(1)} %collective-permute-done.refs_0_.refs_4_, ...), custom_call_target="tpu_custom_call" | custom-call | flops 3932160000 | bytes 11143200 | tf_op jit(solution)/shard_map/stage/pallas_call | solution.py:21
  20.3 0.0 collective-permute-done.5.refs_6_
  20.3 0.0 collective-permute-done.6.refs_7_
  20.3 0.9 %collective-permute-done.4.refs_3_ = bf16[64,512]{1,0:T(8,128)(2,1)S(1)} collective-permute-done((bf16[64,512]{1,0:T(8,128)(2,1)S(1)}, bf16[64,512]{1,0:T(8,128)(2,1)S(1)}, u32[]{:S(2)}, u32[]{:S(2)}) %collective-permute-start.4) | collective-permute-done | bytes 65568 | tf_op jit(solution)/shard_map/ppermute | solution.py:257
  21.3 0.0 collective-permute-done.3.refs_2_
  21.3 0.3 compact.1
  21.6 0.1 collective-permute-start.8
  21.7 1.0 %project_own.1 = (f32[256,2560]{1,0:T(8,128)S(1)}, bf16[128,512]{1,0:T(8,128)(2,1)S(1)}) custom-call(bf16[256,512]{1,0:T(8,128)(2,1)S(1)} %get-tuple-element.47.own, bf16[1024,2560]{1,0:T(8,128)(2,1)S(1)} %get-tuple-element.48.matrix, bf16[128,512]{1,0:T(8,128)(2,1)S(1)} %get-tuple-element.49.even_in), custom_call_target="tpu_custom_call" | custom-call | flops 671088640 | bytes 8388608 | tf_op jit(solution)/shard_map/project_own/pallas_call | solution.py:21
  22.7 1.7 %collective-permute-start.7 = (bf16[128,512]{1,0:T(8,128)(2,1)S(1)}, bf16[128,512]{1,0:T(8,128)(2,1)S(1)}, u32[]{:S(2)}, u32[]{:S(2)}) collective-permute-start(bf16[128,512]{1,0:T(8,128)(2,1)S(1)} %get-tuple-element.50.near), channel_id=1, source_target_pairs={{0,8},{2,10},{4,12},{6,14},{8,0},{10,2},{12,4},{14,6},{1,9},{3,11}... | collective-permute-start | bytes 393224 | tf_op jit(solution)/shard_map/ppermute | solution.py:257
  24.4 0.0 collective-permute-done.8.other
  24.4 0.6 %project.3 = (f32[128,1280]{1,0:T(8,128)S(1)}, bf16[128,1280]{1,0:T(8,128)(2,1)S(1)}) custom-call(f32[256,2560]{1,0:T(8,128)S(1)} %get-tuple-element.52.product, bf16[256,512]{1,0:T(8,128)(2,1)S(1)} %collective-permute-done.8.other, bf16[1024,2560]{1,0:T(8,128)(2,1)S(1)} %get-tuple-element.48.matrix), custom_call_target="tpu_custom_call" | custom-call | flops 335544320 | bytes 9109504 | tf_op jit(solution)/shard_map/project/pallas_call | solution.py:21
  25.0 1.6 %collective-permute-start.10 = (bf16[128,1280]{1,0:T(8,128)(2,1)S(1)}, bf16[128,1280]{1,0:T(8,128)(2,1)S(1)}, u32[]{:S(2)}, u32[]{:S(2)}) collective-permute-start(bf16[128,1280]{1,0:T(8,128)(2,1)S(1)} %get-tuple-element.55), channel_id=1, source_target_pairs={{0,2},{2,0},{4,6},{6,4},{8,10},{10,8},{12,14},{14,12},{1,3},{3,1},... | collective-permute-start | bytes 983048 | tf_op jit(solution)/shard_map/ppermute | solution.py:257
  26.6 0.6 %project.2 = (f32[128,1280]{1,0:T(8,128)S(1)}, bf16[128,1280]{1,0:T(8,128)(2,1)S(1)}) custom-call(f32[256,2560]{1,0:T(8,128)S(1)} %get-tuple-element.52.product, bf16[256,512]{1,0:T(8,128)(2,1)S(1)} %collective-permute-done.8.other, bf16[1024,2560]{1,0:T(8,128)(2,1)S(1)} %get-tuple-element.48.matrix), custom_call_target="tpu_custom_call" | custom-call | flops 335544320 | bytes 9109504 | tf_op jit(solution)/shard_map/project/pallas_call | solution.py:21
  27.2 0.0 copy-start
  27.2 2.2 %collective-permute-start.11 = (bf16[128,1280]{1,0:T(8,128)(2,1)S(1)}, bf16[128,1280]{1,0:T(8,128)(2,1)S(1)}, u32[]{:S(2)}, u32[]{:S(2)}) collective-permute-start(bf16[128,1280]{1,0:T(8,128)(2,1)S(1)} %get-tuple-element.53.after), channel_id=1, source_target_pairs={{0,4},{2,6},{4,0},{6,2},{8,12},{10,14},{12,8},{14,10},{1,5},{3,7},... | collective-permute-start | bytes 983048 | tf_op jit(solution)/shard_map/ppermute | solution.py:257
  29.4 3.1 %collective-permute-done.7.far = bf16[128,512]{1,0:T(8,128)(2,1)S(1)} collective-permute-done((bf16[128,512]{1,0:T(8,128)(2,1)S(1)}, bf16[128,512]{1,0:T(8,128)(2,1)S(1)}, u32[]{:S(2)}, u32[]{:S(2)}) %collective-permute-start.7) | collective-permute-done | bytes 131104 | tf_op jit(solution)/shard_map/ppermute | solution.py:257
  32.5 1.7 %collective-permute-start.9 = (bf16[192,512]{1,0:T(8,128)(2,1)S(1)}, bf16[192,512]{1,0:T(8,128)(2,1)S(1)}, u32[]{:S(2)}, u32[]{:S(2)}) collective-permute-start(bf16[192,512]{1,0:T(8,128)(2,1)S(1)} %gather.1), channel_id=1, source_target_pairs={{0,2},{2,0},{4,6},{6,4},{8,10},{10,8},{12,14},{14,12},{1,3},{3,1},... | collective-permute-start | bytes 589832 | tf_op jit(solution)/shard_map/ppermute | solution.py:257
  34.1 0.8 %collective-permute-done.10.received = bf16[128,1280]{1,0:T(8,128)(2,1)S(1)} collective-permute-done((bf16[128,1280]{1,0:T(8,128)(2,1)S(1)}, bf16[128,1280]{1,0:T(8,128)(2,1)S(1)}, u32[]{:S(2)}, u32[]{:S(2)}) %collective-permute-start.10) | collective-permute-done | bytes 327712 | tf_op jit(solution)/shard_map/ppermute | solution.py:257
  34.9 0.1 hop_sum.2
  35.0 4.3 %collective-permute-done.11.received = bf16[128,1280]{1,0:T(8,128)(2,1)S(1)} collective-permute-done((bf16[128,1280]{1,0:T(8,128)(2,1)S(1)}, bf16[128,1280]{1,0:T(8,128)(2,1)S(1)}, u32[]{:S(2)}, u32[]{:S(2)}) %collective-permute-start.11) | collective-permute-done | bytes 327712 | tf_op jit(solution)/shard_map/ppermute | solution.py:257
  39.3 0.1 hop_sum.3
  39.4 0.7 %collective-permute-start.13 = (bf16[64,1280]{1,0:T(8,128)(2,1)S(1)}, bf16[64,1280]{1,0:T(8,128)(2,1)S(1)}, u32[]{:S(2)}, u32[]{:S(2)}) collective-permute-start(bf16[64,1280]{1,0:T(8,128)(2,1)S(1)} %get-tuple-element.61), channel_id=1, source_target_pairs={{0,2},{2,0},{4,6},{6,4},{8,10},{10,8},{12,14},{14,12},{1,3},{3,1},... | collective-permute-start | bytes 491528 | tf_op jit(solution)/shard_map/ppermute | solution.py:257
  40.0 0.0 collective-permute-start.12
  40.0 0.0 collective-permute-done.9.odd
  40.0 2.0 %attention.1 = (f32[64,2048]{1,0:T(8,128)}, f32[8,64]{1,0:T(8,128)S(1)}) custom-call(bf16[64,2048]{1,0:T(8,128)(2,1)S(1)} %get-tuple-element.37.queries, bf16[128,512]{1,0:T(8,128)(2,1)S(1)} %get-tuple-element.50.near, bf16[128,512]{1,0:T(8,128)(2,1)S(1)} %collective-permute-done.7.far, bf16[64,512]{1,0:T(8,128)(2,1)S(1)} %get-tuple-element.51.pair, ...), custom_call_target="tpu_custom_call" | custom-call | flops 268435456 | bytes 1640448 | tf_op jit(solution)/shard_map/attention/pallas_call | solution.py:21
  42.0 2.0 %collective-permute-start.15 = (f32[2,64]{1,0:T(2,128)S(1)}, f32[2,64]{1,0:T(2,128)S(1)}, u32[]{:S(2)}, u32[]{:S(2)}) collective-permute-start(f32[2,64]{1,0:T(2,128)S(1)} %get-tuple-element.69), channel_id=1, source_target_pairs={{0,4},{2,6},{4,0},{6,2},{8,12},{10,14},{12,8},{14,10},{1,5},{3,7},... | collective-permute-start | bytes 1544 | tf_op jit(solution)/shard_map/ppermute | solution.py:257
  44.1 1.5 %collective-permute-start.16 = (f32[2,64]{1,0:T(2,128)S(1)}, f32[2,64]{1,0:T(2,128)S(1)}, u32[]{:S(2)}, u32[]{:S(2)}) collective-permute-start(f32[2,64]{1,0:T(2,128)S(1)} %get-tuple-element.68), channel_id=1, source_target_pairs={{0,2},{2,0},{4,6},{6,4},{8,10},{10,8},{12,14},{14,12},{1,3},{3,1},... | collective-permute-start | bytes 1544 | tf_op jit(solution)/shard_map/ppermute | solution.py:257
  45.5 0.0 collective-permute-done.12.refs_2_
  45.5 0.1 hop_sum_both.1
  45.6 2.7 %collective-permute-start.14 = (bf16[32,2560]{1,0:T(8,128)(2,1)S(1)}, bf16[32,2560]{1,0:T(8,128)(2,1)S(1)}, u32[]{:S(2)}, u32[]{:S(2)}) collective-permute-start(bf16[32,2560]{1,0:T(8,128)(2,1)S(1)} %get-tuple-element.63), channel_id=1, source_target_pairs={{0,8},{2,10},{4,12},{6,14},{8,0},{10,2},{12,4},{14,6},{1,9},{3,11}... | collective-permute-start | bytes 491528 | tf_op jit(solution)/shard_map/ppermute | solution.py:257
  48.3 1.7 %collective-permute-done.17.refs_3_ = f32[2,64]{1,0:T(2,128)S(1)} collective-permute-done((f32[2,64]{1,0:T(2,128)S(1)}, f32[2,64]{1,0:T(2,128)S(1)}, u32[]{:S(2)}, u32[]{:S(2)}) %collective-permute-start.17) | collective-permute-done | bytes 544 | tf_op jit(solution)/shard_map/ppermute | solution.py:257
  50.0 0.7 %collective-permute-start.18 = (f32[1,64]{1,0:T(1,128)S(1)}, f32[1,64]{1,0:T(1,128)S(1)}, u32[]{:S(2)}, u32[]{:S(2)}) collective-permute-start(f32[1,64]{1,0:T(1,128)S(1)} %get-tuple-element.71), channel_id=1, source_target_pairs={{0,8},{2,10},{4,12},{6,14},{8,0},{10,2},{12,4},{14,6},{1,9},{3,11}... | collective-permute-start | bytes 776 | tf_op jit(solution)/shard_map/ppermute | solution.py:257
  50.8 0.0 collective-permute-start.19
  50.8 2.4 %collective-permute-start.20 = (f32[1,64]{1,0:T(1,128)S(1)}, f32[1,64]{1,0:T(1,128)S(1)}, u32[]{:S(2)}, u32[]{:S(2)}) collective-permute-start(f32[1,64]{1,0:T(1,128)S(1)} %get-tuple-element.71), channel_id=1, source_target_pairs={{0,9},{1,8},{2,11},{3,10},{4,13},{5,12},{6,15},{7,14},{8,1},{9,0},... | collective-permute-start | bytes 776 | tf_op jit(solution)/shard_map/ppermute | solution.py:260
  53.1 2.1 %collective-permute-done.18.refs_1_ = f32[1,64]{1,0:T(1,128)S(1)} collective-permute-done((f32[1,64]{1,0:T(1,128)S(1)}, f32[1,64]{1,0:T(1,128)S(1)}, u32[]{:S(2)}, u32[]{:S(2)}) %collective-permute-start.18) | collective-permute-done | bytes 288 | tf_op jit(solution)/shard_map/ppermute | solution.py:257
  55.3 0.0 collective-permute-done.14.received
  55.3 0.8 %finish.1 = (f32[32,2560]{1,0:T(8,128)}, f32[1,64]{1,0:T(1,128)}) custom-call(f32[1,2560]{1,0:T(1,128)S(1)} %reshape.20.bias, f32[32,2560]{1,0:T(8,128)S(1)} %get-tuple-element.62.after.kept, bf16[32,2560]{1,0:T(8,128)(2,1)S(1)} %collective-permute-done.14.received, f32[1,64]{1,0:T(1,128)S(1)} %get-tuple-element.72.refs_0_, ...), custom_call_target="tpu_custom_call" | custom-call | flops 655360 | bytes 830720 | tf_op jit(solution)/shard_map/finish/pallas_call | solution.py:21
  (13 shorter events, 0.1 us)
Async XLA Ops:
  2.4 10.7 %collective-permute-start.2 = (bf16[64,1024]{1,0:T(8,128)(2,1)S(1)}, bf16[64,1024]{1,0:T(8,128)(2,1)S(1)}, u32[]{:S(2)}, u32[]{:S(2)}) collective-permute-start(bf16[64,1024]{1,0:T(8,128)(2,1)S(1)} %get-tuple-element.40), channel_id=1, source_target_pairs={{0,2},{2,0},{4,6},{6,4},{8,10},{10,8},{12,14},{14,12},{1,3},{3,1},... | collective-permute-start | bytes 393224 | tf_op jit(solution)/shard_map/ppermute | solution.py:257
  5.4 7.8 %collective-permute-start = (bf16[64,512]{1,0:T(8,128)(2,1)S(1)}, bf16[64,512]{1,0:T(8,128)(2,1)S(1)}, u32[]{:S(2)}, u32[]{:S(2)}) collective-permute-start(bf16[64,512]{1,0:T(8,128)(2,1)S(1)} %get-tuple-element.35), channel_id=1, source_target_pairs={{0,8},{2,10},{4,12},{6,14},{8,0},{10,2},{12,4},{14,6},{1,9},{3,11}... | collective-permute-start | bytes 196616 | tf_op jit(solution)/shard_map/ppermute | solution.py:257
  8.0 9.8 %collective-permute-start.1 = (bf16[64,512]{1,0:T(8,128)(2,1)S(1)}, bf16[64,512]{1,0:T(8,128)(2,1)S(1)}, u32[]{:S(2)}, u32[]{:S(2)}) collective-permute-start(bf16[64,512]{1,0:T(8,128)(2,1)S(1)} %get-tuple-element.36), channel_id=1, source_target_pairs={{0,10},{2,8},{4,14},{6,12},{8,2},{10,0},{12,6},{14,4},{1,11},{3,9}... | collective-permute-start | bytes 196616 | tf_op jit(solution)/shard_map/ppermute | solution.py:257
  8.0 12.3 %collective-permute-start.5 = (bf16[64,512]{1,0:T(8,128)(2,1)S(1)}, bf16[64,512]{1,0:T(8,128)(2,1)S(1)}, u32[]{:S(2)}, u32[]{:S(2)}) collective-permute-start(bf16[64,512]{1,0:T(8,128)(2,1)S(1)} %get-tuple-element.45), channel_id=1, source_target_pairs={{0,12},{2,14},{4,8},{6,10},{8,4},{10,6},{12,0},{14,2},{1,13},{3,15... | collective-permute-start | bytes 196616 | tf_op jit(solution)/shard_map/ppermute | solution.py:257
  11.9 8.4 %collective-permute-start.6 = (bf16[64,512]{1,0:T(8,128)(2,1)S(1)}, bf16[64,512]{1,0:T(8,128)(2,1)S(1)}, u32[]{:S(2)}, u32[]{:S(2)}) collective-permute-start(bf16[64,512]{1,0:T(8,128)(2,1)S(1)} %get-tuple-element.46), channel_id=1, source_target_pairs={{0,14},{2,12},{4,10},{6,8},{8,6},{10,4},{12,2},{14,0},{1,15},{3,13... | collective-permute-start | bytes 196616 | tf_op jit(solution)/shard_map/ppermute | solution.py:257
  13.1 8.2 %collective-permute-start.3 = (bf16[64,1024]{1,0:T(8,128)(2,1)S(1)}, bf16[64,1024]{1,0:T(8,128)(2,1)S(1)}, u32[]{:S(2)}, u32[]{:S(2)}) collective-permute-start(bf16[64,1024]{1,0:T(8,128)(2,1)S(1)} %get-tuple-element.43), channel_id=1, source_target_pairs={{0,4},{2,6},{4,0},{6,2},{8,12},{10,14},{12,8},{14,10},{1,5},{3,7},... | collective-permute-start | bytes 393224 | tf_op jit(solution)/shard_map/ppermute | solution.py:257
  13.2 8.1 %collective-permute-start.4 = (bf16[64,512]{1,0:T(8,128)(2,1)S(1)}, bf16[64,512]{1,0:T(8,128)(2,1)S(1)}, u32[]{:S(2)}, u32[]{:S(2)}) collective-permute-start(bf16[64,512]{1,0:T(8,128)(2,1)S(1)} %get-tuple-element.44), channel_id=1, source_target_pairs={{0,6},{2,4},{4,2},{6,0},{8,14},{10,12},{12,10},{14,8},{1,7},{3,5},... | collective-permute-start | bytes 196616 | tf_op jit(solution)/shard_map/ppermute | solution.py:257
  21.6 2.8 %collective-permute-start.8 = (bf16[256,512]{1,0:T(8,128)(2,1)S(1)}, bf16[256,512]{1,0:T(8,128)(2,1)S(1)}, u32[]{:S(2)}, u32[]{:S(2)}) collective-permute-start(bf16[256,512]{1,0:T(8,128)(2,1)S(1)} %get-tuple-element.47.own), channel_id=1, source_target_pairs={{0,1},{1,0},{2,3},{3,2},{4,5},{5,4},{6,7},{7,6},{8,9},{9,8},{10,11... | collective-permute-start | bytes 786440 | tf_op jit(solution)/shard_map/ppermute | solution.py:263
  22.7 9.8 %collective-permute-start.7 = (bf16[128,512]{1,0:T(8,128)(2,1)S(1)}, bf16[128,512]{1,0:T(8,128)(2,1)S(1)}, u32[]{:S(2)}, u32[]{:S(2)}) collective-permute-start(bf16[128,512]{1,0:T(8,128)(2,1)S(1)} %get-tuple-element.50.near), channel_id=1, source_target_pairs={{0,8},{2,10},{4,12},{6,14},{8,0},{10,2},{12,4},{14,6},{1,9},{3,11}... | collective-permute-start | bytes 393224 | tf_op jit(solution)/shard_map/ppermute | solution.py:257
  25.0 9.9 %collective-permute-start.10 = (bf16[128,1280]{1,0:T(8,128)(2,1)S(1)}, bf16[128,1280]{1,0:T(8,128)(2,1)S(1)}, u32[]{:S(2)}, u32[]{:S(2)}) collective-permute-start(bf16[128,1280]{1,0:T(8,128)(2,1)S(1)} %get-tuple-element.55), channel_id=1, source_target_pairs={{0,2},{2,0},{4,6},{6,4},{8,10},{10,8},{12,14},{14,12},{1,3},{3,1},... | collective-permute-start | bytes 983048 | tf_op jit(solution)/shard_map/ppermute | solution.py:257
  27.2 25.9 %copy-start = (f32[2560]{0:T(1024)S(1)}, f32[2560]{0:T(1024)}, u32[]{:S(2)}) copy-start(f32[2560]{0:T(1024)} %param.17) | copy-start | bytes 30724
  27.2 12.1 %collective-permute-start.11 = (bf16[128,1280]{1,0:T(8,128)(2,1)S(1)}, bf16[128,1280]{1,0:T(8,128)(2,1)S(1)}, u32[]{:S(2)}, u32[]{:S(2)}) collective-permute-start(bf16[128,1280]{1,0:T(8,128)(2,1)S(1)} %get-tuple-element.53.after), channel_id=1, source_target_pairs={{0,4},{2,6},{4,0},{6,2},{8,12},{10,14},{12,8},{14,10},{1,5},{3,7},... | collective-permute-start | bytes 983048 | tf_op jit(solution)/shard_map/ppermute | solution.py:257
  32.5 7.5 %collective-permute-start.9 = (bf16[192,512]{1,0:T(8,128)(2,1)S(1)}, bf16[192,512]{1,0:T(8,128)(2,1)S(1)}, u32[]{:S(2)}, u32[]{:S(2)}) collective-permute-start(bf16[192,512]{1,0:T(8,128)(2,1)S(1)} %gather.1), channel_id=1, source_target_pairs={{0,2},{2,0},{4,6},{6,4},{8,10},{10,8},{12,14},{14,12},{1,3},{3,1},... | collective-permute-start | bytes 589832 | tf_op jit(solution)/shard_map/ppermute | solution.py:257
  39.4 6.2 %collective-permute-start.13 = (bf16[64,1280]{1,0:T(8,128)(2,1)S(1)}, bf16[64,1280]{1,0:T(8,128)(2,1)S(1)}, u32[]{:S(2)}, u32[]{:S(2)}) collective-permute-start(bf16[64,1280]{1,0:T(8,128)(2,1)S(1)} %get-tuple-element.61), channel_id=1, source_target_pairs={{0,2},{2,0},{4,6},{6,4},{8,10},{10,8},{12,14},{14,12},{1,3},{3,1},... | collective-permute-start | bytes 491528 | tf_op jit(solution)/shard_map/ppermute | solution.py:257
  40.0 5.5 %collective-permute-start.12 = (bf16[64,1280]{1,0:T(8,128)(2,1)S(1)}, bf16[64,1280]{1,0:T(8,128)(2,1)S(1)}, u32[]{:S(2)}, u32[]{:S(2)}) collective-permute-start(bf16[64,1280]{1,0:T(8,128)(2,1)S(1)} %get-tuple-element.60), channel_id=1, source_target_pairs={{0,4},{2,6},{4,0},{6,2},{8,12},{10,14},{12,8},{14,10},{1,5},{3,7},... | collective-permute-start | bytes 491528 | tf_op jit(solution)/shard_map/ppermute | solution.py:257
  42.0 6.3 %collective-permute-start.15 = (f32[2,64]{1,0:T(2,128)S(1)}, f32[2,64]{1,0:T(2,128)S(1)}, u32[]{:S(2)}, u32[]{:S(2)}) collective-permute-start(f32[2,64]{1,0:T(2,128)S(1)} %get-tuple-element.69), channel_id=1, source_target_pairs={{0,4},{2,6},{4,0},{6,2},{8,12},{10,14},{12,8},{14,10},{1,5},{3,7},... | collective-permute-start | bytes 1544 | tf_op jit(solution)/shard_map/ppermute | solution.py:257
  44.1 4.3 %collective-permute-start.16 = (f32[2,64]{1,0:T(2,128)S(1)}, f32[2,64]{1,0:T(2,128)S(1)}, u32[]{:S(2)}, u32[]{:S(2)}) collective-permute-start(f32[2,64]{1,0:T(2,128)S(1)} %get-tuple-element.68), channel_id=1, source_target_pairs={{0,2},{2,0},{4,6},{6,4},{8,10},{10,8},{12,14},{14,12},{1,3},{3,1},... | collective-permute-start | bytes 1544 | tf_op jit(solution)/shard_map/ppermute | solution.py:257
  45.5 4.5 %collective-permute-start.17 = (f32[2,64]{1,0:T(2,128)S(1)}, f32[2,64]{1,0:T(2,128)S(1)}, u32[]{:S(2)}, u32[]{:S(2)}) collective-permute-start(f32[2,64]{1,0:T(2,128)S(1)} %get-tuple-element.67), channel_id=1, source_target_pairs={{0,6},{2,4},{4,2},{6,0},{8,14},{10,12},{12,10},{14,8},{1,7},{3,5},... | collective-permute-start | bytes 1544 | tf_op jit(solution)/shard_map/ppermute | solution.py:257
  45.6 9.7 %collective-permute-start.14 = (bf16[32,2560]{1,0:T(8,128)(2,1)S(1)}, bf16[32,2560]{1,0:T(8,128)(2,1)S(1)}, u32[]{:S(2)}, u32[]{:S(2)}) collective-permute-start(bf16[32,2560]{1,0:T(8,128)(2,1)S(1)} %get-tuple-element.63), channel_id=1, source_target_pairs={{0,8},{2,10},{4,12},{6,14},{8,0},{10,2},{12,4},{14,6},{1,9},{3,11}... | collective-permute-start | bytes 491528 | tf_op jit(solution)/shard_map/ppermute | solution.py:257
  50.0 5.2 %collective-permute-start.18 = (f32[1,64]{1,0:T(1,128)S(1)}, f32[1,64]{1,0:T(1,128)S(1)}, u32[]{:S(2)}, u32[]{:S(2)}) collective-permute-start(f32[1,64]{1,0:T(1,128)S(1)} %get-tuple-element.71), channel_id=1, source_target_pairs={{0,8},{2,10},{4,12},{6,14},{8,0},{10,2},{12,4},{14,6},{1,9},{3,11}... | collective-permute-start | bytes 776 | tf_op jit(solution)/shard_map/ppermute | solution.py:257
  50.8 4.5 %collective-permute-start.19 = (f32[1,64]{1,0:T(1,128)S(1)}, f32[1,64]{1,0:T(1,128)S(1)}, u32[]{:S(2)}, u32[]{:S(2)}) collective-permute-start(f32[1,64]{1,0:T(1,128)S(1)} %get-tuple-element.72.refs_0_), channel_id=1, source_target_pairs={{0,1},{1,0},{2,3},{3,2},{4,5},{5,4},{6,7},{7,6},{8,9},{9,8},{10,11... | collective-permute-start | bytes 776 | tf_op jit(solution)/shard_map/ppermute | solution.py:263
  50.8 4.5 %collective-permute-start.20 = (f32[1,64]{1,0:T(1,128)S(1)}, f32[1,64]{1,0:T(1,128)S(1)}, u32[]{:S(2)}, u32[]{:S(2)}) collective-permute-start(f32[1,64]{1,0:T(1,128)S(1)} %get-tuple-element.71), channel_id=1, source_target_pairs={{0,9},{1,8},{2,11},{3,10},{4,13},{5,12},{6,15},{7,14},{8,1},{9,0},... | collective-permute-start | bytes 776 | tf_op jit(solution)/shard_map/ppermute | solution.py:260

commit v18 on v15

--- a/solution.py
+++ b/solution.py
@@ -15,14 +15,14 @@
 MIB = 1024 * 1024
 
 
-def call(body, name, inputs, outputs, flops, limit=16, in_specs=None, scratch=(), remote=0):
+def call(body, name, inputs, outputs, flops, limit=16, in_specs=None, scratch=(), remote=0, out_specs=None):
     inputs = [pltpu.with_memory_space_constraint(x, pltpu.HBM) if i < remote else x for i, x in enumerate(inputs)]
     size = sum(math.prod(x.shape) * x.dtype.itemsize for x in list(inputs) + list(outputs))
     return pl.pallas_call(
         body,
         out_shape=list(outputs),
         in_specs=in_specs or [VMEM] * len(inputs),
-        out_specs=[VMEM] * len(outputs),
+        out_specs=out_specs or [VMEM] * len(outputs),
         scratch_shapes=list(scratch),
         compiler_params=pltpu.CompilerParams(vmem_limit_bytes=limit * MIB),
         cost_estimate=pl.CostEstimate(flops=flops, bytes_accessed=size, transcendentals=0),
@@ -229,12 +229,21 @@
 
 
 def finish_kernel(bias, kept, received, *refs):
-    *parts, out, scores = refs
-    out[...] = kept[...] + received[...].astype(jnp.float32) + bias[...]
-    total = parts[0][...]
+    *parts, out, scores, total, sems = refs
+    pieces = sems.shape[0]
+    width = total.shape[1] // pieces
+    stores = []
+    for i in range(pieces):
+        lanes = slice(i * width, (i + 1) * width)
+        total[:, lanes] = kept[:, lanes] + received[:, lanes].astype(jnp.float32) + bias[:, lanes]
+        stores.append(pltpu.make_async_copy(total.at[:, lanes], out.at[:, lanes], sems.at[i]))
+        stores[i].start()
+    columns = parts[0][...]
     for part in parts[1:]:
-        total += part[...]
-    scores[...] = total / QUERY_HEADS
+        columns += part[...]
+    scores[...] = columns / QUERY_HEADS
+    for store in stores:
+        store.wait()
 
 
 def shards(queries, keys, values, hidden, norm_gain, retained_lists, counts, affine_matrix, affine_offset_vector):
@@ -392,6 +401,8 @@
         (affine_offset_vector.reshape(1, width), kept[0], arrived[0], *pieces),
         [shape((lines, width), f32), shape((1, rows), f32)],
         n * lines * width,
+        scratch=[pltpu.VMEM((lines, width), f32), dma((4 if width % 512 == 0 else 1,))],
+        out_specs=[ANY, VMEM],
     )
     return (context, scores.reshape(rows), triples)
 

time: 56.2 us -> 56.7 us (level)
  no operation moved by 1% of the time
where the time goes in v18:
time: 56.7 us; the launch traced here: 56.5 us
  starting transfers between devices  30.5 us (54%)
  waiting for transfers between devices  15.1 us (27%)
  Pallas kernels  10.2 us (18%)
  between operations  0.76 us (1%)
    ppermute x18, starting transfers between devices, trade(): return lax.ppermute(x, 'seq', [(i, i ^ k) for i in range(n)])  27.6 us
    ppermute x18, waiting for transfers between devices, trade(): return lax.ppermute(x, 'seq', [(i, i ^ k) for i in range(n)])  15.1 us
    pallas_call x14, Pallas kernels, call(): pl.pallas_call(body, out_shape=list(outputs), in_specs=in_specs or [VMEM]...  10.2 us
    ppermute x1, starting transfers between devices, trade_across(): lax.ppermute(x, ('seq', 'ten'), [(2 * i + t, 2 * (i ^ k) + 1 - t) for i i...  2.76 us
  transfers between devices with their start and end apart: 21, of which 8 were waited for; matrix products, arithmetic and copies ran while one was open for 0% of the time, Pallas kernels for 12%

profile of v18, /device:TPU:0, one launch (start us, length us, event | category | flops | bytes accessed | tf_op | source)
XLA Modules:
  0.0 56.5 jit_solution(2950697606830765340)
XLA Ops:
  0.6 1.7 %norm_select.1 = (bf16[64,1024]{1,0:T(8,128)(2,1)S(1)}, bf16[64,1024]{1,0:T(8,128)(2,1)S(1)}, bf16[64,1024]{1,0:T(8,128)(2,1)S(1)}, bf16[64,512]{1,0:T(8,128)(2,...) custom-call(bf16[64,8192]{1,0:T(8,128)(2,1)} %hidden_in.1, ...), custom_call_target="tpu_custom_call" | custom-call | flops 2097152 | bytes 1868032 | tf_op jit(solution)/shard_map/norm_select/pallas_call | solution.py:21
  2.4 3.0 %collective-permute-start.2 = (bf16[64,1024]{1,0:T(8,128)(2,1)S(1)}, bf16[64,1024]{1,0:T(8,128)(2,1)S(1)}, u32[]{:S(2)}, u32[]{:S(2)}) collective-permute-start(bf16[64,1024]{1,0:T(8,128)(2,1)S(1)} %get-tuple-element.38), channel_id=1, source_target_pairs={{0,2},{2,0},{4,6},{6,4},{8,10},{10,8},{12,14},{14,12},{1,3},{3,1},... | collective-permute-start | bytes 393224 | tf_op jit(solution)/shard_map/ppermute | solution.py:265
  5.4 2.6 %collective-permute-start = (bf16[64,512]{1,0:T(8,128)(2,1)S(1)}, bf16[64,512]{1,0:T(8,128)(2,1)S(1)}, u32[]{:S(2)}, u32[]{:S(2)}) collective-permute-start(bf16[64,512]{1,0:T(8,128)(2,1)S(1)} %get-tuple-element.33), channel_id=1, source_target_pairs={{0,8},{2,10},{4,12},{6,14},{8,0},{10,2},{12,4},{14,6},{1,9},{3,11}... | collective-permute-start | bytes 196616 | tf_op jit(solution)/shard_map/ppermute | solution.py:265
  8.0 0.0 collective-permute-start.1
  8.0 3.9 %collective-permute-start.5 = (bf16[64,512]{1,0:T(8,128)(2,1)S(1)}, bf16[64,512]{1,0:T(8,128)(2,1)S(1)}, u32[]{:S(2)}, u32[]{:S(2)}) collective-permute-start(bf16[64,512]{1,0:T(8,128)(2,1)S(1)} %get-tuple-element.43), channel_id=1, source_target_pairs={{0,12},{2,14},{4,8},{6,10},{8,4},{10,6},{12,0},{14,2},{1,13},{3,15... | collective-permute-start | bytes 196616 | tf_op jit(solution)/shard_map/ppermute | solution.py:265
  11.9 1.2 %collective-permute-start.6 = (bf16[64,512]{1,0:T(8,128)(2,1)S(1)}, bf16[64,512]{1,0:T(8,128)(2,1)S(1)}, u32[]{:S(2)}, u32[]{:S(2)}) collective-permute-start(bf16[64,512]{1,0:T(8,128)(2,1)S(1)} %get-tuple-element.44), channel_id=1, source_target_pairs={{0,14},{2,12},{4,10},{6,8},{8,6},{10,4},{12,2},{14,0},{1,15},{3,13... | collective-permute-start | bytes 196616 | tf_op jit(solution)/shard_map/ppermute | solution.py:265
  13.1 0.0 collective-permute-done.2.refs_2_.refs_1_
  13.1 0.1 collective-permute-start.3
  13.2 0.0 collective-permute-done.refs_0_.refs_4_
  13.2 1.8 %collective-permute-start.4 = (bf16[64,512]{1,0:T(8,128)(2,1)S(1)}, bf16[64,512]{1,0:T(8,128)(2,1)S(1)}, u32[]{:S(2)}, u32[]{:S(2)}) collective-permute-start(bf16[64,512]{1,0:T(8,128)(2,1)S(1)} %get-tuple-element.42), channel_id=1, source_target_pairs={{0,6},{2,4},{4,2},{6,0},{8,14},{10,12},{12,10},{14,8},{1,7},{3,5},... | collective-permute-start | bytes 196616 | tf_op jit(solution)/shard_map/ppermute | solution.py:265
  15.0 2.8 %collective-permute-done.1.refs_1_.refs_5_ = bf16[64,512]{1,0:T(8,128)(2,1)S(1)} collective-permute-done((bf16[64,512]{1,0:T(8,128)(2,1)S(1)}, bf16[64,512]{1,0:T(8,128)(2,1)S(1)}, u32[]{:S(2)}, u32[]{:S(2)}) %collective-permute-start.1) | collective-permute-done | bytes 65568 | tf_op jit(solution)/shard_map/ppermute | solution.py:265
  17.8 2.5 %stage.1 = (bf16[1024,2560]{1,0:T(8,128)(2,1)S(1)}, bf16[64,2048]{1,0:T(8,128)(2,1)S(1)}, s32[1,512]{1,0:T(1,128)S(1)}) custom-call(s32[8]{0:T(128)} %counts_in.1, bf16[1024,2560]{1,0:T(8,128)(2,1)} %matrix_in.1, bf16[64,2048]{1,0:T(8,128)(2,1)} %queries_in.1, bf16[64,512]{1,0:T(8,128)(2,1)S(1)} %collective-permute-done.refs_0_.refs_4_, ...), custom_call_target="tpu_custom_call" | custom-call | flops 3932160000 | bytes 11143200 | tf_op jit(solution)/shard_map/stage/pallas_call | solution.py:21
  20.3 0.0 collective-permute-done.6.refs_7_
  20.3 0.9 %collective-permute-done.4.refs_3_ = bf16[64,512]{1,0:T(8,128)(2,1)S(1)} collective-permute-done((bf16[64,512]{1,0:T(8,128)(2,1)S(1)}, bf16[64,512]{1,0:T(8,128)(2,1)S(1)}, u32[]{:S(2)}, u32[]{:S(2)}) %collective-permute-start.4) | collective-permute-done | bytes 65568 | tf_op jit(solution)/shard_map/ppermute | solution.py:265
  21.3 0.0 collective-permute-done.3.refs_2_
  21.3 0.3 compact.1
  21.6 0.1 collective-permute-start.8
  21.7 1.7 %collective-permute-start.7 = (bf16[128,512]{1,0:T(8,128)(2,1)S(1)}, bf16[128,512]{1,0:T(8,128)(2,1)S(1)}, u32[]{:S(2)}, u32[]{:S(2)}) collective-permute-start(bf16[128,512]{1,0:T(8,128)(2,1)S(1)} %get-tuple-element.45.near), channel_id=1, source_target_pairs={{0,8},{2,10},{4,12},{6,14},{8,0},{10,2},{12,4},{14,6},{1,9},{3,11}... | collective-permute-start | bytes 393224 | tf_op jit(solution)/shard_map/ppermute | solution.py:265
  23.4 1.0 %project_own.1.product = f32[256,2560]{1,0:T(8,128)S(1)} custom-call(bf16[256,512]{1,0:T(8,128)(2,1)S(1)} %get-tuple-element.47.own, bf16[1024,2560]{1,0:T(8,128)(2,1)S(1)} %get-tuple-element.48.matrix), custom_call_target="tpu_custom_call" | custom-call | flops 671088640 | bytes 8126464 | tf_op jit(solution)/shard_map/project_own/pallas_call | solution.py:21
  24.4 0.0 collective-permute-done.8.other
  24.4 0.6 %project.3 = (f32[128,1280]{1,0:T(8,128)S(1)}, bf16[128,1280]{1,0:T(8,128)(2,1)S(1)}) custom-call(f32[256,2560]{1,0:T(8,128)S(1)} %project_own.1.product, bf16[256,512]{1,0:T(8,128)(2,1)S(1)} %collective-permute-done.8.other, bf16[1024,2560]{1,0:T(8,128)(2,1)S(1)} %get-tuple-element.48.matrix), custom_call_target="tpu_custom_call" | custom-call | flops 335544320 | bytes 9109504 | tf_op jit(solution)/shard_map/project/pallas_call | solution.py:21
  25.0 1.6 %collective-permute-start.10 = (bf16[128,1280]{1,0:T(8,128)(2,1)S(1)}, bf16[128,1280]{1,0:T(8,128)(2,1)S(1)}, u32[]{:S(2)}, u32[]{:S(2)}) collective-permute-start(bf16[128,1280]{1,0:T(8,128)(2,1)S(1)} %get-tuple-element.51), channel_id=1, source_target_pairs={{0,2},{2,0},{4,6},{6,4},{8,10},{10,8},{12,14},{14,12},{1,3},{3,1},... | collective-permute-start | bytes 983048 | tf_op jit(solution)/shard_map/ppermute | solution.py:265
  26.6 0.6 %project.2 = (f32[128,1280]{1,0:T(8,128)S(1)}, bf16[128,1280]{1,0:T(8,128)(2,1)S(1)}) custom-call(f32[256,2560]{1,0:T(8,128)S(1)} %project_own.1.product, bf16[256,512]{1,0:T(8,128)(2,1)S(1)} %collective-permute-done.8.other, bf16[1024,2560]{1,0:T(8,128)(2,1)S(1)} %get-tuple-element.48.matrix), custom_call_target="tpu_custom_call" | custom-call | flops 335544320 | bytes 9109504 | tf_op jit(solution)/shard_map/project/pallas_call | solution.py:21
  27.2 0.0 copy-start
  27.2 2.2 %collective-permute-start.11 = (bf16[128,1280]{1,0:T(8,128)(2,1)S(1)}, bf16[128,1280]{1,0:T(8,128)(2,1)S(1)}, u32[]{:S(2)}, u32[]{:S(2)}) collective-permute-start(bf16[128,1280]{1,0:T(8,128)(2,1)S(1)} %get-tuple-element.49.after), channel_id=1, source_target_pairs={{0,4},{2,6},{4,0},{6,2},{8,12},{10,14},{12,8},{14,10},{1,5},{3,7},... | collective-permute-start | bytes 983048 | tf_op jit(solution)/shard_map/ppermute | solution.py:265
  29.4 2.0 %collective-permute-done.7.far = bf16[128,512]{1,0:T(8,128)(2,1)S(1)} collective-permute-done((bf16[128,512]{1,0:T(8,128)(2,1)S(1)}, bf16[128,512]{1,0:T(8,128)(2,1)S(1)}, u32[]{:S(2)}, u32[]{:S(2)}) %collective-permute-start.7) | collective-permute-done | bytes 131104 | tf_op jit(solution)/shard_map/ppermute | solution.py:265
  31.4 1.7 %collective-permute-start.9 = (bf16[192,512]{1,0:T(8,128)(2,1)S(1)}, bf16[192,512]{1,0:T(8,128)(2,1)S(1)}, u32[]{:S(2)}, u32[]{:S(2)}) collective-permute-start(bf16[192,512]{1,0:T(8,128)(2,1)S(1)} %gather.1), channel_id=1, source_target_pairs={{0,2},{2,0},{4,6},{6,4},{8,10},{10,8},{12,14},{14,12},{1,3},{3,1},... | collective-permute-start | bytes 589832 | tf_op jit(solution)/shard_map/ppermute | solution.py:265
  33.1 2.5 %collective-permute-done.10.received = bf16[128,1280]{1,0:T(8,128)(2,1)S(1)} collective-permute-done((bf16[128,1280]{1,0:T(8,128)(2,1)S(1)}, bf16[128,1280]{1,0:T(8,128)(2,1)S(1)}, u32[]{:S(2)}, u32[]{:S(2)}) %collective-permute-start.10) | collective-permute-done | bytes 327712 | tf_op jit(solution)/shard_map/ppermute | solution.py:265
  35.6 0.1 hop_sum.2
  35.7 2.6 %collective-permute-done.11.received = bf16[128,1280]{1,0:T(8,128)(2,1)S(1)} collective-permute-done((bf16[128,1280]{1,0:T(8,128)(2,1)S(1)}, bf16[128,1280]{1,0:T(8,128)(2,1)S(1)}, u32[]{:S(2)}, u32[]{:S(2)}) %collective-permute-start.11) | collective-permute-done | bytes 327712 | tf_op jit(solution)/shard_map/ppermute | solution.py:265
  38.3 0.1 hop_sum.3
  38.4 1.6 %collective-permute-start.13 = (bf16[64,1280]{1,0:T(8,128)(2,1)S(1)}, bf16[64,1280]{1,0:T(8,128)(2,1)S(1)}, u32[]{:S(2)}, u32[]{:S(2)}) collective-permute-start(bf16[64,1280]{1,0:T(8,128)(2,1)S(1)} %get-tuple-element.57), channel_id=1, source_target_pairs={{0,2},{2,0},{4,6},{6,4},{8,10},{10,8},{12,14},{14,12},{1,3},{3,1},... | collective-permute-start | bytes 491528 | tf_op jit(solution)/shard_map/ppermute | solution.py:265
  40.0 0.0 collective-permute-start.12
  40.0 0.0 collective-permute-done.9.odd
  40.0 2.0 %attention.1 = (f32[64,2048]{1,0:T(8,128)}, f32[8,64]{1,0:T(8,128)S(1)}) custom-call(bf16[64,2048]{1,0:T(8,128)(2,1)S(1)} %get-tuple-element.35.queries, bf16[128,512]{1,0:T(8,128)(2,1)S(1)} %get-tuple-element.45.near, bf16[128,512]{1,0:T(8,128)(2,1)S(1)} %collective-permute-done.7.far, bf16[64,512]{1,0:T(8,128)(2,1)S(1)} %get-tuple-element.46.pair, ...), custom_call_target="tpu_custom_call" | custom-call | flops 268435456 | bytes 1640448 | tf_op jit(solution)/shard_map/attention/pallas_call | solution.py:21
  42.0 2.0 %collective-permute-start.15 = (f32[2,64]{1,0:T(2,128)S(1)}, f32[2,64]{1,0:T(2,128)S(1)}, u32[]{:S(2)}, u32[]{:S(2)}) collective-permute-start(f32[2,64]{1,0:T(2,128)S(1)} %get-tuple-element.65), channel_id=1, source_target_pairs={{0,4},{2,6},{4,0},{6,2},{8,12},{10,14},{12,8},{14,10},{1,5},{3,7},... | collective-permute-start | bytes 1544 | tf_op jit(solution)/shard_map/ppermute | solution.py:265
  44.0 1.3 %collective-permute-start.16 = (f32[2,64]{1,0:T(2,128)S(1)}, f32[2,64]{1,0:T(2,128)S(1)}, u32[]{:S(2)}, u32[]{:S(2)}) collective-permute-start(f32[2,64]{1,0:T(2,128)S(1)} %get-tuple-element.64), channel_id=1, source_target_pairs={{0,2},{2,0},{4,6},{6,4},{8,10},{10,8},{12,14},{14,12},{1,3},{3,1},... | collective-permute-start | bytes 1544 | tf_op jit(solution)/shard_map/ppermute | solution.py:265
  45.4 0.1 collective-permute-start.17
  45.5 0.0 collective-permute-done.13.refs_3_
  45.5 0.3 collective-permute-done.12.refs_2_
  45.8 0.1 hop_sum_both.1
  45.8 2.5 %collective-permute-start.14 = (bf16[32,2560]{1,0:T(8,128)(2,1)S(1)}, bf16[32,2560]{1,0:T(8,128)(2,1)S(1)}, u32[]{:S(2)}, u32[]{:S(2)}) collective-permute-start(bf16[32,2560]{1,0:T(8,128)(2,1)S(1)} %get-tuple-element.59), channel_id=1, source_target_pairs={{0,8},{2,10},{4,12},{6,14},{8,0},{10,2},{12,4},{14,6},{1,9},{3,11}... | collective-permute-start | bytes 491528 | tf_op jit(solution)/shard_map/ppermute | solution.py:265
  48.3 1.5 %collective-permute-done.17.refs_3_ = f32[2,64]{1,0:T(2,128)S(1)} collective-permute-done((f32[2,64]{1,0:T(2,128)S(1)}, f32[2,64]{1,0:T(2,128)S(1)}, u32[]{:S(2)}, u32[]{:S(2)}) %collective-permute-start.17) | collective-permute-done | bytes 544 | tf_op jit(solution)/shard_map/ppermute | solution.py:265
  49.8 0.3 collective-permute-start.18
  50.2 0.0 collective-permute-start.19
  50.2 2.8 %collective-permute-start.20 = (f32[1,64]{1,0:T(1,128)S(1)}, f32[1,64]{1,0:T(1,128)S(1)}, u32[]{:S(2)}, u32[]{:S(2)}) collective-permute-start(f32[1,64]{1,0:T(1,128)S(1)} %get-tuple-element.67), channel_id=1, source_target_pairs={{0,9},{1,8},{2,11},{3,10},{4,13},{5,12},{6,15},{7,14},{8,1},{9,0},... | collective-permute-start | bytes 776 | tf_op jit(solution)/shard_map/ppermute | solution.py:268
  53.0 2.3 %collective-permute-done.18.refs_1_ = f32[1,64]{1,0:T(1,128)S(1)} collective-permute-done((f32[1,64]{1,0:T(1,128)S(1)}, f32[1,64]{1,0:T(1,128)S(1)}, u32[]{:S(2)}, u32[]{:S(2)}) %collective-permute-start.18) | collective-permute-done | bytes 288 | tf_op jit(solution)/shard_map/ppermute | solution.py:265
  55.3 1.3 %finish.1 = (f32[32,2560]{1,0:T(8,128)}, f32[1,64]{1,0:T(1,128)}) custom-call(f32[1,2560]{1,0:T(1,128)S(1)} %reshape.20.bias, f32[32,2560]{1,0:T(8,128)S(1)} %get-tuple-element.58.after.kept, bf16[32,2560]{1,0:T(8,128)(2,1)S(1)} %collective-permute-done.14.received, f32[1,64]{1,0:T(1,128)S(1)} %get-tuple-element.68.refs_0_, ...), custom_call_target="tpu_custom_call" | custom-call | flops 655360 | bytes 830720 | tf_op jit(solution)/shard_map/finish/pallas_call | solution.py:21
  (13 shorter events, 0.1 us)
Async XLA Ops:
  2.4 10.7 %collective-permute-start.2 = (bf16[64,1024]{1,0:T(8,128)(2,1)S(1)}, bf16[64,1024]{1,0:T(8,128)(2,1)S(1)}, u32[]{:S(2)}, u32[]{:S(2)}) collective-permute-start(bf16[64,1024]{1,0:T(8,128)(2,1)S(1)} %get-tuple-element.38), channel_id=1, source_target_pairs={{0,2},{2,0},{4,6},{6,4},{8,10},{10,8},{12,14},{14,12},{1,3},{3,1},... | collective-permute-start | bytes 393224 | tf_op jit(solution)/shard_map/ppermute | solution.py:265
  5.4 7.8 %collective-permute-start = (bf16[64,512]{1,0:T(8,128)(2,1)S(1)}, bf16[64,512]{1,0:T(8,128)(2,1)S(1)}, u32[]{:S(2)}, u32[]{:S(2)}) collective-permute-start(bf16[64,512]{1,0:T(8,128)(2,1)S(1)} %get-tuple-element.33), channel_id=1, source_target_pairs={{0,8},{2,10},{4,12},{6,14},{8,0},{10,2},{12,4},{14,6},{1,9},{3,11}... | collective-permute-start | bytes 196616 | tf_op jit(solution)/shard_map/ppermute | solution.py:265
  8.0 9.8 %collective-permute-start.1 = (bf16[64,512]{1,0:T(8,128)(2,1)S(1)}, bf16[64,512]{1,0:T(8,128)(2,1)S(1)}, u32[]{:S(2)}, u32[]{:S(2)}) collective-permute-start(bf16[64,512]{1,0:T(8,128)(2,1)S(1)} %get-tuple-element.34), channel_id=1, source_target_pairs={{0,10},{2,8},{4,14},{6,12},{8,2},{10,0},{12,6},{14,4},{1,11},{3,9}... | collective-permute-start | bytes 196616 | tf_op jit(solution)/shard_map/ppermute | solution.py:265
  8.0 12.3 %collective-permute-start.5 = (bf16[64,512]{1,0:T(8,128)(2,1)S(1)}, bf16[64,512]{1,0:T(8,128)(2,1)S(1)}, u32[]{:S(2)}, u32[]{:S(2)}) collective-permute-start(bf16[64,512]{1,0:T(8,128)(2,1)S(1)} %get-tuple-element.43), channel_id=1, source_target_pairs={{0,12},{2,14},{4,8},{6,10},{8,4},{10,6},{12,0},{14,2},{1,13},{3,15... | collective-permute-start | bytes 196616 | tf_op jit(solution)/shard_map/ppermute | solution.py:265
  11.9 8.4 %collective-permute-start.6 = (bf16[64,512]{1,0:T(8,128)(2,1)S(1)}, bf16[64,512]{1,0:T(8,128)(2,1)S(1)}, u32[]{:S(2)}, u32[]{:S(2)}) collective-permute-start(bf16[64,512]{1,0:T(8,128)(2,1)S(1)} %get-tuple-element.44), channel_id=1, source_target_pairs={{0,14},{2,12},{4,10},{6,8},{8,6},{10,4},{12,2},{14,0},{1,15},{3,13... | collective-permute-start | bytes 196616 | tf_op jit(solution)/shard_map/ppermute | solution.py:265
  13.1 8.2 %collective-permute-start.3 = (bf16[64,1024]{1,0:T(8,128)(2,1)S(1)}, bf16[64,1024]{1,0:T(8,128)(2,1)S(1)}, u32[]{:S(2)}, u32[]{:S(2)}) collective-permute-start(bf16[64,1024]{1,0:T(8,128)(2,1)S(1)} %get-tuple-element.41), channel_id=1, source_target_pairs={{0,4},{2,6},{4,0},{6,2},{8,12},{10,14},{12,8},{14,10},{1,5},{3,7},... | collective-permute-start | bytes 393224 | tf_op jit(solution)/shard_map/ppermute | solution.py:265
  13.2 8.1 %collective-permute-start.4 = (bf16[64,512]{1,0:T(8,128)(2,1)S(1)}, bf16[64,512]{1,0:T(8,128)(2,1)S(1)}, u32[]{:S(2)}, u32[]{:S(2)}) collective-permute-start(bf16[64,512]{1,0:T(8,128)(2,1)S(1)} %get-tuple-element.42), channel_id=1, source_target_pairs={{0,6},{2,4},{4,2},{6,0},{8,14},{10,12},{12,10},{14,8},{1,7},{3,5},... | collective-permute-start | bytes 196616 | tf_op jit(solution)/shard_map/ppermute | solution.py:265
  21.6 2.8 %collective-permute-start.8 = (bf16[256,512]{1,0:T(8,128)(2,1)S(1)}, bf16[256,512]{1,0:T(8,128)(2,1)S(1)}, u32[]{:S(2)}, u32[]{:S(2)}) collective-permute-start(bf16[256,512]{1,0:T(8,128)(2,1)S(1)} %get-tuple-element.47.own), channel_id=1, source_target_pairs={{0,1},{1,0},{2,3},{3,2},{4,5},{5,4},{6,7},{7,6},{8,9},{9,8},{10,11... | collective-permute-start | bytes 786440 | tf_op jit(solution)/shard_map/ppermute | solution.py:271
  21.7 9.7 %collective-permute-start.7 = (bf16[128,512]{1,0:T(8,128)(2,1)S(1)}, bf16[128,512]{1,0:T(8,128)(2,1)S(1)}, u32[]{:S(2)}, u32[]{:S(2)}) collective-permute-start(bf16[128,512]{1,0:T(8,128)(2,1)S(1)} %get-tuple-element.45.near), channel_id=1, source_target_pairs={{0,8},{2,10},{4,12},{6,14},{8,0},{10,2},{12,4},{14,6},{1,9},{3,11}... | collective-permute-start | bytes 393224 | tf_op jit(solution)/shard_map/ppermute | solution.py:265
  25.0 10.6 %collective-permute-start.10 = (bf16[128,1280]{1,0:T(8,128)(2,1)S(1)}, bf16[128,1280]{1,0:T(8,128)(2,1)S(1)}, u32[]{:S(2)}, u32[]{:S(2)}) collective-permute-start(bf16[128,1280]{1,0:T(8,128)(2,1)S(1)} %get-tuple-element.51), channel_id=1, source_target_pairs={{0,2},{2,0},{4,6},{6,4},{8,10},{10,8},{12,14},{14,12},{1,3},{3,1},... | collective-permute-start | bytes 983048 | tf_op jit(solution)/shard_map/ppermute | solution.py:265
  27.2 25.7 %copy-start = (f32[2560]{0:T(1024)S(1)}, f32[2560]{0:T(1024)}, u32[]{:S(2)}) copy-start(f32[2560]{0:T(1024)} %param.17) | copy-start | bytes 30724
  27.2 11.1 %collective-permute-start.11 = (bf16[128,1280]{1,0:T(8,128)(2,1)S(1)}, bf16[128,1280]{1,0:T(8,128)(2,1)S(1)}, u32[]{:S(2)}, u32[]{:S(2)}) collective-permute-start(bf16[128,1280]{1,0:T(8,128)(2,1)S(1)} %get-tuple-element.49.after), channel_id=1, source_target_pairs={{0,4},{2,6},{4,0},{6,2},{8,12},{10,14},{12,8},{14,10},{1,5},{3,7},... | collective-permute-start | bytes 983048 | tf_op jit(solution)/shard_map/ppermute | solution.py:265
  31.4 8.6 %collective-permute-start.9 = (bf16[192,512]{1,0:T(8,128)(2,1)S(1)}, bf16[192,512]{1,0:T(8,128)(2,1)S(1)}, u32[]{:S(2)}, u32[]{:S(2)}) collective-permute-start(bf16[192,512]{1,0:T(8,128)(2,1)S(1)} %gather.1), channel_id=1, source_target_pairs={{0,2},{2,0},{4,6},{6,4},{8,10},{10,8},{12,14},{14,12},{1,3},{3,1},... | collective-permute-start | bytes 589832 | tf_op jit(solution)/shard_map/ppermute | solution.py:265
  38.4 7.1 %collective-permute-start.13 = (bf16[64,1280]{1,0:T(8,128)(2,1)S(1)}, bf16[64,1280]{1,0:T(8,128)(2,1)S(1)}, u32[]{:S(2)}, u32[]{:S(2)}) collective-permute-start(bf16[64,1280]{1,0:T(8,128)(2,1)S(1)} %get-tuple-element.57), channel_id=1, source_target_pairs={{0,2},{2,0},{4,6},{6,4},{8,10},{10,8},{12,14},{14,12},{1,3},{3,1},... | collective-permute-start | bytes 491528 | tf_op jit(solution)/shard_map/ppermute | solution.py:265
  40.0 5.8 %collective-permute-start.12 = (bf16[64,1280]{1,0:T(8,128)(2,1)S(1)}, bf16[64,1280]{1,0:T(8,128)(2,1)S(1)}, u32[]{:S(2)}, u32[]{:S(2)}) collective-permute-start(bf16[64,1280]{1,0:T(8,128)(2,1)S(1)} %get-tuple-element.56), channel_id=1, source_target_pairs={{0,4},{2,6},{4,0},{6,2},{8,12},{10,14},{12,8},{14,10},{1,5},{3,7},... | collective-permute-start | bytes 491528 | tf_op jit(solution)/shard_map/ppermute | solution.py:265
  42.0 6.3 %collective-permute-start.15 = (f32[2,64]{1,0:T(2,128)S(1)}, f32[2,64]{1,0:T(2,128)S(1)}, u32[]{:S(2)}, u32[]{:S(2)}) collective-permute-start(f32[2,64]{1,0:T(2,128)S(1)} %get-tuple-element.65), channel_id=1, source_target_pairs={{0,4},{2,6},{4,0},{6,2},{8,12},{10,14},{12,8},{14,10},{1,5},{3,7},... | collective-permute-start | bytes 1544 | tf_op jit(solution)/shard_map/ppermute | solution.py:265
  44.0 4.3 %collective-permute-start.16 = (f32[2,64]{1,0:T(2,128)S(1)}, f32[2,64]{1,0:T(2,128)S(1)}, u32[]{:S(2)}, u32[]{:S(2)}) collective-permute-start(f32[2,64]{1,0:T(2,128)S(1)} %get-tuple-element.64), channel_id=1, source_target_pairs={{0,2},{2,0},{4,6},{6,4},{8,10},{10,8},{12,14},{14,12},{1,3},{3,1},... | collective-permute-start | bytes 1544 | tf_op jit(solution)/shard_map/ppermute | solution.py:265
  45.4 4.5 %collective-permute-start.17 = (f32[2,64]{1,0:T(2,128)S(1)}, f32[2,64]{1,0:T(2,128)S(1)}, u32[]{:S(2)}, u32[]{:S(2)}) collective-permute-start(f32[2,64]{1,0:T(2,128)S(1)} %get-tuple-element.63), channel_id=1, source_target_pairs={{0,6},{2,4},{4,2},{6,0},{8,14},{10,12},{12,10},{14,8},{1,7},{3,5},... | collective-permute-start | bytes 1544 | tf_op jit(solution)/shard_map/ppermute | solution.py:265
  45.8 9.4 %collective-permute-start.14 = (bf16[32,2560]{1,0:T(8,128)(2,1)S(1)}, bf16[32,2560]{1,0:T(8,128)(2,1)S(1)}, u32[]{:S(2)}, u32[]{:S(2)}) collective-permute-start(bf16[32,2560]{1,0:T(8,128)(2,1)S(1)} %get-tuple-element.59), channel_id=1, source_target_pairs={{0,8},{2,10},{4,12},{6,14},{8,0},{10,2},{12,4},{14,6},{1,9},{3,11}... | collective-permute-start | bytes 491528 | tf_op jit(solution)/shard_map/ppermute | solution.py:265
  49.8 5.4 %collective-permute-start.18 = (f32[1,64]{1,0:T(1,128)S(1)}, f32[1,64]{1,0:T(1,128)S(1)}, u32[]{:S(2)}, u32[]{:S(2)}) collective-permute-start(f32[1,64]{1,0:T(1,128)S(1)} %get-tuple-element.67), channel_id=1, source_target_pairs={{0,8},{2,10},{4,12},{6,14},{8,0},{10,2},{12,4},{14,6},{1,9},{3,11}... | collective-permute-start | bytes 776 | tf_op jit(solution)/shard_map/ppermute | solution.py:265
  50.2 5.1 %collective-permute-start.19 = (f32[1,64]{1,0:T(1,128)S(1)}, f32[1,64]{1,0:T(1,128)S(1)}, u32[]{:S(2)}, u32[]{:S(2)}) collective-permute-start(f32[1,64]{1,0:T(1,128)S(1)} %get-tuple-element.68.refs_0_), channel_id=1, source_target_pairs={{0,1},{1,0},{2,3},{3,2},{4,5},{5,4},{6,7},{7,6},{8,9},{9,8},{10,11... | collective-permute-start | bytes 776 | tf_op jit(solution)/shard_map/ppermute | solution.py:271
  50.2 5.1 %collective-permute-start.20 = (f32[1,64]{1,0:T(1,128)S(1)}, f32[1,64]{1,0:T(1,128)S(1)}, u32[]{:S(2)}, u32[]{:S(2)}) collective-permute-start(f32[1,64]{1,0:T(1,128)S(1)} %get-tuple-element.67), channel_id=1, source_target_pairs={{0,9},{1,8},{2,11},{3,10},{4,13},{5,12},{6,15},{7,14},{8,1},{9,0},... | collective-permute-start | bytes 776 | tf_op jit(solution)/shard_map/ppermute | solution.py:268
